TPU v7x, 32 devices: a whole 2x2x4 slice. The times are simulated.
32 devices in a mesh: frow: 8 (over z, x), fcol: 4 (over y, core).
Axes of the slice: x: 2, y: 2, z: 4, core: 2. Of those that a mesh axis runs over, the one named last changes fastest.
Arguments:
- facets: float32 [2, 1024, 4096], P(None, 'frow', 'fcol'), may hold values from -6 to 6
- column_start: int32 [1], replicated, may hold values from 0 to 4095
- subgrid_start: int32 [8], replicated, may hold values from 0 to 1023
- vis_count: int32 [8], P('frow'), may hold values from 1 to 64
- vis_row: int32 [8, 64], P('frow'), may hold values from 0 to 511
- vis_weight: float32 [8, 64, 512], P('frow', None, 'fcol'), may hold values from -1 to 1
Outputs:
- corrected: float32 [8, 512, 2, 512], P('frow', 'fcol')
- facet_update: float32 [2, 1024, 4096], P(None, 'frow', 'fcol')
All inputs are finite; a program needn't handle non-finite values.
Results may differ from a plain program's by a relative error of at most 0.0003.
Values sent between devices are 32-bit elements; how exact they have to be, the bound alone decides.
No kernel may reach another device: no remote copies, remote signals or barrier semaphores. Data moves between devices by JAX's collectives and lax.ppermute only.
A program may use at most 64 MiB of HBM per device.

v0:
```python
import functools
import math

import jax
import jax.numpy as jnp
import ml_dtypes
import numpy as np
from jax import lax
from jax.experimental import pallas as pl
from jax.experimental.pallas import tpu as pltpu
from jax.sharding import PartitionSpec as P

SG = 512
MAXB = 64
META = 8

BF = jnp.bfloat16
F32 = jnp.float32
NN = (((1,), (0,)), ((), ()))
NT = (((1,), (1,)), ((), ()))


def halves(value):
    high = value.astype(BF)
    return high, (value - high.astype(F32)).astype(BF)


def dot3(left, right, dims):
    def dot(a, b):
        return lax.dot_general(a, b, dims, preferred_element_type=F32)
    return dot(left[0], right[0]) + (dot(left[0], right[1]) + dot(left[1], right[0]))


def unit(phase, modulus, scale=1.0):
    angle = (phase & (modulus - 1)).astype(F32) * F32(2.0 * math.pi / modulus)
    return jnp.cos(angle) * F32(scale), jnp.sin(angle) * F32(scale)


def lanes(count, rows=1):
    return lax.broadcasted_iota(jnp.int32, (rows, count), 1)


def to_column(row):
    return jnp.transpose(jnp.broadcast_to(row, (8, row.shape[1])))[:, 0:1]


def wave_table(rows, cols, modulus):
    phase = np.arange(rows, dtype=np.int64)[:, None] * np.arange(cols, dtype=np.int64)[None, :] % modulus
    angle = phase * (2.0 * np.pi / modulus)
    parts = np.stack([np.cos(angle), np.sin(angle)])
    high = parts.astype(ml_dtypes.bfloat16)
    low = (parts - high.astype(np.float64)).astype(ml_dtypes.bfloat16)
    return np.concatenate([high, low])


def strip_kernel(cols_total, info, x_ref, e_ref, turn_ref, out_ref, z_hi, z_lo):
    height, width = x_ref.shape[1:]
    count = e_ref.shape[2]

    @pl.when(pl.program_id(0) == 0)
    def _():
        pc, ps = unit(info[1] * (info[0] * width + lanes(width)), cols_total, 1.0 / math.sqrt(cols_total))
        re, im = x_ref[0], x_ref[1]
        z = jnp.concatenate([re * pc + im * ps, im * pc - re * ps])
        z_hi[...], z_lo[...] = halves(z)

    z = (z_hi[...], z_lo[...])
    e = (e_ref[0, 0:2].reshape(2 * count, width), e_ref[0, 2:4].reshape(2 * count, width))
    acc = dot3(e, z, NT)
    cos, sin = acc[:count], acc[count:]
    re = cos[:, :height] + sin[:, height:]
    im = cos[:, height:] - sin[:, :height]
    tc, ts = turn_ref[0, 0], turn_ref[0, 1]
    out_ref[0, 0] = re * tc + im * ts
    out_ref[0, 1] = im * tc - re * ts


def strips(info, facets, table, turn, parity, cols_total):
    blocks, _, count, width = table.shape
    height = facets.shape[1]
    half = blocks // 2
    block = lambda g, info: info[0] ^ (2 * g + parity)
    return pl.pallas_call(
        functools.partial(strip_kernel, cols_total),
        grid_spec=pltpu.PrefetchScalarGridSpec(
            num_scalar_prefetch=1,
            grid=(half,),
            in_specs=[
                pl.BlockSpec((2, height, width), lambda g, info: (0, 0, 0)),
                pl.BlockSpec((1, 4, count, width), lambda g, info: (block(g, info), 0, 0, 0)),
                pl.BlockSpec((1, 2, count, height), lambda g, info: (info[0], 0, block(g, info), 0)),
            ],
            out_specs=pl.BlockSpec((1, 2, count, height), lambda g, info: (g, 0, 0, 0)),
            scratch_shapes=[pltpu.VMEM((2 * height, width), BF)] * 2,
        ),
        out_shape=jax.ShapeDtypeStruct((half, 2, count, height), F32),
        compiler_params=pltpu.CompilerParams(vmem_limit_bytes=32 << 20),
        name="strips",
    )(info, facets, table, turn)


def add_message(info, r, s, message, b_ref, state, height, count, rows_total):
    mine = info[1]
    strip, rest = message[: 2 * count], message[2 * count :]
    pc, ps = unit(mine * (r * height + lanes(height)), rows_total, 1.0 / math.sqrt(rows_total))
    re, im = strip[:count], strip[count:]
    re, im = re * pc + im * ps, im * pc - re * ps
    left = halves(jnp.concatenate([jnp.concatenate([re, im], 1), jnp.concatenate([im, -re], 1)]))
    right = (b_ref[0:2].reshape(2 * height, rows_total), b_ref[2:4].reshape(2 * height, rows_total))
    part = dot3(left, right, NN)
    freq = lanes(rows_total)
    pc, ps = unit(freq * (r * height), rows_total)
    re, im = part[:count], part[count:]
    add_re, add_im = re * pc + im * ps, im * pc - re * ps

    width = message.shape[1]
    flat = jnp.concatenate([rest, jnp.zeros((width - rest.shape[0], width), F32)])
    turned = jnp.transpose(flat)
    weight = turned[:count, :MAXB]
    row = turned[:MAXB, MAXB : MAXB + 1].astype(jnp.int32)
    place = jnp.where(row < 0, -1, (row + (s - mine)) & (rows_total - 1))
    hot = (lanes(rows_total, MAXB) == place).astype(F32).astype(BF)
    gain = lax.dot_general(
        jnp.concatenate(halves(weight), 1), jnp.concatenate([hot, hot]), NN, preferred_element_type=F32
    )
    gain = gain + (((freq + (mine - s)) & (rows_total - 1)) < SG).astype(F32)
    if state is None:
        return add_re, add_im, gain
    return state[0] + add_re, state[1] + add_im, state[2] + gain


def gather_kernel(n_messages, first, height, count, rows_total, info, *refs):
    b_ref, refs = refs[0], refs[1:]
    state = None
    if not first:
        state, refs = (refs[0][0], refs[0][1], refs[0][2]), refs[1:]
    messages, out_ref = refs[:n_messages], refs[n_messages]
    for i in range(n_messages):
        state = add_message(info, info[2 + 2 * i], info[3 + 2 * i], messages[i][...], b_ref, state, height, count, rows_total)
    for i in range(3):
        out_ref[i] = state[i]


def gather_step(info, table, state, messages, count):
    height, rows_total = table.shape[1:]
    first = state is None
    operands = [table] + ([] if first else [state]) + list(messages)
    return pl.pallas_call(
        functools.partial(gather_kernel, len(messages), first, height, count, rows_total),
        in_specs=[pl.BlockSpec(memory_space=pltpu.SMEM)] + [pl.BlockSpec(memory_space=pltpu.VMEM)] * len(operands),
        out_specs=pl.BlockSpec(memory_space=pltpu.VMEM),
        out_shape=jax.ShapeDtypeStruct((3, count, rows_total), F32),
        compiler_params=pltpu.CompilerParams(vmem_limit_bytes=32 << 20),
        cost_estimate=pl.CostEstimate(flops=10**9, bytes_accessed=4 << 20, transcendentals=0),
        name="gather_step",
    )(info, *operands)


def back_kernel(height, count, rows_total, info, b_ref, state_ref, gain_ref, top_ref, bottom_ref, corrected_ref, back_ref):
    state = state_ref[0], state_ref[1], state_ref[2]
    message = jnp.concatenate([top_ref[...], bottom_ref[...]])
    re, im, gain = add_message(info, info[2], info[3], message, b_ref, state, height, count, rows_total)
    mine, r = info[1], info[0]
    corrected_ref[0] = re[:, :SG] * gain_ref[...]
    corrected_ref[1] = im[:, :SG] * gain_ref[...]
    re, im = re * gain, im * gain
    pc, ps = unit(lanes(rows_total) * (r * height), rows_total)
    both = halves(jnp.concatenate([re * pc - im * ps, im * pc + re * ps]))
    table = (b_ref[0:2].reshape(2 * height, rows_total), b_ref[2:4].reshape(2 * height, rows_total))
    acc = dot3(table, both, NT)
    re = acc[:height, :count] - acc[height:, count:]
    im = acc[:height, count:] + acc[height:, :count]
    pc, ps = unit(mine * (r * height + lanes(height)), rows_total, 1.0 / math.sqrt(rows_total))
    pc, ps = to_column(pc), to_column(ps)
    back_ref[0] = re * pc - im * ps
    back_ref[1] = im * pc + re * ps


def back_step(info, table, state, gain, halves_of, count):
    height, rows_total = table.shape[1:]
    vmem = pl.BlockSpec(memory_space=pltpu.VMEM)
    return pl.pallas_call(
        functools.partial(back_kernel, height, count, rows_total),
        in_specs=[pl.BlockSpec(memory_space=pltpu.SMEM)] + [vmem] * 5,
        out_specs=[vmem] * 2,
        out_shape=[
            jax.ShapeDtypeStruct((2, count, SG), F32),
            jax.ShapeDtypeStruct((2, height, count), F32),
        ],
        compiler_params=pltpu.CompilerParams(vmem_limit_bytes=32 << 20),
        name="back_step",
    )(info, table, state, gain, *halves_of)


def image_kernel(gs, first, last, cols_total, blocks, info, e_ref, *refs):
    backs, refs = refs[: len(gs)], refs[len(gs) :]
    if not first:
        acc_ref, refs = refs[0], refs[1:]
    out_ref, tables, sems = refs
    count, width = tables.shape[2:]
    height = out_ref.shape[1]
    own = info[0]
    copies = [pltpu.make_async_copy(e_ref.at[own ^ g], tables.at[i], sems.at[i]) for i, g in enumerate(gs)]
    for copy in copies:
        copy.start()
    acc = None if first else jnp.concatenate([acc_ref[0], acc_ref[1]])
    for i, g in enumerate(gs):
        freq = (own ^ g) * count + lanes(count)
        pc, ps = unit(freq * (own * (cols_total // blocks)), cols_total)
        re, im = backs[i][0], backs[i][1]
        re, im = re * pc - im * ps, im * pc + re * ps
        left = halves(jnp.concatenate([jnp.concatenate([re, -im], 1), jnp.concatenate([im, re], 1)]))
        copies[i].wait()
        right = (tables[i, 0:2].reshape(2 * count, width), tables[i, 2:4].reshape(2 * count, width))
        part = dot3(left, right, NN)
        acc = part if acc is None else acc + part
    re, im = acc[:height], acc[height:]
    if last:
        pc, ps = unit(info[1] * (own * width + lanes(width)), cols_total, 1.0 / math.sqrt(cols_total))
        re, im = re * pc - im * ps, im * pc + re * ps
    out_ref[0] = re
    out_ref[1] = im


def image_step(info, table, gs, backs, acc, last, cols_total):
    blocks, _, count, width = table.shape
    height = backs[0].shape[1]
    first = acc is None
    operands = list(backs) + ([] if first else [acc])
    vmem = pl.BlockSpec(memory_space=pltpu.VMEM)
    return pl.pallas_call(
        functools.partial(image_kernel, gs, first, last, cols_total, blocks),
        in_specs=[pl.BlockSpec(memory_space=pltpu.SMEM), pl.BlockSpec(memory_space=pl.ANY)] + [vmem] * len(operands),
        out_specs=vmem,
        out_shape=jax.ShapeDtypeStruct((2, height, width), F32),
        scratch_shapes=[pltpu.VMEM((len(gs), 4, count, width), BF), pltpu.SemaphoreType.DMA((len(gs),))],
        compiler_params=pltpu.CompilerParams(vmem_limit_bytes=32 << 20),
        cost_estimate=pl.CostEstimate(flops=10**9, bytes_accessed=4 << 20, transcendentals=0),
        name="image_step",
    )(info, table, *operands)


def swap(value, axis, bit):
    return lax.ppermute(value, axis, [(i, i ^ bit) for i in range(lax.axis_size(axis))])


def per_device(facets, column_start, subgrid_start, vis_count, vis_row, vis_weight):
    row = lax.axis_index("frow")
    col = lax.axis_index("fcol")
    rows = lax.axis_size("frow")
    cols = lax.axis_size("fcol")
    height, width = facets.shape[1:]
    rows_total, cols_total = height * rows, width * cols
    count = SG // cols
    assert vis_count.shape[0] == 1 and count <= height

    e_table = jnp.asarray(wave_table(SG, width, cols_total).reshape(4, cols, count, width).transpose(1, 0, 2, 3))
    b_table = jnp.asarray(wave_table(height, rows_total, rows_total))
    angle = np.arange(cols)[:, None] * np.arange(SG)[None, :] % cols * (2.0 * np.pi / cols)
    turn = np.stack([np.cos(angle), np.sin(angle)], 1).astype(np.float32)
    turn = jnp.asarray(np.broadcast_to(turn[..., None], turn.shape + (height,)).copy())

    info = jnp.stack([col, column_start[0]]).astype(jnp.int32)
    sent = strips(info, facets, e_table, turn, 1, cols_total)
    kept = strips(info, facets, e_table, turn, 0, cols_total)
    strip = kept + swap(sent, "fcol", 1)
    bit = 2
    while bit < cols:
        pairs = strip.reshape((-1, 2) + strip.shape[1:])
        strip = pairs[:, 0] + swap(pairs[:, 1], "fcol", bit)
        bit *= 2

    live = jnp.arange(MAXB, dtype=jnp.int32)[None, :] < vis_count[:, None]
    meta = jnp.where(live, vis_row, -1).astype(F32)
    meta = jnp.pad(meta, ((0, META - 1), (0, height - MAXB)))
    weights = jnp.pad(vis_weight[0], ((0, 0), (0, height - count)))
    own = jnp.concatenate([strip.reshape(2 * count, height), weights, meta])

    order = list(range(0, rows, 2)) + list(range(rows - 1, 0, -2))
    place = np.argsort(order)
    ahead = [(order[i], order[(i + 1) % rows]) for i in range(rows)]
    behind = [(b, a) for a, b in ahead]
    order_array, place_array = jnp.asarray(order, jnp.int32), jnp.asarray(place, jnp.int32)
    at = place_array[row]
    mine = subgrid_start[row]

    def facts(*steps):
        found = [row.astype(jnp.int32), mine]
        for step in steps:
            source = order_array[(at + step) % rows]
            found += [source, subgrid_start[source]]
        return jnp.stack(found)

    state = gather_step(facts(0), b_table, None, [own], count)
    gain = state[2, :, :SG]
    up = down = own
    for step in range(1, rows // 2):
        up = lax.ppermute(up, "frow", ahead)
        down = lax.ppermute(down, "frow", behind)
        state = gather_step(facts(-step, step), b_table, state, [up, down], count)
    cut = (own.shape[0] // 2 + 7) // 8 * 8
    top = lax.ppermute(up[:cut], "frow", ahead)
    bottom = lax.ppermute(down[cut:], "frow", behind)
    corrected, back = back_step(facts(rows // 2), b_table, state, gain, [top, bottom], count)

    near, far = [back], None
    bit = 1
    far = [swap(back, "fcol", cols // 2)]
    while bit < cols // 2:
        near += [swap(b, "fcol", bit) for b in near]
        far += [swap(b, "fcol", bit) for b in far]
        bit *= 2
    acc = image_step(info, e_table, tuple(range(cols // 2)), near, None, False, cols_total)
    update = image_step(info, e_table, tuple(range(cols // 2, cols)), far, acc, True, cols_total)
    return jnp.transpose(corrected, (1, 0, 2))[None], update


def solution(mesh):
    return jax.shard_map(
        per_device,
        mesh=mesh,
        in_specs=(
            P(None, "frow", "fcol"),
            P(),
            P(),
            P("frow"),
            P("frow", None),
            P("frow", None, "fcol"),
        ),
        out_specs=(P("frow", "fcol", None, None), P(None, "frow", "fcol")),
        check_vma=False,
    )
```

profile of v0, /device:TPU:0, one launch (start us, length us, event | category | flops | bytes accessed | tf_op | source)
XLA Modules:
  0.0 89.4 jit_solution(8151056122908347736)
XLA Ops:
  1.3 0.1 pad_add_fusion.3.info
  1.4 0.0 copy-start
  1.4 2.2 %copy-done = bf16[4,4,128,1024]{3,2,1,0:T(8,128)(2,1)S(1)} copy-done((bf16[4,4,128,1024]{3,2,1,0:T(8,128)(2,1)S(1)}, bf16[4,4,128,1024]{3,2,1,0:T(8,128)(2,1)}, u32[]{:S(2)}) %copy-start) | copy-done | bytes 4194328
  3.5 0.0 copy-start.3
  3.5 1.6 %copy-done.3 = f32[4,2,512,128]{3,2,1,0:T(8,128)S(1)} copy-done((f32[4,2,512,128]{3,2,1,0:T(8,128)S(1)}, f32[4,2,512,128]{3,2,1,0:T(8,128)}, u32[]{:S(2)}) %copy-start.3) | copy-done | bytes 2097176
  5.1 0.0 copy-start.4
  5.1 1.2 %copy-done.4 = f32[2,128,1024]{2,1,0:T(8,128)S(1)} copy-done((f32[2,128,1024]{2,1,0:T(8,128)S(1)}, f32[2,128,1024]{2,1,0:T(8,128)}, u32[]{:S(2)}) %copy-start.4) | copy-done | bytes 1048600
  6.4 2.2 %strips.3 = f32[2,2,128,128]{3,2,1,0:T(8,128)S(1)} custom-call(s32[2]{0:T(128)S(1)} %pad_add_fusion.3.info, f32[2,128,1024]{2,1,0:T(8,128)S(1)} %copy-done.4, bf16[4,4,128,1024]{3,2,1,0:T(8,128)(2,1)S(1)} %copy-done, f32[4,2,512,128]{3,2,1,0:T(8,128)S(1)} %copy-done.3), custom_call_target="tpu_custom_call" | custom-call | tf_op jit(solution)/shard_map/strips/pallas_call | solution.py:83
  8.6 0.0 copy-start.8
  8.6 0.0 copy-start.9
  8.6 0.0 copy-start.6
  8.6 0.0 copy-start.5
  8.7 0.5 collective-permute-start
  9.2 2.2 %strips.2 = f32[2,2,128,128]{3,2,1,0:T(8,128)S(1)} custom-call(s32[2]{0:T(128)S(1)} %pad_add_fusion.3.info, f32[2,128,1024]{2,1,0:T(8,128)S(1)} %copy-done.4, bf16[4,4,128,1024]{3,2,1,0:T(8,128)(2,1)S(1)} %copy-done, f32[4,2,512,128]{3,2,1,0:T(8,128)S(1)} %copy-done.3), custom_call_target="tpu_custom_call" | custom-call | tf_op jit(solution)/shard_map/strips/pallas_call | solution.py:83
  11.4 0.0 copy-start.7
  11.4 0.0 copy-start.2
  12.2 0.0 collective-permute-done
  12.2 2.6 %collective-permute-start.1 = (f32[1,2,128,128]{3,2,1,0:T(8,128)S(1)}, f32[1,2,128,128]{3,2,1,0:T(8,128)S(1)}, u32[]{:S(2)}, u32[]{:S(2)}) collective-permute-start(f32[1,2,128,128]{3,2,1,0:T(8,128)S(1)} %slice_bitcast_fusion.1), channel_id=1, source_target_pairs={{0,2},{1,3},{2,0},{3,1},{4,6},{5,7},{6,4},{7,5},{8,10},{9,11},{10,... | collective-permute-start | bytes 393224 | tf_op jit(solution)/shard_map/ppermute | solution.py:244
  14.8 0.0 copy-done.8
  14.8 0.0 copy-done.9
  14.8 0.6 dynamic_slice.55
  22.1 0.0 copy-done.6
  22.1 0.7 fusion.3
  38.4 0.0 copy-done.5
  38.4 0.7 fusion.2
  39.1 3.3 %stack.32.info = s32[6]{0:T(128)S(1)} concatenate(s32[1]{0:T(128)} %bitcast, s32[1]{0:T(128)} %get-tuple-element.15, s32[1]{0:T(128)} %get-tuple-element.18, s32[1]{0:T(128)} %get-tuple-element.9, s32[1]{0:T(128)} %get-tuple-element.24, s32[1]{0:T(128)} %get-tuple-element.16), dimensions={0} | concatenate | bytes 48 | tf_op jit(solution)/shard_map/stack | solution.py:292
  42.3 3.3 %stack.31.info = s32[6]{0:T(128)S(1)} concatenate(s32[1]{0:T(128)} %bitcast, s32[1]{0:T(128)} %get-tuple-element.15, s32[1]{0:T(128)} %get-tuple-element.20, s32[1]{0:T(128)} %get-tuple-element.11, s32[1]{0:T(128)} %get-tuple-element.19, s32[1]{0:T(128)} %get-tuple-element.10), dimensions={0} | concatenate | bytes 48 | tf_op jit(solution)/shard_map/stack | solution.py:292
  45.6 3.2 %stack.30.info = s32[6]{0:T(128)S(1)} concatenate(s32[1]{0:T(128)} %bitcast, s32[1]{0:T(128)} %get-tuple-element.15, s32[1]{0:T(128)} %get-tuple-element.22, s32[1]{0:T(128)} %get-tuple-element.13, s32[1]{0:T(128)} %get-tuple-element.21, s32[1]{0:T(128)} %get-tuple-element.12), dimensions={0} | concatenate | bytes 48 | tf_op jit(solution)/shard_map/stack | solution.py:292
  48.8 2.0 %pad_add_fusion.2.info = s32[4]{0:T(128)S(1)} fusion(s32[1]{0:T(128)} %get-tuple-element.8, s32[1]{0:T(128)} %get-tuple-element.17, s32[1]{0:T(128)} %get-tuple-element.15, s32[1]{0:T(128)} %bitcast), kind=kLoop, calls=%fused_computation.11 | loop fusion | flops 12 | bytes 32 | tf_op jit(solution)/shard_map/stack | solution.py:292
  50.8 0.0 collective-permute-done.1
  50.8 0.0 copy-done.7
  50.8 1.5 %collective-permute-start.3 = (f32[328,128]{1,0:T(8,128)S(1)}, f32[328,128]{1,0:T(8,128)S(1)}, u32[]{:S(2)}, u32[]{:S(2)}) collective-permute-start(f32[328,128]{1,0:T(8,128)S(1)} %select_maximum_fusion.refs_1_), channel_id=1, source_target_pairs={{8,0},{16,8},{24,16},{28,24},{20,28},{12,20},{4,12},{0,4},{9,1},{1... | collective-permute-start | bytes 503816 | tf_op jit(solution)/shard_map/ppermute | solution.py:299
  52.4 0.5 collective-permute-start.2
  52.9 2.0 %pad_add_fusion.info = s32[4]{0:T(128)S(1)} fusion(s32[1]{0:T(128)} %get-tuple-element.14, s32[1]{0:T(128)} %get-tuple-element.23, s32[1]{0:T(128)} %get-tuple-element.15, s32[1]{0:T(128)} %bitcast), kind=kLoop, calls=%fused_computation.9 | loop fusion | flops 12 | bytes 32 | tf_op jit(solution)/shard_map/stack | solution.py:292
  54.9 0.0 copy-done.2
  54.9 1.3 %gather_step.4.refs_1_ = f32[3,128,1024]{2,1,0:T(8,128)S(1)} custom-call(s32[4]{0:T(128)S(1)} %pad_add_fusion.2.info, bf16[4,128,1024]{2,1,0:T(8,128)(2,1)S(1)} %copy-done.2, f32[328,128]{1,0:T(8,128)S(1)} %select_maximum_fusion.refs_1_), custom_call_target="tpu_custom_call" | custom-call | flops 1000000000 | bytes 4194304 | tf_op jit(solution)/shard_map/gather_step/pallas_call | solution.py:148
  56.1 1.1 %collective-permute-done.3.refs_3_ = f32[328,128]{1,0:T(8,128)S(1)} collective-permute-done((f32[328,128]{1,0:T(8,128)S(1)}, f32[328,128]{1,0:T(8,128)S(1)}, u32[]{:S(2)}, u32[]{:S(2)}) %collective-permute-start.3) | collective-permute-done | bytes 167968 | tf_op jit(solution)/shard_map/ppermute | solution.py:299
  57.3 1.5 %collective-permute-start.5 = (f32[328,128]{1,0:T(8,128)S(1)}, f32[328,128]{1,0:T(8,128)S(1)}, u32[]{:S(2)}, u32[]{:S(2)}) collective-permute-start(f32[328,128]{1,0:T(8,128)S(1)} %collective-permute-done.3.refs_3_), channel_id=1, source_target_pairs={{8,0},{16,8},{24,16},{28,24},{20,28},{12,20},{4,12},{0,4},{9,1},{1... | collective-permute-start | bytes 503816 | tf_op jit(solution)/shard_map/ppermute | solution.py:299
  58.8 0.0 collective-permute-done.2.refs_2_
  58.8 0.5 collective-permute-start.4
  59.3 3.5 %collective-permute-done.5.refs_3_ = f32[328,128]{1,0:T(8,128)S(1)} collective-permute-done((f32[328,128]{1,0:T(8,128)S(1)}, f32[328,128]{1,0:T(8,128)S(1)}, u32[]{:S(2)}, u32[]{:S(2)}) %collective-permute-start.5) | collective-permute-done | bytes 167968 | tf_op jit(solution)/shard_map/ppermute | solution.py:299
  62.9 1.5 %collective-permute-start.7 = (f32[328,128]{1,0:T(8,128)S(1)}, f32[328,128]{1,0:T(8,128)S(1)}, u32[]{:S(2)}, u32[]{:S(2)}) collective-permute-start(f32[328,128]{1,0:T(8,128)S(1)} %collective-permute-done.5.refs_3_), channel_id=1, source_target_pairs={{8,0},{16,8},{24,16},{28,24},{20,28},{12,20},{4,12},{0,4},{9,1},{1... | collective-permute-start | bytes 503816 | tf_op jit(solution)/shard_map/ppermute | solution.py:299
  64.4 0.0 collective-permute-done.4.refs_2_
  64.4 0.5 collective-permute-start.6
  64.9 2.1 %gather_step.5.refs_1_ = f32[3,128,1024]{2,1,0:T(8,128)S(1)} custom-call(s32[6]{0:T(128)S(1)} %stack.32.info, bf16[4,128,1024]{2,1,0:T(8,128)(2,1)S(1)} %copy-done.2, f32[3,128,1024]{2,1,0:T(8,128)S(1)} %gather_step.4.refs_1_, f32[328,128]{1,0:T(8,128)S(1)} %collective-permute-done.2.refs_2_, f32[328,128]{1,0:T(8,128)S(1)} %collective-permute-done.3.refs_3_), custom_call_target="tpu_custom_call" | custom-call | flops 1000000000 | bytes 4194304 | tf_op jit(solution)/shard_map/gather_step/pallas_call | solution.py:148
  67.0 2.1 %gather_step.6.refs_1_ = f32[3,128,1024]{2,1,0:T(8,128)S(1)} custom-call(s32[6]{0:T(128)S(1)} %stack.31.info, bf16[4,128,1024]{2,1,0:T(8,128)(2,1)S(1)} %copy-done.2, f32[3,128,1024]{2,1,0:T(8,128)S(1)} %gather_step.5.refs_1_, f32[328,128]{1,0:T(8,128)S(1)} %collective-permute-done.4.refs_2_, f32[328,128]{1,0:T(8,128)S(1)} %collective-permute-done.5.refs_3_), custom_call_target="tpu_custom_call" | custom-call | flops 1000000000 | bytes 4194304 | tf_op jit(solution)/shard_map/gather_step/pallas_call | solution.py:148
  69.1 0.0 collective-permute-done.7.refs_3_
  69.1 1.6 %collective-permute-start.9 = (f32[160,128]{1,0:T(8,128)S(1)}, f32[160,128]{1,0:T(8,128)S(1)}, u32[]{:S(2)}, u32[]{:S(2)}) collective-permute-start(f32[160,128]{1,0:T(8,128)S(1)} %slice.24), channel_id=1, source_target_pairs={{8,0},{16,8},{24,16},{28,24},{20,28},{12,20},{4,12},{0,4},{9,1},{1... | collective-permute-start | bytes 245768 | tf_op jit(solution)/shard_map/ppermute | solution.py:303
  70.7 0.0 collective-permute-done.6.refs_2_
  70.7 0.7 collective-permute-start.8
  71.5 2.1 %gather_step.7.state_ref = f32[3,128,1024]{2,1,0:T(8,128)S(1)} custom-call(s32[6]{0:T(128)S(1)} %stack.30.info, bf16[4,128,1024]{2,1,0:T(8,128)(2,1)S(1)} %copy-done.2, f32[3,128,1024]{2,1,0:T(8,128)S(1)} %gather_step.6.refs_1_, f32[328,128]{1,0:T(8,128)S(1)} %collective-permute-done.6.refs_2_, f32[328,128]{1,0:T(8,128)S(1)} %collective-permute-done.7.refs_3_), custom_call_target="tpu_custom_call" | custom-call | flops 1000000000 | bytes 4194304 | tf_op jit(solution)/shard_map/gather_step/pallas_call | solution.py:148
  73.6 0.0 collective-permute-done.9.bottom_ref
  73.6 1.8 %collective-permute-done.8.top_ref = f32[168,128]{1,0:T(8,128)S(1)} collective-permute-done((f32[168,128]{1,0:T(8,128)S(1)}, f32[168,128]{1,0:T(8,128)S(1)}, u32[]{:S(2)}, u32[]{:S(2)}) %collective-permute-start.8) | collective-permute-done | bytes 86048 | tf_op jit(solution)/shard_map/ppermute | solution.py:302
  75.5 2.7 %back_step.1 = (f32[2,128,512]{2,1,0:T(8,128)S(1)}, f32[2,128,128]{2,1,0:T(8,128)S(1)}) custom-call(s32[4]{0:T(128)S(1)} %pad_add_fusion.info, bf16[4,128,1024]{2,1,0:T(8,128)(2,1)S(1)} %copy-done.2, f32[3,128,1024]{2,1,0:T(8,128)S(1)} %gather_step.7.state_ref, f32[128,512]{1,0:T(8,128)S(1)} %slice_bitcast_fusion.gain_ref, ...), custom_call_target="tpu_custom_call" | custom-call | tf_op jit(solution)/shard_map/back_step/pallas_call | solution.py:182
  78.2 0.6 collective-permute-start.10
  78.8 0.0 collective-permute-start.12
  78.8 4.5 %collective-permute-done.10.refs_0_ = f32[2,128,128]{2,1,0:T(8,128)S(1)} collective-permute-done((f32[2,128,128]{2,1,0:T(8,128)S(1)}, f32[2,128,128]{2,1,0:T(8,128)S(1)}, u32[]{:S(2)}, u32[]{:S(2)}) %collective-permute-start.10) | collective-permute-done | bytes 131104 | tf_op jit(solution)/shard_map/ppermute | solution.py:244
  83.2 0.0 collective-permute-start.11
  83.2 1.2 %copy.13 = f32[1,128,2,512]{3,2,1,0:T(2,128)} copy(f32[1,128,2,512]{3,1,2,0:T(8,128)S(1)} %bitcast.28) | data formatting | bytes 1048576
  84.4 0.0 collective-permute-done.12.refs_1_
  84.4 0.0 copy-done.1
  84.4 1.8 %image_step.2.refs_2_ = f32[2,128,1024]{2,1,0:T(8,128)S(1)} custom-call(s32[2]{0:T(128)S(1)} %pad_add_fusion.3.info, bf16[4,4,128,1024]{3,2,1,0:T(8,128)(2,1)S(1)} %copy-done.1, f32[2,128,128]{2,1,0:T(8,128)S(1)} %get-tuple-element.5.refs_0_, f32[2,128,128]{2,1,0:T(8,128)S(1)} %collective-permute-done.12.refs_1_), custom_call_target="tpu_custom_call" | custom-call | flops 1000000000 | bytes 4194304 | tf_op jit(solution)/shard_map/image_step/pallas_call | solution.py:231
  86.3 0.0 collective-permute-done.11.refs_1_
  86.3 2.9 %image_step.3 = f32[2,128,1024]{2,1,0:T(8,128)} custom-call(s32[2]{0:T(128)S(1)} %pad_add_fusion.3.info, bf16[4,4,128,1024]{3,2,1,0:T(8,128)(2,1)S(1)} %copy-done.1, f32[2,128,128]{2,1,0:T(8,128)S(1)} %collective-permute-done.10.refs_0_, f32[2,128,128]{2,1,0:T(8,128)S(1)} %collective-permute-done.11.refs_1_, f32[2,128,1024]{2,1,0:T(8,128)S(1)} %image_step.2.refs_2_), custom_call_target="tpu_custom_call" | custom-call | flops 1000000000 | bytes 4194304 | tf_op jit(solution)/shard_map/image_step/pallas_call | solution.py:231
  (9 shorter events, 0.1 us)
Async XLA Ops:
  1.4 2.2 %copy-start = (bf16[4,4,128,1024]{3,2,1,0:T(8,128)(2,1)S(1)}, bf16[4,4,128,1024]{3,2,1,0:T(8,128)(2,1)}, u32[]{:S(2)}) copy-start(bf16[4,4,128,1024]{3,2,1,0:T(8,128)(2,1)} %constant.77.clone.e_ref) | copy-start | bytes 12582916
  3.5 1.6 %copy-start.3 = (f32[4,2,512,128]{3,2,1,0:T(8,128)S(1)}, f32[4,2,512,128]{3,2,1,0:T(8,128)}, u32[]{:S(2)}) copy-start(f32[4,2,512,128]{3,2,1,0:T(8,128)} %constant.79.clone.turn_ref) | copy-start | bytes 6291460
  5.1 1.2 %copy-start.4 = (f32[2,128,1024]{2,1,0:T(8,128)S(1)}, f32[2,128,1024]{2,1,0:T(8,128)}, u32[]{:S(2)}) copy-start(f32[2,128,1024]{2,1,0:T(8,128)} %x_ref.3) | copy-start | bytes 3145732
  8.6 6.2 %copy-start.8 = (s32[1,64]{1,0:T(1,128)S(1)}, s32[1,64]{1,0:T(1,128)}, u32[]{:S(2)}) copy-start(s32[1,64]{1,0:T(1,128)} %param.15) | copy-start | bytes 772
  8.6 6.2 %copy-start.9 = (s32[8]{0:T(128)S(1)}, s32[8]{0:T(128)}, u32[]{:S(2)}) copy-start(s32[8]{0:T(128)} %constant.81.clone) | copy-start | bytes 100
  8.6 13.4 %copy-start.6 = (s32[8]{0:T(128)S(1)}, s32[8]{0:T(128)}, u32[]{:S(2)}) copy-start(s32[8]{0:T(128)} %constant.80.clone) | copy-start | bytes 100
  8.6 29.7 %copy-start.5 = (s32[8]{0:T(128)S(1)}, s32[8]{0:T(128)}, u32[]{:S(2)}) copy-start(s32[8]{0:T(128)} %param.13) | copy-start | bytes 100
  8.7 3.5 %collective-permute-start = (f32[2,2,128,128]{3,2,1,0:T(8,128)S(1)}, f32[2,2,128,128]{3,2,1,0:T(8,128)S(1)}, u32[]{:S(2)}, u32[]{:S(2)}) collective-permute-start(f32[2,2,128,128]{3,2,1,0:T(8,128)S(1)} %strips.3), channel_id=1, source_target_pairs={{0,1},{1,0},{2,3},{3,2},{4,5},{5,4},{6,7},{7,6},{8,9},{9,8},{10,11... | collective-permute-start | bytes 786440 | tf_op jit(solution)/shard_map/ppermute | solution.py:244
  11.4 39.4 %copy-start.7 = (f32[1,64,128]{2,1,0:T(8,128)S(1)}, f32[1,64,128]{2,1,0:T(8,128)}, u32[]{:S(2)}) copy-start(f32[1,64,128]{2,1,0:T(8,128)} %param.16) | copy-start | bytes 98308
  11.4 43.5 %copy-start.2 = (bf16[4,128,1024]{2,1,0:T(8,128)(2,1)S(1)}, bf16[4,128,1024]{2,1,0:T(8,128)(2,1)}, u32[]{:S(2)}) copy-start(bf16[4,128,1024]{2,1,0:T(8,128)(2,1)} %constant.78.clone.refs_0_.b_ref) | copy-start | bytes 3145732
  12.2 38.5 %collective-permute-start.1 = (f32[1,2,128,128]{3,2,1,0:T(8,128)S(1)}, f32[1,2,128,128]{3,2,1,0:T(8,128)S(1)}, u32[]{:S(2)}, u32[]{:S(2)}) collective-permute-start(f32[1,2,128,128]{3,2,1,0:T(8,128)S(1)} %slice_bitcast_fusion.1), channel_id=1, source_target_pairs={{0,2},{1,3},{2,0},{3,1},{4,6},{5,7},{6,4},{7,5},{8,10},{9,11},{10,... | collective-permute-start | bytes 393224 | tf_op jit(solution)/shard_map/ppermute | solution.py:244
  50.8 6.5 %collective-permute-start.3 = (f32[328,128]{1,0:T(8,128)S(1)}, f32[328,128]{1,0:T(8,128)S(1)}, u32[]{:S(2)}, u32[]{:S(2)}) collective-permute-start(f32[328,128]{1,0:T(8,128)S(1)} %select_maximum_fusion.refs_1_), channel_id=1, source_target_pairs={{8,0},{16,8},{24,16},{28,24},{20,28},{12,20},{4,12},{0,4},{9,1},{1... | collective-permute-start | bytes 503816 | tf_op jit(solution)/shard_map/ppermute | solution.py:299
  52.4 6.4 %collective-permute-start.2 = (f32[328,128]{1,0:T(8,128)S(1)}, f32[328,128]{1,0:T(8,128)S(1)}, u32[]{:S(2)}, u32[]{:S(2)}) collective-permute-start(f32[328,128]{1,0:T(8,128)S(1)} %select_maximum_fusion.refs_1_), channel_id=1, source_target_pairs={{0,8},{8,16},{16,24},{24,28},{28,20},{20,12},{12,4},{4,0},{1,9},{9... | collective-permute-start | bytes 503816 | tf_op jit(solution)/shard_map/ppermute | solution.py:298
  57.3 5.6 %collective-permute-start.5 = (f32[328,128]{1,0:T(8,128)S(1)}, f32[328,128]{1,0:T(8,128)S(1)}, u32[]{:S(2)}, u32[]{:S(2)}) collective-permute-start(f32[328,128]{1,0:T(8,128)S(1)} %collective-permute-done.3.refs_3_), channel_id=1, source_target_pairs={{8,0},{16,8},{24,16},{28,24},{20,28},{12,20},{4,12},{0,4},{9,1},{1... | collective-permute-start | bytes 503816 | tf_op jit(solution)/shard_map/ppermute | solution.py:299
  58.8 5.6 %collective-permute-start.4 = (f32[328,128]{1,0:T(8,128)S(1)}, f32[328,128]{1,0:T(8,128)S(1)}, u32[]{:S(2)}, u32[]{:S(2)}) collective-permute-start(f32[328,128]{1,0:T(8,128)S(1)} %collective-permute-done.2.refs_2_), channel_id=1, source_target_pairs={{0,8},{8,16},{16,24},{24,28},{28,20},{20,12},{12,4},{4,0},{1,9},{9... | collective-permute-start | bytes 503816 | tf_op jit(solution)/shard_map/ppermute | solution.py:298
  62.9 6.3 %collective-permute-start.7 = (f32[328,128]{1,0:T(8,128)S(1)}, f32[328,128]{1,0:T(8,128)S(1)}, u32[]{:S(2)}, u32[]{:S(2)}) collective-permute-start(f32[328,128]{1,0:T(8,128)S(1)} %collective-permute-done.5.refs_3_), channel_id=1, source_target_pairs={{8,0},{16,8},{24,16},{28,24},{20,28},{12,20},{4,12},{0,4},{9,1},{1... | collective-permute-start | bytes 503816 | tf_op jit(solution)/shard_map/ppermute | solution.py:299
  64.4 6.4 %collective-permute-start.6 = (f32[328,128]{1,0:T(8,128)S(1)}, f32[328,128]{1,0:T(8,128)S(1)}, u32[]{:S(2)}, u32[]{:S(2)}) collective-permute-start(f32[328,128]{1,0:T(8,128)S(1)} %collective-permute-done.4.refs_2_), channel_id=1, source_target_pairs={{0,8},{8,16},{16,24},{24,28},{28,20},{20,12},{12,4},{4,0},{1,9},{9... | collective-permute-start | bytes 503816 | tf_op jit(solution)/shard_map/ppermute | solution.py:298
  69.1 4.5 %collective-permute-start.9 = (f32[160,128]{1,0:T(8,128)S(1)}, f32[160,128]{1,0:T(8,128)S(1)}, u32[]{:S(2)}, u32[]{:S(2)}) collective-permute-start(f32[160,128]{1,0:T(8,128)S(1)} %slice.24), channel_id=1, source_target_pairs={{8,0},{16,8},{24,16},{28,24},{20,28},{12,20},{4,12},{0,4},{9,1},{1... | collective-permute-start | bytes 245768 | tf_op jit(solution)/shard_map/ppermute | solution.py:303
  70.7 4.7 %collective-permute-start.8 = (f32[168,128]{1,0:T(8,128)S(1)}, f32[168,128]{1,0:T(8,128)S(1)}, u32[]{:S(2)}, u32[]{:S(2)}) collective-permute-start(f32[168,128]{1,0:T(8,128)S(1)} %slice.23), channel_id=1, source_target_pairs={{0,8},{8,16},{16,24},{24,28},{28,20},{20,12},{12,4},{4,0},{1,9},{9... | collective-permute-start | bytes 258056 | tf_op jit(solution)/shard_map/ppermute | solution.py:302
  71.5 13.0 %copy-start.1 = (bf16[4,4,128,1024]{3,2,1,0:T(8,128)(2,1)S(1)}, bf16[4,4,128,1024]{3,2,1,0:T(8,128)(2,1)}, u32[]{:S(2)}) copy-start(bf16[4,4,128,1024]{3,2,1,0:T(8,128)(2,1)} %constant.77.clone.e_ref) | copy-start | bytes 12582916
  78.2 5.0 %collective-permute-start.10 = (f32[2,128,128]{2,1,0:T(8,128)S(1)}, f32[2,128,128]{2,1,0:T(8,128)S(1)}, u32[]{:S(2)}, u32[]{:S(2)}) collective-permute-start(f32[2,128,128]{2,1,0:T(8,128)S(1)} %get-tuple-element.5.refs_0_), channel_id=1, source_target_pairs={{0,2},{1,3},{2,0},{3,1},{4,6},{5,7},{6,4},{7,5},{8,10},{9,11},{10,... | collective-permute-start | bytes 393224 | tf_op jit(solution)/shard_map/ppermute | solution.py:244
  78.8 5.7 %collective-permute-start.12 = (f32[2,128,128]{2,1,0:T(8,128)S(1)}, f32[2,128,128]{2,1,0:T(8,128)S(1)}, u32[]{:S(2)}, u32[]{:S(2)}) collective-permute-start(f32[2,128,128]{2,1,0:T(8,128)S(1)} %get-tuple-element.5.refs_0_), channel_id=1, source_target_pairs={{0,1},{1,0},{2,3},{3,2},{4,5},{5,4},{6,7},{7,6},{8,9},{9,8},{10,11... | collective-permute-start | bytes 393224 | tf_op jit(solution)/shard_map/ppermute | solution.py:244
  83.2 3.1 %collective-permute-start.11 = (f32[2,128,128]{2,1,0:T(8,128)S(1)}, f32[2,128,128]{2,1,0:T(8,128)S(1)}, u32[]{:S(2)}, u32[]{:S(2)}) collective-permute-start(f32[2,128,128]{2,1,0:T(8,128)S(1)} %collective-permute-done.10.refs_0_), channel_id=1, source_target_pairs={{0,1},{1,0},{2,3},{3,2},{4,5},{5,4},{6,7},{7,6},{8,9},{9,8},{10,11... | collective-permute-start | bytes 393224 | tf_op jit(solution)/shard_map/ppermute | solution.py:244
where the time goes:
time: 90.2 us; the launch traced here: 89.4 us
  between operations  24.6 us (27%)
  Pallas kernels  19.5 us (22%)
  local copies, waits for them, and re-layouts  18 us (20%)
  starting transfers between devices  12.1 us (13%)
  waiting for transfers between devices  11 us (12%)
  other arithmetic  4.07 us (5%)
    another operation x3, local copies, waits for them, and re-layouts, facts(): return jnp.stack(found)  9.72 us
    pallas_call x4, Pallas kernels, gather_step(): pl.pallas_call(functools.partial(gather_kernel, len(messages), first, hei...  7.61 us
    unnamed x21, local copies, waits for them, and re-layouts  6.24 us
    pallas_call x2, Pallas kernels, image_step(): pl.pallas_call(functools.partial(image_kernel, gs, first, last, cols_tota...  4.75 us
    ppermute x3, waiting for transfers between devices, per_device(): down = lax.ppermute(down, 'frow', behind)  4.66 us
    ppermute x3, starting transfers between devices, per_device(): down = lax.ppermute(down, 'frow', behind)  4.54 us
    ppermute x5, waiting for transfers between devices, swap(): lax.ppermute(value, axis, [(i, i ^ bit) for i in range(lax.axis_size(axis...  4.47 us
    pallas_call x2, Pallas kernels, strips(): pl.pallas_call(functools.partial(strip_kernel, cols_total), grid_spec=plt...  4.45 us
  transfers between devices with their start and end apart: 13, of which 4 were waited for; matrix products, arithmetic and copies ran while one was open for 19% of the time, Pallas kernels for 13%

commit v1 on v0

v1 whole, which is shorter than its diff:
```python
import functools
import math

import jax
import jax.numpy as jnp
import ml_dtypes
import numpy as np
from jax import lax
from jax.experimental import pallas as pl
from jax.experimental.pallas import tpu as pltpu
from jax.sharding import PartitionSpec as P

SG = 512
MAXB = 64
META = 8

BF = jnp.bfloat16
F32 = jnp.float32
NN = (((1,), (0,)), ((), ()))
NT = (((1,), (1,)), ((), ()))
VMEM = pl.BlockSpec(memory_space=pltpu.VMEM)
SMEM = pl.BlockSpec(memory_space=pltpu.SMEM)
HBM = pl.BlockSpec(memory_space=pltpu.HBM)
LIMIT = pltpu.CompilerParams(vmem_limit_bytes=32 << 20)


def halves(value):
    high = value.astype(BF)
    return high, (value - high.astype(F32)).astype(BF)


def dot3(left, right, dims):
    def dot(a, b):
        return lax.dot_general(a, b, dims, preferred_element_type=F32)
    return dot(left[0], right[0]) + (dot(left[0], right[1]) + dot(left[1], right[0]))


def unit(phase, modulus, scale=1.0):
    angle = (phase & (modulus - 1)).astype(F32) * F32(2.0 * math.pi / modulus)
    return jnp.cos(angle) * F32(scale), jnp.sin(angle) * F32(scale)


def lanes(count, rows=1):
    return lax.broadcasted_iota(jnp.int32, (rows, count), 1)


def to_column(row):
    return jnp.transpose(jnp.broadcast_to(row, (8, row.shape[1])))[:, 0:1]


def wave_table(rows, cols, modulus):
    phase = np.arange(rows, dtype=np.int64)[:, None] * np.arange(cols, dtype=np.int64)[None, :] % modulus
    angle = phase * (2.0 * np.pi / modulus)
    parts = np.stack([np.cos(angle), np.sin(angle)])
    high = parts.astype(ml_dtypes.bfloat16)
    low = (parts - high.astype(np.float64)).astype(ml_dtypes.bfloat16)
    return np.concatenate([high, low])


def ring_place(r, rows):
    return jnp.where(lax.rem(r, 2) == 0, r // 2, rows - 1 - r // 2)


def ring_block(place, rows):
    place = lax.rem(place + rows, rows)
    return jnp.where(place < rows // 2, 2 * place, 2 * (rows - 1 - place) + 1)


def strip_kernel(gs, cols_total, start_ref, x_ref, e_ref, out_ref, tables, sems):
    height, width = x_ref.shape[1:]
    count = tables.shape[2]
    own = lax.axis_index("fcol")
    copies = [pltpu.make_async_copy(e_ref.at[own ^ g], tables.at[i], sems.at[i]) for i, g in enumerate(gs)]
    for copy in copies:
        copy.start()
    pc, ps = unit(start_ref[0] * (own * width + lanes(width)), cols_total, 1.0 / math.sqrt(cols_total))
    re, im = x_ref[0], x_ref[1]
    z = halves(jnp.concatenate([re * pc + im * ps, im * pc - re * ps]))
    for i, g in enumerate(gs):
        tc, ts = unit(((own ^ g) * count + lanes(count)) * (own * width), cols_total)
        tc, ts = to_column(tc), to_column(ts)
        copies[i].wait()
        e = (tables[i, 0:2].reshape(2 * count, width), tables[i, 2:4].reshape(2 * count, width))
        acc = dot3(e, z, NT)
        cos, sin = acc[:count], acc[count:]
        re = cos[:, :height] + sin[:, height:]
        im = cos[:, height:] - sin[:, :height]
        out_ref[i, 0] = re * tc + im * ts
        out_ref[i, 1] = im * tc - re * ts


def strips(column_start, facets, table, gs, cols_total):
    _, _, count, width = table.shape
    height = facets.shape[1]
    return pl.pallas_call(
        functools.partial(strip_kernel, gs, cols_total),
        in_specs=[SMEM, VMEM, HBM],
        out_specs=VMEM,
        out_shape=jax.ShapeDtypeStruct((len(gs), 2, count, height), F32),
        scratch_shapes=[pltpu.VMEM((len(gs), 4, count, width), BF), pltpu.SemaphoreType.DMA((len(gs),))],
        compiler_params=LIMIT,
        name="strips",
    )(column_start, facets, table)


def add_message(starts, r, message, b_ref, roots_ref, state, height, count, rows_total):
    mine, other = starts[lax.axis_index("frow")], starts[r]
    strip, rest = message[: 2 * count], message[2 * count :]
    pc, ps = unit(mine * (r * height + lanes(height)), rows_total, 1.0 / math.sqrt(rows_total))
    re, im = strip[:count], strip[count:]
    re, im = re * pc + im * ps, im * pc - re * ps
    high, low = halves(jnp.concatenate([jnp.concatenate([re, im], 1), jnp.concatenate([im, -re], 1)]))
    part = lax.dot_general(
        jnp.concatenate([high, low, high], 1), b_ref[...].reshape(6 * height, rows_total), NN, preferred_element_type=F32
    )
    freq = lanes(rows_total)
    pc, ps = roots_ref[r, 0:1], roots_ref[r, 1:2]
    re, im = part[:count], part[count:]
    add_re, add_im = re * pc + im * ps, im * pc - re * ps

    width = message.shape[1]
    flat = jnp.concatenate([rest, jnp.zeros((width - rest.shape[0], width), F32)])
    turned = jnp.transpose(flat)
    weight = turned[:count, :MAXB]
    row = turned[:MAXB, MAXB : MAXB + 1].astype(jnp.int32)
    place = jnp.where(row < 0, -1, (row + (other - mine)) & (rows_total - 1))
    hot = (lanes(rows_total, MAXB) == place).astype(F32).astype(BF)
    gain = lax.dot_general(
        jnp.concatenate(halves(weight), 1), jnp.concatenate([hot, hot]), NN, preferred_element_type=F32
    )
    gain = gain + (((freq + (mine - other)) & (rows_total - 1)) < SG).astype(F32)
    if state is None:
        return add_re, add_im, gain
    return state[0] + add_re, state[1] + add_im, state[2] + gain


def gather_kernel(steps, rows, height, count, starts, b_ref, roots_ref, *refs):
    state = None
    if len(refs) > len(steps) + 1:
        state, refs = (refs[0][0], refs[0][1], refs[0][2]), refs[1:]
    at = ring_place(lax.axis_index("frow"), rows)
    for step, message in zip(steps, refs):
        r = ring_block(at + step, rows)
        state = add_message(starts, r, message[...], b_ref, roots_ref, state, height, count, rows * height)
    for i in range(3):
        refs[-1][i] = state[i]


def gather_step(starts, table, roots, state, messages, steps, count):
    height, rows_total = table.shape[1:]
    operands = [table, roots] + ([] if state is None else [state]) + list(messages)
    return pl.pallas_call(
        functools.partial(gather_kernel, steps, rows_total // height, height, count),
        in_specs=[SMEM] + [VMEM] * len(operands),
        out_specs=VMEM,
        out_shape=jax.ShapeDtypeStruct((3, count, rows_total), F32),
        compiler_params=LIMIT,
        cost_estimate=pl.CostEstimate(flops=10**9, bytes_accessed=4 << 20, transcendentals=0),
        name="gather_step",
    )(starts, *operands)


def back_kernel(rows, height, count, starts, b_ref, roots_ref, state_ref, top_ref, bottom_ref, back_ref, sub_ref):
    state = state_ref[0], state_ref[1], state_ref[2]
    message = jnp.concatenate([top_ref[...], bottom_ref[...]])
    rows_total = rows * height
    own = lax.axis_index("frow")
    r = ring_block(ring_place(own, rows) + rows // 2, rows)
    re, im, gain = add_message(starts, r, message, b_ref, roots_ref, state, height, count, rows_total)
    sub_ref[0] = re[:, :SG]
    sub_ref[1] = im[:, :SG]
    re, im = re * gain, im * gain
    pc, ps = roots_ref[own, 0:1], roots_ref[own, 1:2]
    both = halves(jnp.concatenate([re * pc - im * ps, im * pc + re * ps]))
    table = (b_ref[0:2].reshape(2 * height, rows_total), b_ref[4:6].reshape(2 * height, rows_total))
    acc = dot3(table, both, NT)
    re = acc[:height, :count] - acc[height:, count:]
    im = acc[:height, count:] + acc[height:, :count]
    pc, ps = unit(starts[own] * (own * height + lanes(height)), rows_total, 1.0 / math.sqrt(rows_total))
    pc, ps = to_column(pc), to_column(ps)
    back_ref[0] = re * pc - im * ps
    back_ref[1] = im * pc + re * ps


def back_step(starts, table, roots, state, parts, count):
    height, rows_total = table.shape[1:]
    return pl.pallas_call(
        functools.partial(back_kernel, rows_total // height, height, count),
        in_specs=[SMEM] + [VMEM] * 5,
        out_specs=[VMEM] * 2,
        out_shape=[
            jax.ShapeDtypeStruct((2, height, count), F32),
            jax.ShapeDtypeStruct((2, count, SG), F32),
        ],
        compiler_params=LIMIT,
        name="back_step",
    )(starts, table, roots, state, *parts)


def correct_kernel(sub_ref, gain_ref, out_ref):
    count = sub_ref.shape[1]
    pieces = SG // 128
    for part in range(2):
        value = sub_ref[part] * gain_ref[2, :, :SG]
        for i in range(pieces):
            out_ref[pl.ds(2 * i + part, count, stride=2 * pieces), :] = value[:, 128 * i : 128 * (i + 1)]


def correct_step(sub, first_state):
    count = sub.shape[1]
    out = pl.pallas_call(
        correct_kernel,
        in_specs=[VMEM] * 2,
        out_specs=VMEM,
        out_shape=jax.ShapeDtypeStruct((count * 2 * SG // 128, 128), F32),
        compiler_params=LIMIT,
        cost_estimate=pl.CostEstimate(flops=10**9, bytes_accessed=4 << 20, transcendentals=0),
        name="correct_step",
    )(sub, first_state)
    out = out.reshape(count, SG // 128, 2, 128)
    return jnp.transpose(out, (0, 2, 1, 3)).reshape(1, count, 2, SG)


def image_kernel(gs, cols_total, blocks, start_ref, e_ref, *refs):
    backs, refs = refs[: len(gs)], refs[len(gs) :]
    out_ref = refs[-1]
    _, height, width = out_ref.shape
    count = e_ref.shape[2]
    own = lax.axis_index("fcol")
    last = len(refs) > 1
    acc = jnp.concatenate([refs[0][0], refs[0][1]]) if last else None
    for back, g in zip(backs, gs):
        freq = (own ^ g) * count + lanes(count)
        pc, ps = unit(freq * (own * width), cols_total)
        re, im = back[0], back[1]
        re, im = re * pc - im * ps, im * pc + re * ps
        left = halves(jnp.concatenate([jnp.concatenate([re, -im], 1), jnp.concatenate([im, re], 1)]))
        right = (e_ref[own ^ g, 0:2].reshape(2 * count, width), e_ref[own ^ g, 2:4].reshape(2 * count, width))
        part = dot3(left, right, NN)
        acc = part if acc is None else acc + part
    re, im = acc[:height], acc[height:]
    if last:
        pc, ps = unit(start_ref[0] * (own * width + lanes(width)), cols_total, 1.0 / math.sqrt(cols_total))
        re, im = re * pc - im * ps, im * pc + re * ps
    out_ref[0] = re
    out_ref[1] = im


def image_step(column_start, table, gs, backs, acc, cols_total):
    blocks, _, _, width = table.shape
    height = backs[0].shape[1]
    operands = list(backs) + ([] if acc is None else [acc])
    return pl.pallas_call(
        functools.partial(image_kernel, gs, cols_total, blocks),
        in_specs=[SMEM] + [VMEM] * (1 + len(operands)),
        out_specs=VMEM,
        out_shape=jax.ShapeDtypeStruct((2, height, width), F32),
        compiler_params=LIMIT,
        cost_estimate=pl.CostEstimate(flops=10**9, bytes_accessed=4 << 20, transcendentals=0),
        name="image_step",
    )(column_start, table, *operands)


def swap(value, axis, bit):
    return lax.ppermute(value, axis, [(i, i ^ bit) for i in range(lax.axis_size(axis))])


def per_device(facets, column_start, subgrid_start, vis_count, vis_row, vis_weight):
    rows = lax.axis_size("frow")
    cols = lax.axis_size("fcol")
    height, width = facets.shape[1:]
    rows_total, cols_total = height * rows, width * cols
    count = SG // cols
    assert vis_count.shape[0] == 1 and count <= height

    e_table = jnp.asarray(wave_table(SG, width, cols_total).reshape(4, cols, count, width).transpose(1, 0, 2, 3))
    b_table = wave_table(height, rows_total, rows_total)
    b_table = jnp.asarray(np.concatenate([b_table[:2], b_table]))
    angle = np.arange(rows)[:, None] * np.arange(rows_total)[None, :] % rows * (2.0 * np.pi / rows)
    roots = jnp.asarray(np.stack([np.cos(angle), np.sin(angle)], 1).astype(np.float32))

    sent = strips(column_start, facets, e_table, tuple(range(1, cols, 2)), cols_total)
    kept = strips(column_start, facets, e_table, tuple(range(0, cols, 2)), cols_total)
    strip = kept + swap(sent, "fcol", 1)
    bit = 2
    while bit < cols:
        pairs = strip.reshape((-1, 2) + strip.shape[1:])
        strip = pairs[:, 0] + swap(pairs[:, 1], "fcol", bit)
        bit *= 2

    live = jnp.arange(MAXB, dtype=jnp.int32)[None, :] < vis_count[:, None]
    meta = jnp.where(live, vis_row, -1).astype(F32)
    meta = jnp.pad(meta, ((0, META - 1), (0, height - MAXB)))
    weights = jnp.pad(vis_weight[0], ((0, 0), (0, height - count)))
    own = jnp.concatenate([strip.reshape(2 * count, height), weights, meta])

    order = list(range(0, rows, 2)) + list(range(rows - 1, 0, -2))
    ahead = [(order[i], order[(i + 1) % rows]) for i in range(rows)]
    behind = [(b, a) for a, b in ahead]
    first_state = state = gather_step(subgrid_start, b_table, roots, None, [own], (0,), count)
    up = down = own
    for step in range(1, rows // 2):
        up = lax.ppermute(up, "frow", ahead)
        down = lax.ppermute(down, "frow", behind)
        state = gather_step(subgrid_start, b_table, roots, state, [up, down], (-step, step), count)
    cut = (own.shape[0] // 2 + 7) // 8 * 8
    top = lax.ppermute(up[:cut], "frow", ahead)
    bottom = lax.ppermute(down[cut:], "frow", behind)
    back, sub = back_step(subgrid_start, b_table, roots, state, [top, bottom], count)

    near, far = [back], [swap(back, "fcol", cols // 2)]
    bit = 1
    while bit < cols // 2:
        near += [swap(b, "fcol", bit) for b in near]
        bit *= 2
    acc = image_step(column_start, e_table, tuple(range(cols // 2)), near, None, cols_total)
    corrected = correct_step(sub, first_state)
    far[0], acc, corrected = lax.optimization_barrier((far[0], acc, corrected))
    bit = 1
    while bit < cols // 2:
        far += [swap(b, "fcol", bit) for b in far]
        bit *= 2
    update = image_step(column_start, e_table, tuple(range(cols // 2, cols)), far, acc, cols_total)
    return corrected, update


def solution(mesh):
    return jax.shard_map(
        per_device,
        mesh=mesh,
        in_specs=(
            P(None, "frow", "fcol"),
            P(),
            P(),
            P("frow"),
            P("frow", None),
            P("frow", None, "fcol"),
        ),
        out_specs=(P("frow", "fcol", None, None), P(None, "frow", "fcol")),
        check_vma=False,
    )
```

time: 90.2 us -> 54.4 us (0.60)
  between operations: 24.6 us -> 2.24 us
  local copies, waits for them, and re-layouts: 18 us -> 3.47 us
  waiting for transfers between devices: 11 us -> 16 us
  other arithmetic: 4.07 us -> 0.07 us
  starting transfers between devices: 12.1 us -> 13.2 us
    another operation x3 -> x0, local copies, waits for them, and re-layouts: 9.72 us -> none  [facts(): return jnp.stack(found)]
    ppermute x3, waiting for transfers between devices: 0.01 us -> 6.14 us  [per_device(): up = lax.ppermute(up, 'frow', ahead)]
    ppermute x3, waiting for transfers between devices: 4.66 us -> 0.01 us  [per_device(): down = lax.ppermute(down, 'frow', behind)]
    another operation x3 -> x0, other arithmetic: 4.01 us -> none  [the longest x2 3.93 us: facts(): return jnp.stack(found)]
    ppermute x3, starting transfers between devices: 4.54 us -> 1.11 us  [per_device(): down = lax.ppermute(down, 'frow', behind)]
    ppermute x3, starting transfers between devices: 1.59 us -> 5.02 us  [per_device(): up = lax.ppermute(up, 'frow', ahead)]
    ppermute x5, waiting for transfers between devices: 4.47 us -> 7.85 us  [swap(): lax.ppermute(value, axis, [(i, i ^ bit) for i in range(lax.axis_size(axis...]
    unnamed x21 -> x16, local copies, waits for them, and re-layouts: 6.24 us -> 3.44 us
  transfers between devices with their start and end apart: 13 -> 13, of which waited for: 4 -> 6; matrix products, arithmetic and copies ran while one was open for 19% -> 0% of each run, Pallas kernels for 13% -> 22%
where the time goes in v1:
time: 54.4 us; the launch traced here: 54.2 us
  Pallas kernels  19.2 us (35%)
  waiting for transfers between devices  16 us (29%)
  starting transfers between devices  13.2 us (24%)
  local copies, waits for them, and re-layouts  3.47 us (6%)
  between operations  2.24 us (4%)
    ppermute x5, waiting for transfers between devices, swap(): lax.ppermute(value, axis, [(i, i ^ bit) for i in range(lax.axis_size(axis...  7.85 us
    pallas_call x4, Pallas kernels, gather_step(): pl.pallas_call(functools.partial(gather_kernel, steps, rows_total // heig...  7.08 us
    ppermute x3, waiting for transfers between devices, per_device(): up = lax.ppermute(up, 'frow', ahead)  6.14 us
    pallas_call x2, Pallas kernels, strips(): pl.pallas_call(functools.partial(strip_kernel, gs, cols_total), in_specs=...  5.52 us
    ppermute x3, starting transfers between devices, per_device(): up = lax.ppermute(up, 'frow', ahead)  5.02 us
    ppermute x5, starting transfers between devices, swap(): lax.ppermute(value, axis, [(i, i ^ bit) for i in range(lax.axis_size(axis...  4.79 us
    unnamed x16, local copies, waits for them, and re-layouts  3.44 us
    pallas_call x2, Pallas kernels, image_step(): pl.pallas_call(functools.partial(image_kernel, gs, cols_total, blocks), i...  3.01 us
  transfers between devices with their start and end apart: 13, of which 6 were waited for; matrix products, arithmetic and copies ran while one was open for 0% of the time, Pallas kernels for 22%

profile of v1, /device:TPU:0, one launch (start us, length us, event | category | flops | bytes accessed | tf_op | source)
XLA Modules:
  0.0 54.2 jit_solution(6003062825594496429)
XLA Ops:
  1.3 0.0 copy-start
  1.3 2.2 %copy-done = bf16[4,4,128,1024]{3,2,1,0:T(8,128)(2,1)S(1)} copy-done((bf16[4,4,128,1024]{3,2,1,0:T(8,128)(2,1)S(1)}, bf16[4,4,128,1024]{3,2,1,0:T(8,128)(2,1)}, u32[]{:S(2)}) %copy-start) | copy-done | bytes 4194328
  3.5 0.0 copy-start.3
  3.5 1.2 %copy-done.3 = f32[2,128,1024]{2,1,0:T(8,128)S(1)} copy-done((f32[2,128,1024]{2,1,0:T(8,128)S(1)}, f32[2,128,1024]{2,1,0:T(8,128)}, u32[]{:S(2)}) %copy-start.3) | copy-done | bytes 1048600
  4.7 2.8 %strips.3 = f32[2,2,128,128]{3,2,1,0:T(8,128)S(1)} custom-call(s32[1]{0:T(128)S(6)} %copy.12.start_ref, f32[2,128,1024]{2,1,0:T(8,128)S(1)} %copy-done.3, bf16[4,4,128,1024]{3,2,1,0:T(8,128)(2,1)S(1)} %copy-done), custom_call_target="tpu_custom_call" | custom-call | tf_op jit(solution)/shard_map/strips/pallas_call | solution.py:95
  7.5 0.0 copy-start.7
  7.5 0.0 copy-start.6
  7.5 0.5 collective-permute-start
  8.0 2.8 %strips.2 = f32[2,2,128,128]{3,2,1,0:T(8,128)S(1)} custom-call(s32[1]{0:T(128)S(6)} %copy.12.start_ref, f32[2,128,1024]{2,1,0:T(8,128)S(1)} %copy-done.3, bf16[4,4,128,1024]{3,2,1,0:T(8,128)(2,1)S(1)} %copy-done), custom_call_target="tpu_custom_call" | custom-call | tf_op jit(solution)/shard_map/strips/pallas_call | solution.py:95
  10.8 0.0 copy-start.2
  10.8 0.0 copy-start.4
  10.8 0.0 copy-start.5
  11.6 0.0 collective-permute-done
  11.6 2.6 %collective-permute-start.1 = (f32[1,2,128,128]{3,2,1,0:T(8,128)S(1)}, f32[1,2,128,128]{3,2,1,0:T(8,128)S(1)}, u32[]{:S(2)}, u32[]{:S(2)}) collective-permute-start(f32[1,2,128,128]{3,2,1,0:T(8,128)S(1)} %slice_bitcast_fusion), channel_id=1, source_target_pairs={{0,2},{1,3},{2,0},{3,1},{4,6},{5,7},{6,4},{7,5},{8,10},{9,11},{10,... | collective-permute-start | bytes 393224 | tf_op jit(solution)/shard_map/ppermute | solution.py:265
  14.2 0.0 copy-done.7
  14.3 4.1 %collective-permute-done.1 = f32[1,2,128,128]{3,2,1,0:T(8,128)S(1)} collective-permute-done((f32[1,2,128,128]{3,2,1,0:T(8,128)S(1)}, f32[1,2,128,128]{3,2,1,0:T(8,128)S(1)}, u32[]{:S(2)}, u32[]{:S(2)}) %collective-permute-start.1) | collective-permute-done | bytes 131104 | tf_op jit(solution)/shard_map/ppermute | solution.py:265
  18.4 0.0 copy-done.6
  18.4 1.8 %collective-permute-start.2 = (f32[328,128]{1,0:T(8,128)S(1)}, f32[328,128]{1,0:T(8,128)S(1)}, u32[]{:S(2)}, u32[]{:S(2)}) collective-permute-start(f32[328,128]{1,0:T(8,128)S(1)} %select_maximum_fusion.refs_0_), channel_id=1, source_target_pairs={{0,8},{8,16},{16,24},{24,28},{28,20},{20,12},{12,4},{4,0},{1,9},{9... | collective-permute-start | bytes 503816 | tf_op jit(solution)/shard_map/ppermute | solution.py:303
  20.3 0.2 collective-permute-start.3
  20.5 4.1 %collective-permute-done.2.refs_1_ = f32[328,128]{1,0:T(8,128)S(1)} collective-permute-done((f32[328,128]{1,0:T(8,128)S(1)}, f32[328,128]{1,0:T(8,128)S(1)}, u32[]{:S(2)}, u32[]{:S(2)}) %collective-permute-start.2) | collective-permute-done | bytes 167968 | tf_op jit(solution)/shard_map/ppermute | solution.py:303
  24.6 1.6 %collective-permute-start.4 = (f32[328,128]{1,0:T(8,128)S(1)}, f32[328,128]{1,0:T(8,128)S(1)}, u32[]{:S(2)}, u32[]{:S(2)}) collective-permute-start(f32[328,128]{1,0:T(8,128)S(1)} %collective-permute-done.2.refs_1_), channel_id=1, source_target_pairs={{0,8},{8,16},{16,24},{24,28},{28,20},{20,12},{12,4},{4,0},{1,9},{9... | collective-permute-start | bytes 503816 | tf_op jit(solution)/shard_map/ppermute | solution.py:303
  26.2 0.0 collective-permute-done.3.refs_2_
  26.2 0.4 collective-permute-start.5
  26.6 0.0 copy-done.2
  26.6 0.0 copy-done.4
  26.6 0.0 copy-done.5
  26.6 1.3 %gather_step.4.refs_0_.gain_ref = f32[3,128,1024]{2,1,0:T(8,128)S(1)} custom-call(s32[8]{0:T(128)S(1)} %copy-done.5, bf16[6,128,1024]{2,1,0:T(8,128)(2,1)S(1)} %copy-done.2, f32[8,2,1024]{2,1,0:T(2,128)S(1)} %copy-done.4, f32[328,128]{1,0:T(8,128)S(1)} %select_maximum_fusion.refs_0_), custom_call_target="tpu_custom_call" | custom-call | flops 1000000000 | bytes 4194304 | tf_op jit(solution)/shard_map/gather_step/pallas_call | solution.py:152
  27.9 2.1 %collective-permute-done.4.refs_1_ = f32[328,128]{1,0:T(8,128)S(1)} collective-permute-done((f32[328,128]{1,0:T(8,128)S(1)}, f32[328,128]{1,0:T(8,128)S(1)}, u32[]{:S(2)}, u32[]{:S(2)}) %collective-permute-start.4) | collective-permute-done | bytes 167968 | tf_op jit(solution)/shard_map/ppermute | solution.py:303
  30.0 1.6 %collective-permute-start.6 = (f32[328,128]{1,0:T(8,128)S(1)}, f32[328,128]{1,0:T(8,128)S(1)}, u32[]{:S(2)}, u32[]{:S(2)}) collective-permute-start(f32[328,128]{1,0:T(8,128)S(1)} %collective-permute-done.4.refs_1_), channel_id=1, source_target_pairs={{0,8},{8,16},{16,24},{24,28},{28,20},{20,12},{12,4},{4,0},{1,9},{9... | collective-permute-start | bytes 503816 | tf_op jit(solution)/shard_map/ppermute | solution.py:303
  31.5 0.0 collective-permute-done.5.refs_2_
  31.6 0.4 collective-permute-start.7
  32.0 1.9 %gather_step.5.refs_0_ = f32[3,128,1024]{2,1,0:T(8,128)S(1)} custom-call(s32[8]{0:T(128)S(1)} %copy-done.5, bf16[6,128,1024]{2,1,0:T(8,128)(2,1)S(1)} %copy-done.2, f32[8,2,1024]{2,1,0:T(2,128)S(1)} %copy-done.4, f32[3,128,1024]{2,1,0:T(8,128)S(1)} %gather_step.4.refs_0_.gain_ref, f32[328,128]{1,0:T(8,128)S(1)} %collective-permute-done.2.refs_1_, ...), custom_call_target="tpu_custom_call" | custom-call | flops 1000000000 | bytes 4194304 | tf_op jit(solution)/shard_map/gather_step/pallas_call | solution.py:152
  33.9 2.0 %gather_step.6.refs_0_ = f32[3,128,1024]{2,1,0:T(8,128)S(1)} custom-call(s32[8]{0:T(128)S(1)} %copy-done.5, bf16[6,128,1024]{2,1,0:T(8,128)(2,1)S(1)} %copy-done.2, f32[8,2,1024]{2,1,0:T(2,128)S(1)} %copy-done.4, f32[3,128,1024]{2,1,0:T(8,128)S(1)} %gather_step.5.refs_0_, f32[328,128]{1,0:T(8,128)S(1)} %collective-permute-done.4.refs_1_, ...), custom_call_target="tpu_custom_call" | custom-call | flops 1000000000 | bytes 4194304 | tf_op jit(solution)/shard_map/gather_step/pallas_call | solution.py:152
  35.9 0.0 collective-permute-done.6.refs_1_
  35.9 1.6 %collective-permute-start.8 = (f32[168,128]{1,0:T(8,128)S(1)}, f32[168,128]{1,0:T(8,128)S(1)}, u32[]{:S(2)}, u32[]{:S(2)}) collective-permute-start(f32[168,128]{1,0:T(8,128)S(1)} %slice.18), channel_id=1, source_target_pairs={{0,8},{8,16},{16,24},{24,28},{28,20},{20,12},{12,4},{4,0},{1,9},{9... | collective-permute-start | bytes 258056 | tf_op jit(solution)/shard_map/ppermute | solution.py:307
  37.6 0.0 collective-permute-done.7.refs_2_
  37.6 0.7 %collective-permute-start.9 = (f32[160,128]{1,0:T(8,128)S(1)}, f32[160,128]{1,0:T(8,128)S(1)}, u32[]{:S(2)}, u32[]{:S(2)}) collective-permute-start(f32[160,128]{1,0:T(8,128)S(1)} %slice.19), channel_id=1, source_target_pairs={{8,0},{16,8},{24,16},{28,24},{20,28},{12,20},{4,12},{0,4},{9,1},{1... | collective-permute-start | bytes 245768 | tf_op jit(solution)/shard_map/ppermute | solution.py:308
  38.2 2.0 %gather_step.7.state_ref = f32[3,128,1024]{2,1,0:T(8,128)S(1)} custom-call(s32[8]{0:T(128)S(1)} %copy-done.5, bf16[6,128,1024]{2,1,0:T(8,128)(2,1)S(1)} %copy-done.2, f32[8,2,1024]{2,1,0:T(2,128)S(1)} %copy-done.4, f32[3,128,1024]{2,1,0:T(8,128)S(1)} %gather_step.6.refs_0_, f32[328,128]{1,0:T(8,128)S(1)} %collective-permute-done.6.refs_1_, ...), custom_call_target="tpu_custom_call" | custom-call | flops 1000000000 | bytes 4194304 | tf_op jit(solution)/shard_map/gather_step/pallas_call | solution.py:152
  40.2 2.0 %collective-permute-done.9.bottom_ref = f32[160,128]{1,0:T(8,128)S(1)} collective-permute-done((f32[160,128]{1,0:T(8,128)S(1)}, f32[160,128]{1,0:T(8,128)S(1)}, u32[]{:S(2)}, u32[]{:S(2)}) %collective-permute-start.9) | collective-permute-done | bytes 81952 | tf_op jit(solution)/shard_map/ppermute | solution.py:308
  42.2 0.0 collective-permute-done.8.top_ref
  42.2 0.0 copy-start.1
  42.2 2.6 %back_step.1 = (f32[2,128,128]{2,1,0:T(8,128)S(1)}, f32[2,128,512]{2,1,0:T(8,128)S(1)}) custom-call(s32[8]{0:T(128)S(1)} %copy-done.5, bf16[6,128,1024]{2,1,0:T(8,128)(2,1)S(1)} %copy-done.2, f32[8,2,1024]{2,1,0:T(2,128)S(1)} %copy-done.4, f32[3,128,1024]{2,1,0:T(8,128)S(1)} %gather_step.7.state_ref, f32[168,128]{1,0:T(8,128)S(1)} %collective-permute-done.8.top_ref, ...), custom_call_target="tpu_custom_call" | custom-call | tf_op jit(solution)/shard_map/back_step/pallas_call | solution.py:187
  44.9 0.1 collective-permute-start.11
  45.0 1.6 %collective-permute-start.10 = (f32[2,128,128]{2,1,0:T(8,128)S(1)}, f32[2,128,128]{2,1,0:T(8,128)S(1)}, u32[]{:S(2)}, u32[]{:S(2)}) collective-permute-start(f32[2,128,128]{2,1,0:T(8,128)S(1)} %get-tuple-element.7.refs_0_), channel_id=1, source_target_pairs={{0,2},{1,3},{2,0},{3,1},{4,6},{5,7},{6,4},{7,5},{8,10},{9,11},{10,... | collective-permute-start | bytes 393224 | tf_op jit(solution)/shard_map/ppermute | solution.py:265
  46.5 0.9 %correct_step.1 = f32[1024,128]{1,0:T(8,128)} custom-call(f32[2,128,512]{2,1,0:T(8,128)S(1)} %get-tuple-element.8.sub_ref, f32[3,128,1024]{2,1,0:T(8,128)S(1)} %gather_step.4.refs_0_.gain_ref), custom_call_target="tpu_custom_call" | custom-call | flops 1000000000 | bytes 4194304 | tf_op jit(solution)/shard_map/correct_step/pallas_call | solution.py:211
  47.5 0.0 collective-permute-done.11.refs_1_
  47.5 0.0 copy-done.1
  47.5 1.0 %image_step.2.refs_2_ = f32[2,128,1024]{2,1,0:T(8,128)S(1)} custom-call(s32[1]{0:T(128)S(6)} %copy.12.start_ref, bf16[4,4,128,1024]{3,2,1,0:T(8,128)(2,1)S(1)} %copy-done.1, f32[2,128,128]{2,1,0:T(8,128)S(1)} %get-tuple-element.7.refs_0_, f32[2,128,128]{2,1,0:T(8,128)S(1)} %collective-permute-done.11.refs_1_), custom_call_target="tpu_custom_call" | custom-call | flops 1000000000 | bytes 4194304 | tf_op jit(solution)/shard_map/image_step/pallas_call | solution.py:253
  48.5 2.4 %collective-permute-done.10.refs_0_ = f32[2,128,128]{2,1,0:T(8,128)S(1)} collective-permute-done((f32[2,128,128]{2,1,0:T(8,128)S(1)}, f32[2,128,128]{2,1,0:T(8,128)S(1)}, u32[]{:S(2)}, u32[]{:S(2)}) %collective-permute-start.10) | collective-permute-done | bytes 131104 | tf_op jit(solution)/shard_map/ppermute | solution.py:265
  50.9 0.0 collective-permute-start.12
  50.9 1.3 %collective-permute-done.12.refs_1_ = f32[2,128,128]{2,1,0:T(8,128)S(1)} collective-permute-done((f32[2,128,128]{2,1,0:T(8,128)S(1)}, f32[2,128,128]{2,1,0:T(8,128)S(1)}, u32[]{:S(2)}, u32[]{:S(2)}) %collective-permute-start.12) | collective-permute-done | bytes 131104 | tf_op jit(solution)/shard_map/ppermute | solution.py:265
  52.2 2.0 %image_step.3 = f32[2,128,1024]{2,1,0:T(8,128)} custom-call(s32[1]{0:T(128)S(6)} %copy.12.start_ref, bf16[4,4,128,1024]{3,2,1,0:T(8,128)(2,1)S(1)} %copy-done.1, f32[2,128,128]{2,1,0:T(8,128)S(1)} %collective-permute-done.10.refs_0_, f32[2,128,128]{2,1,0:T(8,128)S(1)} %collective-permute-done.12.refs_1_, f32[2,128,1024]{2,1,0:T(8,128)S(1)} %image_step.2.refs_2_), custom_call_target="tpu_custom_call" | custom-call | flops 1000000000 | bytes 4194304 | tf_op jit(solution)/shard_map/image_step/pallas_call | solution.py:253
  (7 shorter events, 0.1 us)
Async XLA Ops:
  1.3 2.2 %copy-start = (bf16[4,4,128,1024]{3,2,1,0:T(8,128)(2,1)S(1)}, bf16[4,4,128,1024]{3,2,1,0:T(8,128)(2,1)}, u32[]{:S(2)}) copy-start(bf16[4,4,128,1024]{3,2,1,0:T(8,128)(2,1)} %constant.11.clone.e_ref) | copy-start | bytes 12582916
  3.5 1.2 %copy-start.3 = (f32[2,128,1024]{2,1,0:T(8,128)S(1)}, f32[2,128,1024]{2,1,0:T(8,128)}, u32[]{:S(2)}) copy-start(f32[2,128,1024]{2,1,0:T(8,128)} %x_ref.3) | copy-start | bytes 3145732
  7.5 6.8 %copy-start.7 = (s32[1,64]{1,0:T(1,128)S(1)}, s32[1,64]{1,0:T(1,128)}, u32[]{:S(2)}) copy-start(s32[1,64]{1,0:T(1,128)} %param.13) | copy-start | bytes 772
  7.5 10.9 %copy-start.6 = (f32[1,64,128]{2,1,0:T(8,128)S(1)}, f32[1,64,128]{2,1,0:T(8,128)}, u32[]{:S(2)}) copy-start(f32[1,64,128]{2,1,0:T(8,128)} %param.14) | copy-start | bytes 98308
  7.5 4.1 %collective-permute-start = (f32[2,2,128,128]{3,2,1,0:T(8,128)S(1)}, f32[2,2,128,128]{3,2,1,0:T(8,128)S(1)}, u32[]{:S(2)}, u32[]{:S(2)}) collective-permute-start(f32[2,2,128,128]{3,2,1,0:T(8,128)S(1)} %strips.3), channel_id=1, source_target_pairs={{0,1},{1,0},{2,3},{3,2},{4,5},{5,4},{6,7},{7,6},{8,9},{9,8},{10,11... | collective-permute-start | bytes 786440 | tf_op jit(solution)/shard_map/ppermute | solution.py:265
  10.8 15.9 %copy-start.2 = (bf16[6,128,1024]{2,1,0:T(8,128)(2,1)S(1)}, bf16[6,128,1024]{2,1,0:T(8,128)(2,1)}, u32[]{:S(2)}) copy-start(bf16[6,128,1024]{2,1,0:T(8,128)(2,1)} %constant.12.clone.b_ref) | copy-start | bytes 4718596
  10.8 15.8 %copy-start.4 = (f32[8,2,1024]{2,1,0:T(2,128)S(1)}, f32[8,2,1024]{2,1,0:T(2,128)}, u32[]{:S(2)}) copy-start(f32[8,2,1024]{2,1,0:T(2,128)} %constant.13.clone.roots_ref) | copy-start | bytes 196612
  10.8 15.8 %copy-start.5 = (s32[8]{0:T(128)S(1)}, s32[8]{0:T(128)}, u32[]{:S(2)}) copy-start(s32[8]{0:T(128)} %starts.9) | copy-start | bytes 100
  11.6 6.8 %collective-permute-start.1 = (f32[1,2,128,128]{3,2,1,0:T(8,128)S(1)}, f32[1,2,128,128]{3,2,1,0:T(8,128)S(1)}, u32[]{:S(2)}, u32[]{:S(2)}) collective-permute-start(f32[1,2,128,128]{3,2,1,0:T(8,128)S(1)} %slice_bitcast_fusion), channel_id=1, source_target_pairs={{0,2},{1,3},{2,0},{3,1},{4,6},{5,7},{6,4},{7,5},{8,10},{9,11},{10,... | collective-permute-start | bytes 393224 | tf_op jit(solution)/shard_map/ppermute | solution.py:265
  18.4 6.2 %collective-permute-start.2 = (f32[328,128]{1,0:T(8,128)S(1)}, f32[328,128]{1,0:T(8,128)S(1)}, u32[]{:S(2)}, u32[]{:S(2)}) collective-permute-start(f32[328,128]{1,0:T(8,128)S(1)} %select_maximum_fusion.refs_0_), channel_id=1, source_target_pairs={{0,8},{8,16},{16,24},{24,28},{28,20},{20,12},{12,4},{4,0},{1,9},{9... | collective-permute-start | bytes 503816 | tf_op jit(solution)/shard_map/ppermute | solution.py:303
  20.3 5.9 %collective-permute-start.3 = (f32[328,128]{1,0:T(8,128)S(1)}, f32[328,128]{1,0:T(8,128)S(1)}, u32[]{:S(2)}, u32[]{:S(2)}) collective-permute-start(f32[328,128]{1,0:T(8,128)S(1)} %select_maximum_fusion.refs_0_), channel_id=1, source_target_pairs={{8,0},{16,8},{24,16},{28,24},{20,28},{12,20},{4,12},{0,4},{9,1},{1... | collective-permute-start | bytes 503816 | tf_op jit(solution)/shard_map/ppermute | solution.py:304
  24.6 5.4 %collective-permute-start.4 = (f32[328,128]{1,0:T(8,128)S(1)}, f32[328,128]{1,0:T(8,128)S(1)}, u32[]{:S(2)}, u32[]{:S(2)}) collective-permute-start(f32[328,128]{1,0:T(8,128)S(1)} %collective-permute-done.2.refs_1_), channel_id=1, source_target_pairs={{0,8},{8,16},{16,24},{24,28},{28,20},{20,12},{12,4},{4,0},{1,9},{9... | collective-permute-start | bytes 503816 | tf_op jit(solution)/shard_map/ppermute | solution.py:303
  26.2 5.4 %collective-permute-start.5 = (f32[328,128]{1,0:T(8,128)S(1)}, f32[328,128]{1,0:T(8,128)S(1)}, u32[]{:S(2)}, u32[]{:S(2)}) collective-permute-start(f32[328,128]{1,0:T(8,128)S(1)} %collective-permute-done.3.refs_2_), channel_id=1, source_target_pairs={{8,0},{16,8},{24,16},{28,24},{20,28},{12,20},{4,12},{0,4},{9,1},{1... | collective-permute-start | bytes 503816 | tf_op jit(solution)/shard_map/ppermute | solution.py:304
  30.0 5.9 %collective-permute-start.6 = (f32[328,128]{1,0:T(8,128)S(1)}, f32[328,128]{1,0:T(8,128)S(1)}, u32[]{:S(2)}, u32[]{:S(2)}) collective-permute-start(f32[328,128]{1,0:T(8,128)S(1)} %collective-permute-done.4.refs_1_), channel_id=1, source_target_pairs={{0,8},{8,16},{16,24},{24,28},{28,20},{20,12},{12,4},{4,0},{1,9},{9... | collective-permute-start | bytes 503816 | tf_op jit(solution)/shard_map/ppermute | solution.py:303
  31.6 6.0 %collective-permute-start.7 = (f32[328,128]{1,0:T(8,128)S(1)}, f32[328,128]{1,0:T(8,128)S(1)}, u32[]{:S(2)}, u32[]{:S(2)}) collective-permute-start(f32[328,128]{1,0:T(8,128)S(1)} %collective-permute-done.5.refs_2_), channel_id=1, source_target_pairs={{8,0},{16,8},{24,16},{28,24},{20,28},{12,20},{4,12},{0,4},{9,1},{1... | collective-permute-start | bytes 503816 | tf_op jit(solution)/shard_map/ppermute | solution.py:304
  35.9 6.3 %collective-permute-start.8 = (f32[168,128]{1,0:T(8,128)S(1)}, f32[168,128]{1,0:T(8,128)S(1)}, u32[]{:S(2)}, u32[]{:S(2)}) collective-permute-start(f32[168,128]{1,0:T(8,128)S(1)} %slice.18), channel_id=1, source_target_pairs={{0,8},{8,16},{16,24},{24,28},{28,20},{20,12},{12,4},{4,0},{1,9},{9... | collective-permute-start | bytes 258056 | tf_op jit(solution)/shard_map/ppermute | solution.py:307
  37.6 4.7 %collective-permute-start.9 = (f32[160,128]{1,0:T(8,128)S(1)}, f32[160,128]{1,0:T(8,128)S(1)}, u32[]{:S(2)}, u32[]{:S(2)}) collective-permute-start(f32[160,128]{1,0:T(8,128)S(1)} %slice.19), channel_id=1, source_target_pairs={{8,0},{16,8},{24,16},{28,24},{20,28},{12,20},{4,12},{0,4},{9,1},{1... | collective-permute-start | bytes 245768 | tf_op jit(solution)/shard_map/ppermute | solution.py:308
  42.2 5.3 %copy-start.1 = (bf16[4,4,128,1024]{3,2,1,0:T(8,128)(2,1)S(1)}, bf16[4,4,128,1024]{3,2,1,0:T(8,128)(2,1)}, u32[]{:S(2)}) copy-start(bf16[4,4,128,1024]{3,2,1,0:T(8,128)(2,1)} %constant.11.clone.e_ref) | copy-start | bytes 12582916
  44.9 2.6 %collective-permute-start.11 = (f32[2,128,128]{2,1,0:T(8,128)S(1)}, f32[2,128,128]{2,1,0:T(8,128)S(1)}, u32[]{:S(2)}, u32[]{:S(2)}) collective-permute-start(f32[2,128,128]{2,1,0:T(8,128)S(1)} %get-tuple-element.7.refs_0_), channel_id=1, source_target_pairs={{0,1},{1,0},{2,3},{3,2},{4,5},{5,4},{6,7},{7,6},{8,9},{9,8},{10,11... | collective-permute-start | bytes 393224 | tf_op jit(solution)/shard_map/ppermute | solution.py:265
  45.0 5.9 %collective-permute-start.10 = (f32[2,128,128]{2,1,0:T(8,128)S(1)}, f32[2,128,128]{2,1,0:T(8,128)S(1)}, u32[]{:S(2)}, u32[]{:S(2)}) collective-permute-start(f32[2,128,128]{2,1,0:T(8,128)S(1)} %get-tuple-element.7.refs_0_), channel_id=1, source_target_pairs={{0,2},{1,3},{2,0},{3,1},{4,6},{5,7},{6,4},{7,5},{8,10},{9,11},{10,... | collective-permute-start | bytes 393224 | tf_op jit(solution)/shard_map/ppermute | solution.py:265
  50.9 1.3 %collective-permute-start.12 = (f32[2,128,128]{2,1,0:T(8,128)S(1)}, f32[2,128,128]{2,1,0:T(8,128)S(1)}, u32[]{:S(2)}, u32[]{:S(2)}) collective-permute-start(f32[2,128,128]{2,1,0:T(8,128)S(1)} %collective-permute-done.10.refs_0_), channel_id=1, source_target_pairs={{0,1},{1,0},{2,3},{3,2},{4,5},{5,4},{6,7},{7,6},{8,9},{9,8},{10,11... | collective-permute-start | bytes 393224 | tf_op jit(solution)/shard_map/ppermute | solution.py:265

commit v2 on v1

v2 whole, which is shorter than its diff:
```python
import functools
import math

import jax
import jax.numpy as jnp
import ml_dtypes
import numpy as np
from jax import lax
from jax.experimental import pallas as pl
from jax.experimental.pallas import tpu as pltpu
from jax.sharding import PartitionSpec as P

SG = 512
MAXB = 64
META = 8

BF = jnp.bfloat16
F32 = jnp.float32
NN = (((1,), (0,)), ((), ()))
NT = (((1,), (1,)), ((), ()))
VMEM = pl.BlockSpec(memory_space=pltpu.VMEM)
SMEM = pl.BlockSpec(memory_space=pltpu.SMEM)
LIMIT = pltpu.CompilerParams(vmem_limit_bytes=32 << 20)


def halves(value):
    high = value.astype(BF)
    return high, (value - high.astype(F32)).astype(BF)


def dot3(left, right, dims):
    def dot(a, b):
        return lax.dot_general(a, b, dims, preferred_element_type=F32)
    return dot(left[0], right[0]) + (dot(left[0], right[1]) + dot(left[1], right[0]))


def unit(phase, modulus, scale=1.0):
    angle = (phase & (modulus - 1)).astype(F32) * F32(2.0 * math.pi / modulus)
    return jnp.cos(angle) * F32(scale), jnp.sin(angle) * F32(scale)


def lanes(count, rows=1):
    return lax.broadcasted_iota(jnp.int32, (rows, count), 1)


def wave_parts(rows, stride, cols, modulus):
    phase = np.arange(rows, dtype=np.int64)[:, None] * (stride * np.arange(cols, dtype=np.int64))[None, :] % modulus
    angle = phase * (2.0 * np.pi / modulus)
    return np.stack([np.cos(angle), np.sin(angle)])


def wave_table(rows, cols, modulus):
    parts = wave_parts(rows, 1, cols, modulus)
    high = parts.astype(ml_dtypes.bfloat16)
    low = (parts - high.astype(np.float64)).astype(ml_dtypes.bfloat16)
    return np.concatenate([high, low])


def ring_place(r, rows):
    return jnp.where(lax.rem(r, 2) == 0, r // 2, rows - 1 - r // 2)


def ring_block(place, rows):
    place = lax.rem(place + rows, rows)
    return jnp.where(place < rows // 2, 2 * place, 2 * (rows - 1 - place) + 1)


def wave_kernel(width, cols_total, base_ref, steps_ref):
    own = lax.axis_index("fcol")
    blocks, _, count, _ = base_ref.shape
    row = lax.broadcasted_iota(jnp.int32, (count, 128), 0)
    for ref, coord in ((base_ref, lanes(128)), (steps_ref, lanes(128) * 128 + own * width)):
        cos, sin = unit(row * coord, cols_total)
        for g in range(blocks):
            pc, ps = unit((own ^ g) * count * coord, cols_total)
            ref[g, 0] = cos * pc - sin * ps
            ref[g, 1] = sin * pc + cos * ps


def waves_of(count, width, cols_total):
    shape = jax.ShapeDtypeStruct((SG // count, 2, count, 128), F32)
    return pl.pallas_call(
        functools.partial(wave_kernel, width, cols_total),
        out_specs=[VMEM] * 2,
        out_shape=[shape] * 2,
        compiler_params=LIMIT,
        cost_estimate=pl.CostEstimate(flops=10**9, bytes_accessed=2 << 20, transcendentals=0),
        name="waves",
    )()


def strip_kernel(gs, cols_total, first, *refs):
    source_ref, base_ref, steps_ref, out_ref = refs[1:5] if first else refs
    own = lax.axis_index("fcol")
    height, width = out_ref.shape[-1], source_ref.shape[-1]
    if first:
        pc, ps = unit(refs[0][0:1, 0:1] * (own * width + lanes(width)), cols_total, 1.0 / math.sqrt(cols_total))
        re, im = source_ref[0], source_ref[1]
        z = halves(jnp.concatenate([re * pc + im * ps, im * pc - re * ps]))
        z_ref, phase_ref = refs[5:]
        z_ref[0], z_ref[1] = z
        phase_ref[0:1], phase_ref[1:2] = pc, ps
    else:
        z = source_ref[0], source_ref[1]
    for i, g in enumerate(gs):
        turn_cos, turn_sin, base_cos, base_sin = steps_ref[g, 0], steps_ref[g, 1], base_ref[g, 0], base_ref[g, 1]
        cos, sin = [], []
        for t in range(width // 128):
            tc, ts = turn_cos[:, t : t + 1], turn_sin[:, t : t + 1]
            cos.append(tc * base_cos - ts * base_sin)
            sin.append(ts * base_cos + tc * base_sin)
        waves = halves(jnp.concatenate([jnp.concatenate(cos, 1), jnp.concatenate(sin, 1)]))
        acc = dot3(waves, z, NT)
        count = out_ref.shape[2]
        cos, sin = acc[:count], acc[count:]
        out_ref[i, 0] = cos[:, :height] + sin[:, height:]
        out_ref[i, 1] = cos[:, height:] - sin[:, :height]


def strips(column_start, source, waves, gs, cols_total, first=False, cost=10**9):
    count = waves[0].shape[2]
    height, width = source.shape[1] // (1 if first else 2), source.shape[2]
    operands = ([column_start] if first else []) + [source, *waves]
    out = pl.pallas_call(
        functools.partial(strip_kernel, gs, cols_total, int(first)),
        in_specs=[VMEM] * len(operands),
        out_specs=[VMEM] * (3 if first else 1),
        out_shape=[jax.ShapeDtypeStruct((len(gs), 2, count, height), F32)]
        + ([jax.ShapeDtypeStruct((2, 2 * height, width), BF), jax.ShapeDtypeStruct((2, width), F32)] if first else []),
        compiler_params=LIMIT,
        cost_estimate=pl.CostEstimate(flops=cost, bytes_accessed=cost // 1000, transcendentals=0),
        name="strips",
    )(*operands)
    return out if first else out[0]


def pack_kernel(terms, *refs):
    weight_ref, row_ref, live_ref, out_ref = refs[terms:]
    count = refs[0].shape[2]
    strip = sum(ref[0] for ref in refs[:terms])
    out_ref[:count], out_ref[count : 2 * count] = strip[0], strip[1]
    width = out_ref.shape[1]
    weight = weight_ref[0]
    if count < width:
        weight = jnp.concatenate([weight, jnp.zeros((MAXB, width - count), F32)], 1)
    out_ref[2 * count : 2 * count + MAXB] = weight
    row = jnp.where(lanes(MAXB) < live_ref[0:1, 0:1], row_ref[...], -1).astype(F32)
    row = jnp.concatenate([row, jnp.zeros((1, width - MAXB), F32)], 1)
    out_ref[2 * count + MAXB :] = jnp.broadcast_to(row, (META, width))


def pack(terms, weight, row, live, count, height):
    return pl.pallas_call(
        functools.partial(pack_kernel, len(terms)),
        in_specs=[VMEM] * (len(terms) + 3),
        out_specs=VMEM,
        out_shape=jax.ShapeDtypeStruct((2 * count + MAXB + META, height), F32),
        compiler_params=LIMIT,
        name="pack",
    )(*terms, weight, row, live)


def add_message(starts, r, message, b_ref, roots_ref, state, height, count, rows_total):
    mine, other = starts[lax.axis_index("frow")], starts[r]
    strip, rest = message[: 2 * count], message[2 * count :]
    pc, ps = unit(mine * (r * height + lanes(height)), rows_total, 1.0 / math.sqrt(rows_total))
    re, im = strip[:count], strip[count:]
    re, im = re * pc + im * ps, im * pc - re * ps
    high, low = halves(jnp.concatenate([jnp.concatenate([re, im], 1), jnp.concatenate([im, -re], 1)]))
    part = lax.dot_general(
        jnp.concatenate([high, low, high], 1), b_ref[...].reshape(6 * height, rows_total), NN, preferred_element_type=F32
    )
    freq = lanes(rows_total)
    turn = lax.rem(r - lax.axis_index("frow") + rows_total // height, rows_total // height)
    pc, ps = roots_ref[turn, 0:1], roots_ref[turn, 1:2]
    re, im = part[:count], part[count:]
    add_re, add_im = re * pc + im * ps, im * pc - re * ps

    width = message.shape[1]
    flat = jnp.concatenate([rest, jnp.zeros((width - rest.shape[0], width), F32)])
    turned = jnp.transpose(flat)
    weight = turned[:count, :MAXB]
    row = turned[:MAXB, MAXB : MAXB + 1].astype(jnp.int32)
    place = jnp.where(row < 0, -1, (row + (other - mine)) & (rows_total - 1))
    hot = (lanes(rows_total, MAXB) == place).astype(F32).astype(BF)
    gain = lax.dot_general(
        jnp.concatenate(halves(weight), 1), jnp.concatenate([hot, hot]), NN, preferred_element_type=F32
    )
    gain = gain + (((freq + (mine - other)) & (rows_total - 1)) < SG).astype(F32)
    if state is None:
        return add_re, add_im, gain
    return state[0] + add_re, state[1] + add_im, state[2] + gain


def gather_kernel(steps, rows, height, count, starts, b_ref, roots_ref, *refs):
    state = None
    if len(refs) > len(steps) + 1:
        state, refs = (refs[0][0], refs[0][1], refs[0][2]), refs[1:]
    at = ring_place(lax.axis_index("frow"), rows)
    for step, message in zip(steps, refs):
        r = ring_block(at + step, rows)
        state = add_message(starts, r, message[...], b_ref, roots_ref, state, height, count, rows * height)
    for i in range(3):
        refs[-1][i] = state[i]


def gather_step(starts, table, roots, state, messages, steps, count):
    height, rows_total = table.shape[1:]
    operands = [table, roots] + ([] if state is None else [state]) + list(messages)
    return pl.pallas_call(
        functools.partial(gather_kernel, steps, rows_total // height, height, count),
        in_specs=[SMEM] + [VMEM] * len(operands),
        out_specs=VMEM,
        out_shape=jax.ShapeDtypeStruct((3, count, rows_total), F32),
        compiler_params=LIMIT,
        cost_estimate=pl.CostEstimate(flops=10**9, bytes_accessed=4 << 20, transcendentals=0),
        name="gather_step",
    )(starts, *operands)


def back_kernel(rows, height, count, starts, b_ref, turned_ref, roots_ref, state_ref, top_ref, bottom_ref, back_ref, sub_ref):
    state = state_ref[0], state_ref[1], state_ref[2]
    message = jnp.concatenate([top_ref[...], bottom_ref[...]])
    rows_total = rows * height
    own = lax.axis_index("frow")
    r = ring_block(ring_place(own, rows) + rows // 2, rows)
    re, im, gain = add_message(starts, r, message, b_ref, roots_ref, state, height, count, rows_total)
    sub_ref[0] = re[:, :SG]
    sub_ref[1] = im[:, :SG]
    high, low = halves(jnp.concatenate([re * gain, im * gain]))
    acc = lax.dot_general(high, turned_ref[...], NN, preferred_element_type=F32)
    acc = acc[:, : 2 * height] + (
        acc[:, 2 * height :] + lax.dot_general(low, turned_ref[:, : 2 * height], NN, preferred_element_type=F32)
    )
    re = acc[:count, :height] - acc[count:, height:]
    im = acc[count:, :height] + acc[:count, height:]
    pc, ps = unit(starts[own] * (own * height + lanes(height)), rows_total, 1.0 / math.sqrt(rows_total))
    back_ref[0] = jnp.transpose(re * pc - im * ps)
    back_ref[1] = jnp.transpose(im * pc + re * ps)


def back_step(starts, table, turned, roots, state, parts, count):
    height, rows_total = table.shape[1:]
    return pl.pallas_call(
        functools.partial(back_kernel, rows_total // height, height, count),
        in_specs=[SMEM] + [VMEM] * 6,
        out_specs=[VMEM] * 2,
        out_shape=[
            jax.ShapeDtypeStruct((2, height, count), F32),
            jax.ShapeDtypeStruct((2, count, SG), F32),
        ],
        compiler_params=LIMIT,
        name="back_step",
    )(starts, table, turned, roots, state, *parts)


def correct_kernel(sub_ref, gain_ref, roots_ref, out_ref):
    count = sub_ref.shape[1]
    pieces = SG // 128
    own = lax.axis_index("frow")
    pc, ps = roots_ref[own, 0:1, :SG], roots_ref[own, 1:2, :SG]
    re, im, gain = sub_ref[0], sub_ref[1], gain_ref[2, :, :SG]
    for part, value in enumerate([(re * pc + im * ps) * gain, (im * pc - re * ps) * gain]):
        for i in range(pieces):
            out_ref[pl.ds(2 * i + part, count, stride=2 * pieces), :] = value[:, 128 * i : 128 * (i + 1)]


def correct_step(sub, first_state, roots):
    count = sub.shape[1]
    out = pl.pallas_call(
        correct_kernel,
        in_specs=[VMEM] * 3,
        out_specs=VMEM,
        out_shape=jax.ShapeDtypeStruct((count * 2 * SG // 128, 128), F32),
        compiler_params=LIMIT,
        cost_estimate=pl.CostEstimate(flops=10**9, bytes_accessed=4 << 20, transcendentals=0),
        name="correct_step",
    )(sub, first_state, roots)
    out = out.reshape(count, SG // 128, 2, 128)
    return jnp.transpose(out, (0, 2, 1, 3)).reshape(1, count, 2, SG)


def image_kernel(gs, cols_total, first, last, phase_ref, e_ref, *refs):
    backs, refs = refs[: len(gs)], refs[len(gs) :]
    out_ref = refs[-1]
    _, height, width = out_ref.shape
    count = e_ref.shape[2]
    own = lax.axis_index("fcol")
    acc = None if first else jnp.concatenate([refs[0][0], refs[0][1]])
    for back, g in zip(backs, gs):
        freq = (own ^ g) * count + lanes(count)
        pc, ps = unit(freq * (own * width), cols_total)
        re, im = back[0], back[1]
        re, im = re * pc - im * ps, im * pc + re * ps
        left = halves(jnp.concatenate([jnp.concatenate([re, -im], 1), jnp.concatenate([im, re], 1)]))
        right = (e_ref[own ^ g, 0:2].reshape(2 * count, width), e_ref[own ^ g, 2:4].reshape(2 * count, width))
        part = dot3(left, right, NN)
        acc = part if acc is None else acc + part
    re, im = acc[:height], acc[height:]
    if last:
        pc, ps = phase_ref[0:1], phase_ref[1:2]
        re, im = re * pc - im * ps, im * pc + re * ps
    out_ref[0] = re
    out_ref[1] = im


def image_step(phase, table, gs, backs, acc, last, cols_total):
    width = table.shape[-1]
    height = backs[0].shape[1]
    first = acc is None
    operands = list(backs) + ([] if first else [acc])
    return pl.pallas_call(
        functools.partial(image_kernel, tuple(gs), cols_total, first, last),
        in_specs=[VMEM] * (2 + len(operands)),
        out_specs=VMEM,
        out_shape=jax.ShapeDtypeStruct((2, height, width), F32),
        compiler_params=LIMIT,
        cost_estimate=pl.CostEstimate(flops=10**9, bytes_accessed=4 << 20, transcendentals=0),
        name="image_step",
    )(phase, table, *operands)


def swap(value, axis, bit):
    return lax.ppermute(value, axis, [(i, i ^ bit) for i in range(lax.axis_size(axis))])


def per_device(facets, column_start, subgrid_start, vis_count, vis_row, vis_weight):
    rows = lax.axis_size("frow")
    cols = lax.axis_size("fcol")
    height, width = facets.shape[1:]
    rows_total, cols_total = height * rows, width * cols
    count = SG // cols
    assert vis_count.shape[0] == 1 and count <= height

    e_table = jnp.asarray(wave_table(SG, width, cols_total).reshape(4, cols, count, width).transpose(1, 0, 2, 3))
    b_table = wave_table(height, rows_total, rows_total)
    turned = jnp.asarray(b_table.reshape(4 * height, rows_total).T.copy())
    b_table = jnp.asarray(np.concatenate([b_table[:2], b_table]))
    angle = np.arange(rows)[:, None] * np.arange(rows_total)[None, :] % rows * (2.0 * np.pi / rows)
    roots = jnp.asarray(np.stack([np.cos(angle), np.sin(angle)], 1).astype(np.float32))

    top = cols // 2
    groups = [range(top + 1, cols, 2), range(top, cols, 2), range(1, top, 2), range(0, top, 2)]
    groups = [tuple(group) for group in groups]
    column_start = column_start.reshape(1, 1)
    waves = waves_of(count, width, cols_total)
    sent, z, phase = strips(column_start, facets, waves, groups[0], cols_total, first=True)
    far = strips(column_start, z, waves, groups[1], cols_total) + swap(sent, "fcol", 1)
    far, z = lax.optimization_barrier((far, z))
    far = swap(far, "fcol", top)
    sent = strips(column_start, z, waves, groups[2], cols_total, cost=10**6)
    terms = [strips(column_start, z, waves, groups[3], cols_total, cost=10**6), swap(sent, "fcol", 1), far]
    bit = 2
    while bit < top:
        pairs = sum(terms).reshape((-1, 2) + far.shape[1:])
        terms = [pairs[:, 0], swap(pairs[:, 1], "fcol", bit)]
        bit *= 2

    own = pack(terms, vis_weight, vis_row, vis_count.reshape(1, 1), count, height)
    order = list(range(0, rows, 2)) + list(range(rows - 1, 0, -2))
    ahead = [(order[i], order[(i + 1) % rows]) for i in range(rows)]
    behind = [(b, a) for a, b in ahead]
    first_state = state = gather_step(subgrid_start, b_table, roots, None, [own], (0,), count)
    up = down = own
    for step in range(1, rows // 2):
        up = lax.ppermute(up, "frow", ahead)
        down = lax.ppermute(down, "frow", behind)
        up, state = lax.optimization_barrier((up, state))
        state = gather_step(subgrid_start, b_table, roots, state, [up, down], (-step, step), count)
    cut = (own.shape[0] // 2 + 7) // 8 * 8
    parts = [lax.ppermute(up[:cut], "frow", ahead), lax.ppermute(down[cut:], "frow", behind)]
    back, sub = back_step(subgrid_start, b_table, turned, roots, state, parts, count)

    near, far = {0: back}, {top: swap(back, "fcol", top)}

    def spread(blocks, bit):
        return {g ^ bit: swap(b, "fcol", bit) for g, b in blocks.items()}

    def image(blocks, acc, last=False):
        return image_step(phase, e_table, blocks.keys(), list(blocks.values()), acc, last, cols_total)

    bit = top // 2
    while bit >= 1:
        near |= spread(near, bit)
        bit //= 2
    acc = image(near, None)
    corrected = correct_step(sub, first_state, roots)
    far[top], acc, corrected = lax.optimization_barrier((far[top], acc, corrected))
    bit = top // 2
    while bit > 1:
        far |= spread(far, bit)
        bit //= 2
    rest = spread(far, 1)
    acc = image(far, acc)
    return corrected, image(rest, acc, last=True)


def solution(mesh):
    return jax.shard_map(
        per_device,
        mesh=mesh,
        in_specs=(
            P(None, "frow", "fcol"),
            P(),
            P(),
            P("frow"),
            P("frow", None),
            P("frow", None, "fcol"),
        ),
        out_specs=(P("frow", "fcol", None, None), P(None, "frow", "fcol")),
        check_vma=False,
    )
```

time: 54.4 us -> 48.5 us (0.89)
  local copies, waits for them, and re-layouts: 3.47 us -> 0.06 us
  waiting for transfers between devices: 16 us -> 14 us
  Pallas kernels: 19.2 us -> 18.5 us
    unnamed x16, local copies, waits for them, and re-layouts: 3.44 us -> 0.05 us
    ppermute x5 -> x6, waiting for transfers between devices: 7.85 us -> 5.6 us  [swap(): lax.ppermute(value, axis, [(i, i ^ bit) for i in range(lax.axis_size(axis...]
    pallas_call x5 -> x10, Pallas kernels: 9.47 us -> 8.83 us  [the longest x4 3.81 us: strips(): pl.pallas_call(functools.partial(strip_kernel, gs, cols_total, int(first)...]
    ppermute x5 -> x6, starting transfers between devices: 4.79 us -> 5.28 us  [swap(): lax.ppermute(value, axis, [(i, i ^ bit) for i in range(lax.axis_size(axis...]
  transfers between devices with their start and end apart: 13 -> 14, of which waited for: 6 -> 8; matrix products, arithmetic and copies ran while one was open for 0% -> 0% of each run, Pallas kernels for 22% -> 24%
where the time goes in v2:
time: 48.5 us; the launch traced here: 48.4 us
  Pallas kernels  18.5 us (38%)
  waiting for transfers between devices  14 us (29%)
  starting transfers between devices  13.7 us (28%)
  between operations  2.13 us (4%)
    pallas_call x4, Pallas kernels, gather_step(): pl.pallas_call(functools.partial(gather_kernel, steps, rows_total // heig...  7.12 us
    ppermute x3, waiting for transfers between devices, per_device(): up = lax.ppermute(up, 'frow', ahead)  6.15 us
    ppermute x6, waiting for transfers between devices, swap(): lax.ppermute(value, axis, [(i, i ^ bit) for i in range(lax.axis_size(axis...  5.6 us
    ppermute x6, starting transfers between devices, swap(): lax.ppermute(value, axis, [(i, i ^ bit) for i in range(lax.axis_size(axis...  5.28 us
    ppermute x3, starting transfers between devices, per_device(): up = lax.ppermute(up, 'frow', ahead)  4.93 us
    pallas_call x4, Pallas kernels, strips(): pl.pallas_call(functools.partial(strip_kernel, gs, cols_total, int(first)...  3.81 us
    pallas_call x3, Pallas kernels, image_step(): pl.pallas_call(functools.partial(image_kernel, tuple(gs), cols_total, fir...  3.22 us
    pallas_call x1, Pallas kernels, back_step(): pl.pallas_call(functools.partial(back_kernel, rows_total // height, heigh...  2.59 us
  transfers between devices with their start and end apart: 14, of which 8 were waited for; matrix products, arithmetic and copies ran while one was open for 0% of the time, Pallas kernels for 24%

profile of v2, /device:TPU:0, one launch (start us, length us, event | category | flops | bytes accessed | tf_op | source)
XLA Modules:
  0.0 48.4 jit_solution(14651563071289380617)
XLA Ops:
  0.6 0.0 copy-start.7
  0.6 0.7 %waves.1 = (f32[4,2,128,128]{3,2,1,0:T(8,128)S(1)}, f32[4,2,128,128]{3,2,1,0:T(8,128)S(1)}) custom-call(), custom_call_target="tpu_custom_call" | custom-call | flops 1000000000 | bytes 2097152 | tf_op jit(solution)/shard_map/waves/pallas_call | solution.py:82
  2.0 0.0 copy-done.7
  2.0 1.1 %strips.4 = (f32[1,2,128,128]{3,2,1,0:T(8,128)S(1)}, bf16[2,256,1024]{2,1,0:T(8,128)(2,1)S(1)}, f32[2,1024]{1,0:T(2,128)S(1)}) custom-call(s32[1,1]{1,0:T(1,128)} %bitcast.7.refs_0_, f32[2,128,1024]{2,1,0:T(8,128)S(1)} %copy-done.7, f32[4,2,128,128]{3,2,1,0:T(8,128)S(1)} %get-tuple-element.20.refs_2_.refs_1_, ...), custom_call_target="tpu_custom_call" | custom-call | flops 1000000000 | bytes 1000000 | tf_op jit(solution)/shard_map/strips/pallas_call | solution.py:124
  3.2 0.5 %collective-permute-start = (f32[1,2,128,128]{3,2,1,0:T(8,128)S(1)}, f32[1,2,128,128]{3,2,1,0:T(8,128)S(1)}, u32[]{:S(2)}, u32[]{:S(2)}) collective-permute-start(f32[1,2,128,128]{3,2,1,0:T(8,128)S(1)} %get-tuple-element.23), channel_id=1, source_target_pairs={{0,1},{1,0},{2,3},{3,2},{4,5},{5,4},{6,7},{7,6},{8,9},{9,8},{10,11... | collective-permute-start | bytes 393224 | tf_op jit(solution)/shard_map/ppermute | solution.py:324
  3.7 0.9 %strips.5 = f32[1,2,128,128]{3,2,1,0:T(8,128)S(1)} custom-call(bf16[2,256,1024]{2,1,0:T(8,128)(2,1)S(1)} %get-tuple-element.24.refs_0_, f32[4,2,128,128]{3,2,1,0:T(8,128)S(1)} %get-tuple-element.20.refs_2_.refs_1_, f32[4,2,128,128]{3,2,1,0:T(8,128)S(1)} %get-tuple-element.21.refs_3_.refs_2_), custom_call_target="tpu_custom_call" | custom-call | flops 1000000000 | bytes 1000000 | tf_op jit(solution)/shard_map/strips/pallas_call | solution.py:124
  4.6 0.1 collective-permute-done
  4.7 0.9 %strips.7 = f32[1,2,128,128]{3,2,1,0:T(8,128)S(1)} custom-call(bf16[2,256,1024]{2,1,0:T(8,128)(2,1)S(1)} %get-tuple-element.24.refs_0_, f32[4,2,128,128]{3,2,1,0:T(8,128)S(1)} %get-tuple-element.20.refs_2_.refs_1_, f32[4,2,128,128]{3,2,1,0:T(8,128)S(1)} %get-tuple-element.21.refs_3_.refs_2_), custom_call_target="tpu_custom_call" | custom-call | flops 1000000 | bytes 1000 | tf_op jit(solution)/shard_map/strips/pallas_call | solution.py:124
  5.6 0.0 copy-start.4
  5.6 0.0 copy-start.6
  5.6 0.0 copy-start.1
  5.6 0.0 copy-start.2
  5.6 0.0 copy-start.5
  5.7 0.4 collective-permute-start.1
  6.1 2.7 %collective-permute-start.2 = (f32[1,2,128,128]{3,2,1,0:T(8,128)S(1)}, f32[1,2,128,128]{3,2,1,0:T(8,128)S(1)}, u32[]{:S(2)}, u32[]{:S(2)}) collective-permute-start(f32[1,2,128,128]{3,2,1,0:T(8,128)S(1)} %add.3), channel_id=1, source_target_pairs={{0,2},{1,3},{2,0},{3,1},{4,6},{5,7},{6,4},{7,5},{8,10},{9,11},{10,... | collective-permute-start | bytes 393224 | tf_op jit(solution)/shard_map/ppermute | solution.py:324
  9.4 0.9 %strips.6.refs_0_ = f32[1,2,128,128]{3,2,1,0:T(8,128)S(1)} custom-call(bf16[2,256,1024]{2,1,0:T(8,128)(2,1)S(1)} %get-tuple-element.24.refs_0_, f32[4,2,128,128]{3,2,1,0:T(8,128)S(1)} %get-tuple-element.20.refs_2_.refs_1_, f32[4,2,128,128]{3,2,1,0:T(8,128)S(1)} %get-tuple-element.21.refs_3_.refs_2_), custom_call_target="tpu_custom_call" | custom-call | flops 1000000 | bytes 1000 | tf_op jit(solution)/shard_map/strips/pallas_call | solution.py:124
  10.3 0.0 collective-permute-done.1.refs_1_
  10.3 2.4 %collective-permute-done.2.refs_2_ = f32[1,2,128,128]{3,2,1,0:T(8,128)S(1)} collective-permute-done((f32[1,2,128,128]{3,2,1,0:T(8,128)S(1)}, f32[1,2,128,128]{3,2,1,0:T(8,128)S(1)}, u32[]{:S(2)}, u32[]{:S(2)}) %collective-permute-start.2) | collective-permute-done | bytes 131104 | tf_op jit(solution)/shard_map/ppermute | solution.py:324
  12.8 0.0 copy-done.4
  12.8 0.0 copy-done.6
  12.8 0.1 pack.1.refs_0_
  12.9 1.8 %collective-permute-start.3 = (f32[328,128]{1,0:T(8,128)S(1)}, f32[328,128]{1,0:T(8,128)S(1)}, u32[]{:S(2)}, u32[]{:S(2)}) collective-permute-start(f32[328,128]{1,0:T(8,128)S(1)} %pack.1.refs_0_), channel_id=1, source_target_pairs={{0,8},{8,16},{16,24},{24,28},{28,20},{20,12},{12,4},{4,0},{1,9},{9... | collective-permute-start | bytes 503816 | tf_op jit(solution)/shard_map/ppermute | solution.py:366
  14.7 0.2 collective-permute-start.5
  14.9 0.0 copy-done.1
  14.9 0.0 copy-done.2
  14.9 0.0 copy-done.5
  14.9 1.3 %gather_step.4.refs_0_.gain_ref = f32[3,128,1024]{2,1,0:T(8,128)S(1)} custom-call(s32[8]{0:T(128)S(1)} %copy-done.5, bf16[6,128,1024]{2,1,0:T(8,128)(2,1)S(1)} %copy-done.1, f32[8,2,1024]{2,1,0:T(2,128)S(1)} %copy-done.2, f32[328,128]{1,0:T(8,128)S(1)} %pack.1.refs_0_), custom_call_target="tpu_custom_call" | custom-call | flops 1000000000 | bytes 4194304 | tf_op jit(solution)/shard_map/gather_step/pallas_call | solution.py:210
  16.2 2.7 %collective-permute-done.3.refs_1_ = f32[328,128]{1,0:T(8,128)S(1)} collective-permute-done((f32[328,128]{1,0:T(8,128)S(1)}, f32[328,128]{1,0:T(8,128)S(1)}, u32[]{:S(2)}, u32[]{:S(2)}) %collective-permute-start.3) | collective-permute-done | bytes 167968 | tf_op jit(solution)/shard_map/ppermute | solution.py:366
  18.8 1.6 %collective-permute-start.4 = (f32[328,128]{1,0:T(8,128)S(1)}, f32[328,128]{1,0:T(8,128)S(1)}, u32[]{:S(2)}, u32[]{:S(2)}) collective-permute-start(f32[328,128]{1,0:T(8,128)S(1)} %collective-permute-done.3.refs_1_), channel_id=1, source_target_pairs={{0,8},{8,16},{16,24},{24,28},{28,20},{20,12},{12,4},{4,0},{1,9},{9... | collective-permute-start | bytes 503816 | tf_op jit(solution)/shard_map/ppermute | solution.py:366
  20.4 0.0 collective-permute-done.5.refs_2_
  20.4 0.5 collective-permute-start.7
  20.9 2.0 %gather_step.5.refs_0_ = f32[3,128,1024]{2,1,0:T(8,128)S(1)} custom-call(s32[8]{0:T(128)S(1)} %copy-done.5, bf16[6,128,1024]{2,1,0:T(8,128)(2,1)S(1)} %copy-done.1, f32[8,2,1024]{2,1,0:T(2,128)S(1)} %copy-done.2, f32[3,128,1024]{2,1,0:T(8,128)S(1)} %gather_step.4.refs_0_.gain_ref, f32[328,128]{1,0:T(8,128)S(1)} %collective-permute-done.3.refs_1_, ...), custom_call_target="tpu_custom_call" | custom-call | flops 1000000000 | bytes 4194304 | tf_op jit(solution)/shard_map/gather_step/pallas_call | solution.py:210
  22.8 1.4 %collective-permute-done.4.refs_1_ = f32[328,128]{1,0:T(8,128)S(1)} collective-permute-done((f32[328,128]{1,0:T(8,128)S(1)}, f32[328,128]{1,0:T(8,128)S(1)}, u32[]{:S(2)}, u32[]{:S(2)}) %collective-permute-start.4) | collective-permute-done | bytes 167968 | tf_op jit(solution)/shard_map/ppermute | solution.py:366
  24.2 1.6 %collective-permute-start.6 = (f32[328,128]{1,0:T(8,128)S(1)}, f32[328,128]{1,0:T(8,128)S(1)}, u32[]{:S(2)}, u32[]{:S(2)}) collective-permute-start(f32[328,128]{1,0:T(8,128)S(1)} %collective-permute-done.4.refs_1_), channel_id=1, source_target_pairs={{0,8},{8,16},{16,24},{24,28},{28,20},{20,12},{12,4},{4,0},{1,9},{9... | collective-permute-start | bytes 503816 | tf_op jit(solution)/shard_map/ppermute | solution.py:366
  25.8 0.0 collective-permute-done.7.refs_2_
  25.8 0.5 collective-permute-start.8
  26.2 2.0 %gather_step.6.refs_0_ = f32[3,128,1024]{2,1,0:T(8,128)S(1)} custom-call(s32[8]{0:T(128)S(1)} %copy-done.5, bf16[6,128,1024]{2,1,0:T(8,128)(2,1)S(1)} %copy-done.1, f32[8,2,1024]{2,1,0:T(2,128)S(1)} %copy-done.2, f32[3,128,1024]{2,1,0:T(8,128)S(1)} %gather_step.5.refs_0_, f32[328,128]{1,0:T(8,128)S(1)} %collective-permute-done.4.refs_1_, ...), custom_call_target="tpu_custom_call" | custom-call | flops 1000000000 | bytes 4194304 | tf_op jit(solution)/shard_map/gather_step/pallas_call | solution.py:210
  28.2 2.1 %collective-permute-done.6.refs_1_ = f32[328,128]{1,0:T(8,128)S(1)} collective-permute-done((f32[328,128]{1,0:T(8,128)S(1)}, f32[328,128]{1,0:T(8,128)S(1)}, u32[]{:S(2)}, u32[]{:S(2)}) %collective-permute-start.6) | collective-permute-done | bytes 167968 | tf_op jit(solution)/shard_map/ppermute | solution.py:366
  30.3 1.8 %collective-permute-start.9 = (f32[168,128]{1,0:T(8,128)S(1)}, f32[168,128]{1,0:T(8,128)S(1)}, u32[]{:S(2)}, u32[]{:S(2)}) collective-permute-start(f32[168,128]{1,0:T(8,128)S(1)} %slice.6), channel_id=1, source_target_pairs={{0,8},{8,16},{16,24},{24,28},{28,20},{20,12},{12,4},{4,0},{1,9},{9... | collective-permute-start | bytes 258056 | tf_op jit(solution)/shard_map/ppermute | solution.py:371
  32.1 0.0 collective-permute-done.8.refs_2_
  32.1 0.0 copy-start.3
  32.1 0.5 %collective-permute-start.10 = (f32[160,128]{1,0:T(8,128)S(1)}, f32[160,128]{1,0:T(8,128)S(1)}, u32[]{:S(2)}, u32[]{:S(2)}) collective-permute-start(f32[160,128]{1,0:T(8,128)S(1)} %slice.8), channel_id=1, source_target_pairs={{8,0},{16,8},{24,16},{28,24},{20,28},{12,20},{4,12},{0,4},{9,1},{1... | collective-permute-start | bytes 245768 | tf_op jit(solution)/shard_map/ppermute | solution.py:371
  32.6 2.0 %gather_step.7.state_ref = f32[3,128,1024]{2,1,0:T(8,128)S(1)} custom-call(s32[8]{0:T(128)S(1)} %copy-done.5, bf16[6,128,1024]{2,1,0:T(8,128)(2,1)S(1)} %copy-done.1, f32[8,2,1024]{2,1,0:T(2,128)S(1)} %copy-done.2, f32[3,128,1024]{2,1,0:T(8,128)S(1)} %gather_step.6.refs_0_, f32[328,128]{1,0:T(8,128)S(1)} %collective-permute-done.6.refs_1_, ...), custom_call_target="tpu_custom_call" | custom-call | flops 1000000000 | bytes 4194304 | tf_op jit(solution)/shard_map/gather_step/pallas_call | solution.py:210
  34.6 2.2 %collective-permute-done.10.bottom_ref = f32[160,128]{1,0:T(8,128)S(1)} collective-permute-done((f32[160,128]{1,0:T(8,128)S(1)}, f32[160,128]{1,0:T(8,128)S(1)}, u32[]{:S(2)}, u32[]{:S(2)}) %collective-permute-start.10) | collective-permute-done | bytes 81952 | tf_op jit(solution)/shard_map/ppermute | solution.py:371
  36.8 0.0 collective-permute-done.9.top_ref
  36.8 0.0 copy-done.3
  36.8 0.0 copy-start
  36.8 2.6 %back_step.1 = (f32[2,128,128]{2,1,0:T(8,128)S(1)}, f32[2,128,512]{2,1,0:T(8,128)S(1)}) custom-call(s32[8]{0:T(128)S(1)} %copy-done.5, bf16[6,128,1024]{2,1,0:T(8,128)(2,1)S(1)} %copy-done.1, bf16[1024,512]{1,0:T(8,128)(2,1)S(1)} %copy-done.3, f32[8,2,1024]{2,1,0:T(2,128)S(1)} %copy-done.2, f32[3,128,1024]{2,1,0:T(8,128)S(1)} %gather_step.7.state_ref, ...), custom_call_target="tpu_custom_call" | custom-call | tf_op jit(solution)/shard_map/back_step/pallas_call | solution.py:244
  39.4 0.1 collective-permute-start.12
  39.5 1.6 %collective-permute-start.11 = (f32[2,128,128]{2,1,0:T(8,128)S(1)}, f32[2,128,128]{2,1,0:T(8,128)S(1)}, u32[]{:S(2)}, u32[]{:S(2)}) collective-permute-start(f32[2,128,128]{2,1,0:T(8,128)S(1)} %get-tuple-element.32.refs_0_), channel_id=1, source_target_pairs={{0,2},{1,3},{2,0},{3,1},{4,6},{5,7},{6,4},{7,5},{8,10},{9,11},{10,... | collective-permute-start | bytes 393224 | tf_op jit(solution)/shard_map/ppermute | solution.py:324
  41.1 1.0 %correct_step.1 = f32[1024,128]{1,0:T(8,128)} custom-call(f32[2,128,512]{2,1,0:T(8,128)S(1)} %get-tuple-element.34.sub_ref, f32[3,128,1024]{2,1,0:T(8,128)S(1)} %gather_step.4.refs_0_.gain_ref, f32[8,2,1024]{2,1,0:T(2,128)S(1)} %copy-done.2), custom_call_target="tpu_custom_call" | custom-call | flops 1000000000 | bytes 4194304 | tf_op jit(solution)/shard_map/correct_step/pallas_call | solution.py:270
  42.1 0.0 collective-permute-done.12.refs_1_
  42.1 0.0 copy-done
  42.1 1.0 %image_step.3.refs_1_ = f32[2,128,1024]{2,1,0:T(8,128)S(1)} custom-call(f32[2,1024]{1,0:T(2,128)S(1)} %get-tuple-element.33.phase_ref, bf16[4,4,128,1024]{3,2,1,0:T(8,128)(2,1)S(1)} %copy-done, f32[2,128,128]{2,1,0:T(8,128)S(1)} %get-tuple-element.32.refs_0_, f32[2,128,128]{2,1,0:T(8,128)S(1)} %collective-permute-done.12.refs_1_), custom_call_target="tpu_custom_call" | custom-call | flops 1000000000 | bytes 4194304 | tf_op jit(solution)/shard_map/image_step/pallas_call | solution.py:312
  43.1 2.3 %collective-permute-done.11.refs_0_ = f32[2,128,128]{2,1,0:T(8,128)S(1)} collective-permute-done((f32[2,128,128]{2,1,0:T(8,128)S(1)}, f32[2,128,128]{2,1,0:T(8,128)S(1)}, u32[]{:S(2)}, u32[]{:S(2)}) %collective-permute-start.11) | collective-permute-done | bytes 131104 | tf_op jit(solution)/shard_map/ppermute | solution.py:324
  45.4 0.0 collective-permute-start.13
  45.4 0.6 %image_step.4.refs_1_ = f32[2,128,1024]{2,1,0:T(8,128)S(1)} custom-call(f32[2,1024]{1,0:T(2,128)S(1)} %get-tuple-element.33.phase_ref, bf16[4,4,128,1024]{3,2,1,0:T(8,128)(2,1)S(1)} %copy-done, f32[2,128,128]{2,1,0:T(8,128)S(1)} %collective-permute-done.11.refs_0_, f32[2,128,1024]{2,1,0:T(8,128)S(1)} %image_step.3.refs_1_), custom_call_target="tpu_custom_call" | custom-call | flops 1000000000 | bytes 4194304 | tf_op jit(solution)/shard_map/image_step/pallas_call | solution.py:312
  46.0 0.7 %collective-permute-done.13.refs_0_ = f32[2,128,128]{2,1,0:T(8,128)S(1)} collective-permute-done((f32[2,128,128]{2,1,0:T(8,128)S(1)}, f32[2,128,128]{2,1,0:T(8,128)S(1)}, u32[]{:S(2)}, u32[]{:S(2)}) %collective-permute-start.13) | collective-permute-done | bytes 131104 | tf_op jit(solution)/shard_map/ppermute | solution.py:324
  46.8 1.6 %image_step.5 = f32[2,128,1024]{2,1,0:T(8,128)} custom-call(f32[2,1024]{1,0:T(2,128)S(1)} %get-tuple-element.33.phase_ref, bf16[4,4,128,1024]{3,2,1,0:T(8,128)(2,1)S(1)} %copy-done, f32[2,128,128]{2,1,0:T(8,128)S(1)} %collective-permute-done.13.refs_0_, f32[2,128,1024]{2,1,0:T(8,128)S(1)} %image_step.4.refs_1_), custom_call_target="tpu_custom_call" | custom-call | flops 1000000000 | bytes 4194304 | tf_op jit(solution)/shard_map/image_step/pallas_call | solution.py:312
  (3 shorter events, 0.0 us)
Async XLA Ops:
  0.6 1.4 %copy-start.7 = (f32[2,128,1024]{2,1,0:T(8,128)S(1)}, f32[2,128,1024]{2,1,0:T(8,128)}, u32[]{:S(2)}) copy-start(f32[2,128,1024]{2,1,0:T(8,128)} %refs_1_.1) | copy-start | bytes 3145732
  3.2 1.5 %collective-permute-start = (f32[1,2,128,128]{3,2,1,0:T(8,128)S(1)}, f32[1,2,128,128]{3,2,1,0:T(8,128)S(1)}, u32[]{:S(2)}, u32[]{:S(2)}) collective-permute-start(f32[1,2,128,128]{3,2,1,0:T(8,128)S(1)} %get-tuple-element.23), channel_id=1, source_target_pairs={{0,1},{1,0},{2,3},{3,2},{4,5},{5,4},{6,7},{7,6},{8,9},{9,8},{10,11... | collective-permute-start | bytes 393224 | tf_op jit(solution)/shard_map/ppermute | solution.py:324
  5.6 7.2 %copy-start.4 = (f32[1,64,128]{2,1,0:T(8,128)S(1)}, f32[1,64,128]{2,1,0:T(8,128)}, u32[]{:S(2)}) copy-start(f32[1,64,128]{2,1,0:T(8,128)} %refs_3_.1) | copy-start | bytes 98308
  5.6 7.2 %copy-start.6 = (s32[1,64]{1,0:T(1,128)S(1)}, s32[1,64]{1,0:T(1,128)}, u32[]{:S(2)}) copy-start(s32[1,64]{1,0:T(1,128)} %refs_4_.1) | copy-start | bytes 772
  5.6 9.3 %copy-start.1 = (bf16[6,128,1024]{2,1,0:T(8,128)(2,1)S(1)}, bf16[6,128,1024]{2,1,0:T(8,128)(2,1)}, u32[]{:S(2)}) copy-start(bf16[6,128,1024]{2,1,0:T(8,128)(2,1)} %constant.10.clone.b_ref) | copy-start | bytes 4718596
  5.6 9.3 %copy-start.2 = (f32[8,2,1024]{2,1,0:T(2,128)S(1)}, f32[8,2,1024]{2,1,0:T(2,128)}, u32[]{:S(2)}) copy-start(f32[8,2,1024]{2,1,0:T(2,128)} %constant.11.clone.roots_ref) | copy-start | bytes 196612
  5.6 9.3 %copy-start.5 = (s32[8]{0:T(128)S(1)}, s32[8]{0:T(128)}, u32[]{:S(2)}) copy-start(s32[8]{0:T(128)} %starts.9) | copy-start | bytes 100
  5.7 4.7 %collective-permute-start.1 = (f32[1,2,128,128]{3,2,1,0:T(8,128)S(1)}, f32[1,2,128,128]{3,2,1,0:T(8,128)S(1)}, u32[]{:S(2)}, u32[]{:S(2)}) collective-permute-start(f32[1,2,128,128]{3,2,1,0:T(8,128)S(1)} %strips.7), channel_id=1, source_target_pairs={{0,1},{1,0},{2,3},{3,2},{4,5},{5,4},{6,7},{7,6},{8,9},{9,8},{10,11... | collective-permute-start | bytes 393224 | tf_op jit(solution)/shard_map/ppermute | solution.py:324
  6.1 6.7 %collective-permute-start.2 = (f32[1,2,128,128]{3,2,1,0:T(8,128)S(1)}, f32[1,2,128,128]{3,2,1,0:T(8,128)S(1)}, u32[]{:S(2)}, u32[]{:S(2)}) collective-permute-start(f32[1,2,128,128]{3,2,1,0:T(8,128)S(1)} %add.3), channel_id=1, source_target_pairs={{0,2},{1,3},{2,0},{3,1},{4,6},{5,7},{6,4},{7,5},{8,10},{9,11},{10,... | collective-permute-start | bytes 393224 | tf_op jit(solution)/shard_map/ppermute | solution.py:324
  12.9 6.0 %collective-permute-start.3 = (f32[328,128]{1,0:T(8,128)S(1)}, f32[328,128]{1,0:T(8,128)S(1)}, u32[]{:S(2)}, u32[]{:S(2)}) collective-permute-start(f32[328,128]{1,0:T(8,128)S(1)} %pack.1.refs_0_), channel_id=1, source_target_pairs={{0,8},{8,16},{16,24},{24,28},{28,20},{20,12},{12,4},{4,0},{1,9},{9... | collective-permute-start | bytes 503816 | tf_op jit(solution)/shard_map/ppermute | solution.py:366
  14.7 5.7 %collective-permute-start.5 = (f32[328,128]{1,0:T(8,128)S(1)}, f32[328,128]{1,0:T(8,128)S(1)}, u32[]{:S(2)}, u32[]{:S(2)}) collective-permute-start(f32[328,128]{1,0:T(8,128)S(1)} %pack.1.refs_0_), channel_id=1, source_target_pairs={{8,0},{16,8},{24,16},{28,24},{20,28},{12,20},{4,12},{0,4},{9,1},{1... | collective-permute-start | bytes 503816 | tf_op jit(solution)/shard_map/ppermute | solution.py:367
  18.8 5.4 %collective-permute-start.4 = (f32[328,128]{1,0:T(8,128)S(1)}, f32[328,128]{1,0:T(8,128)S(1)}, u32[]{:S(2)}, u32[]{:S(2)}) collective-permute-start(f32[328,128]{1,0:T(8,128)S(1)} %collective-permute-done.3.refs_1_), channel_id=1, source_target_pairs={{0,8},{8,16},{16,24},{24,28},{28,20},{20,12},{12,4},{4,0},{1,9},{9... | collective-permute-start | bytes 503816 | tf_op jit(solution)/shard_map/ppermute | solution.py:366
  20.4 5.4 %collective-permute-start.7 = (f32[328,128]{1,0:T(8,128)S(1)}, f32[328,128]{1,0:T(8,128)S(1)}, u32[]{:S(2)}, u32[]{:S(2)}) collective-permute-start(f32[328,128]{1,0:T(8,128)S(1)} %collective-permute-done.5.refs_2_), channel_id=1, source_target_pairs={{8,0},{16,8},{24,16},{28,24},{20,28},{12,20},{4,12},{0,4},{9,1},{1... | collective-permute-start | bytes 503816 | tf_op jit(solution)/shard_map/ppermute | solution.py:367
  24.2 6.1 %collective-permute-start.6 = (f32[328,128]{1,0:T(8,128)S(1)}, f32[328,128]{1,0:T(8,128)S(1)}, u32[]{:S(2)}, u32[]{:S(2)}) collective-permute-start(f32[328,128]{1,0:T(8,128)S(1)} %collective-permute-done.4.refs_1_), channel_id=1, source_target_pairs={{0,8},{8,16},{16,24},{24,28},{28,20},{20,12},{12,4},{4,0},{1,9},{9... | collective-permute-start | bytes 503816 | tf_op jit(solution)/shard_map/ppermute | solution.py:366
  25.8 6.3 %collective-permute-start.8 = (f32[328,128]{1,0:T(8,128)S(1)}, f32[328,128]{1,0:T(8,128)S(1)}, u32[]{:S(2)}, u32[]{:S(2)}) collective-permute-start(f32[328,128]{1,0:T(8,128)S(1)} %collective-permute-done.7.refs_2_), channel_id=1, source_target_pairs={{8,0},{16,8},{24,16},{28,24},{20,28},{12,20},{4,12},{0,4},{9,1},{1... | collective-permute-start | bytes 503816 | tf_op jit(solution)/shard_map/ppermute | solution.py:367
  30.3 6.5 %collective-permute-start.9 = (f32[168,128]{1,0:T(8,128)S(1)}, f32[168,128]{1,0:T(8,128)S(1)}, u32[]{:S(2)}, u32[]{:S(2)}) collective-permute-start(f32[168,128]{1,0:T(8,128)S(1)} %slice.6), channel_id=1, source_target_pairs={{0,8},{8,16},{16,24},{24,28},{28,20},{20,12},{12,4},{4,0},{1,9},{9... | collective-permute-start | bytes 258056 | tf_op jit(solution)/shard_map/ppermute | solution.py:371
  32.1 4.7 %copy-start.3 = (bf16[1024,512]{1,0:T(8,128)(2,1)S(1)}, bf16[1024,512]{1,0:T(8,128)(2,1)}, u32[]{:S(2)}) copy-start(bf16[1024,512]{1,0:T(8,128)(2,1)} %constant.9.clone.turned_ref) | copy-start | bytes 3145732
  32.1 4.7 %collective-permute-start.10 = (f32[160,128]{1,0:T(8,128)S(1)}, f32[160,128]{1,0:T(8,128)S(1)}, u32[]{:S(2)}, u32[]{:S(2)}) collective-permute-start(f32[160,128]{1,0:T(8,128)S(1)} %slice.8), channel_id=1, source_target_pairs={{8,0},{16,8},{24,16},{28,24},{20,28},{12,20},{4,12},{0,4},{9,1},{1... | collective-permute-start | bytes 245768 | tf_op jit(solution)/shard_map/ppermute | solution.py:371
  36.8 5.3 %copy-start = (bf16[4,4,128,1024]{3,2,1,0:T(8,128)(2,1)S(1)}, bf16[4,4,128,1024]{3,2,1,0:T(8,128)(2,1)}, u32[]{:S(2)}) copy-start(bf16[4,4,128,1024]{3,2,1,0:T(8,128)(2,1)} %constant.8.clone.e_ref) | copy-start | bytes 12582916
  39.4 2.6 %collective-permute-start.12 = (f32[2,128,128]{2,1,0:T(8,128)S(1)}, f32[2,128,128]{2,1,0:T(8,128)S(1)}, u32[]{:S(2)}, u32[]{:S(2)}) collective-permute-start(f32[2,128,128]{2,1,0:T(8,128)S(1)} %get-tuple-element.32.refs_0_), channel_id=1, source_target_pairs={{0,1},{1,0},{2,3},{3,2},{4,5},{5,4},{6,7},{7,6},{8,9},{9,8},{10,11... | collective-permute-start | bytes 393224 | tf_op jit(solution)/shard_map/ppermute | solution.py:324
  39.5 5.9 %collective-permute-start.11 = (f32[2,128,128]{2,1,0:T(8,128)S(1)}, f32[2,128,128]{2,1,0:T(8,128)S(1)}, u32[]{:S(2)}, u32[]{:S(2)}) collective-permute-start(f32[2,128,128]{2,1,0:T(8,128)S(1)} %get-tuple-element.32.refs_0_), channel_id=1, source_target_pairs={{0,2},{1,3},{2,0},{3,1},{4,6},{5,7},{6,4},{7,5},{8,10},{9,11},{10,... | collective-permute-start | bytes 393224 | tf_op jit(solution)/shard_map/ppermute | solution.py:324
  45.4 1.3 %collective-permute-start.13 = (f32[2,128,128]{2,1,0:T(8,128)S(1)}, f32[2,128,128]{2,1,0:T(8,128)S(1)}, u32[]{:S(2)}, u32[]{:S(2)}) collective-permute-start(f32[2,128,128]{2,1,0:T(8,128)S(1)} %collective-permute-done.11.refs_0_), channel_id=1, source_target_pairs={{0,1},{1,0},{2,3},{3,2},{4,5},{5,4},{6,7},{7,6},{8,9},{9,8},{10,11... | collective-permute-start | bytes 393224 | tf_op jit(solution)/shard_map/ppermute | solution.py:324

commit v3 on v2

--- a/solution.py
+++ b/solution.py
@@ -117,7 +117,7 @@
         out_ref[i, 1] = cos[:, height:] - sin[:, :height]
 
 
-def strips(column_start, source, waves, gs, cols_total, first=False, cost=10**9):
+def strips(column_start, source, waves, gs, cols_total, first=False):
     count = waves[0].shape[2]
     height, width = source.shape[1] // (1 if first else 2), source.shape[2]
     operands = ([column_start] if first else []) + [source, *waves]
@@ -128,7 +128,7 @@
         out_shape=[jax.ShapeDtypeStruct((len(gs), 2, count, height), F32)]
         + ([jax.ShapeDtypeStruct((2, 2 * height, width), BF), jax.ShapeDtypeStruct((2, width), F32)] if first else []),
         compiler_params=LIMIT,
-        cost_estimate=pl.CostEstimate(flops=cost, bytes_accessed=cost // 1000, transcendentals=0),
+        cost_estimate=pl.CostEstimate(flops=10**9, bytes_accessed=2 << 20, transcendentals=0),
         name="strips",
     )(*operands)
     return out if first else out[0]
@@ -160,52 +160,64 @@
     )(*terms, weight, row, live)
 
 
-def add_message(starts, r, message, b_ref, roots_ref, state, height, count, rows_total):
-    mine, other = starts[lax.axis_index("frow")], starts[r]
-    strip, rest = message[: 2 * count], message[2 * count :]
-    pc, ps = unit(mine * (r * height + lanes(height)), rows_total, 1.0 / math.sqrt(rows_total))
-    re, im = strip[:count], strip[count:]
-    re, im = re * pc + im * ps, im * pc - re * ps
-    high, low = halves(jnp.concatenate([jnp.concatenate([re, im], 1), jnp.concatenate([im, -re], 1)]))
-    part = lax.dot_general(
-        jnp.concatenate([high, low, high], 1), b_ref[...].reshape(6 * height, rows_total), NN, preferred_element_type=F32
-    )
-    freq = lanes(rows_total)
-    turn = lax.rem(r - lax.axis_index("frow") + rows_total // height, rows_total // height)
-    pc, ps = roots_ref[turn, 0:1], roots_ref[turn, 1:2]
-    re, im = part[:count], part[count:]
-    add_re, add_im = re * pc + im * ps, im * pc - re * ps
-
-    width = message.shape[1]
-    flat = jnp.concatenate([rest, jnp.zeros((width - rest.shape[0], width), F32)])
-    turned = jnp.transpose(flat)
-    weight = turned[:count, :MAXB]
-    row = turned[:MAXB, MAXB : MAXB + 1].astype(jnp.int32)
-    place = jnp.where(row < 0, -1, (row + (other - mine)) & (rows_total - 1))
-    hot = (lanes(rows_total, MAXB) == place).astype(F32).astype(BF)
-    gain = lax.dot_general(
-        jnp.concatenate(halves(weight), 1), jnp.concatenate([hot, hot]), NN, preferred_element_type=F32
-    )
-    gain = gain + (((freq + (mine - other)) & (rows_total - 1)) < SG).astype(F32)
-    if state is None:
-        return add_re, add_im, gain
-    return state[0] + add_re, state[1] + add_im, state[2] + gain
+class Message:
+    def __init__(self, starts, r, message, b_ref, roots_ref, height, count, rows_total):
+        own = lax.axis_index("frow")
+        mine, other = starts[own], starts[r]
+        strip, rest = message[: 2 * count], message[2 * count :]
+        pc, ps = unit(mine * (r * height + lanes(height)), rows_total, 1.0 / math.sqrt(rows_total))
+        re, im = strip[:count], strip[count:]
+        re, im = re * pc + im * ps, im * pc - re * ps
+        high, low = halves(jnp.concatenate([jnp.concatenate([re, im], 1), jnp.concatenate([im, -re], 1)]))
+        self.left = jnp.concatenate([high, low, high], 1)
+
+        width = message.shape[1]
+        flat = jnp.concatenate([rest, jnp.zeros((width - rest.shape[0], width), F32)])
+        turned = jnp.transpose(flat)
+        self.weight = jnp.concatenate(halves(turned[:count, :MAXB]), 1)
+        row = turned[:MAXB, MAXB : MAXB + 1].astype(jnp.int32)
+        self.place = jnp.where(row < 0, -1, (row + (other - mine)) & (rows_total - 1))
+        self.away = mine - other
+        self.turn = lax.rem(r - own + rows_total // height, rows_total // height)
+        self.refs, self.count, self.rows_total = (b_ref, roots_ref), count, rows_total
+
+    def chunk(self, begin, size):
+        b_ref, roots_ref = self.refs
+        part = lax.dot_general(self.left, b_ref[:, begin : begin + size], NN, preferred_element_type=F32)
+        pc, ps = roots_ref[self.turn, 0:1, begin : begin + size], roots_ref[self.turn, 1:2, begin : begin + size]
+        re, im = part[: self.count], part[self.count :]
+        freq = begin + lanes(size)
+        hot = (begin + lanes(size, MAXB) == self.place).astype(F32).astype(BF)
+        gain = lax.dot_general(self.weight, jnp.concatenate([hot, hot]), NN, preferred_element_type=F32)
+        seen = (((freq + self.away) & (self.rows_total - 1)) < SG).astype(F32)
+        return re * pc + im * ps, im * pc - re * ps, gain + seen
+
+
+def chunks(total, size=256):
+    return [(begin, min(size, total - begin)) for begin in range(0, total, size)]
 
 
 def gather_kernel(steps, rows, height, count, starts, b_ref, roots_ref, *refs):
-    state = None
+    state_ref = None
     if len(refs) > len(steps) + 1:
-        state, refs = (refs[0][0], refs[0][1], refs[0][2]), refs[1:]
+        state_ref, refs = refs[0], refs[1:]
     at = ring_place(lax.axis_index("frow"), rows)
-    for step, message in zip(steps, refs):
-        r = ring_block(at + step, rows)
-        state = add_message(starts, r, message[...], b_ref, roots_ref, state, height, count, rows * height)
-    for i in range(3):
-        refs[-1][i] = state[i]
-
-
-def gather_step(starts, table, roots, state, messages, steps, count):
-    height, rows_total = table.shape[1:]
+    found = [
+        Message(starts, ring_block(at + step, rows), message[...], b_ref, roots_ref, height, count, rows * height)
+        for step, message in zip(steps, refs)
+    ]
+    for begin, size in chunks(rows * height):
+        terms = [message.chunk(begin, size) for message in found]
+        for i in range(3):
+            value = sum(term[i] for term in terms)
+            if state_ref is not None:
+                value = value + state_ref[i, :, begin : begin + size]
+            refs[-1][i, :, begin : begin + size] = value
+
+
+def gather_step(starts, table, roots, state, messages, steps, height):
+    rows_total = table.shape[1]
+    count = (messages[0].shape[0] - MAXB - META) // 2
     operands = [table, roots] + ([] if state is None else [state]) + list(messages)
     return pl.pallas_call(
         functools.partial(gather_kernel, steps, rows_total // height, height, count),
@@ -218,20 +230,25 @@
     )(starts, *operands)
 
 
-def back_kernel(rows, height, count, starts, b_ref, turned_ref, roots_ref, state_ref, top_ref, bottom_ref, back_ref, sub_ref):
-    state = state_ref[0], state_ref[1], state_ref[2]
-    message = jnp.concatenate([top_ref[...], bottom_ref[...]])
+def back_kernel(rows, height, count, starts, b_ref, turned_ref, roots_ref, state_ref, message_ref, back_ref, sub_ref):
     rows_total = rows * height
     own = lax.axis_index("frow")
     r = ring_block(ring_place(own, rows) + rows // 2, rows)
-    re, im, gain = add_message(starts, r, message, b_ref, roots_ref, state, height, count, rows_total)
-    sub_ref[0] = re[:, :SG]
-    sub_ref[1] = im[:, :SG]
-    high, low = halves(jnp.concatenate([re * gain, im * gain]))
-    acc = lax.dot_general(high, turned_ref[...], NN, preferred_element_type=F32)
-    acc = acc[:, : 2 * height] + (
-        acc[:, 2 * height :] + lax.dot_general(low, turned_ref[:, : 2 * height], NN, preferred_element_type=F32)
-    )
+    message = Message(starts, r, message_ref[...], b_ref, roots_ref, height, count, rows_total)
+    acc = None
+    for begin, size in chunks(rows_total):
+        terms = message.chunk(begin, size)
+        re, im, gain = [term + state_ref[i, :, begin : begin + size] for i, term in enumerate(terms)]
+        if begin < SG:
+            sub_ref[0, :, begin : begin + size] = re
+            sub_ref[1, :, begin : begin + size] = im
+        high, low = halves(jnp.concatenate([re * gain, im * gain]))
+        table = turned_ref[begin : begin + size]
+        part = lax.dot_general(high, table, NN, preferred_element_type=F32)
+        part = part[:, : 2 * height] + (
+            part[:, 2 * height :] + lax.dot_general(low, table[:, : 2 * height], NN, preferred_element_type=F32)
+        )
+        acc = part if acc is None else acc + part
     re = acc[:count, :height] - acc[count:, height:]
     im = acc[count:, :height] + acc[:count, height:]
     pc, ps = unit(starts[own] * (own * height + lanes(height)), rows_total, 1.0 / math.sqrt(rows_total))
@@ -239,11 +256,11 @@
     back_ref[1] = jnp.transpose(im * pc + re * ps)
 
 
-def back_step(starts, table, turned, roots, state, parts, count):
-    height, rows_total = table.shape[1:]
+def back_step(starts, table, turned, roots, state, message, height):
+    count, rows_total = state.shape[1:]
     return pl.pallas_call(
         functools.partial(back_kernel, rows_total // height, height, count),
-        in_specs=[SMEM] + [VMEM] * 6,
+        in_specs=[SMEM] + [VMEM] * 5,
         out_specs=[VMEM] * 2,
         out_shape=[
             jax.ShapeDtypeStruct((2, height, count), F32),
@@ -251,7 +268,7 @@
         ],
         compiler_params=LIMIT,
         name="back_step",
-    )(starts, table, turned, roots, state, *parts)
+    )(starts, table, turned, roots, state, message)
 
 
 def correct_kernel(sub_ref, gain_ref, roots_ref, out_ref):
@@ -280,40 +297,57 @@
     return jnp.transpose(out, (0, 2, 1, 3)).reshape(1, count, 2, SG)
 
 
-def image_kernel(gs, cols_total, first, last, phase_ref, e_ref, *refs):
+def image_kernel(gs, first, last, phase_ref, e_ref, *refs):
     backs, refs = refs[: len(gs)], refs[len(gs) :]
-    out_ref = refs[-1]
-    _, height, width = out_ref.shape
-    count = e_ref.shape[2]
+    acc_ref = None if first else refs[0]
+    out_ref = refs[0 if first else 1]
+    if last:
+        scratch, sems = refs[-2:]
+    width = e_ref.shape[-1]
+    height, count = backs[0].shape[1:]
     own = lax.axis_index("fcol")
-    acc = None if first else jnp.concatenate([refs[0][0], refs[0][1]])
+    left = []
     for back, g in zip(backs, gs):
         freq = (own ^ g) * count + lanes(count)
-        pc, ps = unit(freq * (own * width), cols_total)
+        pc, ps = unit(freq * (own * width), e_ref.shape[0] * width)
         re, im = back[0], back[1]
         re, im = re * pc - im * ps, im * pc + re * ps
-        left = halves(jnp.concatenate([jnp.concatenate([re, -im], 1), jnp.concatenate([im, re], 1)]))
-        right = (e_ref[own ^ g, 0:2].reshape(2 * count, width), e_ref[own ^ g, 2:4].reshape(2 * count, width))
-        part = dot3(left, right, NN)
-        acc = part if acc is None else acc + part
-    re, im = acc[:height], acc[height:]
-    if last:
-        pc, ps = phase_ref[0:1], phase_ref[1:2]
-        re, im = re * pc - im * ps, im * pc + re * ps
-    out_ref[0] = re
-    out_ref[1] = im
-
-
-def image_step(phase, table, gs, backs, acc, last, cols_total):
+        left.append(halves(jnp.concatenate([jnp.concatenate([re, -im], 1), jnp.concatenate([im, re], 1)])))
+    copies = []
+    for begin, size in chunks(width):
+        columns = slice(begin, begin + size)
+        acc = None if first else jnp.concatenate([acc_ref[0, :, columns], acc_ref[1, :, columns]])
+        for (high, low), g in zip(left, gs):
+            e = e_ref[own ^ g, 0:2, :, columns], e_ref[own ^ g, 2:4, :, columns]
+            part = dot3((high, low), [value.reshape(2 * count, size) for value in e], NN)
+            acc = part if acc is None else acc + part
+        re, im = acc[:height], acc[height:]
+        if last:
+            pc, ps = phase_ref[0:1, columns], phase_ref[1:2, columns]
+            scratch[0, :, columns] = re * pc - im * ps
+            scratch[1, :, columns] = im * pc + re * ps
+            copies.append(
+                pltpu.make_async_copy(scratch.at[:, :, columns], out_ref.at[:, :, columns], sems.at[len(copies)])
+            )
+            copies[-1].start()
+        else:
+            out_ref[0, :, columns] = re
+            out_ref[1, :, columns] = im
+    for copy in copies:
+        copy.wait()
+
+
+def image_step(phase, table, gs, backs, acc, last):
     width = table.shape[-1]
     height = backs[0].shape[1]
     first = acc is None
     operands = list(backs) + ([] if first else [acc])
     return pl.pallas_call(
-        functools.partial(image_kernel, tuple(gs), cols_total, first, last),
+        functools.partial(image_kernel, tuple(gs), first, last),
         in_specs=[VMEM] * (2 + len(operands)),
-        out_specs=VMEM,
+        out_specs=pl.BlockSpec(memory_space=pl.ANY) if last else VMEM,
         out_shape=jax.ShapeDtypeStruct((2, height, width), F32),
+        scratch_shapes=[pltpu.VMEM((2, height, width), F32), pltpu.SemaphoreType.DMA((len(chunks(width)),))] if last else [],
         compiler_params=LIMIT,
         cost_estimate=pl.CostEstimate(flops=10**9, bytes_accessed=4 << 20, transcendentals=0),
         name="image_step",
@@ -335,23 +369,22 @@
     e_table = jnp.asarray(wave_table(SG, width, cols_total).reshape(4, cols, count, width).transpose(1, 0, 2, 3))
     b_table = wave_table(height, rows_total, rows_total)
     turned = jnp.asarray(b_table.reshape(4 * height, rows_total).T.copy())
-    b_table = jnp.asarray(np.concatenate([b_table[:2], b_table]))
+    b_table = jnp.asarray(np.concatenate([b_table[:2], b_table]).reshape(6 * height, rows_total))
     angle = np.arange(rows)[:, None] * np.arange(rows_total)[None, :] % rows * (2.0 * np.pi / rows)
     roots = jnp.asarray(np.stack([np.cos(angle), np.sin(angle)], 1).astype(np.float32))
 
     top = cols // 2
-    groups = [range(top + 1, cols, 2), range(top, cols, 2), range(1, top, 2), range(0, top, 2)]
-    groups = [tuple(group) for group in groups]
     column_start = column_start.reshape(1, 1)
     waves = waves_of(count, width, cols_total)
+    groups = [tuple(range(1, cols, 2)), tuple(range(top, cols, 2)), tuple(range(0, top, 2))]
     sent, z, phase = strips(column_start, facets, waves, groups[0], cols_total, first=True)
-    far = strips(column_start, z, waves, groups[1], cols_total) + swap(sent, "fcol", 1)
-    far, z = lax.optimization_barrier((far, z))
-    far = swap(far, "fcol", top)
-    sent = strips(column_start, z, waves, groups[2], cols_total, cost=10**6)
-    terms = [strips(column_start, z, waves, groups[3], cols_total, cost=10**6), swap(sent, "fcol", 1), far]
+    far = strips(column_start, z, waves, groups[1], cols_total)
+    got = swap(sent, "fcol", 1)
+    far, got = lax.optimization_barrier((far + got[top // 2 :], got))
+    terms = [strips(column_start, z, waves, groups[2], cols_total), got, swap(far, "fcol", top)]
     bit = 2
     while bit < top:
+        terms[1] = terms[1][: terms[0].shape[0]]
         pairs = sum(terms).reshape((-1, 2) + far.shape[1:])
         terms = [pairs[:, 0], swap(pairs[:, 1], "fcol", bit)]
         bit *= 2
@@ -360,16 +393,15 @@
     order = list(range(0, rows, 2)) + list(range(rows - 1, 0, -2))
     ahead = [(order[i], order[(i + 1) % rows]) for i in range(rows)]
     behind = [(b, a) for a, b in ahead]
-    first_state = state = gather_step(subgrid_start, b_table, roots, None, [own], (0,), count)
+    first_state = state = gather_step(subgrid_start, b_table, roots, None, [own], (0,), height)
     up = down = own
     for step in range(1, rows // 2):
         up = lax.ppermute(up, "frow", ahead)
         down = lax.ppermute(down, "frow", behind)
         up, state = lax.optimization_barrier((up, state))
-        state = gather_step(subgrid_start, b_table, roots, state, [up, down], (-step, step), count)
-    cut = (own.shape[0] // 2 + 7) // 8 * 8
-    parts = [lax.ppermute(up[:cut], "frow", ahead), lax.ppermute(down[cut:], "frow", behind)]
-    back, sub = back_step(subgrid_start, b_table, turned, roots, state, parts, count)
+        state = gather_step(subgrid_start, b_table, roots, state, [up, down], (-step, step), height)
+    up = lax.ppermute(up, "frow", ahead)
+    back, sub = back_step(subgrid_start, b_table, turned, roots, state, up, height)
 
     near, far = {0: back}, {top: swap(back, "fcol", top)}
 
@@ -377,7 +409,7 @@
         return {g ^ bit: swap(b, "fcol", bit) for g, b in blocks.items()}
 
     def image(blocks, acc, last=False):
-        return image_step(phase, e_table, blocks.keys(), list(blocks.values()), acc, last, cols_total)
+        return image_step(phase, e_table, blocks.keys(), list(blocks.values()), acc, last)
 
     bit = top // 2
     while bit >= 1:

time: 48.5 us -> 46.7 us (0.963)
  Pallas kernels: 18.5 us -> 17.8 us
  starting transfers between devices: 13.7 us -> 13.1 us
  waiting for transfers between devices: 14 us -> 13.4 us
    ppermute x2 -> x0, starting transfers between devices: 2.31 us -> none  [the longest x1 1.79 us: per_device(): lax.ppermute(up[:cut], 'frow', ahead)]
    ppermute x2 -> x0, waiting for transfers between devices: 2.2 us -> none  [the longest x1 2.2 us: per_device(): lax.ppermute(down[cut:], 'frow', behind)]
    ppermute x3 -> x4, waiting for transfers between devices: 6.15 us -> 7.99 us  [per_device(): up = lax.ppermute(up, 'frow', ahead)]
    ppermute x3 -> x4, starting transfers between devices: 4.93 us -> 6.57 us  [per_device(): up = lax.ppermute(up, 'frow', ahead)]
    pallas_call x4 -> x3, Pallas kernels: 3.81 us -> 3.51 us  [strips(): pl.pallas_call(functools.partial(strip_kernel, gs, cols_total, int(first)...]
    ppermute x6 -> x5, waiting for transfers between devices: 5.6 us -> 5.37 us  [swap(): lax.ppermute(value, axis, [(i, i ^ bit) for i in range(lax.axis_size(axis...]
    ppermute x6 -> x5, starting transfers between devices: 5.28 us -> 5.25 us  [swap(): lax.ppermute(value, axis, [(i, i ^ bit) for i in range(lax.axis_size(axis...]
  transfers between devices with their start and end apart: 14 -> 12, of which waited for: 8 -> 8; matrix products, arithmetic and copies ran while one was open for 0% -> 0% of each run, Pallas kernels for 24% -> 25%
where the time goes in v3:
time: 46.7 us; the launch traced here: 46.5 us
  Pallas kernels  17.8 us (38%)
  waiting for transfers between devices  13.4 us (29%)
  starting transfers between devices  13.1 us (28%)
  between operations  2.26 us (5%)
    ppermute x4, waiting for transfers between devices, per_device(): up = lax.ppermute(up, 'frow', ahead)  7.99 us
    pallas_call x4, Pallas kernels, gather_step(): pl.pallas_call(functools.partial(gather_kernel, steps, rows_total // heig...  7.05 us
    ppermute x4, starting transfers between devices, per_device(): up = lax.ppermute(up, 'frow', ahead)  6.57 us
    ppermute x5, waiting for transfers between devices, swap(): lax.ppermute(value, axis, [(i, i ^ bit) for i in range(lax.axis_size(axis...  5.37 us
    ppermute x5, starting transfers between devices, swap(): lax.ppermute(value, axis, [(i, i ^ bit) for i in range(lax.axis_size(axis...  5.25 us
    pallas_call x3, Pallas kernels, strips(): pl.pallas_call(functools.partial(strip_kernel, gs, cols_total, int(first)...  3.51 us
    pallas_call x3, Pallas kernels, image_step(): pl.pallas_call(functools.partial(image_kernel, tuple(gs), first, last), i...  3.12 us
    pallas_call x1, Pallas kernels, back_step(): pl.pallas_call(functools.partial(back_kernel, rows_total // height, heigh...  2.31 us
  transfers between devices with their start and end apart: 12, of which 8 were waited for; matrix products, arithmetic and copies ran while one was open for 0% of the time, Pallas kernels for 25%

profile of v3, /device:TPU:0, one launch (start us, length us, event | category | flops | bytes accessed | tf_op | source)
XLA Modules:
  0.0 46.5 jit_solution(13386250415811862544)
XLA Ops:
  0.6 0.0 copy-start.7
  0.6 0.7 %waves.1 = (f32[4,2,128,128]{3,2,1,0:T(8,128)S(1)}, f32[4,2,128,128]{3,2,1,0:T(8,128)S(1)}) custom-call(), custom_call_target="tpu_custom_call" | custom-call | flops 1000000000 | bytes 2097152 | tf_op jit(solution)/shard_map/waves/pallas_call | solution.py:82
  2.0 0.0 copy-done.7
  2.0 1.7 %strips.3 = (f32[2,2,128,128]{3,2,1,0:T(8,128)S(1)}, bf16[2,256,1024]{2,1,0:T(8,128)(2,1)S(1)}, f32[2,1024]{1,0:T(2,128)S(1)}) custom-call(s32[1,1]{1,0:T(1,128)} %bitcast.7.refs_0_, f32[2,128,1024]{2,1,0:T(8,128)S(1)} %copy-done.7, f32[4,2,128,128]{3,2,1,0:T(8,128)S(1)} %get-tuple-element.20.refs_2_.refs_1_, ...), custom_call_target="tpu_custom_call" | custom-call | flops 1000000000 | bytes 2097152 | tf_op jit(solution)/shard_map/strips/pallas_call | solution.py:124
  3.8 0.5 %collective-permute-start = (f32[2,2,128,128]{3,2,1,0:T(8,128)S(1)}, f32[2,2,128,128]{3,2,1,0:T(8,128)S(1)}, u32[]{:S(2)}, u32[]{:S(2)}) collective-permute-start(f32[2,2,128,128]{3,2,1,0:T(8,128)S(1)} %get-tuple-element.23), channel_id=1, source_target_pairs={{0,1},{1,0},{2,3},{3,2},{4,5},{5,4},{6,7},{7,6},{8,9},{9,8},{10,11... | collective-permute-start | bytes 786440 | tf_op jit(solution)/shard_map/ppermute | solution.py:358
  4.3 0.9 %strips.5 = f32[1,2,128,128]{3,2,1,0:T(8,128)S(1)} custom-call(bf16[2,256,1024]{2,1,0:T(8,128)(2,1)S(1)} %get-tuple-element.22.refs_0_, f32[4,2,128,128]{3,2,1,0:T(8,128)S(1)} %get-tuple-element.20.refs_2_.refs_1_, f32[4,2,128,128]{3,2,1,0:T(8,128)S(1)} %get-tuple-element.21.refs_3_.refs_2_), custom_call_target="tpu_custom_call" | custom-call | flops 1000000000 | bytes 2097152 | tf_op jit(solution)/shard_map/strips/pallas_call | solution.py:124
  5.2 0.3 collective-permute-done.refs_1_
  5.5 3.0 %collective-permute-start.1 = (f32[1,2,128,128]{3,2,1,0:T(8,128)S(1)}, f32[1,2,128,128]{3,2,1,0:T(8,128)S(1)}, u32[]{:S(2)}, u32[]{:S(2)}) collective-permute-start(f32[1,2,128,128]{3,2,1,0:T(8,128)S(1)} %slice_add_fusion), channel_id=1, source_target_pairs={{0,2},{1,3},{2,0},{3,1},{4,6},{5,7},{6,4},{7,5},{8,10},{9,11},{10,... | collective-permute-start | bytes 393224 | tf_op jit(solution)/shard_map/ppermute | solution.py:358
  9.1 0.0 copy-start.4
  9.1 0.0 copy-start.6
  9.1 0.0 copy-start.1
  9.1 0.0 copy-start.2
  9.1 0.0 copy-start.5
  9.1 0.9 %strips.4.refs_0_ = f32[1,2,128,128]{3,2,1,0:T(8,128)S(1)} custom-call(bf16[2,256,1024]{2,1,0:T(8,128)(2,1)S(1)} %get-tuple-element.22.refs_0_, f32[4,2,128,128]{3,2,1,0:T(8,128)S(1)} %get-tuple-element.20.refs_2_.refs_1_, f32[4,2,128,128]{3,2,1,0:T(8,128)S(1)} %get-tuple-element.21.refs_3_.refs_2_), custom_call_target="tpu_custom_call" | custom-call | flops 1000000000 | bytes 2097152 | tf_op jit(solution)/shard_map/strips/pallas_call | solution.py:124
  10.0 2.2 %collective-permute-done.1.refs_2_ = f32[1,2,128,128]{3,2,1,0:T(8,128)S(1)} collective-permute-done((f32[1,2,128,128]{3,2,1,0:T(8,128)S(1)}, f32[1,2,128,128]{3,2,1,0:T(8,128)S(1)}, u32[]{:S(2)}, u32[]{:S(2)}) %collective-permute-start.1) | collective-permute-done | bytes 131104 | tf_op jit(solution)/shard_map/ppermute | solution.py:358
  12.2 0.0 copy-done.4
  12.2 0.0 copy-done.6
  12.2 0.1 pack.1.refs_0_
  12.3 1.8 %collective-permute-start.2 = (f32[328,128]{1,0:T(8,128)S(1)}, f32[328,128]{1,0:T(8,128)S(1)}, u32[]{:S(2)}, u32[]{:S(2)}) collective-permute-start(f32[328,128]{1,0:T(8,128)S(1)} %pack.1.refs_0_), channel_id=1, source_target_pairs={{0,8},{8,16},{16,24},{24,28},{28,20},{20,12},{12,4},{4,0},{1,9},{9... | collective-permute-start | bytes 503816 | tf_op jit(solution)/shard_map/ppermute | solution.py:399
  14.1 0.2 collective-permute-start.4
  14.3 0.0 copy-done.1
  14.3 0.0 copy-done.2
  14.3 0.0 copy-done.5
  14.3 1.3 %gather_step.4.refs_0_.gain_ref = f32[3,128,1024]{2,1,0:T(8,128)S(1)} custom-call(s32[8]{0:T(128)S(1)} %copy-done.5, bf16[768,1024]{1,0:T(8,128)(2,1)S(1)} %copy-done.1, f32[8,2,1024]{2,1,0:T(2,128)S(1)} %copy-done.2, f32[328,128]{1,0:T(8,128)S(1)} %pack.1.refs_0_), custom_call_target="tpu_custom_call" | custom-call | flops 1000000000 | bytes 4194304 | tf_op jit(solution)/shard_map/gather_step/pallas_call | solution.py:222
  15.7 2.5 %collective-permute-done.2.refs_1_ = f32[328,128]{1,0:T(8,128)S(1)} collective-permute-done((f32[328,128]{1,0:T(8,128)S(1)}, f32[328,128]{1,0:T(8,128)S(1)}, u32[]{:S(2)}, u32[]{:S(2)}) %collective-permute-start.2) | collective-permute-done | bytes 167968 | tf_op jit(solution)/shard_map/ppermute | solution.py:399
  18.1 1.5 %collective-permute-start.3 = (f32[328,128]{1,0:T(8,128)S(1)}, f32[328,128]{1,0:T(8,128)S(1)}, u32[]{:S(2)}, u32[]{:S(2)}) collective-permute-start(f32[328,128]{1,0:T(8,128)S(1)} %collective-permute-done.2.refs_1_), channel_id=1, source_target_pairs={{0,8},{8,16},{16,24},{24,28},{28,20},{20,12},{12,4},{4,0},{1,9},{9... | collective-permute-start | bytes 503816 | tf_op jit(solution)/shard_map/ppermute | solution.py:399
  19.6 0.0 collective-permute-done.4.refs_2_
  19.6 0.5 %collective-permute-start.6 = (f32[328,128]{1,0:T(8,128)S(1)}, f32[328,128]{1,0:T(8,128)S(1)}, u32[]{:S(2)}, u32[]{:S(2)}) collective-permute-start(f32[328,128]{1,0:T(8,128)S(1)} %collective-permute-done.4.refs_2_), channel_id=1, source_target_pairs={{8,0},{16,8},{24,16},{28,24},{20,28},{12,20},{4,12},{0,4},{9,1},{1... | collective-permute-start | bytes 503816 | tf_op jit(solution)/shard_map/ppermute | solution.py:400
  20.2 1.9 %gather_step.5.refs_0_ = f32[3,128,1024]{2,1,0:T(8,128)S(1)} custom-call(s32[8]{0:T(128)S(1)} %copy-done.5, bf16[768,1024]{1,0:T(8,128)(2,1)S(1)} %copy-done.1, f32[8,2,1024]{2,1,0:T(2,128)S(1)} %copy-done.2, f32[3,128,1024]{2,1,0:T(8,128)S(1)} %gather_step.4.refs_0_.gain_ref, f32[328,128]{1,0:T(8,128)S(1)} %collective-permute-done.2.refs_1_, ...), custom_call_target="tpu_custom_call" | custom-call | flops 1000000000 | bytes 4194304 | tf_op jit(solution)/shard_map/gather_step/pallas_call | solution.py:222
  22.1 1.4 %collective-permute-done.3.refs_1_ = f32[328,128]{1,0:T(8,128)S(1)} collective-permute-done((f32[328,128]{1,0:T(8,128)S(1)}, f32[328,128]{1,0:T(8,128)S(1)}, u32[]{:S(2)}, u32[]{:S(2)}) %collective-permute-start.3) | collective-permute-done | bytes 167968 | tf_op jit(solution)/shard_map/ppermute | solution.py:399
  23.5 1.6 %collective-permute-start.5 = (f32[328,128]{1,0:T(8,128)S(1)}, f32[328,128]{1,0:T(8,128)S(1)}, u32[]{:S(2)}, u32[]{:S(2)}) collective-permute-start(f32[328,128]{1,0:T(8,128)S(1)} %collective-permute-done.3.refs_1_), channel_id=1, source_target_pairs={{0,8},{8,16},{16,24},{24,28},{28,20},{20,12},{12,4},{4,0},{1,9},{9... | collective-permute-start | bytes 503816 | tf_op jit(solution)/shard_map/ppermute | solution.py:399
  25.1 0.0 collective-permute-done.6.refs_2_
  25.1 0.5 %collective-permute-start.7 = (f32[328,128]{1,0:T(8,128)S(1)}, f32[328,128]{1,0:T(8,128)S(1)}, u32[]{:S(2)}, u32[]{:S(2)}) collective-permute-start(f32[328,128]{1,0:T(8,128)S(1)} %collective-permute-done.6.refs_2_), channel_id=1, source_target_pairs={{8,0},{16,8},{24,16},{28,24},{20,28},{12,20},{4,12},{0,4},{9,1},{1... | collective-permute-start | bytes 503816 | tf_op jit(solution)/shard_map/ppermute | solution.py:400
  25.6 1.9 %gather_step.6.refs_0_ = f32[3,128,1024]{2,1,0:T(8,128)S(1)} custom-call(s32[8]{0:T(128)S(1)} %copy-done.5, bf16[768,1024]{1,0:T(8,128)(2,1)S(1)} %copy-done.1, f32[8,2,1024]{2,1,0:T(2,128)S(1)} %copy-done.2, f32[3,128,1024]{2,1,0:T(8,128)S(1)} %gather_step.5.refs_0_, f32[328,128]{1,0:T(8,128)S(1)} %collective-permute-done.3.refs_1_, ...), custom_call_target="tpu_custom_call" | custom-call | flops 1000000000 | bytes 4194304 | tf_op jit(solution)/shard_map/gather_step/pallas_call | solution.py:222
  27.5 0.0 copy-start.3
  27.5 2.4 %collective-permute-done.5.refs_1_ = f32[328,128]{1,0:T(8,128)S(1)} collective-permute-done((f32[328,128]{1,0:T(8,128)S(1)}, f32[328,128]{1,0:T(8,128)S(1)}, u32[]{:S(2)}, u32[]{:S(2)}) %collective-permute-start.5) | collective-permute-done | bytes 167968 | tf_op jit(solution)/shard_map/ppermute | solution.py:399
  29.9 1.7 %collective-permute-start.8 = (f32[328,128]{1,0:T(8,128)S(1)}, f32[328,128]{1,0:T(8,128)S(1)}, u32[]{:S(2)}, u32[]{:S(2)}) collective-permute-start(f32[328,128]{1,0:T(8,128)S(1)} %collective-permute-done.5.refs_1_), channel_id=1, source_target_pairs={{0,8},{8,16},{16,24},{24,28},{28,20},{20,12},{12,4},{4,0},{1,9},{9... | collective-permute-start | bytes 503816 | tf_op jit(solution)/shard_map/ppermute | solution.py:403
  31.6 0.0 collective-permute-done.7.refs_2_
  31.6 1.9 %gather_step.7.state_ref = f32[3,128,1024]{2,1,0:T(8,128)S(1)} custom-call(s32[8]{0:T(128)S(1)} %copy-done.5, bf16[768,1024]{1,0:T(8,128)(2,1)S(1)} %copy-done.1, f32[8,2,1024]{2,1,0:T(2,128)S(1)} %copy-done.2, f32[3,128,1024]{2,1,0:T(8,128)S(1)} %gather_step.6.refs_0_, f32[328,128]{1,0:T(8,128)S(1)} %collective-permute-done.5.refs_1_, ...), custom_call_target="tpu_custom_call" | custom-call | flops 1000000000 | bytes 4194304 | tf_op jit(solution)/shard_map/gather_step/pallas_call | solution.py:222
  33.5 1.7 %collective-permute-done.8.message_ref = f32[328,128]{1,0:T(8,128)S(1)} collective-permute-done((f32[328,128]{1,0:T(8,128)S(1)}, f32[328,128]{1,0:T(8,128)S(1)}, u32[]{:S(2)}, u32[]{:S(2)}) %collective-permute-start.8) | collective-permute-done | bytes 167968 | tf_op jit(solution)/shard_map/ppermute | solution.py:403
  35.2 0.0 copy-done.3
  35.2 0.0 copy-start
  35.2 2.3 %back_step.1 = (f32[2,128,128]{2,1,0:T(8,128)S(1)}, f32[2,128,512]{2,1,0:T(8,128)S(1)}) custom-call(s32[8]{0:T(128)S(1)} %copy-done.5, bf16[768,1024]{1,0:T(8,128)(2,1)S(1)} %copy-done.1, bf16[1024,512]{1,0:T(8,128)(2,1)S(1)} %copy-done.3, f32[8,2,1024]{2,1,0:T(2,128)S(1)} %copy-done.2, f32[3,128,1024]{2,1,0:T(8,128)S(1)} %gather_step.7.state_ref, ...), custom_call_target="tpu_custom_call" | custom-call | tf_op jit(solution)/shard_map/back_step/pallas_call | solution.py:261
  37.5 0.1 collective-permute-start.10
  37.6 1.7 %collective-permute-start.9 = (f32[2,128,128]{2,1,0:T(8,128)S(1)}, f32[2,128,128]{2,1,0:T(8,128)S(1)}, u32[]{:S(2)}, u32[]{:S(2)}) collective-permute-start(f32[2,128,128]{2,1,0:T(8,128)S(1)} %get-tuple-element.32.refs_0_), channel_id=1, source_target_pairs={{0,2},{1,3},{2,0},{3,1},{4,6},{5,7},{6,4},{7,5},{8,10},{9,11},{10,... | collective-permute-start | bytes 393224 | tf_op jit(solution)/shard_map/ppermute | solution.py:358
  39.3 1.0 %correct_step.1 = f32[1024,128]{1,0:T(8,128)} custom-call(f32[2,128,512]{2,1,0:T(8,128)S(1)} %get-tuple-element.34.sub_ref, f32[3,128,1024]{2,1,0:T(8,128)S(1)} %gather_step.4.refs_0_.gain_ref, f32[8,2,1024]{2,1,0:T(2,128)S(1)} %copy-done.2), custom_call_target="tpu_custom_call" | custom-call | flops 1000000000 | bytes 4194304 | tf_op jit(solution)/shard_map/correct_step/pallas_call | solution.py:287
  40.3 0.0 collective-permute-done.10.refs_1_
  40.3 0.0 copy-done
  40.3 1.0 %image_step.3.refs_1_ = f32[2,128,1024]{2,1,0:T(8,128)S(1)} custom-call(f32[2,1024]{1,0:T(2,128)S(1)} %get-tuple-element.33.phase_ref, bf16[4,4,128,1024]{3,2,1,0:T(8,128)(2,1)S(1)} %copy-done, f32[2,128,128]{2,1,0:T(8,128)S(1)} %get-tuple-element.32.refs_0_, f32[2,128,128]{2,1,0:T(8,128)S(1)} %collective-permute-done.10.refs_1_), custom_call_target="tpu_custom_call" | custom-call | flops 1000000000 | bytes 4194304 | tf_op jit(solution)/shard_map/image_step/pallas_call | solution.py:345
  41.3 2.2 %collective-permute-done.9.refs_0_ = f32[2,128,128]{2,1,0:T(8,128)S(1)} collective-permute-done((f32[2,128,128]{2,1,0:T(8,128)S(1)}, f32[2,128,128]{2,1,0:T(8,128)S(1)}, u32[]{:S(2)}, u32[]{:S(2)}) %collective-permute-start.9) | collective-permute-done | bytes 131104 | tf_op jit(solution)/shard_map/ppermute | solution.py:358
  43.5 0.0 collective-permute-start.11
  43.5 0.6 %image_step.4.refs_1_ = f32[2,128,1024]{2,1,0:T(8,128)S(1)} custom-call(f32[2,1024]{1,0:T(2,128)S(1)} %get-tuple-element.33.phase_ref, bf16[4,4,128,1024]{3,2,1,0:T(8,128)(2,1)S(1)} %copy-done, f32[2,128,128]{2,1,0:T(8,128)S(1)} %collective-permute-done.9.refs_0_, f32[2,128,1024]{2,1,0:T(8,128)S(1)} %image_step.3.refs_1_), custom_call_target="tpu_custom_call" | custom-call | flops 1000000000 | bytes 4194304 | tf_op jit(solution)/shard_map/image_step/pallas_call | solution.py:345
  44.1 0.7 %collective-permute-done.11.refs_0_ = f32[2,128,128]{2,1,0:T(8,128)S(1)} collective-permute-done((f32[2,128,128]{2,1,0:T(8,128)S(1)}, f32[2,128,128]{2,1,0:T(8,128)S(1)}, u32[]{:S(2)}, u32[]{:S(2)}) %collective-permute-start.11) | collective-permute-done | bytes 131104 | tf_op jit(solution)/shard_map/ppermute | solution.py:358
  44.9 1.5 %image_step.5 = f32[2,128,1024]{2,1,0:T(8,128)} custom-call(f32[2,1024]{1,0:T(2,128)S(1)} %get-tuple-element.33.phase_ref, bf16[4,4,128,1024]{3,2,1,0:T(8,128)(2,1)S(1)} %copy-done, f32[2,128,128]{2,1,0:T(8,128)S(1)} %collective-permute-done.11.refs_0_, f32[2,128,1024]{2,1,0:T(8,128)S(1)} %image_step.4.refs_1_), custom_call_target="tpu_custom_call" | custom-call | flops 1000000000 | bytes 4194304 | tf_op jit(solution)/shard_map/image_step/pallas_call | solution.py:345
  (1 shorter events, 0.0 us)
Async XLA Ops:
  0.6 1.4 %copy-start.7 = (f32[2,128,1024]{2,1,0:T(8,128)S(1)}, f32[2,128,1024]{2,1,0:T(8,128)}, u32[]{:S(2)}) copy-start(f32[2,128,1024]{2,1,0:T(8,128)} %refs_1_.1) | copy-start | bytes 3145732
  3.8 1.7 %collective-permute-start = (f32[2,2,128,128]{3,2,1,0:T(8,128)S(1)}, f32[2,2,128,128]{3,2,1,0:T(8,128)S(1)}, u32[]{:S(2)}, u32[]{:S(2)}) collective-permute-start(f32[2,2,128,128]{3,2,1,0:T(8,128)S(1)} %get-tuple-element.23), channel_id=1, source_target_pairs={{0,1},{1,0},{2,3},{3,2},{4,5},{5,4},{6,7},{7,6},{8,9},{9,8},{10,11... | collective-permute-start | bytes 786440 | tf_op jit(solution)/shard_map/ppermute | solution.py:358
  5.5 6.7 %collective-permute-start.1 = (f32[1,2,128,128]{3,2,1,0:T(8,128)S(1)}, f32[1,2,128,128]{3,2,1,0:T(8,128)S(1)}, u32[]{:S(2)}, u32[]{:S(2)}) collective-permute-start(f32[1,2,128,128]{3,2,1,0:T(8,128)S(1)} %slice_add_fusion), channel_id=1, source_target_pairs={{0,2},{1,3},{2,0},{3,1},{4,6},{5,7},{6,4},{7,5},{8,10},{9,11},{10,... | collective-permute-start | bytes 393224 | tf_op jit(solution)/shard_map/ppermute | solution.py:358
  9.1 3.1 %copy-start.4 = (f32[1,64,128]{2,1,0:T(8,128)S(1)}, f32[1,64,128]{2,1,0:T(8,128)}, u32[]{:S(2)}) copy-start(f32[1,64,128]{2,1,0:T(8,128)} %refs_3_.1) | copy-start | bytes 98308
  9.1 3.1 %copy-start.6 = (s32[1,64]{1,0:T(1,128)S(1)}, s32[1,64]{1,0:T(1,128)}, u32[]{:S(2)}) copy-start(s32[1,64]{1,0:T(1,128)} %refs_4_.1) | copy-start | bytes 772
  9.1 5.2 %copy-start.1 = (bf16[768,1024]{1,0:T(8,128)(2,1)S(1)}, bf16[768,1024]{1,0:T(8,128)(2,1)}, u32[]{:S(2)}) copy-start(bf16[768,1024]{1,0:T(8,128)(2,1)} %constant.10.clone.b_ref) | copy-start | bytes 4718596
  9.1 5.2 %copy-start.2 = (f32[8,2,1024]{2,1,0:T(2,128)S(1)}, f32[8,2,1024]{2,1,0:T(2,128)}, u32[]{:S(2)}) copy-start(f32[8,2,1024]{2,1,0:T(2,128)} %constant.11.clone.roots_ref) | copy-start | bytes 196612
  9.1 5.2 %copy-start.5 = (s32[8]{0:T(128)S(1)}, s32[8]{0:T(128)}, u32[]{:S(2)}) copy-start(s32[8]{0:T(128)} %starts.9) | copy-start | bytes 100
  12.3 5.8 %collective-permute-start.2 = (f32[328,128]{1,0:T(8,128)S(1)}, f32[328,128]{1,0:T(8,128)S(1)}, u32[]{:S(2)}, u32[]{:S(2)}) collective-permute-start(f32[328,128]{1,0:T(8,128)S(1)} %pack.1.refs_0_), channel_id=1, source_target_pairs={{0,8},{8,16},{16,24},{24,28},{28,20},{20,12},{12,4},{4,0},{1,9},{9... | collective-permute-start | bytes 503816 | tf_op jit(solution)/shard_map/ppermute | solution.py:399
  14.1 5.5 %collective-permute-start.4 = (f32[328,128]{1,0:T(8,128)S(1)}, f32[328,128]{1,0:T(8,128)S(1)}, u32[]{:S(2)}, u32[]{:S(2)}) collective-permute-start(f32[328,128]{1,0:T(8,128)S(1)} %pack.1.refs_0_), channel_id=1, source_target_pairs={{8,0},{16,8},{24,16},{28,24},{20,28},{12,20},{4,12},{0,4},{9,1},{1... | collective-permute-start | bytes 503816 | tf_op jit(solution)/shard_map/ppermute | solution.py:400
  18.1 5.4 %collective-permute-start.3 = (f32[328,128]{1,0:T(8,128)S(1)}, f32[328,128]{1,0:T(8,128)S(1)}, u32[]{:S(2)}, u32[]{:S(2)}) collective-permute-start(f32[328,128]{1,0:T(8,128)S(1)} %collective-permute-done.2.refs_1_), channel_id=1, source_target_pairs={{0,8},{8,16},{16,24},{24,28},{28,20},{20,12},{12,4},{4,0},{1,9},{9... | collective-permute-start | bytes 503816 | tf_op jit(solution)/shard_map/ppermute | solution.py:399
  19.6 5.5 %collective-permute-start.6 = (f32[328,128]{1,0:T(8,128)S(1)}, f32[328,128]{1,0:T(8,128)S(1)}, u32[]{:S(2)}, u32[]{:S(2)}) collective-permute-start(f32[328,128]{1,0:T(8,128)S(1)} %collective-permute-done.4.refs_2_), channel_id=1, source_target_pairs={{8,0},{16,8},{24,16},{28,24},{20,28},{12,20},{4,12},{0,4},{9,1},{1... | collective-permute-start | bytes 503816 | tf_op jit(solution)/shard_map/ppermute | solution.py:400
  23.5 6.4 %collective-permute-start.5 = (f32[328,128]{1,0:T(8,128)S(1)}, f32[328,128]{1,0:T(8,128)S(1)}, u32[]{:S(2)}, u32[]{:S(2)}) collective-permute-start(f32[328,128]{1,0:T(8,128)S(1)} %collective-permute-done.3.refs_1_), channel_id=1, source_target_pairs={{0,8},{8,16},{16,24},{24,28},{28,20},{20,12},{12,4},{4,0},{1,9},{9... | collective-permute-start | bytes 503816 | tf_op jit(solution)/shard_map/ppermute | solution.py:399
  25.1 6.5 %collective-permute-start.7 = (f32[328,128]{1,0:T(8,128)S(1)}, f32[328,128]{1,0:T(8,128)S(1)}, u32[]{:S(2)}, u32[]{:S(2)}) collective-permute-start(f32[328,128]{1,0:T(8,128)S(1)} %collective-permute-done.6.refs_2_), channel_id=1, source_target_pairs={{8,0},{16,8},{24,16},{28,24},{20,28},{12,20},{4,12},{0,4},{9,1},{1... | collective-permute-start | bytes 503816 | tf_op jit(solution)/shard_map/ppermute | solution.py:400
  27.5 7.7 %copy-start.3 = (bf16[1024,512]{1,0:T(8,128)(2,1)S(1)}, bf16[1024,512]{1,0:T(8,128)(2,1)}, u32[]{:S(2)}) copy-start(bf16[1024,512]{1,0:T(8,128)(2,1)} %constant.9.clone.turned_ref) | copy-start | bytes 3145732
  29.9 5.4 %collective-permute-start.8 = (f32[328,128]{1,0:T(8,128)S(1)}, f32[328,128]{1,0:T(8,128)S(1)}, u32[]{:S(2)}, u32[]{:S(2)}) collective-permute-start(f32[328,128]{1,0:T(8,128)S(1)} %collective-permute-done.5.refs_1_), channel_id=1, source_target_pairs={{0,8},{8,16},{16,24},{24,28},{28,20},{20,12},{12,4},{4,0},{1,9},{9... | collective-permute-start | bytes 503816 | tf_op jit(solution)/shard_map/ppermute | solution.py:403
  35.2 5.1 %copy-start = (bf16[4,4,128,1024]{3,2,1,0:T(8,128)(2,1)S(1)}, bf16[4,4,128,1024]{3,2,1,0:T(8,128)(2,1)}, u32[]{:S(2)}) copy-start(bf16[4,4,128,1024]{3,2,1,0:T(8,128)(2,1)} %constant.8.clone.e_ref) | copy-start | bytes 12582916
  37.5 2.8 %collective-permute-start.10 = (f32[2,128,128]{2,1,0:T(8,128)S(1)}, f32[2,128,128]{2,1,0:T(8,128)S(1)}, u32[]{:S(2)}, u32[]{:S(2)}) collective-permute-start(f32[2,128,128]{2,1,0:T(8,128)S(1)} %get-tuple-element.32.refs_0_), channel_id=1, source_target_pairs={{0,1},{1,0},{2,3},{3,2},{4,5},{5,4},{6,7},{7,6},{8,9},{9,8},{10,11... | collective-permute-start | bytes 393224 | tf_op jit(solution)/shard_map/ppermute | solution.py:358
  37.6 5.9 %collective-permute-start.9 = (f32[2,128,128]{2,1,0:T(8,128)S(1)}, f32[2,128,128]{2,1,0:T(8,128)S(1)}, u32[]{:S(2)}, u32[]{:S(2)}) collective-permute-start(f32[2,128,128]{2,1,0:T(8,128)S(1)} %get-tuple-element.32.refs_0_), channel_id=1, source_target_pairs={{0,2},{1,3},{2,0},{3,1},{4,6},{5,7},{6,4},{7,5},{8,10},{9,11},{10,... | collective-permute-start | bytes 393224 | tf_op jit(solution)/shard_map/ppermute | solution.py:358
  43.5 1.3 %collective-permute-start.11 = (f32[2,128,128]{2,1,0:T(8,128)S(1)}, f32[2,128,128]{2,1,0:T(8,128)S(1)}, u32[]{:S(2)}, u32[]{:S(2)}) collective-permute-start(f32[2,128,128]{2,1,0:T(8,128)S(1)} %collective-permute-done.9.refs_0_), channel_id=1, source_target_pairs={{0,1},{1,0},{2,3},{3,2},{4,5},{5,4},{6,7},{7,6},{8,9},{9,8},{10,11... | collective-permute-start | bytes 393224 | tf_op jit(solution)/shard_map/ppermute | solution.py:358

commit v4 on v3

--- a/solution.py
+++ b/solution.py
@@ -89,49 +89,52 @@
     )()
 
 
-def strip_kernel(gs, cols_total, first, *refs):
-    source_ref, base_ref, steps_ref, out_ref = refs[1:5] if first else refs
-    own = lax.axis_index("fcol")
-    height, width = out_ref.shape[-1], source_ref.shape[-1]
+def strip_kernel(groups, cols_total, *refs):
+    first = len(refs) == 6 + len(groups)
+    source_ref, base_ref, steps_ref, out_refs = refs[0], refs[1], refs[2], refs[3 : 3 + len(groups)]
     if first:
-        pc, ps = unit(refs[0][0:1, 0:1] * (own * width + lanes(width)), cols_total, 1.0 / math.sqrt(cols_total))
+        start_ref, (source_ref, base_ref, steps_ref), out_refs = refs[0], refs[1:4], refs[4 : 4 + len(groups)]
+    width = source_ref.shape[-1]
+    if first:
+        own = lax.axis_index("fcol")
+        pc, ps = unit(start_ref[0:1, 0:1] * (own * width + lanes(width)), cols_total, 1.0 / math.sqrt(cols_total))
         re, im = source_ref[0], source_ref[1]
         z = halves(jnp.concatenate([re * pc + im * ps, im * pc - re * ps]))
-        z_ref, phase_ref = refs[5:]
+        z_ref, phase_ref = refs[-2:]
         z_ref[0], z_ref[1] = z
         phase_ref[0:1], phase_ref[1:2] = pc, ps
     else:
         z = source_ref[0], source_ref[1]
-    for i, g in enumerate(gs):
-        turn_cos, turn_sin, base_cos, base_sin = steps_ref[g, 0], steps_ref[g, 1], base_ref[g, 0], base_ref[g, 1]
-        cos, sin = [], []
-        for t in range(width // 128):
-            tc, ts = turn_cos[:, t : t + 1], turn_sin[:, t : t + 1]
-            cos.append(tc * base_cos - ts * base_sin)
-            sin.append(ts * base_cos + tc * base_sin)
-        waves = halves(jnp.concatenate([jnp.concatenate(cos, 1), jnp.concatenate(sin, 1)]))
-        acc = dot3(waves, z, NT)
-        count = out_ref.shape[2]
-        cos, sin = acc[:count], acc[count:]
-        out_ref[i, 0] = cos[:, :height] + sin[:, height:]
-        out_ref[i, 1] = cos[:, height:] - sin[:, :height]
-
-
-def strips(column_start, source, waves, gs, cols_total, first=False):
-    count = waves[0].shape[2]
+    for gs, out_ref in zip(groups, out_refs):
+        count, height = out_ref.shape[-2:]
+        for i, g in enumerate(gs):
+            turn_cos, turn_sin, base_cos, base_sin = steps_ref[g, 0], steps_ref[g, 1], base_ref[g, 0], base_ref[g, 1]
+            cos, sin = [], []
+            for t in range(width // 128):
+                tc, ts = turn_cos[:, t : t + 1], turn_sin[:, t : t + 1]
+                cos.append(tc * base_cos - ts * base_sin)
+                sin.append(ts * base_cos + tc * base_sin)
+            waves = halves(jnp.concatenate([jnp.concatenate(cos, 1), jnp.concatenate(sin, 1)]))
+            acc = dot3(waves, z, NT)
+            cos, sin = acc[:count], acc[count:]
+            out_ref[i, 0] = cos[:, :height] + sin[:, height:]
+            out_ref[i, 1] = cos[:, height:] - sin[:, :height]
+
+
+def strips(column_start, source, waves, *groups, first=False, cost=10**9):
+    cols, _, count, _ = waves[0].shape
     height, width = source.shape[1] // (1 if first else 2), source.shape[2]
     operands = ([column_start] if first else []) + [source, *waves]
-    out = pl.pallas_call(
-        functools.partial(strip_kernel, gs, cols_total, int(first)),
+    return pl.pallas_call(
+        functools.partial(strip_kernel, groups, cols * width),
         in_specs=[VMEM] * len(operands),
-        out_specs=[VMEM] * (3 if first else 1),
-        out_shape=[jax.ShapeDtypeStruct((len(gs), 2, count, height), F32)]
+        out_specs=[VMEM] * (len(groups) + (2 if first else 0)),
+        out_shape=[jax.ShapeDtypeStruct((len(gs), 2, count, height), F32) for gs in groups]
         + ([jax.ShapeDtypeStruct((2, 2 * height, width), BF), jax.ShapeDtypeStruct((2, width), F32)] if first else []),
         compiler_params=LIMIT,
-        cost_estimate=pl.CostEstimate(flops=10**9, bytes_accessed=2 << 20, transcendentals=0),
+        cost_estimate=pl.CostEstimate(flops=cost, bytes_accessed=2 << 20, transcendentals=0),
         name="strips",
     )(*operands)
-    return out if first else out[0]
 
 
 def pack_kernel(terms, *refs):
@@ -290,7 +293,7 @@
         out_specs=VMEM,
         out_shape=jax.ShapeDtypeStruct((count * 2 * SG // 128, 128), F32),
         compiler_params=LIMIT,
-        cost_estimate=pl.CostEstimate(flops=10**9, bytes_accessed=4 << 20, transcendentals=0),
+        cost_estimate=pl.CostEstimate(flops=4 * 10**9, bytes_accessed=4 << 20, transcendentals=0),
         name="correct_step",
     )(sub, first_state, roots)
     out = out.reshape(count, SG // 128, 2, 128)
@@ -349,7 +352,7 @@
         out_shape=jax.ShapeDtypeStruct((2, height, width), F32),
         scratch_shapes=[pltpu.VMEM((2, height, width), F32), pltpu.SemaphoreType.DMA((len(chunks(width)),))] if last else [],
         compiler_params=LIMIT,
-        cost_estimate=pl.CostEstimate(flops=10**9, bytes_accessed=4 << 20, transcendentals=0),
+        cost_estimate=pl.CostEstimate(flops=4 * 10**9, bytes_accessed=4 << 20, transcendentals=0),
         name="image_step",
     )(phase, table, *operands)
 
@@ -376,15 +379,13 @@
     top = cols // 2
     column_start = column_start.reshape(1, 1)
     waves = waves_of(count, width, cols_total)
-    groups = [tuple(range(1, cols, 2)), tuple(range(top, cols, 2)), tuple(range(0, top, 2))]
-    sent, z, phase = strips(column_start, facets, waves, groups[0], cols_total, first=True)
-    far = strips(column_start, z, waves, groups[1], cols_total)
-    got = swap(sent, "fcol", 1)
-    far, got = lax.optimization_barrier((far + got[top // 2 :], got))
-    terms = [strips(column_start, z, waves, groups[2], cols_total), got, swap(far, "fcol", top)]
+    sent, z, phase = strips(column_start, facets, waves, range(top + 1, cols, 2), first=True)
+    far = strips(column_start, z, waves, range(top, cols, 2))[0] + swap(sent, "fcol", 1)
+    far, z = lax.optimization_barrier((far, z))
+    sent, near = strips(column_start, z, waves, range(1, top, 2), range(0, top, 2), cost=4 * 10**9)
+    terms = [near + swap(far, "fcol", top), swap(sent, "fcol", 1)]
     bit = 2
     while bit < top:
-        terms[1] = terms[1][: terms[0].shape[0]]
         pairs = sum(terms).reshape((-1, 2) + far.shape[1:])
         terms = [pairs[:, 0], swap(pairs[:, 1], "fcol", bit)]
         bit *= 2
@@ -411,11 +412,14 @@
     def image(blocks, acc, last=False):
         return image_step(phase, e_table, blocks.keys(), list(blocks.values()), acc, last)
 
+    acc = image(near, None)
+    near[0], acc = lax.optimization_barrier((back, acc))
     bit = top // 2
     while bit >= 1:
         near |= spread(near, bit)
         bit //= 2
-    acc = image(near, None)
+    del near[0]
+    acc = image(near, acc)
     corrected = correct_step(sub, first_state, roots)
     far[top], acc, corrected = lax.optimization_barrier((far[top], acc, corrected))
     bit = top // 2

time: 46.7 us -> 45.1 us (0.966)
  waiting for transfers between devices: 13.4 us -> 11.4 us
    ppermute x5 -> x6, waiting for transfers between devices: 5.37 us -> 3.4 us  [swap(): lax.ppermute(value, axis, [(i, i ^ bit) for i in range(lax.axis_size(axis...]
    pallas_call x3 -> x4, Pallas kernels: 3.12 us -> 3.31 us  [image_step(): pl.pallas_call(functools.partial(image_kernel, tuple(gs), first, last), i...]
    ppermute x5 -> x6, starting transfers between devices: 5.25 us -> 5.32 us  [swap(): lax.ppermute(value, axis, [(i, i ^ bit) for i in range(lax.axis_size(axis...]
  transfers between devices with their start and end apart: 12 -> 13, of which waited for: 8 -> 9; matrix products, arithmetic and copies ran while one was open for 0% -> 0% of each run, Pallas kernels for 25% -> 27%
where the time goes in v4:
time: 45.1 us; the launch traced here: 44.9 us
  Pallas kernels  18 us (40%)
  starting transfers between devices  13.1 us (29%)
  waiting for transfers between devices  11.4 us (25%)
  between operations  2.31 us (5%)
    ppermute x4, waiting for transfers between devices, per_device(): up = lax.ppermute(up, 'frow', ahead)  7.95 us
    pallas_call x4, Pallas kernels, gather_step(): pl.pallas_call(functools.partial(gather_kernel, steps, rows_total // heig...  7.08 us
    ppermute x4, starting transfers between devices, per_device(): up = lax.ppermute(up, 'frow', ahead)  6.55 us
    ppermute x6, starting transfers between devices, swap(): lax.ppermute(value, axis, [(i, i ^ bit) for i in range(lax.axis_size(axis...  5.32 us
    pallas_call x3, Pallas kernels, strips(): pl.pallas_call(functools.partial(strip_kernel, groups, cols * width), in_...  3.54 us
    ppermute x6, waiting for transfers between devices, swap(): lax.ppermute(value, axis, [(i, i ^ bit) for i in range(lax.axis_size(axis...  3.4 us
    pallas_call x4, Pallas kernels, image_step(): pl.pallas_call(functools.partial(image_kernel, tuple(gs), first, last), i...  3.31 us
    pallas_call x1, Pallas kernels, back_step(): pl.pallas_call(functools.partial(back_kernel, rows_total // height, heigh...  2.32 us
  transfers between devices with their start and end apart: 13, of which 9 were waited for; matrix products, arithmetic and copies ran while one was open for 0% of the time, Pallas kernels for 27%

profile of v4, /device:TPU:0, one launch (start us, length us, event | category | flops | bytes accessed | tf_op | source)
XLA Modules:
  0.0 44.9 jit_solution(333118727341820080)
XLA Ops:
  0.6 0.0 copy-start.6
  0.6 0.7 %waves.1 = (f32[4,2,128,128]{3,2,1,0:T(8,128)S(1)}, f32[4,2,128,128]{3,2,1,0:T(8,128)S(1)}) custom-call(), custom_call_target="tpu_custom_call" | custom-call | flops 1000000000 | bytes 2097152 | tf_op jit(solution)/shard_map/waves/pallas_call | solution.py:82
  2.0 0.0 copy-done.6
  2.0 1.1 %strips.3 = (f32[1,2,128,128]{3,2,1,0:T(8,128)S(1)}, bf16[2,256,1024]{2,1,0:T(8,128)(2,1)S(1)}, f32[2,1024]{1,0:T(2,128)S(1)}) custom-call(s32[1,1]{1,0:T(1,128)} %bitcast.7.refs_0_, f32[2,128,1024]{2,1,0:T(8,128)S(1)} %copy-done.6, f32[4,2,128,128]{3,2,1,0:T(8,128)S(1)} %get-tuple-element.24.refs_2_.refs_1_, ...), custom_call_target="tpu_custom_call" | custom-call | flops 1000000000 | bytes 2097152 | tf_op jit(solution)/shard_map/strips/pallas_call | solution.py:128
  3.2 0.5 %collective-permute-start = (f32[1,2,128,128]{3,2,1,0:T(8,128)S(1)}, f32[1,2,128,128]{3,2,1,0:T(8,128)S(1)}, u32[]{:S(2)}, u32[]{:S(2)}) collective-permute-start(f32[1,2,128,128]{3,2,1,0:T(8,128)S(1)} %get-tuple-element.27), channel_id=1, source_target_pairs={{0,1},{1,0},{2,3},{3,2},{4,5},{5,4},{6,7},{7,6},{8,9},{9,8},{10,11... | collective-permute-start | bytes 393224 | tf_op jit(solution)/shard_map/ppermute | solution.py:361
  3.7 0.9 %strips.4 = f32[1,2,128,128]{3,2,1,0:T(8,128)S(1)} custom-call(bf16[2,256,1024]{2,1,0:T(8,128)(2,1)S(1)} %get-tuple-element.28.refs_0_, f32[4,2,128,128]{3,2,1,0:T(8,128)S(1)} %get-tuple-element.24.refs_2_.refs_1_, f32[4,2,128,128]{3,2,1,0:T(8,128)S(1)} %get-tuple-element.25.refs_3_.refs_2_), custom_call_target="tpu_custom_call" | custom-call | flops 1000000000 | bytes 2097152 | tf_op jit(solution)/shard_map/strips/pallas_call | solution.py:128
  4.6 0.1 collective-permute-done
  4.7 0.0 copy-start.3
  4.7 0.0 copy-start.5
  4.7 0.0 copy-start
  4.7 0.0 copy-start.1
  4.7 0.0 copy-start.4
  4.8 2.9 %collective-permute-start.1 = (f32[1,2,128,128]{3,2,1,0:T(8,128)S(1)}, f32[1,2,128,128]{3,2,1,0:T(8,128)S(1)}, u32[]{:S(2)}, u32[]{:S(2)}) collective-permute-start(f32[1,2,128,128]{3,2,1,0:T(8,128)S(1)} %add.6), channel_id=1, source_target_pairs={{0,2},{1,3},{2,0},{3,1},{4,6},{5,7},{6,4},{7,5},{8,10},{9,11},{10,... | collective-permute-start | bytes 393224 | tf_op jit(solution)/shard_map/ppermute | solution.py:361
  7.7 1.5 %strips.5 = (f32[1,2,128,128]{3,2,1,0:T(8,128)S(1)}, f32[1,2,128,128]{3,2,1,0:T(8,128)S(1)}) custom-call(bf16[2,256,1024]{2,1,0:T(8,128)(2,1)S(1)} %get-tuple-element.28.refs_0_, f32[4,2,128,128]{3,2,1,0:T(8,128)S(1)} %get-tuple-element.24.refs_2_.refs_1_, f32[4,2,128,128]{3,2,1,0:T(8,128)S(1)} %get-tuple-element.25.refs_3_.refs_2_), custom_call_target="tpu_custom_call" | custom-call | flops 4000000000 | bytes 2097152 | tf_op jit(solution)/shard_map/strips/pallas_call | solution.py:128
  9.2 0.1 collective-permute-start.2
  9.9 1.6 %collective-permute-done.1 = f32[1,2,128,128]{3,2,1,0:T(8,128)S(1)} collective-permute-done((f32[1,2,128,128]{3,2,1,0:T(8,128)S(1)}, f32[1,2,128,128]{3,2,1,0:T(8,128)S(1)}, u32[]{:S(2)}, u32[]{:S(2)}) %collective-permute-start.1) | collective-permute-done | bytes 131104 | tf_op jit(solution)/shard_map/ppermute | solution.py:361
  11.5 0.0 collective-permute-done.2.refs_1_
  11.5 0.0 copy-done.3
  11.5 0.0 copy-done.5
  11.6 0.1 pack.1.refs_0_
  11.6 1.8 %collective-permute-start.3 = (f32[328,128]{1,0:T(8,128)S(1)}, f32[328,128]{1,0:T(8,128)S(1)}, u32[]{:S(2)}, u32[]{:S(2)}) collective-permute-start(f32[328,128]{1,0:T(8,128)S(1)} %pack.1.refs_0_), channel_id=1, source_target_pairs={{0,8},{8,16},{16,24},{24,28},{28,20},{20,12},{12,4},{4,0},{1,9},{9... | collective-permute-start | bytes 503816 | tf_op jit(solution)/shard_map/ppermute | solution.py:400
  13.4 0.2 collective-permute-start.5
  13.7 0.0 copy-done
  13.7 0.0 copy-done.1
  13.7 0.0 copy-done.4
  13.7 1.3 %gather_step.4.refs_0_.gain_ref = f32[3,128,1024]{2,1,0:T(8,128)S(1)} custom-call(s32[8]{0:T(128)S(1)} %copy-done.4, bf16[768,1024]{1,0:T(8,128)(2,1)S(1)} %copy-done, f32[8,2,1024]{2,1,0:T(2,128)S(1)} %copy-done.1, f32[328,128]{1,0:T(8,128)S(1)} %pack.1.refs_0_), custom_call_target="tpu_custom_call" | custom-call | flops 1000000000 | bytes 4194304 | tf_op jit(solution)/shard_map/gather_step/pallas_call | solution.py:225
  15.0 2.5 %collective-permute-done.3.refs_1_ = f32[328,128]{1,0:T(8,128)S(1)} collective-permute-done((f32[328,128]{1,0:T(8,128)S(1)}, f32[328,128]{1,0:T(8,128)S(1)}, u32[]{:S(2)}, u32[]{:S(2)}) %collective-permute-start.3) | collective-permute-done | bytes 167968 | tf_op jit(solution)/shard_map/ppermute | solution.py:400
  17.5 1.5 %collective-permute-start.4 = (f32[328,128]{1,0:T(8,128)S(1)}, f32[328,128]{1,0:T(8,128)S(1)}, u32[]{:S(2)}, u32[]{:S(2)}) collective-permute-start(f32[328,128]{1,0:T(8,128)S(1)} %collective-permute-done.3.refs_1_), channel_id=1, source_target_pairs={{0,8},{8,16},{16,24},{24,28},{28,20},{20,12},{12,4},{4,0},{1,9},{9... | collective-permute-start | bytes 503816 | tf_op jit(solution)/shard_map/ppermute | solution.py:400
  18.9 0.0 collective-permute-done.5.refs_2_
  19.0 0.5 %collective-permute-start.7 = (f32[328,128]{1,0:T(8,128)S(1)}, f32[328,128]{1,0:T(8,128)S(1)}, u32[]{:S(2)}, u32[]{:S(2)}) collective-permute-start(f32[328,128]{1,0:T(8,128)S(1)} %collective-permute-done.5.refs_2_), channel_id=1, source_target_pairs={{8,0},{16,8},{24,16},{28,24},{20,28},{12,20},{4,12},{0,4},{9,1},{1... | collective-permute-start | bytes 503816 | tf_op jit(solution)/shard_map/ppermute | solution.py:401
  19.5 1.9 %gather_step.5.refs_0_ = f32[3,128,1024]{2,1,0:T(8,128)S(1)} custom-call(s32[8]{0:T(128)S(1)} %copy-done.4, bf16[768,1024]{1,0:T(8,128)(2,1)S(1)} %copy-done, f32[8,2,1024]{2,1,0:T(2,128)S(1)} %copy-done.1, f32[3,128,1024]{2,1,0:T(8,128)S(1)} %gather_step.4.refs_0_.gain_ref, f32[328,128]{1,0:T(8,128)S(1)} %collective-permute-done.3.refs_1_, ...), custom_call_target="tpu_custom_call" | custom-call | flops 1000000000 | bytes 4194304 | tf_op jit(solution)/shard_map/gather_step/pallas_call | solution.py:225
  21.4 1.4 %collective-permute-done.4.refs_1_ = f32[328,128]{1,0:T(8,128)S(1)} collective-permute-done((f32[328,128]{1,0:T(8,128)S(1)}, f32[328,128]{1,0:T(8,128)S(1)}, u32[]{:S(2)}, u32[]{:S(2)}) %collective-permute-start.4) | collective-permute-done | bytes 167968 | tf_op jit(solution)/shard_map/ppermute | solution.py:400
  22.8 1.6 %collective-permute-start.6 = (f32[328,128]{1,0:T(8,128)S(1)}, f32[328,128]{1,0:T(8,128)S(1)}, u32[]{:S(2)}, u32[]{:S(2)}) collective-permute-start(f32[328,128]{1,0:T(8,128)S(1)} %collective-permute-done.4.refs_1_), channel_id=1, source_target_pairs={{0,8},{8,16},{16,24},{24,28},{28,20},{20,12},{12,4},{4,0},{1,9},{9... | collective-permute-start | bytes 503816 | tf_op jit(solution)/shard_map/ppermute | solution.py:400
  24.4 0.0 collective-permute-done.7.refs_2_
  24.4 0.5 %collective-permute-start.8 = (f32[328,128]{1,0:T(8,128)S(1)}, f32[328,128]{1,0:T(8,128)S(1)}, u32[]{:S(2)}, u32[]{:S(2)}) collective-permute-start(f32[328,128]{1,0:T(8,128)S(1)} %collective-permute-done.7.refs_2_), channel_id=1, source_target_pairs={{8,0},{16,8},{24,16},{28,24},{20,28},{12,20},{4,12},{0,4},{9,1},{1... | collective-permute-start | bytes 503816 | tf_op jit(solution)/shard_map/ppermute | solution.py:401
  24.9 1.9 %gather_step.6.refs_0_ = f32[3,128,1024]{2,1,0:T(8,128)S(1)} custom-call(s32[8]{0:T(128)S(1)} %copy-done.4, bf16[768,1024]{1,0:T(8,128)(2,1)S(1)} %copy-done, f32[8,2,1024]{2,1,0:T(2,128)S(1)} %copy-done.1, f32[3,128,1024]{2,1,0:T(8,128)S(1)} %gather_step.5.refs_0_, f32[328,128]{1,0:T(8,128)S(1)} %collective-permute-done.4.refs_1_, ...), custom_call_target="tpu_custom_call" | custom-call | flops 1000000000 | bytes 4194304 | tf_op jit(solution)/shard_map/gather_step/pallas_call | solution.py:225
  26.8 0.0 copy-start.2
  26.8 2.4 %collective-permute-done.6.refs_1_ = f32[328,128]{1,0:T(8,128)S(1)} collective-permute-done((f32[328,128]{1,0:T(8,128)S(1)}, f32[328,128]{1,0:T(8,128)S(1)}, u32[]{:S(2)}, u32[]{:S(2)}) %collective-permute-start.6) | collective-permute-done | bytes 167968 | tf_op jit(solution)/shard_map/ppermute | solution.py:400
  29.2 1.7 %collective-permute-start.9 = (f32[328,128]{1,0:T(8,128)S(1)}, f32[328,128]{1,0:T(8,128)S(1)}, u32[]{:S(2)}, u32[]{:S(2)}) collective-permute-start(f32[328,128]{1,0:T(8,128)S(1)} %collective-permute-done.6.refs_1_), channel_id=1, source_target_pairs={{0,8},{8,16},{16,24},{24,28},{28,20},{20,12},{12,4},{4,0},{1,9},{9... | collective-permute-start | bytes 503816 | tf_op jit(solution)/shard_map/ppermute | solution.py:404
  30.9 0.0 collective-permute-done.8.refs_2_
  30.9 1.9 %gather_step.7.state_ref = f32[3,128,1024]{2,1,0:T(8,128)S(1)} custom-call(s32[8]{0:T(128)S(1)} %copy-done.4, bf16[768,1024]{1,0:T(8,128)(2,1)S(1)} %copy-done, f32[8,2,1024]{2,1,0:T(2,128)S(1)} %copy-done.1, f32[3,128,1024]{2,1,0:T(8,128)S(1)} %gather_step.6.refs_0_, f32[328,128]{1,0:T(8,128)S(1)} %collective-permute-done.6.refs_1_, ...), custom_call_target="tpu_custom_call" | custom-call | flops 1000000000 | bytes 4194304 | tf_op jit(solution)/shard_map/gather_step/pallas_call | solution.py:225
  32.8 0.0 copy-start.7
  32.8 1.7 %collective-permute-done.9.message_ref = f32[328,128]{1,0:T(8,128)S(1)} collective-permute-done((f32[328,128]{1,0:T(8,128)S(1)}, f32[328,128]{1,0:T(8,128)S(1)}, u32[]{:S(2)}, u32[]{:S(2)}) %collective-permute-start.9) | collective-permute-done | bytes 167968 | tf_op jit(solution)/shard_map/ppermute | solution.py:404
  34.6 0.0 copy-done.2
  34.6 2.3 %back_step.1 = (f32[2,128,128]{2,1,0:T(8,128)S(1)}, f32[2,128,512]{2,1,0:T(8,128)S(1)}) custom-call(s32[8]{0:T(128)S(1)} %copy-done.4, bf16[768,1024]{1,0:T(8,128)(2,1)S(1)} %copy-done, bf16[1024,512]{1,0:T(8,128)(2,1)S(1)} %copy-done.2, f32[8,2,1024]{2,1,0:T(2,128)S(1)} %copy-done.1, f32[3,128,1024]{2,1,0:T(8,128)S(1)} %gather_step.7.state_ref, ...), custom_call_target="tpu_custom_call" | custom-call | tf_op jit(solution)/shard_map/back_step/pallas_call | solution.py:264
  36.9 1.7 %collective-permute-start.10 = (f32[2,128,128]{2,1,0:T(8,128)S(1)}, f32[2,128,128]{2,1,0:T(8,128)S(1)}, u32[]{:S(2)}, u32[]{:S(2)}) collective-permute-start(f32[2,128,128]{2,1,0:T(8,128)S(1)} %get-tuple-element.40.refs_0_), channel_id=1, source_target_pairs={{0,2},{1,3},{2,0},{3,1},{4,6},{5,7},{6,4},{7,5},{8,10},{9,11},{10,... | collective-permute-start | bytes 393224 | tf_op jit(solution)/shard_map/ppermute | solution.py:361
  38.6 0.0 copy-done.7
  38.6 0.6 %image_step.4.refs_1_ = f32[2,128,1024]{2,1,0:T(8,128)S(1)} custom-call(f32[2,1024]{1,0:T(2,128)S(1)} %get-tuple-element.39.phase_ref, bf16[4,4,128,1024]{3,2,1,0:T(8,128)(2,1)S(1)} %copy-done.7, f32[2,128,128]{2,1,0:T(8,128)S(1)} %get-tuple-element.40.refs_0_), custom_call_target="tpu_custom_call" | custom-call | flops 4000000000 | bytes 4194304 | tf_op jit(solution)/shard_map/image_step/pallas_call | solution.py:348
  39.2 0.1 collective-permute-start.11
  39.3 1.0 %correct_step.1 = f32[1024,128]{1,0:T(8,128)} custom-call(f32[2,128,512]{2,1,0:T(8,128)S(1)} %get-tuple-element.42.sub_ref, f32[3,128,1024]{2,1,0:T(8,128)S(1)} %gather_step.4.refs_0_.gain_ref, f32[8,2,1024]{2,1,0:T(2,128)S(1)} %copy-done.1), custom_call_target="tpu_custom_call" | custom-call | flops 4000000000 | bytes 4194304 | tf_op jit(solution)/shard_map/correct_step/pallas_call | solution.py:290
  40.3 0.3 collective-permute-done.11.refs_0_
  40.6 0.6 %image_step.5.refs_1_ = f32[2,128,1024]{2,1,0:T(8,128)S(1)} custom-call(f32[2,1024]{1,0:T(2,128)S(1)} %get-tuple-element.39.phase_ref, bf16[4,4,128,1024]{3,2,1,0:T(8,128)(2,1)S(1)} %copy-done.7, f32[2,128,128]{2,1,0:T(8,128)S(1)} %collective-permute-done.11.refs_0_, f32[2,128,1024]{2,1,0:T(8,128)S(1)} %image_step.4.refs_1_), custom_call_target="tpu_custom_call" | custom-call | flops 4000000000 | bytes 4194304 | tf_op jit(solution)/shard_map/image_step/pallas_call | solution.py:348
  41.2 0.7 %collective-permute-done.10.refs_0_ = f32[2,128,128]{2,1,0:T(8,128)S(1)} collective-permute-done((f32[2,128,128]{2,1,0:T(8,128)S(1)}, f32[2,128,128]{2,1,0:T(8,128)S(1)}, u32[]{:S(2)}, u32[]{:S(2)}) %collective-permute-start.10) | collective-permute-done | bytes 131104 | tf_op jit(solution)/shard_map/ppermute | solution.py:361
  41.9 0.0 collective-permute-start.12
  41.9 0.6 %image_step.6.refs_1_ = f32[2,128,1024]{2,1,0:T(8,128)S(1)} custom-call(f32[2,1024]{1,0:T(2,128)S(1)} %get-tuple-element.39.phase_ref, bf16[4,4,128,1024]{3,2,1,0:T(8,128)(2,1)S(1)} %copy-done.7, f32[2,128,128]{2,1,0:T(8,128)S(1)} %collective-permute-done.10.refs_0_, f32[2,128,1024]{2,1,0:T(8,128)S(1)} %image_step.5.refs_1_), custom_call_target="tpu_custom_call" | custom-call | flops 4000000000 | bytes 4194304 | tf_op jit(solution)/shard_map/image_step/pallas_call | solution.py:348
  42.5 0.7 %collective-permute-done.12.refs_0_ = f32[2,128,128]{2,1,0:T(8,128)S(1)} collective-permute-done((f32[2,128,128]{2,1,0:T(8,128)S(1)}, f32[2,128,128]{2,1,0:T(8,128)S(1)}, u32[]{:S(2)}, u32[]{:S(2)}) %collective-permute-start.12) | collective-permute-done | bytes 131104 | tf_op jit(solution)/shard_map/ppermute | solution.py:361
  43.3 1.5 %image_step.7 = f32[2,128,1024]{2,1,0:T(8,128)} custom-call(f32[2,1024]{1,0:T(2,128)S(1)} %get-tuple-element.39.phase_ref, bf16[4,4,128,1024]{3,2,1,0:T(8,128)(2,1)S(1)} %copy-done.7, f32[2,128,128]{2,1,0:T(8,128)S(1)} %collective-permute-done.12.refs_0_, f32[2,128,1024]{2,1,0:T(8,128)S(1)} %image_step.6.refs_1_), custom_call_target="tpu_custom_call" | custom-call | flops 4000000000 | bytes 4194304 | tf_op jit(solution)/shard_map/image_step/pallas_call | solution.py:348
  (2 shorter events, 0.0 us)
Async XLA Ops:
  0.6 1.4 %copy-start.6 = (f32[2,128,1024]{2,1,0:T(8,128)S(1)}, f32[2,128,1024]{2,1,0:T(8,128)}, u32[]{:S(2)}) copy-start(f32[2,128,1024]{2,1,0:T(8,128)} %refs_1_.1) | copy-start | bytes 3145732
  3.2 1.5 %collective-permute-start = (f32[1,2,128,128]{3,2,1,0:T(8,128)S(1)}, f32[1,2,128,128]{3,2,1,0:T(8,128)S(1)}, u32[]{:S(2)}, u32[]{:S(2)}) collective-permute-start(f32[1,2,128,128]{3,2,1,0:T(8,128)S(1)} %get-tuple-element.27), channel_id=1, source_target_pairs={{0,1},{1,0},{2,3},{3,2},{4,5},{5,4},{6,7},{7,6},{8,9},{9,8},{10,11... | collective-permute-start | bytes 393224 | tf_op jit(solution)/shard_map/ppermute | solution.py:361
  4.7 6.8 %copy-start.3 = (f32[1,64,128]{2,1,0:T(8,128)S(1)}, f32[1,64,128]{2,1,0:T(8,128)}, u32[]{:S(2)}) copy-start(f32[1,64,128]{2,1,0:T(8,128)} %refs_2_.1) | copy-start | bytes 98308
  4.7 6.8 %copy-start.5 = (s32[1,64]{1,0:T(1,128)S(1)}, s32[1,64]{1,0:T(1,128)}, u32[]{:S(2)}) copy-start(s32[1,64]{1,0:T(1,128)} %refs_3_.1) | copy-start | bytes 772
  4.7 9.0 %copy-start = (bf16[768,1024]{1,0:T(8,128)(2,1)S(1)}, bf16[768,1024]{1,0:T(8,128)(2,1)}, u32[]{:S(2)}) copy-start(bf16[768,1024]{1,0:T(8,128)(2,1)} %constant.10.clone.b_ref) | copy-start | bytes 4718596
  4.7 8.9 %copy-start.1 = (f32[8,2,1024]{2,1,0:T(2,128)S(1)}, f32[8,2,1024]{2,1,0:T(2,128)}, u32[]{:S(2)}) copy-start(f32[8,2,1024]{2,1,0:T(2,128)} %constant.11.clone.roots_ref) | copy-start | bytes 196612
  4.7 8.9 %copy-start.4 = (s32[8]{0:T(128)S(1)}, s32[8]{0:T(128)}, u32[]{:S(2)}) copy-start(s32[8]{0:T(128)} %starts.9) | copy-start | bytes 100
  4.8 6.8 %collective-permute-start.1 = (f32[1,2,128,128]{3,2,1,0:T(8,128)S(1)}, f32[1,2,128,128]{3,2,1,0:T(8,128)S(1)}, u32[]{:S(2)}, u32[]{:S(2)}) collective-permute-start(f32[1,2,128,128]{3,2,1,0:T(8,128)S(1)} %add.6), channel_id=1, source_target_pairs={{0,2},{1,3},{2,0},{3,1},{4,6},{5,7},{6,4},{7,5},{8,10},{9,11},{10,... | collective-permute-start | bytes 393224 | tf_op jit(solution)/shard_map/ppermute | solution.py:361
  9.2 2.3 %collective-permute-start.2 = (f32[1,2,128,128]{3,2,1,0:T(8,128)S(1)}, f32[1,2,128,128]{3,2,1,0:T(8,128)S(1)}, u32[]{:S(2)}, u32[]{:S(2)}) collective-permute-start(f32[1,2,128,128]{3,2,1,0:T(8,128)S(1)} %get-tuple-element.31), channel_id=1, source_target_pairs={{0,1},{1,0},{2,3},{3,2},{4,5},{5,4},{6,7},{7,6},{8,9},{9,8},{10,11... | collective-permute-start | bytes 393224 | tf_op jit(solution)/shard_map/ppermute | solution.py:361
  11.6 5.8 %collective-permute-start.3 = (f32[328,128]{1,0:T(8,128)S(1)}, f32[328,128]{1,0:T(8,128)S(1)}, u32[]{:S(2)}, u32[]{:S(2)}) collective-permute-start(f32[328,128]{1,0:T(8,128)S(1)} %pack.1.refs_0_), channel_id=1, source_target_pairs={{0,8},{8,16},{16,24},{24,28},{28,20},{20,12},{12,4},{4,0},{1,9},{9... | collective-permute-start | bytes 503816 | tf_op jit(solution)/shard_map/ppermute | solution.py:400
  13.4 5.5 %collective-permute-start.5 = (f32[328,128]{1,0:T(8,128)S(1)}, f32[328,128]{1,0:T(8,128)S(1)}, u32[]{:S(2)}, u32[]{:S(2)}) collective-permute-start(f32[328,128]{1,0:T(8,128)S(1)} %pack.1.refs_0_), channel_id=1, source_target_pairs={{8,0},{16,8},{24,16},{28,24},{20,28},{12,20},{4,12},{0,4},{9,1},{1... | collective-permute-start | bytes 503816 | tf_op jit(solution)/shard_map/ppermute | solution.py:401
  17.5 5.4 %collective-permute-start.4 = (f32[328,128]{1,0:T(8,128)S(1)}, f32[328,128]{1,0:T(8,128)S(1)}, u32[]{:S(2)}, u32[]{:S(2)}) collective-permute-start(f32[328,128]{1,0:T(8,128)S(1)} %collective-permute-done.3.refs_1_), channel_id=1, source_target_pairs={{0,8},{8,16},{16,24},{24,28},{28,20},{20,12},{12,4},{4,0},{1,9},{9... | collective-permute-start | bytes 503816 | tf_op jit(solution)/shard_map/ppermute | solution.py:400
  19.0 5.5 %collective-permute-start.7 = (f32[328,128]{1,0:T(8,128)S(1)}, f32[328,128]{1,0:T(8,128)S(1)}, u32[]{:S(2)}, u32[]{:S(2)}) collective-permute-start(f32[328,128]{1,0:T(8,128)S(1)} %collective-permute-done.5.refs_2_), channel_id=1, source_target_pairs={{8,0},{16,8},{24,16},{28,24},{20,28},{12,20},{4,12},{0,4},{9,1},{1... | collective-permute-start | bytes 503816 | tf_op jit(solution)/shard_map/ppermute | solution.py:401
  22.8 6.4 %collective-permute-start.6 = (f32[328,128]{1,0:T(8,128)S(1)}, f32[328,128]{1,0:T(8,128)S(1)}, u32[]{:S(2)}, u32[]{:S(2)}) collective-permute-start(f32[328,128]{1,0:T(8,128)S(1)} %collective-permute-done.4.refs_1_), channel_id=1, source_target_pairs={{0,8},{8,16},{16,24},{24,28},{28,20},{20,12},{12,4},{4,0},{1,9},{9... | collective-permute-start | bytes 503816 | tf_op jit(solution)/shard_map/ppermute | solution.py:400
  24.4 6.5 %collective-permute-start.8 = (f32[328,128]{1,0:T(8,128)S(1)}, f32[328,128]{1,0:T(8,128)S(1)}, u32[]{:S(2)}, u32[]{:S(2)}) collective-permute-start(f32[328,128]{1,0:T(8,128)S(1)} %collective-permute-done.7.refs_2_), channel_id=1, source_target_pairs={{8,0},{16,8},{24,16},{28,24},{20,28},{12,20},{4,12},{0,4},{9,1},{1... | collective-permute-start | bytes 503816 | tf_op jit(solution)/shard_map/ppermute | solution.py:401
  26.8 7.7 %copy-start.2 = (bf16[1024,512]{1,0:T(8,128)(2,1)S(1)}, bf16[1024,512]{1,0:T(8,128)(2,1)}, u32[]{:S(2)}) copy-start(bf16[1024,512]{1,0:T(8,128)(2,1)} %constant.9.clone.turned_ref) | copy-start | bytes 3145732
  29.2 5.4 %collective-permute-start.9 = (f32[328,128]{1,0:T(8,128)S(1)}, f32[328,128]{1,0:T(8,128)S(1)}, u32[]{:S(2)}, u32[]{:S(2)}) collective-permute-start(f32[328,128]{1,0:T(8,128)S(1)} %collective-permute-done.6.refs_1_), channel_id=1, source_target_pairs={{0,8},{8,16},{16,24},{24,28},{28,20},{20,12},{12,4},{4,0},{1,9},{9... | collective-permute-start | bytes 503816 | tf_op jit(solution)/shard_map/ppermute | solution.py:404
  32.8 5.8 %copy-start.7 = (bf16[4,4,128,1024]{3,2,1,0:T(8,128)(2,1)S(1)}, bf16[4,4,128,1024]{3,2,1,0:T(8,128)(2,1)}, u32[]{:S(2)}) copy-start(bf16[4,4,128,1024]{3,2,1,0:T(8,128)(2,1)} %constant.8.clone.e_ref) | copy-start | bytes 12582916
  36.9 5.0 %collective-permute-start.10 = (f32[2,128,128]{2,1,0:T(8,128)S(1)}, f32[2,128,128]{2,1,0:T(8,128)S(1)}, u32[]{:S(2)}, u32[]{:S(2)}) collective-permute-start(f32[2,128,128]{2,1,0:T(8,128)S(1)} %get-tuple-element.40.refs_0_), channel_id=1, source_target_pairs={{0,2},{1,3},{2,0},{3,1},{4,6},{5,7},{6,4},{7,5},{8,10},{9,11},{10,... | collective-permute-start | bytes 393224 | tf_op jit(solution)/shard_map/ppermute | solution.py:361
  39.2 1.4 %collective-permute-start.11 = (f32[2,128,128]{2,1,0:T(8,128)S(1)}, f32[2,128,128]{2,1,0:T(8,128)S(1)}, u32[]{:S(2)}, u32[]{:S(2)}) collective-permute-start(f32[2,128,128]{2,1,0:T(8,128)S(1)} %get-tuple-element.40.refs_0_), channel_id=1, source_target_pairs={{0,1},{1,0},{2,3},{3,2},{4,5},{5,4},{6,7},{7,6},{8,9},{9,8},{10,11... | collective-permute-start | bytes 393224 | tf_op jit(solution)/shard_map/ppermute | solution.py:361
  41.9 1.3 %collective-permute-start.12 = (f32[2,128,128]{2,1,0:T(8,128)S(1)}, f32[2,128,128]{2,1,0:T(8,128)S(1)}, u32[]{:S(2)}, u32[]{:S(2)}) collective-permute-start(f32[2,128,128]{2,1,0:T(8,128)S(1)} %collective-permute-done.10.refs_0_), channel_id=1, source_target_pairs={{0,1},{1,0},{2,3},{3,2},{4,5},{5,4},{6,7},{7,6},{8,9},{9,8},{10,11... | collective-permute-start | bytes 393224 | tf_op jit(solution)/shard_map/ppermute | solution.py:361

commit v5 on v4

--- a/solution.py
+++ b/solution.py
@@ -89,52 +89,98 @@
     )()
 
 
-def strip_kernel(groups, cols_total, *refs):
-    first = len(refs) == 6 + len(groups)
-    source_ref, base_ref, steps_ref, out_refs = refs[0], refs[1], refs[2], refs[3 : 3 + len(groups)]
-    if first:
-        start_ref, (source_ref, base_ref, steps_ref), out_refs = refs[0], refs[1:4], refs[4 : 4 + len(groups)]
-    width = source_ref.shape[-1]
-    if first:
-        own = lax.axis_index("fcol")
-        pc, ps = unit(start_ref[0:1, 0:1] * (own * width + lanes(width)), cols_total, 1.0 / math.sqrt(cols_total))
-        re, im = source_ref[0], source_ref[1]
-        z = halves(jnp.concatenate([re * pc + im * ps, im * pc - re * ps]))
-        z_ref, phase_ref = refs[-2:]
-        z_ref[0], z_ref[1] = z
-        phase_ref[0:1], phase_ref[1:2] = pc, ps
-    else:
-        z = source_ref[0], source_ref[1]
-    for gs, out_ref in zip(groups, out_refs):
-        count, height = out_ref.shape[-2:]
-        for i, g in enumerate(gs):
-            turn_cos, turn_sin, base_cos, base_sin = steps_ref[g, 0], steps_ref[g, 1], base_ref[g, 0], base_ref[g, 1]
+def strip_sums(gs, z_ref, base_ref, steps_ref, out_ref):
+    count, height = out_ref.shape[-2:]
+    z = z_ref[0], z_ref[1]
+    for i, g in enumerate(gs):
+        turn_cos, turn_sin, base_cos, base_sin = steps_ref[g, 0], steps_ref[g, 1], base_ref[g, 0], base_ref[g, 1]
+        acc = None
+        for begin, size in chunks(z_ref.shape[-1]):
             cos, sin = [], []
-            for t in range(width // 128):
+            for t in range(begin // 128, (begin + size) // 128):
                 tc, ts = turn_cos[:, t : t + 1], turn_sin[:, t : t + 1]
                 cos.append(tc * base_cos - ts * base_sin)
                 sin.append(ts * base_cos + tc * base_sin)
             waves = halves(jnp.concatenate([jnp.concatenate(cos, 1), jnp.concatenate(sin, 1)]))
-            acc = dot3(waves, z, NT)
-            cos, sin = acc[:count], acc[count:]
-            out_ref[i, 0] = cos[:, :height] + sin[:, height:]
-            out_ref[i, 1] = cos[:, height:] - sin[:, :height]
-
-
-def strips(column_start, source, waves, *groups, first=False, cost=10**9):
+            part = dot3(waves, [value[:, begin : begin + size] for value in z], NT)
+            acc = part if acc is None else acc + part
+        cos, sin = acc[:count], acc[count:]
+        out_ref[i, 0] = cos[:, :height] + sin[:, height:]
+        out_ref[i, 1] = cos[:, height:] - sin[:, :height]
+
+
+def first_strip_kernel(gs, cols_total, start_ref, x_ref, base_ref, steps_ref, out_ref, z_ref, phase_ref):
+    own = lax.axis_index("fcol")
+    width = x_ref.shape[-1]
+    pc, ps = unit(start_ref[0:1, 0:1] * (own * width + lanes(width)), cols_total, 1.0 / math.sqrt(cols_total))
+    re, im = x_ref[0], x_ref[1]
+    z_ref[0], z_ref[1] = halves(jnp.concatenate([re * pc + im * ps, im * pc - re * ps]))
+    phase_ref[0:1], phase_ref[1:2] = pc, ps
+    strip_sums(gs, z_ref, base_ref, steps_ref, out_ref)
+
+
+def first_strips(column_start, facets, waves, gs):
     cols, _, count, _ = waves[0].shape
-    height, width = source.shape[1] // (1 if first else 2), source.shape[2]
-    operands = ([column_start] if first else []) + [source, *waves]
-    return pl.pallas_call(
-        functools.partial(strip_kernel, groups, cols * width),
-        in_specs=[VMEM] * len(operands),
-        out_specs=[VMEM] * (len(groups) + (2 if first else 0)),
+    _, height, width = facets.shape
+    return pl.pallas_call(
+        functools.partial(first_strip_kernel, tuple(gs), cols * width),
+        in_specs=[VMEM] * 4,
+        out_specs=[VMEM] * 3,
+        out_shape=[
+            jax.ShapeDtypeStruct((len(gs), 2, count, height), F32),
+            jax.ShapeDtypeStruct((2, 2 * height, width), BF),
+            jax.ShapeDtypeStruct((2, width), F32),
+        ],
+        compiler_params=LIMIT,
+        cost_estimate=pl.CostEstimate(flops=10**9, bytes_accessed=2 << 20, transcendentals=0),
+        name="first_strips",
+    )(column_start, facets, *waves)
+
+
+def far_strip_kernel(gs, z_ref, base_ref, steps_ref, out_ref):
+    strip_sums(gs, z_ref, base_ref, steps_ref, out_ref)
+
+
+def far_strips(z, waves, gs):
+    return pl.pallas_call(
+        functools.partial(far_strip_kernel, tuple(gs)),
+        in_specs=[VMEM] * 3,
+        out_specs=VMEM,
+        out_shape=jax.ShapeDtypeStruct((len(gs), 2, waves[0].shape[2], z.shape[1] // 2), F32),
+        compiler_params=LIMIT,
+        cost_estimate=pl.CostEstimate(flops=10**9, bytes_accessed=2 << 20, transcendentals=0),
+        name="far_strips",
+    )(z, *waves)
+
+
+def near_strip_kernel(groups, starts_ref, z_ref, base_ref, steps_ref, *refs):
+    out_refs, (turn_ref, away_ref, starts, sem) = refs[: len(groups)], refs[len(groups) :]
+    copy = pltpu.make_async_copy(starts_ref, starts, sem)
+    copy.start()
+    for gs, out_ref in zip(groups, out_refs):
+        strip_sums(gs, z_ref, base_ref, steps_ref, out_ref)
+    copy.wait()
+    rows, _, height = turn_ref.shape
+    rows_total = rows * height
+    mine = starts[lax.axis_index("frow")]
+    for r in range(rows):
+        turn_ref[r, 0:1], turn_ref[r, 1:2] = unit(mine * (r * height + lanes(height)), rows_total, 1.0 / math.sqrt(rows_total))
+        away_ref[r] = jnp.full((1, 128), mine - starts[r], jnp.int32)
+
+
+def near_strips(starts, z, waves, groups):
+    rows, count, height = starts.shape[0], waves[0].shape[2], z.shape[1] // 2
+    return pl.pallas_call(
+        functools.partial(near_strip_kernel, groups),
+        in_specs=[pl.BlockSpec(memory_space=pl.ANY)] + [VMEM] * 3,
+        out_specs=[VMEM] * (len(groups) + 2),
         out_shape=[jax.ShapeDtypeStruct((len(gs), 2, count, height), F32) for gs in groups]
-        + ([jax.ShapeDtypeStruct((2, 2 * height, width), BF), jax.ShapeDtypeStruct((2, width), F32)] if first else []),
-        compiler_params=LIMIT,
-        cost_estimate=pl.CostEstimate(flops=cost, bytes_accessed=2 << 20, transcendentals=0),
-        name="strips",
-    )(*operands)
+        + [jax.ShapeDtypeStruct((rows, 2, height), F32), jax.ShapeDtypeStruct((rows, 1, 128), jnp.int32)],
+        scratch_shapes=[pltpu.SMEM((rows,), jnp.int32), pltpu.SemaphoreType.DMA],
+        compiler_params=LIMIT,
+        cost_estimate=pl.CostEstimate(flops=4 * 10**9, bytes_accessed=2 << 20, transcendentals=0),
+        name="near_strips",
+    )(starts, z, *waves)
 
 
 def pack_kernel(terms, *refs):
@@ -164,11 +210,11 @@
 
 
 class Message:
-    def __init__(self, starts, r, message, b_ref, roots_ref, height, count, rows_total):
+    def __init__(self, r, message, refs, height, count, rows_total):
+        b_ref, roots_ref, turn_ref, away_ref = refs
         own = lax.axis_index("frow")
-        mine, other = starts[own], starts[r]
         strip, rest = message[: 2 * count], message[2 * count :]
-        pc, ps = unit(mine * (r * height + lanes(height)), rows_total, 1.0 / math.sqrt(rows_total))
+        pc, ps = turn_ref[r, 0:1], turn_ref[r, 1:2]
         re, im = strip[:count], strip[count:]
         re, im = re * pc + im * ps, im * pc - re * ps
         high, low = halves(jnp.concatenate([jnp.concatenate([re, im], 1), jnp.concatenate([im, -re], 1)]))
@@ -179,8 +225,8 @@
         turned = jnp.transpose(flat)
         self.weight = jnp.concatenate(halves(turned[:count, :MAXB]), 1)
         row = turned[:MAXB, MAXB : MAXB + 1].astype(jnp.int32)
-        self.place = jnp.where(row < 0, -1, (row + (other - mine)) & (rows_total - 1))
-        self.away = mine - other
+        self.away = away_ref[r][0:1, 0:1]
+        self.place = jnp.where(row < 0, -1, (row - self.away) & (rows_total - 1))
         self.turn = lax.rem(r - own + rows_total // height, rows_total // height)
         self.refs, self.count, self.rows_total = (b_ref, roots_ref), count, rows_total
 
@@ -200,13 +246,14 @@
     return [(begin, min(size, total - begin)) for begin in range(0, total, size)]
 
 
-def gather_kernel(steps, rows, height, count, starts, b_ref, roots_ref, *refs):
+def gather_kernel(steps, rows, height, count, *refs):
+    tables, refs = refs[:4], refs[4:]
     state_ref = None
     if len(refs) > len(steps) + 1:
         state_ref, refs = refs[0], refs[1:]
     at = ring_place(lax.axis_index("frow"), rows)
     found = [
-        Message(starts, ring_block(at + step, rows), message[...], b_ref, roots_ref, height, count, rows * height)
+        Message(ring_block(at + step, rows), message[...], tables, height, count, rows * height)
         for step, message in zip(steps, refs)
     ]
     for begin, size in chunks(rows * height):
@@ -218,26 +265,27 @@
             refs[-1][i, :, begin : begin + size] = value
 
 
-def gather_step(starts, table, roots, state, messages, steps, height):
-    rows_total = table.shape[1]
+def gather_step(tables, state, messages, steps, height):
+    rows_total = tables[0].shape[1]
     count = (messages[0].shape[0] - MAXB - META) // 2
-    operands = [table, roots] + ([] if state is None else [state]) + list(messages)
+    operands = [*tables] + ([] if state is None else [state]) + list(messages)
     return pl.pallas_call(
         functools.partial(gather_kernel, steps, rows_total // height, height, count),
-        in_specs=[SMEM] + [VMEM] * len(operands),
+        in_specs=[VMEM] * len(operands),
         out_specs=VMEM,
         out_shape=jax.ShapeDtypeStruct((3, count, rows_total), F32),
         compiler_params=LIMIT,
         cost_estimate=pl.CostEstimate(flops=10**9, bytes_accessed=4 << 20, transcendentals=0),
         name="gather_step",
-    )(starts, *operands)
-
-
-def back_kernel(rows, height, count, starts, b_ref, turned_ref, roots_ref, state_ref, message_ref, back_ref, sub_ref):
+    )(*operands)
+
+
+def back_kernel(rows, height, count, *refs):
+    tables, (turned_ref, state_ref, message_ref, back_ref, sub_ref) = refs[:4], refs[4:]
     rows_total = rows * height
     own = lax.axis_index("frow")
     r = ring_block(ring_place(own, rows) + rows // 2, rows)
-    message = Message(starts, r, message_ref[...], b_ref, roots_ref, height, count, rows_total)
+    message = Message(r, message_ref[...], tables, height, count, rows_total)
     acc = None
     for begin, size in chunks(rows_total):
         terms = message.chunk(begin, size)
@@ -254,16 +302,16 @@
         acc = part if acc is None else acc + part
     re = acc[:count, :height] - acc[count:, height:]
     im = acc[count:, :height] + acc[:count, height:]
-    pc, ps = unit(starts[own] * (own * height + lanes(height)), rows_total, 1.0 / math.sqrt(rows_total))
+    pc, ps = tables[2][own, 0:1], tables[2][own, 1:2]
     back_ref[0] = jnp.transpose(re * pc - im * ps)
     back_ref[1] = jnp.transpose(im * pc + re * ps)
 
 
-def back_step(starts, table, turned, roots, state, message, height):
+def back_step(tables, turned, state, message, height):
     count, rows_total = state.shape[1:]
     return pl.pallas_call(
         functools.partial(back_kernel, rows_total // height, height, count),
-        in_specs=[SMEM] + [VMEM] * 5,
+        in_specs=[VMEM] * 7,
         out_specs=[VMEM] * 2,
         out_shape=[
             jax.ShapeDtypeStruct((2, height, count), F32),
@@ -271,7 +319,7 @@
         ],
         compiler_params=LIMIT,
         name="back_step",
-    )(starts, table, turned, roots, state, message)
+    )(*tables, turned, state, message)
 
 
 def correct_kernel(sub_ref, gain_ref, roots_ref, out_ref):
@@ -379,10 +427,10 @@
     top = cols // 2
     column_start = column_start.reshape(1, 1)
     waves = waves_of(count, width, cols_total)
-    sent, z, phase = strips(column_start, facets, waves, range(top + 1, cols, 2), first=True)
-    far = strips(column_start, z, waves, range(top, cols, 2))[0] + swap(sent, "fcol", 1)
+    sent, z, phase = first_strips(column_start, facets, waves, range(top + 1, cols, 2))
+    far = far_strips(z, waves, range(top, cols, 2)) + swap(sent, "fcol", 1)
     far, z = lax.optimization_barrier((far, z))
-    sent, near = strips(column_start, z, waves, range(1, top, 2), range(0, top, 2), cost=4 * 10**9)
+    sent, near, *turns = near_strips(subgrid_start, z, waves, [tuple(range(1, top, 2)), tuple(range(0, top, 2))])
     terms = [near + swap(far, "fcol", top), swap(sent, "fcol", 1)]
     bit = 2
     while bit < top:
@@ -391,18 +439,19 @@
         bit *= 2
 
     own = pack(terms, vis_weight, vis_row, vis_count.reshape(1, 1), count, height)
+    tables = b_table, roots, *turns
     order = list(range(0, rows, 2)) + list(range(rows - 1, 0, -2))
     ahead = [(order[i], order[(i + 1) % rows]) for i in range(rows)]
     behind = [(b, a) for a, b in ahead]
-    first_state = state = gather_step(subgrid_start, b_table, roots, None, [own], (0,), height)
+    first_state = state = gather_step(tables, None, [own], (0,), height)
     up = down = own
     for step in range(1, rows // 2):
         up = lax.ppermute(up, "frow", ahead)
         down = lax.ppermute(down, "frow", behind)
         up, state = lax.optimization_barrier((up, state))
-        state = gather_step(subgrid_start, b_table, roots, state, [up, down], (-step, step), height)
+        state = gather_step(tables, state, [up, down], (-step, step), height)
     up = lax.ppermute(up, "frow", ahead)
-    back, sub = back_step(subgrid_start, b_table, turned, roots, state, up, height)
+    back, sub = back_step(tables, turned, state, up, height)
 
     near, far = {0: back}, {top: swap(back, "fcol", top)}
 

time: 45.1 us -> 44.4 us (0.984)
  Pallas kernels: 18 us -> 15.1 us
  waiting for transfers between devices: 11.4 us -> 13.7 us
    pallas_call x4, Pallas kernels: 7.08 us -> 4.94 us  [gather_step(): pl.pallas_call(functools.partial(gather_kernel, steps, rows_total // heig...]
    ppermute x4, waiting for transfers between devices: 7.95 us -> 10.1 us  [per_device(): up = lax.ppermute(up, 'frow', ahead)]
    pallas_call x1, Pallas kernels: 2.32 us -> 1.74 us  [back_step(): pl.pallas_call(functools.partial(back_kernel, rows_total // height, heigh...]
  transfers between devices with their start and end apart: 13 -> 13, of which waited for: 9 -> 9; matrix products, arithmetic and copies ran while one was open for 0% -> 0% of each run, Pallas kernels for 27% -> 23%
where the time goes in v5:
time: 44.4 us; the launch traced here: 44.2 us
  Pallas kernels  15.1 us (34%)
  waiting for transfers between devices  13.7 us (31%)
  starting transfers between devices  13.1 us (30%)
  between operations  2.3 us (5%)
    ppermute x4, waiting for transfers between devices, per_device(): up = lax.ppermute(up, 'frow', ahead)  10.1 us
    ppermute x4, starting transfers between devices, per_device(): up = lax.ppermute(up, 'frow', ahead)  6.55 us
    ppermute x6, starting transfers between devices, swap(): lax.ppermute(value, axis, [(i, i ^ bit) for i in range(lax.axis_size(axis...  5.32 us
    pallas_call x4, Pallas kernels, gather_step(): pl.pallas_call(functools.partial(gather_kernel, steps, rows_total // heig...  4.94 us
    ppermute x6, waiting for transfers between devices, swap(): lax.ppermute(value, axis, [(i, i ^ bit) for i in range(lax.axis_size(axis...  3.56 us
    pallas_call x4, Pallas kernels, image_step(): pl.pallas_call(functools.partial(image_kernel, tuple(gs), first, last), i...  3.3 us
    pallas_call x1, Pallas kernels, back_step(): pl.pallas_call(functools.partial(back_kernel, rows_total // height, heigh...  1.74 us
    pallas_call x1, Pallas kernels, near_strips(): pl.pallas_call(functools.partial(near_strip_kernel, groups), in_specs=[pl...  1.45 us
  transfers between devices with their start and end apart: 13, of which 9 were waited for; matrix products, arithmetic and copies ran while one was open for 0% of the time, Pallas kernels for 23%

profile of v5, /device:TPU:0, one launch (start us, length us, event | category | flops | bytes accessed | tf_op | source)
XLA Modules:
  0.0 44.2 jit_solution(8712577993449543789)
XLA Ops:
  0.6 0.0 copy-start.5
  0.6 0.7 %waves.1 = (f32[4,2,128,128]{3,2,1,0:T(8,128)S(1)}, f32[4,2,128,128]{3,2,1,0:T(8,128)S(1)}) custom-call(), custom_call_target="tpu_custom_call" | custom-call | flops 1000000000 | bytes 2097152 | tf_op jit(solution)/shard_map/waves/pallas_call | solution.py:82
  2.0 0.0 copy-done.5
  2.0 1.0 %first_strips.1 = (f32[1,2,128,128]{3,2,1,0:T(8,128)S(1)}, bf16[2,256,1024]{2,1,0:T(8,128)(2,1)S(1)}, f32[2,1024]{1,0:T(2,128)S(1)}) custom-call(s32[1,1]{1,0:T(1,128)} %bitcast.7.start_ref, f32[2,128,1024]{2,1,0:T(8,128)S(1)} %copy-done.5, f32[4,2,128,128]{3,2,1,0:T(8,128)S(1)} %get-tuple-element.26.base_ref, f32[4,2,128,128]{3,2,1,0:T(8,128)S(1)} %get-tuple-element.27.steps_ref), custom_call_target="tpu_custom_call" | custom-call | flops 1000000000 | bytes 2097152 | tf_op jit(solution)/shard_map/first_strips/pallas_call | solution.py:125
  3.1 0.5 %collective-permute-start = (f32[1,2,128,128]{3,2,1,0:T(8,128)S(1)}, f32[1,2,128,128]{3,2,1,0:T(8,128)S(1)}, u32[]{:S(2)}, u32[]{:S(2)}) collective-permute-start(f32[1,2,128,128]{3,2,1,0:T(8,128)S(1)} %get-tuple-element.29), channel_id=1, source_target_pairs={{0,1},{1,0},{2,3},{3,2},{4,5},{5,4},{6,7},{7,6},{8,9},{9,8},{10,11... | collective-permute-start | bytes 393224 | tf_op jit(solution)/shard_map/ppermute | solution.py:409
  3.6 0.0 copy-start.6
  3.6 0.8 %far_strips.1 = f32[1,2,128,128]{3,2,1,0:T(8,128)S(1)} custom-call(bf16[2,256,1024]{2,1,0:T(8,128)(2,1)S(1)} %get-tuple-element.30.z_ref, f32[4,2,128,128]{3,2,1,0:T(8,128)S(1)} %get-tuple-element.26.base_ref, f32[4,2,128,128]{3,2,1,0:T(8,128)S(1)} %get-tuple-element.27.steps_ref), custom_call_target="tpu_custom_call" | custom-call | flops 1000000000 | bytes 2097152 | tf_op jit(solution)/shard_map/far_strips/pallas_call | solution.py:145
  4.4 0.2 collective-permute-done
  4.6 0.0 copy-start.3
  4.6 0.0 copy-start.4
  4.6 0.0 copy-start
  4.6 0.0 copy-start.1
  4.6 2.9 %collective-permute-start.1 = (f32[1,2,128,128]{3,2,1,0:T(8,128)S(1)}, f32[1,2,128,128]{3,2,1,0:T(8,128)S(1)}, u32[]{:S(2)}, u32[]{:S(2)}) collective-permute-start(f32[1,2,128,128]{3,2,1,0:T(8,128)S(1)} %add.6), channel_id=1, source_target_pairs={{0,2},{1,3},{2,0},{3,1},{4,6},{5,7},{6,4},{7,5},{8,10},{9,11},{10,... | collective-permute-start | bytes 393224 | tf_op jit(solution)/shard_map/ppermute | solution.py:409
  7.6 0.0 copy-done.6
  7.6 1.4 %near_strips.1 = (f32[1,2,128,128]{3,2,1,0:T(8,128)S(1)}, f32[1,2,128,128]{3,2,1,0:T(8,128)S(1)}, f32[8,2,128]{2,1,0:T(2,128)S(1)}, s32[8,1,128]{2,1,0:T(1,128)S(1)}) custom-call(s32[8]{0:T(128)S(1)} %copy-done.6, bf16[2,256,1024]{2,1,0:T(8,128)(2,1)S(1)} %get-tuple-element.30.z_ref, f32[4,2,128,128]{3,2,1,0:T(8,128)S(1)} %get-tuple-element.26.base_ref, ...), custom_call_target="tpu_custom_call" | custom-call | flops 4000000000 | bytes 2097152 | tf_op jit(solution)/shard_map/near_strips/pallas_call | solution.py:173
  9.0 0.1 collective-permute-start.2
  9.8 1.6 %collective-permute-done.1 = f32[1,2,128,128]{3,2,1,0:T(8,128)S(1)} collective-permute-done((f32[1,2,128,128]{3,2,1,0:T(8,128)S(1)}, f32[1,2,128,128]{3,2,1,0:T(8,128)S(1)}, u32[]{:S(2)}, u32[]{:S(2)}) %collective-permute-start.1) | collective-permute-done | bytes 131104 | tf_op jit(solution)/shard_map/ppermute | solution.py:409
  11.4 0.0 collective-permute-done.2.refs_1_
  11.4 0.0 copy-done.3
  11.4 0.0 copy-done.4
  11.4 0.1 pack.1.refs_4_
  11.5 1.8 %collective-permute-start.3 = (f32[328,128]{1,0:T(8,128)S(1)}, f32[328,128]{1,0:T(8,128)S(1)}, u32[]{:S(2)}, u32[]{:S(2)}) collective-permute-start(f32[328,128]{1,0:T(8,128)S(1)} %pack.1.refs_4_), channel_id=1, source_target_pairs={{0,8},{8,16},{16,24},{24,28},{28,20},{20,12},{12,4},{4,0},{1,9},{9... | collective-permute-start | bytes 503816 | tf_op jit(solution)/shard_map/ppermute | solution.py:449
  13.3 0.2 collective-permute-start.5
  13.5 0.0 copy-done
  13.5 0.0 copy-done.1
  13.6 0.8 %gather_step.4.refs_4_.gain_ref = f32[3,128,1024]{2,1,0:T(8,128)S(1)} custom-call(bf16[768,1024]{1,0:T(8,128)(2,1)S(1)} %copy-done, f32[8,2,1024]{2,1,0:T(2,128)S(1)} %copy-done.1, f32[8,2,128]{2,1,0:T(2,128)S(1)} %get-tuple-element.31.refs_2_, s32[8,1,128]{2,1,0:T(1,128)S(1)} %get-tuple-element.32.refs_3_, f32[328,128]{1,0:T(8,128)S(1)} %pack.1.refs_4_), custom_call_target="tpu_custom_call" | custom-call | flops 1000000000 | bytes 4194304 | tf_op jit(solution)/shard_map/gather_step/pallas_call | solution.py:272
  14.4 3.0 %collective-permute-done.3.refs_5_ = f32[328,128]{1,0:T(8,128)S(1)} collective-permute-done((f32[328,128]{1,0:T(8,128)S(1)}, f32[328,128]{1,0:T(8,128)S(1)}, u32[]{:S(2)}, u32[]{:S(2)}) %collective-permute-start.3) | collective-permute-done | bytes 167968 | tf_op jit(solution)/shard_map/ppermute | solution.py:449
  17.3 1.5 %collective-permute-start.4 = (f32[328,128]{1,0:T(8,128)S(1)}, f32[328,128]{1,0:T(8,128)S(1)}, u32[]{:S(2)}, u32[]{:S(2)}) collective-permute-start(f32[328,128]{1,0:T(8,128)S(1)} %collective-permute-done.3.refs_5_), channel_id=1, source_target_pairs={{0,8},{8,16},{16,24},{24,28},{28,20},{20,12},{12,4},{4,0},{1,9},{9... | collective-permute-start | bytes 503816 | tf_op jit(solution)/shard_map/ppermute | solution.py:449
  18.8 0.0 collective-permute-done.5.refs_6_
  18.8 0.5 %collective-permute-start.7 = (f32[328,128]{1,0:T(8,128)S(1)}, f32[328,128]{1,0:T(8,128)S(1)}, u32[]{:S(2)}, u32[]{:S(2)}) collective-permute-start(f32[328,128]{1,0:T(8,128)S(1)} %collective-permute-done.5.refs_6_), channel_id=1, source_target_pairs={{8,0},{16,8},{24,16},{28,24},{20,28},{12,20},{4,12},{0,4},{9,1},{1... | collective-permute-start | bytes 503816 | tf_op jit(solution)/shard_map/ppermute | solution.py:450
  19.4 1.4 %gather_step.5.refs_4_ = f32[3,128,1024]{2,1,0:T(8,128)S(1)} custom-call(bf16[768,1024]{1,0:T(8,128)(2,1)S(1)} %copy-done, f32[8,2,1024]{2,1,0:T(2,128)S(1)} %copy-done.1, f32[8,2,128]{2,1,0:T(2,128)S(1)} %get-tuple-element.31.refs_2_, s32[8,1,128]{2,1,0:T(1,128)S(1)} %get-tuple-element.32.refs_3_, f32[3,128,1024]{2,1,0:T(8,128)S(1)} %gather_step.4.refs_4_.gain_ref, ...), custom_call_target="tpu_custom_call" | custom-call | flops 1000000000 | bytes 4194304 | tf_op jit(solution)/shard_map/gather_step/pallas_call | solution.py:272
  20.8 2.0 %collective-permute-done.4.refs_5_ = f32[328,128]{1,0:T(8,128)S(1)} collective-permute-done((f32[328,128]{1,0:T(8,128)S(1)}, f32[328,128]{1,0:T(8,128)S(1)}, u32[]{:S(2)}, u32[]{:S(2)}) %collective-permute-start.4) | collective-permute-done | bytes 167968 | tf_op jit(solution)/shard_map/ppermute | solution.py:449
  22.7 1.6 %collective-permute-start.6 = (f32[328,128]{1,0:T(8,128)S(1)}, f32[328,128]{1,0:T(8,128)S(1)}, u32[]{:S(2)}, u32[]{:S(2)}) collective-permute-start(f32[328,128]{1,0:T(8,128)S(1)} %collective-permute-done.4.refs_5_), channel_id=1, source_target_pairs={{0,8},{8,16},{16,24},{24,28},{28,20},{20,12},{12,4},{4,0},{1,9},{9... | collective-permute-start | bytes 503816 | tf_op jit(solution)/shard_map/ppermute | solution.py:449
  24.3 0.0 collective-permute-done.7.refs_6_
  24.3 0.5 %collective-permute-start.8 = (f32[328,128]{1,0:T(8,128)S(1)}, f32[328,128]{1,0:T(8,128)S(1)}, u32[]{:S(2)}, u32[]{:S(2)}) collective-permute-start(f32[328,128]{1,0:T(8,128)S(1)} %collective-permute-done.7.refs_6_), channel_id=1, source_target_pairs={{8,0},{16,8},{24,16},{28,24},{20,28},{12,20},{4,12},{0,4},{9,1},{1... | collective-permute-start | bytes 503816 | tf_op jit(solution)/shard_map/ppermute | solution.py:450
  24.8 1.4 %gather_step.6.refs_4_ = f32[3,128,1024]{2,1,0:T(8,128)S(1)} custom-call(bf16[768,1024]{1,0:T(8,128)(2,1)S(1)} %copy-done, f32[8,2,1024]{2,1,0:T(2,128)S(1)} %copy-done.1, f32[8,2,128]{2,1,0:T(2,128)S(1)} %get-tuple-element.31.refs_2_, s32[8,1,128]{2,1,0:T(1,128)S(1)} %get-tuple-element.32.refs_3_, f32[3,128,1024]{2,1,0:T(8,128)S(1)} %gather_step.5.refs_4_, ...), custom_call_target="tpu_custom_call" | custom-call | flops 1000000000 | bytes 4194304 | tf_op jit(solution)/shard_map/gather_step/pallas_call | solution.py:272
  26.2 0.0 copy-start.2
  26.2 2.9 %collective-permute-done.6.refs_5_ = f32[328,128]{1,0:T(8,128)S(1)} collective-permute-done((f32[328,128]{1,0:T(8,128)S(1)}, f32[328,128]{1,0:T(8,128)S(1)}, u32[]{:S(2)}, u32[]{:S(2)}) %collective-permute-start.6) | collective-permute-done | bytes 167968 | tf_op jit(solution)/shard_map/ppermute | solution.py:449
  29.1 1.7 %collective-permute-start.9 = (f32[328,128]{1,0:T(8,128)S(1)}, f32[328,128]{1,0:T(8,128)S(1)}, u32[]{:S(2)}, u32[]{:S(2)}) collective-permute-start(f32[328,128]{1,0:T(8,128)S(1)} %collective-permute-done.6.refs_5_), channel_id=1, source_target_pairs={{0,8},{8,16},{16,24},{24,28},{28,20},{20,12},{12,4},{4,0},{1,9},{9... | collective-permute-start | bytes 503816 | tf_op jit(solution)/shard_map/ppermute | solution.py:453
  30.8 0.0 collective-permute-done.8.refs_6_
  30.8 1.4 %gather_step.7.refs_5_ = f32[3,128,1024]{2,1,0:T(8,128)S(1)} custom-call(bf16[768,1024]{1,0:T(8,128)(2,1)S(1)} %copy-done, f32[8,2,1024]{2,1,0:T(2,128)S(1)} %copy-done.1, f32[8,2,128]{2,1,0:T(2,128)S(1)} %get-tuple-element.31.refs_2_, s32[8,1,128]{2,1,0:T(1,128)S(1)} %get-tuple-element.32.refs_3_, f32[3,128,1024]{2,1,0:T(8,128)S(1)} %gather_step.6.refs_4_, ...), custom_call_target="tpu_custom_call" | custom-call | flops 1000000000 | bytes 4194304 | tf_op jit(solution)/shard_map/gather_step/pallas_call | solution.py:272
  32.2 0.0 copy-start.7
  32.2 2.3 %collective-permute-done.9.refs_6_ = f32[328,128]{1,0:T(8,128)S(1)} collective-permute-done((f32[328,128]{1,0:T(8,128)S(1)}, f32[328,128]{1,0:T(8,128)S(1)}, u32[]{:S(2)}, u32[]{:S(2)}) %collective-permute-start.9) | collective-permute-done | bytes 167968 | tf_op jit(solution)/shard_map/ppermute | solution.py:453
  34.4 0.0 copy-done.2
  34.4 1.7 %back_step.1 = (f32[2,128,128]{2,1,0:T(8,128)S(1)}, f32[2,128,512]{2,1,0:T(8,128)S(1)}) custom-call(bf16[768,1024]{1,0:T(8,128)(2,1)S(1)} %copy-done, f32[8,2,1024]{2,1,0:T(2,128)S(1)} %copy-done.1, f32[8,2,128]{2,1,0:T(2,128)S(1)} %get-tuple-element.31.refs_2_, s32[8,1,128]{2,1,0:T(1,128)S(1)} %get-tuple-element.32.refs_3_, ...), custom_call_target="tpu_custom_call" | custom-call | tf_op jit(solution)/shard_map/back_step/pallas_call | solution.py:312
  36.2 1.7 %collective-permute-start.10 = (f32[2,128,128]{2,1,0:T(8,128)S(1)}, f32[2,128,128]{2,1,0:T(8,128)S(1)}, u32[]{:S(2)}, u32[]{:S(2)}) collective-permute-start(f32[2,128,128]{2,1,0:T(8,128)S(1)} %get-tuple-element.44.refs_0_), channel_id=1, source_target_pairs={{0,2},{1,3},{2,0},{3,1},{4,6},{5,7},{6,4},{7,5},{8,10},{9,11},{10,... | collective-permute-start | bytes 393224 | tf_op jit(solution)/shard_map/ppermute | solution.py:409
  37.9 0.0 copy-done.7
  37.9 0.6 %image_step.4.refs_1_ = f32[2,128,1024]{2,1,0:T(8,128)S(1)} custom-call(f32[2,1024]{1,0:T(2,128)S(1)} %get-tuple-element.43.phase_ref, bf16[4,4,128,1024]{3,2,1,0:T(8,128)(2,1)S(1)} %copy-done.7, f32[2,128,128]{2,1,0:T(8,128)S(1)} %get-tuple-element.44.refs_0_), custom_call_target="tpu_custom_call" | custom-call | flops 4000000000 | bytes 4194304 | tf_op jit(solution)/shard_map/image_step/pallas_call | solution.py:396
  38.5 0.1 collective-permute-start.11
  38.6 1.0 %correct_step.1 = f32[1024,128]{1,0:T(8,128)} custom-call(f32[2,128,512]{2,1,0:T(8,128)S(1)} %get-tuple-element.46.sub_ref, f32[3,128,1024]{2,1,0:T(8,128)S(1)} %gather_step.4.refs_4_.gain_ref, f32[8,2,1024]{2,1,0:T(2,128)S(1)} %copy-done.1), custom_call_target="tpu_custom_call" | custom-call | flops 4000000000 | bytes 4194304 | tf_op jit(solution)/shard_map/correct_step/pallas_call | solution.py:338
  39.6 0.3 collective-permute-done.11.refs_0_
  39.9 0.6 %image_step.5.refs_1_ = f32[2,128,1024]{2,1,0:T(8,128)S(1)} custom-call(f32[2,1024]{1,0:T(2,128)S(1)} %get-tuple-element.43.phase_ref, bf16[4,4,128,1024]{3,2,1,0:T(8,128)(2,1)S(1)} %copy-done.7, f32[2,128,128]{2,1,0:T(8,128)S(1)} %collective-permute-done.11.refs_0_, f32[2,128,1024]{2,1,0:T(8,128)S(1)} %image_step.4.refs_1_), custom_call_target="tpu_custom_call" | custom-call | flops 4000000000 | bytes 4194304 | tf_op jit(solution)/shard_map/image_step/pallas_call | solution.py:396
  40.5 0.7 %collective-permute-done.10.refs_0_ = f32[2,128,128]{2,1,0:T(8,128)S(1)} collective-permute-done((f32[2,128,128]{2,1,0:T(8,128)S(1)}, f32[2,128,128]{2,1,0:T(8,128)S(1)}, u32[]{:S(2)}, u32[]{:S(2)}) %collective-permute-start.10) | collective-permute-done | bytes 131104 | tf_op jit(solution)/shard_map/ppermute | solution.py:409
  41.2 0.0 collective-permute-start.12
  41.2 0.6 %image_step.6.refs_1_ = f32[2,128,1024]{2,1,0:T(8,128)S(1)} custom-call(f32[2,1024]{1,0:T(2,128)S(1)} %get-tuple-element.43.phase_ref, bf16[4,4,128,1024]{3,2,1,0:T(8,128)(2,1)S(1)} %copy-done.7, f32[2,128,128]{2,1,0:T(8,128)S(1)} %collective-permute-done.10.refs_0_, f32[2,128,1024]{2,1,0:T(8,128)S(1)} %image_step.5.refs_1_), custom_call_target="tpu_custom_call" | custom-call | flops 4000000000 | bytes 4194304 | tf_op jit(solution)/shard_map/image_step/pallas_call | solution.py:396
  41.8 0.7 %collective-permute-done.12.refs_0_ = f32[2,128,128]{2,1,0:T(8,128)S(1)} collective-permute-done((f32[2,128,128]{2,1,0:T(8,128)S(1)}, f32[2,128,128]{2,1,0:T(8,128)S(1)}, u32[]{:S(2)}, u32[]{:S(2)}) %collective-permute-start.12) | collective-permute-done | bytes 131104 | tf_op jit(solution)/shard_map/ppermute | solution.py:409
  42.6 1.5 %image_step.7 = f32[2,128,1024]{2,1,0:T(8,128)} custom-call(f32[2,1024]{1,0:T(2,128)S(1)} %get-tuple-element.43.phase_ref, bf16[4,4,128,1024]{3,2,1,0:T(8,128)(2,1)S(1)} %copy-done.7, f32[2,128,128]{2,1,0:T(8,128)S(1)} %collective-permute-done.12.refs_0_, f32[2,128,1024]{2,1,0:T(8,128)S(1)} %image_step.6.refs_1_), custom_call_target="tpu_custom_call" | custom-call | flops 4000000000 | bytes 4194304 | tf_op jit(solution)/shard_map/image_step/pallas_call | solution.py:396
  (2 shorter events, 0.0 us)
Async XLA Ops:
  0.6 1.4 %copy-start.5 = (f32[2,128,1024]{2,1,0:T(8,128)S(1)}, f32[2,128,1024]{2,1,0:T(8,128)}, u32[]{:S(2)}) copy-start(f32[2,128,1024]{2,1,0:T(8,128)} %x_ref.1) | copy-start | bytes 3145732
  3.1 1.5 %collective-permute-start = (f32[1,2,128,128]{3,2,1,0:T(8,128)S(1)}, f32[1,2,128,128]{3,2,1,0:T(8,128)S(1)}, u32[]{:S(2)}, u32[]{:S(2)}) collective-permute-start(f32[1,2,128,128]{3,2,1,0:T(8,128)S(1)} %get-tuple-element.29), channel_id=1, source_target_pairs={{0,1},{1,0},{2,3},{3,2},{4,5},{5,4},{6,7},{7,6},{8,9},{9,8},{10,11... | collective-permute-start | bytes 393224 | tf_op jit(solution)/shard_map/ppermute | solution.py:409
  3.6 4.0 %copy-start.6 = (s32[8]{0:T(128)S(1)}, s32[8]{0:T(128)}, u32[]{:S(2)}) copy-start(s32[8]{0:T(128)} %starts_ref.1) | copy-start | bytes 100
  4.6 6.8 %copy-start.3 = (f32[1,64,128]{2,1,0:T(8,128)S(1)}, f32[1,64,128]{2,1,0:T(8,128)}, u32[]{:S(2)}) copy-start(f32[1,64,128]{2,1,0:T(8,128)} %refs_2_.1) | copy-start | bytes 98308
  4.6 6.8 %copy-start.4 = (s32[1,64]{1,0:T(1,128)S(1)}, s32[1,64]{1,0:T(1,128)}, u32[]{:S(2)}) copy-start(s32[1,64]{1,0:T(1,128)} %refs_3_.1) | copy-start | bytes 772
  4.6 8.9 %copy-start = (bf16[768,1024]{1,0:T(8,128)(2,1)S(1)}, bf16[768,1024]{1,0:T(8,128)(2,1)}, u32[]{:S(2)}) copy-start(bf16[768,1024]{1,0:T(8,128)(2,1)} %constant.10.clone.refs_0_) | copy-start | bytes 4718596
  4.6 8.9 %copy-start.1 = (f32[8,2,1024]{2,1,0:T(2,128)S(1)}, f32[8,2,1024]{2,1,0:T(2,128)}, u32[]{:S(2)}) copy-start(f32[8,2,1024]{2,1,0:T(2,128)} %constant.11.clone.refs_1_.roots_ref) | copy-start | bytes 196612
  4.6 6.8 %collective-permute-start.1 = (f32[1,2,128,128]{3,2,1,0:T(8,128)S(1)}, f32[1,2,128,128]{3,2,1,0:T(8,128)S(1)}, u32[]{:S(2)}, u32[]{:S(2)}) collective-permute-start(f32[1,2,128,128]{3,2,1,0:T(8,128)S(1)} %add.6), channel_id=1, source_target_pairs={{0,2},{1,3},{2,0},{3,1},{4,6},{5,7},{6,4},{7,5},{8,10},{9,11},{10,... | collective-permute-start | bytes 393224 | tf_op jit(solution)/shard_map/ppermute | solution.py:409
  9.0 2.4 %collective-permute-start.2 = (f32[1,2,128,128]{3,2,1,0:T(8,128)S(1)}, f32[1,2,128,128]{3,2,1,0:T(8,128)S(1)}, u32[]{:S(2)}, u32[]{:S(2)}) collective-permute-start(f32[1,2,128,128]{3,2,1,0:T(8,128)S(1)} %get-tuple-element.35), channel_id=1, source_target_pairs={{0,1},{1,0},{2,3},{3,2},{4,5},{5,4},{6,7},{7,6},{8,9},{9,8},{10,11... | collective-permute-start | bytes 393224 | tf_op jit(solution)/shard_map/ppermute | solution.py:409
  11.5 5.8 %collective-permute-start.3 = (f32[328,128]{1,0:T(8,128)S(1)}, f32[328,128]{1,0:T(8,128)S(1)}, u32[]{:S(2)}, u32[]{:S(2)}) collective-permute-start(f32[328,128]{1,0:T(8,128)S(1)} %pack.1.refs_4_), channel_id=1, source_target_pairs={{0,8},{8,16},{16,24},{24,28},{28,20},{20,12},{12,4},{4,0},{1,9},{9... | collective-permute-start | bytes 503816 | tf_op jit(solution)/shard_map/ppermute | solution.py:449
  13.3 5.5 %collective-permute-start.5 = (f32[328,128]{1,0:T(8,128)S(1)}, f32[328,128]{1,0:T(8,128)S(1)}, u32[]{:S(2)}, u32[]{:S(2)}) collective-permute-start(f32[328,128]{1,0:T(8,128)S(1)} %pack.1.refs_4_), channel_id=1, source_target_pairs={{8,0},{16,8},{24,16},{28,24},{20,28},{12,20},{4,12},{0,4},{9,1},{1... | collective-permute-start | bytes 503816 | tf_op jit(solution)/shard_map/ppermute | solution.py:450
  17.3 5.4 %collective-permute-start.4 = (f32[328,128]{1,0:T(8,128)S(1)}, f32[328,128]{1,0:T(8,128)S(1)}, u32[]{:S(2)}, u32[]{:S(2)}) collective-permute-start(f32[328,128]{1,0:T(8,128)S(1)} %collective-permute-done.3.refs_5_), channel_id=1, source_target_pairs={{0,8},{8,16},{16,24},{24,28},{28,20},{20,12},{12,4},{4,0},{1,9},{9... | collective-permute-start | bytes 503816 | tf_op jit(solution)/shard_map/ppermute | solution.py:449
  18.8 5.5 %collective-permute-start.7 = (f32[328,128]{1,0:T(8,128)S(1)}, f32[328,128]{1,0:T(8,128)S(1)}, u32[]{:S(2)}, u32[]{:S(2)}) collective-permute-start(f32[328,128]{1,0:T(8,128)S(1)} %collective-permute-done.5.refs_6_), channel_id=1, source_target_pairs={{8,0},{16,8},{24,16},{28,24},{20,28},{12,20},{4,12},{0,4},{9,1},{1... | collective-permute-start | bytes 503816 | tf_op jit(solution)/shard_map/ppermute | solution.py:450
  22.7 6.4 %collective-permute-start.6 = (f32[328,128]{1,0:T(8,128)S(1)}, f32[328,128]{1,0:T(8,128)S(1)}, u32[]{:S(2)}, u32[]{:S(2)}) collective-permute-start(f32[328,128]{1,0:T(8,128)S(1)} %collective-permute-done.4.refs_5_), channel_id=1, source_target_pairs={{0,8},{8,16},{16,24},{24,28},{28,20},{20,12},{12,4},{4,0},{1,9},{9... | collective-permute-start | bytes 503816 | tf_op jit(solution)/shard_map/ppermute | solution.py:449
  24.3 6.5 %collective-permute-start.8 = (f32[328,128]{1,0:T(8,128)S(1)}, f32[328,128]{1,0:T(8,128)S(1)}, u32[]{:S(2)}, u32[]{:S(2)}) collective-permute-start(f32[328,128]{1,0:T(8,128)S(1)} %collective-permute-done.7.refs_6_), channel_id=1, source_target_pairs={{8,0},{16,8},{24,16},{28,24},{20,28},{12,20},{4,12},{0,4},{9,1},{1... | collective-permute-start | bytes 503816 | tf_op jit(solution)/shard_map/ppermute | solution.py:450
  26.2 8.3 %copy-start.2 = (bf16[1024,512]{1,0:T(8,128)(2,1)S(1)}, bf16[1024,512]{1,0:T(8,128)(2,1)}, u32[]{:S(2)}) copy-start(bf16[1024,512]{1,0:T(8,128)(2,1)} %constant.9.clone.refs_4_) | copy-start | bytes 3145732
  29.1 5.4 %collective-permute-start.9 = (f32[328,128]{1,0:T(8,128)S(1)}, f32[328,128]{1,0:T(8,128)S(1)}, u32[]{:S(2)}, u32[]{:S(2)}) collective-permute-start(f32[328,128]{1,0:T(8,128)S(1)} %collective-permute-done.6.refs_5_), channel_id=1, source_target_pairs={{0,8},{8,16},{16,24},{24,28},{28,20},{20,12},{12,4},{4,0},{1,9},{9... | collective-permute-start | bytes 503816 | tf_op jit(solution)/shard_map/ppermute | solution.py:453
  32.2 5.7 %copy-start.7 = (bf16[4,4,128,1024]{3,2,1,0:T(8,128)(2,1)S(1)}, bf16[4,4,128,1024]{3,2,1,0:T(8,128)(2,1)}, u32[]{:S(2)}) copy-start(bf16[4,4,128,1024]{3,2,1,0:T(8,128)(2,1)} %constant.8.clone.e_ref) | copy-start | bytes 12582916
  36.2 5.0 %collective-permute-start.10 = (f32[2,128,128]{2,1,0:T(8,128)S(1)}, f32[2,128,128]{2,1,0:T(8,128)S(1)}, u32[]{:S(2)}, u32[]{:S(2)}) collective-permute-start(f32[2,128,128]{2,1,0:T(8,128)S(1)} %get-tuple-element.44.refs_0_), channel_id=1, source_target_pairs={{0,2},{1,3},{2,0},{3,1},{4,6},{5,7},{6,4},{7,5},{8,10},{9,11},{10,... | collective-permute-start | bytes 393224 | tf_op jit(solution)/shard_map/ppermute | solution.py:409
  38.5 1.4 %collective-permute-start.11 = (f32[2,128,128]{2,1,0:T(8,128)S(1)}, f32[2,128,128]{2,1,0:T(8,128)S(1)}, u32[]{:S(2)}, u32[]{:S(2)}) collective-permute-start(f32[2,128,128]{2,1,0:T(8,128)S(1)} %get-tuple-element.44.refs_0_), channel_id=1, source_target_pairs={{0,1},{1,0},{2,3},{3,2},{4,5},{5,4},{6,7},{7,6},{8,9},{9,8},{10,11... | collective-permute-start | bytes 393224 | tf_op jit(solution)/shard_map/ppermute | solution.py:409
  41.2 1.3 %collective-permute-start.12 = (f32[2,128,128]{2,1,0:T(8,128)S(1)}, f32[2,128,128]{2,1,0:T(8,128)S(1)}, u32[]{:S(2)}, u32[]{:S(2)}) collective-permute-start(f32[2,128,128]{2,1,0:T(8,128)S(1)} %collective-permute-done.10.refs_0_), channel_id=1, source_target_pairs={{0,1},{1,0},{2,3},{3,2},{4,5},{5,4},{6,7},{7,6},{8,9},{9,8},{10,11... | collective-permute-start | bytes 393224 | tf_op jit(solution)/shard_map/ppermute | solution.py:409

commit v6 on v5

--- a/solution.py
+++ b/solution.py
@@ -89,19 +89,23 @@
     )()
 
 
+def waves_in(base, turn, begin, size):
+    cos, sin = [], []
+    for t in range(begin // 128, (begin + size) // 128):
+        tc, ts = turn[0][:, t : t + 1], turn[1][:, t : t + 1]
+        cos.append(tc * base[0] - ts * base[1])
+        sin.append(ts * base[0] + tc * base[1])
+    return halves(jnp.concatenate([jnp.concatenate(cos, 1), jnp.concatenate(sin, 1)]))
+
+
 def strip_sums(gs, z_ref, base_ref, steps_ref, out_ref):
     count, height = out_ref.shape[-2:]
     z = z_ref[0], z_ref[1]
     for i, g in enumerate(gs):
-        turn_cos, turn_sin, base_cos, base_sin = steps_ref[g, 0], steps_ref[g, 1], base_ref[g, 0], base_ref[g, 1]
+        base, turn = (base_ref[g, 0], base_ref[g, 1]), (steps_ref[g, 0], steps_ref[g, 1])
         acc = None
         for begin, size in chunks(z_ref.shape[-1]):
-            cos, sin = [], []
-            for t in range(begin // 128, (begin + size) // 128):
-                tc, ts = turn_cos[:, t : t + 1], turn_sin[:, t : t + 1]
-                cos.append(tc * base_cos - ts * base_sin)
-                sin.append(ts * base_cos + tc * base_sin)
-            waves = halves(jnp.concatenate([jnp.concatenate(cos, 1), jnp.concatenate(sin, 1)]))
+            waves = waves_in(base, turn, begin, size)
             part = dot3(waves, [value[:, begin : begin + size] for value in z], NT)
             acc = part if acc is None else acc + part
         cos, sin = acc[:count], acc[count:]
@@ -109,13 +113,15 @@
         out_ref[i, 1] = cos[:, height:] - sin[:, :height]
 
 
-def first_strip_kernel(gs, cols_total, start_ref, x_ref, base_ref, steps_ref, out_ref, z_ref, phase_ref):
+def first_strip_kernel(gs, cols_total, start_ref, x_ref, base_ref, steps_ref, out_ref, z_ref, tilt_ref):
     own = lax.axis_index("fcol")
     width = x_ref.shape[-1]
-    pc, ps = unit(start_ref[0:1, 0:1] * (own * width + lanes(width)), cols_total, 1.0 / math.sqrt(cols_total))
+    start, scale = start_ref[0:1, 0:1], 1.0 / math.sqrt(cols_total)
+    pc, ps = unit(start * (own * width + lanes(width)), cols_total, scale)
     re, im = x_ref[0], x_ref[1]
     z_ref[0], z_ref[1] = halves(jnp.concatenate([re * pc + im * ps, im * pc - re * ps]))
-    phase_ref[0:1], phase_ref[1:2] = pc, ps
+    tilt_ref[0:1], tilt_ref[1:2] = unit(start * lanes(128), cols_total)
+    tilt_ref[2:3], tilt_ref[3:4] = unit(start * (own * width + 128 * lanes(128)), cols_total, scale)
     strip_sums(gs, z_ref, base_ref, steps_ref, out_ref)
 
 
@@ -129,7 +135,7 @@
         out_shape=[
             jax.ShapeDtypeStruct((len(gs), 2, count, height), F32),
             jax.ShapeDtypeStruct((2, 2 * height, width), BF),
-            jax.ShapeDtypeStruct((2, width), F32),
+            jax.ShapeDtypeStruct((4, 128), F32),
         ],
         compiler_params=LIMIT,
         cost_estimate=pl.CostEstimate(flops=10**9, bytes_accessed=2 << 20, transcendentals=0),
@@ -246,38 +252,86 @@
     return [(begin, min(size, total - begin)) for begin in range(0, total, size)]
 
 
-def gather_kernel(steps, rows, height, count, *refs):
+def image_waves(base_ref, steps_ref, tilt_ref, out_ref):
+    def tilted(cos, sin, row):
+        pc, ps = tilt_ref[row : row + 1], tilt_ref[row + 1 : row + 2]
+        return cos * pc - sin * ps, sin * pc + cos * ps
+
+    for g in range(out_ref.shape[0]):
+        base, turn = tilted(base_ref[g, 0], base_ref[g, 1], 0), tilted(steps_ref[g, 0], steps_ref[g, 1], 2)
+        for begin, size in chunks(out_ref.shape[-1]):
+            columns = slice(begin, begin + size)
+            out_ref[g, 0, :, columns], out_ref[g, 1, :, columns] = waves_in(base, turn, begin, size)
+
+
+def gather_kernel(kind, steps, rows, height, count, *refs):
     tables, refs = refs[:4], refs[4:]
-    state_ref = None
-    if len(refs) > len(steps) + 1:
-        state_ref, refs = refs[0], refs[1:]
+    odd = lax.rem(lax.axis_index("fcol"), 2) == 1
     at = ring_place(lax.axis_index("frow"), rows)
-    found = [
-        Message(ring_block(at + step, rows), message[...], tables, height, count, rows * height)
-        for step, message in zip(steps, refs)
-    ]
-    for begin, size in chunks(rows * height):
-        terms = [message.chunk(begin, size) for message in found]
-        for i in range(3):
-            value = sum(term[i] for term in terms)
-            if state_ref is not None:
-                value = value + state_ref[i, :, begin : begin + size]
-            refs[-1][i, :, begin : begin + size] = value
-
-
-def gather_step(tables, state, messages, steps, height):
-    rows_total = tables[0].shape[1]
-    count = (messages[0].shape[0] - MAXB - META) // 2
-    operands = [*tables] + ([] if state is None else [state]) + list(messages)
-    return pl.pallas_call(
-        functools.partial(gather_kernel, steps, rows_total // height, height, count),
-        in_specs=[VMEM] * len(operands),
-        out_specs=VMEM,
-        out_shape=jax.ShapeDtypeStruct((3, count, rows_total), F32),
+
+    def add(state_ref, arrived, out_ref):
+        found = [
+            Message(ring_block(at + step, rows), message[...], tables, height, count, rows * height)
+            for step, message in arrived
+        ]
+        for begin, size in chunks(rows * height):
+            terms = [message.chunk(begin, size) for message in found]
+            for i in range(3):
+                value = sum(term[i] for term in terms)
+                if state_ref is not None:
+                    value = value + state_ref[i, :, begin : begin + size]
+                out_ref[i, :, begin : begin + size] = value
+
+    if kind == "first":
+        add(None, zip(steps, refs), refs[-1])
+    elif kind == "plain":
+        add(refs[0], zip(steps, refs[1:]), refs[-1])
+    elif kind == "skip":
+
+        @pl.when(jnp.logical_not(odd))
+        def _():
+            add(refs[0], zip(steps, refs[1:]), refs[-1])
+
+    elif kind == "late":
+        state_ref, before_ref, early, now, waves, (out_ref, made_ref) = (
+            refs[0], refs[1], refs[2:4], refs[4:6], refs[6:9], refs[9:]
+        )
+
+        @pl.when(jnp.logical_not(odd))
+        def _():
+            add(state_ref, zip(steps[2:], now), out_ref)
+
+        @pl.when(odd)
+        def _():
+            add(before_ref, zip(steps, [*early, *now]), out_ref)
+            image_waves(*waves, made_ref)
+
+    else:
+        state_ref, now, waves, made_ref, (out_ref, waves_ref) = refs[0], refs[1:3], refs[3:6], refs[6], refs[7:]
+        add(state_ref, zip(steps, now), out_ref)
+
+        @pl.when(odd)
+        def _():
+            waves_ref[...] = made_ref[...]
+
+        @pl.when(jnp.logical_not(odd))
+        def _():
+            image_waves(*waves, waves_ref)
+
+
+def gather_step(kind, tables, operands, steps, count, made=None):
+    height, rows_total = tables[2].shape[2], tables[0].shape[1]
+    shapes = [jax.ShapeDtypeStruct((3, count, rows_total), F32)] + ([made] if made else [])
+    out = pl.pallas_call(
+        functools.partial(gather_kernel, kind, steps, rows_total // height, height, count),
+        in_specs=[VMEM] * (len(tables) + len(operands)),
+        out_specs=[VMEM] * len(shapes),
+        out_shape=shapes,
         compiler_params=LIMIT,
         cost_estimate=pl.CostEstimate(flops=10**9, bytes_accessed=4 << 20, transcendentals=0),
         name="gather_step",
-    )(*operands)
+    )(*tables, *operands)
+    return out if made else out[0]
 
 
 def back_kernel(rows, height, count, *refs):
@@ -348,35 +402,29 @@
     return jnp.transpose(out, (0, 2, 1, 3)).reshape(1, count, 2, SG)
 
 
-def image_kernel(gs, first, last, phase_ref, e_ref, *refs):
+def image_kernel(gs, first, last, e_ref, *refs):
     backs, refs = refs[: len(gs)], refs[len(gs) :]
     acc_ref = None if first else refs[0]
     out_ref = refs[0 if first else 1]
     if last:
         scratch, sems = refs[-2:]
     width = e_ref.shape[-1]
-    height, count = backs[0].shape[1:]
-    own = lax.axis_index("fcol")
+    height = backs[0].shape[1]
     left = []
-    for back, g in zip(backs, gs):
-        freq = (own ^ g) * count + lanes(count)
-        pc, ps = unit(freq * (own * width), e_ref.shape[0] * width)
+    for back in backs:
         re, im = back[0], back[1]
-        re, im = re * pc - im * ps, im * pc + re * ps
         left.append(halves(jnp.concatenate([jnp.concatenate([re, -im], 1), jnp.concatenate([im, re], 1)])))
     copies = []
     for begin, size in chunks(width):
         columns = slice(begin, begin + size)
         acc = None if first else jnp.concatenate([acc_ref[0, :, columns], acc_ref[1, :, columns]])
         for (high, low), g in zip(left, gs):
-            e = e_ref[own ^ g, 0:2, :, columns], e_ref[own ^ g, 2:4, :, columns]
-            part = dot3((high, low), [value.reshape(2 * count, size) for value in e], NN)
+            part = dot3((high, low), (e_ref[g, 0, :, columns], e_ref[g, 1, :, columns]), NN)
             acc = part if acc is None else acc + part
         re, im = acc[:height], acc[height:]
         if last:
-            pc, ps = phase_ref[0:1, columns], phase_ref[1:2, columns]
-            scratch[0, :, columns] = re * pc - im * ps
-            scratch[1, :, columns] = im * pc + re * ps
+            scratch[0, :, columns] = re
+            scratch[1, :, columns] = im
             copies.append(
                 pltpu.make_async_copy(scratch.at[:, :, columns], out_ref.at[:, :, columns], sems.at[len(copies)])
             )
@@ -388,21 +436,21 @@
         copy.wait()
 
 
-def image_step(phase, table, gs, backs, acc, last):
+def image_step(table, gs, backs, acc, last):
     width = table.shape[-1]
     height = backs[0].shape[1]
     first = acc is None
     operands = list(backs) + ([] if first else [acc])
     return pl.pallas_call(
         functools.partial(image_kernel, tuple(gs), first, last),
-        in_specs=[VMEM] * (2 + len(operands)),
+        in_specs=[VMEM] * (1 + len(operands)),
         out_specs=pl.BlockSpec(memory_space=pl.ANY) if last else VMEM,
         out_shape=jax.ShapeDtypeStruct((2, height, width), F32),
         scratch_shapes=[pltpu.VMEM((2, height, width), F32), pltpu.SemaphoreType.DMA((len(chunks(width)),))] if last else [],
         compiler_params=LIMIT,
         cost_estimate=pl.CostEstimate(flops=4 * 10**9, bytes_accessed=4 << 20, transcendentals=0),
         name="image_step",
-    )(phase, table, *operands)
+    )(table, *operands)
 
 
 def swap(value, axis, bit):
@@ -417,7 +465,6 @@
     count = SG // cols
     assert vis_count.shape[0] == 1 and count <= height
 
-    e_table = jnp.asarray(wave_table(SG, width, cols_total).reshape(4, cols, count, width).transpose(1, 0, 2, 3))
     b_table = wave_table(height, rows_total, rows_total)
     turned = jnp.asarray(b_table.reshape(4 * height, rows_total).T.copy())
     b_table = jnp.asarray(np.concatenate([b_table[:2], b_table]).reshape(6 * height, rows_total))
@@ -427,7 +474,7 @@
     top = cols // 2
     column_start = column_start.reshape(1, 1)
     waves = waves_of(count, width, cols_total)
-    sent, z, phase = first_strips(column_start, facets, waves, range(top + 1, cols, 2))
+    sent, z, tilt = first_strips(column_start, facets, waves, range(top + 1, cols, 2))
     far = far_strips(z, waves, range(top, cols, 2)) + swap(sent, "fcol", 1)
     far, z = lax.optimization_barrier((far, z))
     sent, near, *turns = near_strips(subgrid_start, z, waves, [tuple(range(1, top, 2)), tuple(range(0, top, 2))])
@@ -443,13 +490,27 @@
     order = list(range(0, rows, 2)) + list(range(rows - 1, 0, -2))
     ahead = [(order[i], order[(i + 1) % rows]) for i in range(rows)]
     behind = [(b, a) for a, b in ahead]
-    first_state = state = gather_step(tables, None, [own], (0,), height)
+    first_state = state = gather_step("first", tables, [own], (0,), count)
+    last = rows // 2 - 1
+    assert last >= 3
+    made = jax.ShapeDtypeStruct((cols, 2, 2 * count, width), BF)
     up = down = own
-    for step in range(1, rows // 2):
+    for step in range(1, last + 1):
         up = lax.ppermute(up, "frow", ahead)
         down = lax.ppermute(down, "frow", behind)
         up, state = lax.optimization_barrier((up, state))
-        state = gather_step(tables, state, [up, down], (-step, step), height)
+        if step == last - 2:
+            before, early = state, [up, down]
+            state = gather_step("skip", tables, [state, up, down], (-step, step), count)
+        elif step == last - 1:
+            steps = (1 - step, step - 1, -step, step)
+            operands = [state, before, *early, up, down, *waves, tilt]
+            state, image_table = gather_step("late", tables, operands, steps, count, made)
+        elif step == last:
+            operands = [state, up, down, *waves, tilt, image_table]
+            state, image_table = gather_step("last", tables, operands, (-step, step), count, made)
+        else:
+            state = gather_step("plain", tables, [state, up, down], (-step, step), count)
     up = lax.ppermute(up, "frow", ahead)
     back, sub = back_step(tables, turned, state, up, height)
 
@@ -459,7 +520,7 @@
         return {g ^ bit: swap(b, "fcol", bit) for g, b in blocks.items()}
 
     def image(blocks, acc, last=False):
-        return image_step(phase, e_table, blocks.keys(), list(blocks.values()), acc, last)
+        return image_step(image_table, blocks.keys(), list(blocks.values()), acc, last)
 
     acc = image(near, None)
     near[0], acc = lax.optimization_barrier((back, acc))

time: 44.4 us -> 43.5 us (0.980)
  waiting for transfers between devices: 13.7 us -> 11.3 us
  Pallas kernels: 15.1 us -> 16.4 us
    ppermute x4, waiting for transfers between devices: 10.1 us -> 7.85 us  [per_device(): up = lax.ppermute(up, 'frow', ahead)]
    pallas_call x4, Pallas kernels: 4.94 us -> 6.33 us  [gather_step(): pl.pallas_call(functools.partial(gather_kernel, kind, steps, rows_total /...]
  transfers between devices with their start and end apart: 13 -> 13, of which waited for: 9 -> 9; matrix products, arithmetic and copies ran while one was open for 0% -> 0% of each run, Pallas kernels for 23% -> 26%
where the time goes in v6:
time: 43.5 us; the launch traced here: 43.3 us
  Pallas kernels  16.4 us (38%)
  starting transfers between devices  13.3 us (31%)
  waiting for transfers between devices  11.3 us (26%)
  between operations  2.29 us (5%)
    ppermute x4, waiting for transfers between devices, per_device(): up = lax.ppermute(up, 'frow', ahead)  7.85 us
    ppermute x4, starting transfers between devices, per_device(): up = lax.ppermute(up, 'frow', ahead)  6.55 us
    pallas_call x4, Pallas kernels, gather_step(): pl.pallas_call(functools.partial(gather_kernel, kind, steps, rows_total /...  6.33 us
    ppermute x6, starting transfers between devices, swap(): lax.ppermute(value, axis, [(i, i ^ bit) for i in range(lax.axis_size(axis...  5.51 us
    ppermute x6, waiting for transfers between devices, swap(): lax.ppermute(value, axis, [(i, i ^ bit) for i in range(lax.axis_size(axis...  3.43 us
    pallas_call x4, Pallas kernels, image_step(): pl.pallas_call(functools.partial(image_kernel, tuple(gs), first, last), i...  3.16 us
    pallas_call x1, Pallas kernels, back_step(): pl.pallas_call(functools.partial(back_kernel, rows_total // height, heigh...  1.72 us
    pallas_call x1, Pallas kernels, near_strips(): pl.pallas_call(functools.partial(near_strip_kernel, groups), in_specs=[pl...  1.47 us
  transfers between devices with their start and end apart: 13, of which 9 were waited for; matrix products, arithmetic and copies ran while one was open for 0% of the time, Pallas kernels for 26%

profile of v6, /device:TPU:0, one launch (start us, length us, event | category | flops | bytes accessed | tf_op | source)
XLA Modules:
  0.0 43.3 jit_solution(14495165574032281186)
XLA Ops:
  0.6 0.0 copy-start.5
  0.6 0.7 %waves.1 = (f32[4,2,128,128]{3,2,1,0:T(8,128)S(1)}, f32[4,2,128,128]{3,2,1,0:T(8,128)S(1)}) custom-call(), custom_call_target="tpu_custom_call" | custom-call | flops 1000000000 | bytes 2097152 | tf_op jit(solution)/shard_map/waves/pallas_call | solution.py:82
  2.0 0.0 copy-done.5
  2.0 1.1 %first_strips.1 = (f32[1,2,128,128]{3,2,1,0:T(8,128)S(1)}, bf16[2,256,1024]{2,1,0:T(8,128)(2,1)S(1)}, f32[4,128]{1,0:T(4,128)S(1)}) custom-call(s32[1,1]{1,0:T(1,128)} %bitcast.7.start_ref, f32[2,128,1024]{2,1,0:T(8,128)S(1)} %copy-done.5, f32[4,2,128,128]{3,2,1,0:T(8,128)S(1)} %get-tuple-element.30.base_ref.refs_10_.refs_7_, ...), custom_call_target="tpu_custom_call" | custom-call | flops 1000000000 | bytes 2097152 | tf_op jit(solution)/shard_map/first_strips/pallas_call | solution.py:131
  3.1 0.5 %collective-permute-start = (f32[1,2,128,128]{3,2,1,0:T(8,128)S(1)}, f32[1,2,128,128]{3,2,1,0:T(8,128)S(1)}, u32[]{:S(2)}, u32[]{:S(2)}) collective-permute-start(f32[1,2,128,128]{3,2,1,0:T(8,128)S(1)} %get-tuple-element.33), channel_id=1, source_target_pairs={{0,1},{1,0},{2,3},{3,2},{4,5},{5,4},{6,7},{7,6},{8,9},{9,8},{10,11... | collective-permute-start | bytes 393224 | tf_op jit(solution)/shard_map/ppermute | solution.py:457
  3.6 0.0 copy-start.6
  3.6 0.8 %far_strips.1 = f32[1,2,128,128]{3,2,1,0:T(8,128)S(1)} custom-call(bf16[2,256,1024]{2,1,0:T(8,128)(2,1)S(1)} %get-tuple-element.34.z_ref, f32[4,2,128,128]{3,2,1,0:T(8,128)S(1)} %get-tuple-element.30.base_ref.refs_10_.refs_7_, f32[4,2,128,128]{3,2,1,0:T(8,128)S(1)} %get-tuple-element.31.steps_ref.refs_11_.refs_8_), custom_call_target="tpu_custom_call" | custom-call | flops 1000000000 | bytes 2097152 | tf_op jit(solution)/shard_map/far_strips/pallas_call | solution.py:151
  4.5 0.2 collective-permute-done
  4.6 0.0 copy-start.3
  4.7 0.0 copy-start.4
  4.7 0.0 copy-start
  4.7 0.0 copy-start.1
  4.7 2.9 %collective-permute-start.1 = (f32[1,2,128,128]{3,2,1,0:T(8,128)S(1)}, f32[1,2,128,128]{3,2,1,0:T(8,128)S(1)}, u32[]{:S(2)}, u32[]{:S(2)}) collective-permute-start(f32[1,2,128,128]{3,2,1,0:T(8,128)S(1)} %add.6), channel_id=1, source_target_pairs={{0,2},{1,3},{2,0},{3,1},{4,6},{5,7},{6,4},{7,5},{8,10},{9,11},{10,... | collective-permute-start | bytes 393224 | tf_op jit(solution)/shard_map/ppermute | solution.py:457
  7.6 0.0 copy-done.6
  7.6 1.5 %near_strips.1 = (f32[1,2,128,128]{3,2,1,0:T(8,128)S(1)}, f32[1,2,128,128]{3,2,1,0:T(8,128)S(1)}, f32[8,2,128]{2,1,0:T(2,128)S(1)}, s32[8,1,128]{2,1,0:T(1,128)S(1)}) custom-call(s32[8]{0:T(128)S(1)} %copy-done.6, bf16[2,256,1024]{2,1,0:T(8,128)(2,1)S(1)} %get-tuple-element.34.z_ref, f32[4,2,128,128]{3,2,1,0:T(8,128)S(1)} %get-tuple-element.30.base_ref.refs_10_.refs_7_, ...), custom_call_target="tpu_custom_call" | custom-call | flops 4000000000 | bytes 2097152 | tf_op jit(solution)/shard_map/near_strips/pallas_call | solution.py:179
  9.1 0.1 collective-permute-start.2
  9.8 1.6 %collective-permute-done.1 = f32[1,2,128,128]{3,2,1,0:T(8,128)S(1)} collective-permute-done((f32[1,2,128,128]{3,2,1,0:T(8,128)S(1)}, f32[1,2,128,128]{3,2,1,0:T(8,128)S(1)}, u32[]{:S(2)}, u32[]{:S(2)}) %collective-permute-start.1) | collective-permute-done | bytes 131104 | tf_op jit(solution)/shard_map/ppermute | solution.py:457
  11.5 0.0 collective-permute-done.2.refs_1_
  11.5 0.0 copy-done.3
  11.5 0.0 copy-done.4
  11.5 0.1 pack.1.refs_4_
  11.6 1.8 %collective-permute-start.3 = (f32[328,128]{1,0:T(8,128)S(1)}, f32[328,128]{1,0:T(8,128)S(1)}, u32[]{:S(2)}, u32[]{:S(2)}) collective-permute-start(f32[328,128]{1,0:T(8,128)S(1)} %pack.1.refs_4_), channel_id=1, source_target_pairs={{0,8},{8,16},{16,24},{24,28},{28,20},{20,12},{12,4},{4,0},{1,9},{9... | collective-permute-start | bytes 503816 | tf_op jit(solution)/shard_map/ppermute | solution.py:499
  13.4 0.2 collective-permute-start.5
  13.6 0.0 copy-done
  13.6 0.0 copy-done.1
  13.6 0.8 %gather_step.4.refs_4_.refs_5_.gain_ref = f32[3,128,1024]{2,1,0:T(8,128)S(1)} custom-call(bf16[768,1024]{1,0:T(8,128)(2,1)S(1)} %copy-done, f32[8,2,1024]{2,1,0:T(2,128)S(1)} %copy-done.1, f32[8,2,128]{2,1,0:T(2,128)S(1)} %get-tuple-element.35.refs_2_, s32[8,1,128]{2,1,0:T(1,128)S(1)} %get-tuple-element.36.refs_3_, f32[328,128]{1,0:T(8,128)S(1)} %pack.1.refs_4_), custom_call_target="tpu_custom_call" | custom-call | flops 1000000000 | bytes 4194304 | tf_op jit(solution)/shard_map/gather_step/pallas_call | solution.py:325
  14.4 3.0 %collective-permute-done.3.refs_5_.refs_6_ = f32[328,128]{1,0:T(8,128)S(1)} collective-permute-done((f32[328,128]{1,0:T(8,128)S(1)}, f32[328,128]{1,0:T(8,128)S(1)}, u32[]{:S(2)}, u32[]{:S(2)}) %collective-permute-start.3) | collective-permute-done | bytes 167968 | tf_op jit(solution)/shard_map/ppermute | solution.py:499
  17.4 1.5 %collective-permute-start.4 = (f32[328,128]{1,0:T(8,128)S(1)}, f32[328,128]{1,0:T(8,128)S(1)}, u32[]{:S(2)}, u32[]{:S(2)}) collective-permute-start(f32[328,128]{1,0:T(8,128)S(1)} %collective-permute-done.3.refs_5_.refs_6_), channel_id=1, source_target_pairs={{0,8},{8,16},{16,24},{24,28},{28,20},{20,12},{12,4},{4,0},{1,9},{9... | collective-permute-start | bytes 503816 | tf_op jit(solution)/shard_map/ppermute | solution.py:499
  18.9 0.0 collective-permute-done.5.refs_6_.refs_7_
  18.9 0.5 %collective-permute-start.7 = (f32[328,128]{1,0:T(8,128)S(1)}, f32[328,128]{1,0:T(8,128)S(1)}, u32[]{:S(2)}, u32[]{:S(2)}) collective-permute-start(f32[328,128]{1,0:T(8,128)S(1)} %collective-permute-done.5.refs_6_.refs_7_), channel_id=1, source_target_pairs={{8,0},{16,8},{24,16},{28,24},{20,28},{12,20},{4,12},{0,4},{9,1},{1... | collective-permute-start | bytes 503816 | tf_op jit(solution)/shard_map/ppermute | solution.py:500
  19.4 1.4 %gather_step.5.refs_4_ = f32[3,128,1024]{2,1,0:T(8,128)S(1)} custom-call(bf16[768,1024]{1,0:T(8,128)(2,1)S(1)} %copy-done, f32[8,2,1024]{2,1,0:T(2,128)S(1)} %copy-done.1, f32[8,2,128]{2,1,0:T(2,128)S(1)} %get-tuple-element.35.refs_2_, s32[8,1,128]{2,1,0:T(1,128)S(1)} %get-tuple-element.36.refs_3_, f32[3,128,1024]{2,1,0:T(8,128)S(1)} %gather_step.4.refs_4_.refs_5_.gain_ref, ...), custom_call_target="tpu_custom_call" | custom-call | flops 1000000000 | bytes 4194304 | tf_op jit(solution)/shard_map/gather_step/pallas_call | solution.py:325
  20.8 2.0 %collective-permute-done.4.refs_8_ = f32[328,128]{1,0:T(8,128)S(1)} collective-permute-done((f32[328,128]{1,0:T(8,128)S(1)}, f32[328,128]{1,0:T(8,128)S(1)}, u32[]{:S(2)}, u32[]{:S(2)}) %collective-permute-start.4) | collective-permute-done | bytes 167968 | tf_op jit(solution)/shard_map/ppermute | solution.py:499
  22.8 1.6 %collective-permute-start.6 = (f32[328,128]{1,0:T(8,128)S(1)}, f32[328,128]{1,0:T(8,128)S(1)}, u32[]{:S(2)}, u32[]{:S(2)}) collective-permute-start(f32[328,128]{1,0:T(8,128)S(1)} %collective-permute-done.4.refs_8_), channel_id=1, source_target_pairs={{0,8},{8,16},{16,24},{24,28},{28,20},{20,12},{12,4},{4,0},{1,9},{9... | collective-permute-start | bytes 503816 | tf_op jit(solution)/shard_map/ppermute | solution.py:499
  24.3 0.0 collective-permute-done.7.refs_9_
  24.3 0.5 %collective-permute-start.8 = (f32[328,128]{1,0:T(8,128)S(1)}, f32[328,128]{1,0:T(8,128)S(1)}, u32[]{:S(2)}, u32[]{:S(2)}) collective-permute-start(f32[328,128]{1,0:T(8,128)S(1)} %collective-permute-done.7.refs_9_), channel_id=1, source_target_pairs={{8,0},{16,8},{24,16},{28,24},{20,28},{12,20},{4,12},{0,4},{9,1},{1... | collective-permute-start | bytes 503816 | tf_op jit(solution)/shard_map/ppermute | solution.py:500
  24.8 1.4 %gather_step.6 = (f32[3,128,1024]{2,1,0:T(8,128)S(1)}, bf16[4,2,256,1024]{3,2,1,0:T(8,128)(2,1)S(1)}) custom-call(bf16[768,1024]{1,0:T(8,128)(2,1)S(1)} %copy-done, f32[8,2,1024]{2,1,0:T(2,128)S(1)} %copy-done.1, f32[8,2,128]{2,1,0:T(2,128)S(1)} %get-tuple-element.35.refs_2_, s32[8,1,128]{2,1,0:T(1,128)S(1)} %get-tuple-element.36.refs_3_, ...), custom_call_target="tpu_custom_call" | custom-call | flops 1000000000 | bytes 4194304 | tf_op jit(solution)/shard_map/gather_step/pallas_call | solution.py:325
  26.2 2.1 %collective-permute-done.6.refs_5_ = f32[328,128]{1,0:T(8,128)S(1)} collective-permute-done((f32[328,128]{1,0:T(8,128)S(1)}, f32[328,128]{1,0:T(8,128)S(1)}, u32[]{:S(2)}, u32[]{:S(2)}) %collective-permute-start.6) | collective-permute-done | bytes 167968 | tf_op jit(solution)/shard_map/ppermute | solution.py:499
  28.3 1.7 %collective-permute-start.9 = (f32[328,128]{1,0:T(8,128)S(1)}, f32[328,128]{1,0:T(8,128)S(1)}, u32[]{:S(2)}, u32[]{:S(2)}) collective-permute-start(f32[328,128]{1,0:T(8,128)S(1)} %collective-permute-done.6.refs_5_), channel_id=1, source_target_pairs={{0,8},{8,16},{16,24},{24,28},{28,20},{20,12},{12,4},{4,0},{1,9},{9... | collective-permute-start | bytes 503816 | tf_op jit(solution)/shard_map/ppermute | solution.py:514
  30.0 0.0 collective-permute-done.8.refs_6_
  30.0 0.0 copy-start.2
  30.0 2.8 %gather_step.7 = (f32[3,128,1024]{2,1,0:T(8,128)S(1)}, bf16[4,2,256,1024]{3,2,1,0:T(8,128)(2,1)S(1)}) custom-call(bf16[768,1024]{1,0:T(8,128)(2,1)S(1)} %copy-done, f32[8,2,1024]{2,1,0:T(2,128)S(1)} %copy-done.1, f32[8,2,128]{2,1,0:T(2,128)S(1)} %get-tuple-element.35.refs_2_, s32[8,1,128]{2,1,0:T(1,128)S(1)} %get-tuple-element.36.refs_3_, ...), custom_call_target="tpu_custom_call" | custom-call | flops 1000000000 | bytes 4194304 | tf_op jit(solution)/shard_map/gather_step/pallas_call | solution.py:325
  32.8 0.8 %collective-permute-done.9.refs_6_ = f32[328,128]{1,0:T(8,128)S(1)} collective-permute-done((f32[328,128]{1,0:T(8,128)S(1)}, f32[328,128]{1,0:T(8,128)S(1)}, u32[]{:S(2)}, u32[]{:S(2)}) %collective-permute-start.9) | collective-permute-done | bytes 167968 | tf_op jit(solution)/shard_map/ppermute | solution.py:514
  33.6 0.0 copy-done.2
  33.6 1.7 %back_step.1 = (f32[2,128,128]{2,1,0:T(8,128)S(1)}, f32[2,128,512]{2,1,0:T(8,128)S(1)}) custom-call(bf16[768,1024]{1,0:T(8,128)(2,1)S(1)} %copy-done, f32[8,2,1024]{2,1,0:T(2,128)S(1)} %copy-done.1, f32[8,2,128]{2,1,0:T(2,128)S(1)} %get-tuple-element.35.refs_2_, s32[8,1,128]{2,1,0:T(1,128)S(1)} %get-tuple-element.36.refs_3_, ...), custom_call_target="tpu_custom_call" | custom-call | tf_op jit(solution)/shard_map/back_step/pallas_call | solution.py:366
  35.4 1.9 %collective-permute-start.10 = (f32[2,128,128]{2,1,0:T(8,128)S(1)}, f32[2,128,128]{2,1,0:T(8,128)S(1)}, u32[]{:S(2)}, u32[]{:S(2)}) collective-permute-start(f32[2,128,128]{2,1,0:T(8,128)S(1)} %get-tuple-element.52.refs_0_), channel_id=1, source_target_pairs={{0,2},{1,3},{2,0},{3,1},{4,6},{5,7},{6,4},{7,5},{8,10},{9,11},{10,... | collective-permute-start | bytes 393224 | tf_op jit(solution)/shard_map/ppermute | solution.py:457
  37.3 0.6 %image_step.4.refs_1_ = f32[2,128,1024]{2,1,0:T(8,128)S(1)} custom-call(bf16[4,2,256,1024]{3,2,1,0:T(8,128)(2,1)S(1)} %get-tuple-element.51.e_ref, f32[2,128,128]{2,1,0:T(8,128)S(1)} %get-tuple-element.52.refs_0_), custom_call_target="tpu_custom_call" | custom-call | flops 4000000000 | bytes 4194304 | tf_op jit(solution)/shard_map/image_step/pallas_call | solution.py:444
  37.9 0.1 collective-permute-start.11
  37.9 1.0 %correct_step.1 = f32[1024,128]{1,0:T(8,128)} custom-call(f32[2,128,512]{2,1,0:T(8,128)S(1)} %get-tuple-element.54.sub_ref, f32[3,128,1024]{2,1,0:T(8,128)S(1)} %gather_step.4.refs_4_.refs_5_.gain_ref, f32[8,2,1024]{2,1,0:T(2,128)S(1)} %copy-done.1), custom_call_target="tpu_custom_call" | custom-call | flops 4000000000 | bytes 4194304 | tf_op jit(solution)/shard_map/correct_step/pallas_call | solution.py:392
  38.9 0.4 collective-permute-done.11.refs_0_
  39.3 0.6 %image_step.5.refs_1_ = f32[2,128,1024]{2,1,0:T(8,128)S(1)} custom-call(bf16[4,2,256,1024]{3,2,1,0:T(8,128)(2,1)S(1)} %get-tuple-element.51.e_ref, f32[2,128,128]{2,1,0:T(8,128)S(1)} %collective-permute-done.11.refs_0_, f32[2,128,1024]{2,1,0:T(8,128)S(1)} %image_step.4.refs_1_), custom_call_target="tpu_custom_call" | custom-call | flops 4000000000 | bytes 4194304 | tf_op jit(solution)/shard_map/image_step/pallas_call | solution.py:444
  39.9 0.5 %collective-permute-done.10.refs_0_ = f32[2,128,128]{2,1,0:T(8,128)S(1)} collective-permute-done((f32[2,128,128]{2,1,0:T(8,128)S(1)}, f32[2,128,128]{2,1,0:T(8,128)S(1)}, u32[]{:S(2)}, u32[]{:S(2)}) %collective-permute-start.10) | collective-permute-done | bytes 131104 | tf_op jit(solution)/shard_map/ppermute | solution.py:457
  40.4 0.0 collective-permute-start.12
  40.4 0.6 %image_step.6.refs_1_ = f32[2,128,1024]{2,1,0:T(8,128)S(1)} custom-call(bf16[4,2,256,1024]{3,2,1,0:T(8,128)(2,1)S(1)} %get-tuple-element.51.e_ref, f32[2,128,128]{2,1,0:T(8,128)S(1)} %collective-permute-done.10.refs_0_, f32[2,128,1024]{2,1,0:T(8,128)S(1)} %image_step.5.refs_1_), custom_call_target="tpu_custom_call" | custom-call | flops 4000000000 | bytes 4194304 | tf_op jit(solution)/shard_map/image_step/pallas_call | solution.py:444
  41.0 0.8 %collective-permute-done.12.refs_0_ = f32[2,128,128]{2,1,0:T(8,128)S(1)} collective-permute-done((f32[2,128,128]{2,1,0:T(8,128)S(1)}, f32[2,128,128]{2,1,0:T(8,128)S(1)}, u32[]{:S(2)}, u32[]{:S(2)}) %collective-permute-start.12) | collective-permute-done | bytes 131104 | tf_op jit(solution)/shard_map/ppermute | solution.py:457
  41.7 1.4 %image_step.7 = f32[2,128,1024]{2,1,0:T(8,128)} custom-call(bf16[4,2,256,1024]{3,2,1,0:T(8,128)(2,1)S(1)} %get-tuple-element.51.e_ref, f32[2,128,128]{2,1,0:T(8,128)S(1)} %collective-permute-done.12.refs_0_, f32[2,128,1024]{2,1,0:T(8,128)S(1)} %image_step.6.refs_1_), custom_call_target="tpu_custom_call" | custom-call | flops 4000000000 | bytes 4194304 | tf_op jit(solution)/shard_map/image_step/pallas_call | solution.py:444
  (2 shorter events, 0.0 us)
Async XLA Ops:
  0.6 1.4 %copy-start.5 = (f32[2,128,1024]{2,1,0:T(8,128)S(1)}, f32[2,128,1024]{2,1,0:T(8,128)}, u32[]{:S(2)}) copy-start(f32[2,128,1024]{2,1,0:T(8,128)} %x_ref.1) | copy-start | bytes 3145732
  3.1 1.5 %collective-permute-start = (f32[1,2,128,128]{3,2,1,0:T(8,128)S(1)}, f32[1,2,128,128]{3,2,1,0:T(8,128)S(1)}, u32[]{:S(2)}, u32[]{:S(2)}) collective-permute-start(f32[1,2,128,128]{3,2,1,0:T(8,128)S(1)} %get-tuple-element.33), channel_id=1, source_target_pairs={{0,1},{1,0},{2,3},{3,2},{4,5},{5,4},{6,7},{7,6},{8,9},{9,8},{10,11... | collective-permute-start | bytes 393224 | tf_op jit(solution)/shard_map/ppermute | solution.py:457
  3.6 4.0 %copy-start.6 = (s32[8]{0:T(128)S(1)}, s32[8]{0:T(128)}, u32[]{:S(2)}) copy-start(s32[8]{0:T(128)} %starts_ref.1) | copy-start | bytes 100
  4.6 6.8 %copy-start.3 = (f32[1,64,128]{2,1,0:T(8,128)S(1)}, f32[1,64,128]{2,1,0:T(8,128)}, u32[]{:S(2)}) copy-start(f32[1,64,128]{2,1,0:T(8,128)} %refs_2_.1) | copy-start | bytes 98308
  4.7 6.8 %copy-start.4 = (s32[1,64]{1,0:T(1,128)S(1)}, s32[1,64]{1,0:T(1,128)}, u32[]{:S(2)}) copy-start(s32[1,64]{1,0:T(1,128)} %refs_3_.1) | copy-start | bytes 772
  4.7 8.9 %copy-start = (bf16[768,1024]{1,0:T(8,128)(2,1)S(1)}, bf16[768,1024]{1,0:T(8,128)(2,1)}, u32[]{:S(2)}) copy-start(bf16[768,1024]{1,0:T(8,128)(2,1)} %constant.7.clone.refs_0_) | copy-start | bytes 4718596
  4.7 8.9 %copy-start.1 = (f32[8,2,1024]{2,1,0:T(2,128)S(1)}, f32[8,2,1024]{2,1,0:T(2,128)}, u32[]{:S(2)}) copy-start(f32[8,2,1024]{2,1,0:T(2,128)} %constant.8.clone.refs_1_.roots_ref) | copy-start | bytes 196612
  4.7 6.8 %collective-permute-start.1 = (f32[1,2,128,128]{3,2,1,0:T(8,128)S(1)}, f32[1,2,128,128]{3,2,1,0:T(8,128)S(1)}, u32[]{:S(2)}, u32[]{:S(2)}) collective-permute-start(f32[1,2,128,128]{3,2,1,0:T(8,128)S(1)} %add.6), channel_id=1, source_target_pairs={{0,2},{1,3},{2,0},{3,1},{4,6},{5,7},{6,4},{7,5},{8,10},{9,11},{10,... | collective-permute-start | bytes 393224 | tf_op jit(solution)/shard_map/ppermute | solution.py:457
  9.1 2.3 %collective-permute-start.2 = (f32[1,2,128,128]{3,2,1,0:T(8,128)S(1)}, f32[1,2,128,128]{3,2,1,0:T(8,128)S(1)}, u32[]{:S(2)}, u32[]{:S(2)}) collective-permute-start(f32[1,2,128,128]{3,2,1,0:T(8,128)S(1)} %get-tuple-element.39), channel_id=1, source_target_pairs={{0,1},{1,0},{2,3},{3,2},{4,5},{5,4},{6,7},{7,6},{8,9},{9,8},{10,11... | collective-permute-start | bytes 393224 | tf_op jit(solution)/shard_map/ppermute | solution.py:457
  11.6 5.8 %collective-permute-start.3 = (f32[328,128]{1,0:T(8,128)S(1)}, f32[328,128]{1,0:T(8,128)S(1)}, u32[]{:S(2)}, u32[]{:S(2)}) collective-permute-start(f32[328,128]{1,0:T(8,128)S(1)} %pack.1.refs_4_), channel_id=1, source_target_pairs={{0,8},{8,16},{16,24},{24,28},{28,20},{20,12},{12,4},{4,0},{1,9},{9... | collective-permute-start | bytes 503816 | tf_op jit(solution)/shard_map/ppermute | solution.py:499
  13.4 5.5 %collective-permute-start.5 = (f32[328,128]{1,0:T(8,128)S(1)}, f32[328,128]{1,0:T(8,128)S(1)}, u32[]{:S(2)}, u32[]{:S(2)}) collective-permute-start(f32[328,128]{1,0:T(8,128)S(1)} %pack.1.refs_4_), channel_id=1, source_target_pairs={{8,0},{16,8},{24,16},{28,24},{20,28},{12,20},{4,12},{0,4},{9,1},{1... | collective-permute-start | bytes 503816 | tf_op jit(solution)/shard_map/ppermute | solution.py:500
  17.4 5.4 %collective-permute-start.4 = (f32[328,128]{1,0:T(8,128)S(1)}, f32[328,128]{1,0:T(8,128)S(1)}, u32[]{:S(2)}, u32[]{:S(2)}) collective-permute-start(f32[328,128]{1,0:T(8,128)S(1)} %collective-permute-done.3.refs_5_.refs_6_), channel_id=1, source_target_pairs={{0,8},{8,16},{16,24},{24,28},{28,20},{20,12},{12,4},{4,0},{1,9},{9... | collective-permute-start | bytes 503816 | tf_op jit(solution)/shard_map/ppermute | solution.py:499
  18.9 5.5 %collective-permute-start.7 = (f32[328,128]{1,0:T(8,128)S(1)}, f32[328,128]{1,0:T(8,128)S(1)}, u32[]{:S(2)}, u32[]{:S(2)}) collective-permute-start(f32[328,128]{1,0:T(8,128)S(1)} %collective-permute-done.5.refs_6_.refs_7_), channel_id=1, source_target_pairs={{8,0},{16,8},{24,16},{28,24},{20,28},{12,20},{4,12},{0,4},{9,1},{1... | collective-permute-start | bytes 503816 | tf_op jit(solution)/shard_map/ppermute | solution.py:500
  22.8 5.5 %collective-permute-start.6 = (f32[328,128]{1,0:T(8,128)S(1)}, f32[328,128]{1,0:T(8,128)S(1)}, u32[]{:S(2)}, u32[]{:S(2)}) collective-permute-start(f32[328,128]{1,0:T(8,128)S(1)} %collective-permute-done.4.refs_8_), channel_id=1, source_target_pairs={{0,8},{8,16},{16,24},{24,28},{28,20},{20,12},{12,4},{4,0},{1,9},{9... | collective-permute-start | bytes 503816 | tf_op jit(solution)/shard_map/ppermute | solution.py:499
  24.3 5.6 %collective-permute-start.8 = (f32[328,128]{1,0:T(8,128)S(1)}, f32[328,128]{1,0:T(8,128)S(1)}, u32[]{:S(2)}, u32[]{:S(2)}) collective-permute-start(f32[328,128]{1,0:T(8,128)S(1)} %collective-permute-done.7.refs_9_), channel_id=1, source_target_pairs={{8,0},{16,8},{24,16},{28,24},{20,28},{12,20},{4,12},{0,4},{9,1},{1... | collective-permute-start | bytes 503816 | tf_op jit(solution)/shard_map/ppermute | solution.py:500
  28.3 5.4 %collective-permute-start.9 = (f32[328,128]{1,0:T(8,128)S(1)}, f32[328,128]{1,0:T(8,128)S(1)}, u32[]{:S(2)}, u32[]{:S(2)}) collective-permute-start(f32[328,128]{1,0:T(8,128)S(1)} %collective-permute-done.6.refs_5_), channel_id=1, source_target_pairs={{0,8},{8,16},{16,24},{24,28},{28,20},{20,12},{12,4},{4,0},{1,9},{9... | collective-permute-start | bytes 503816 | tf_op jit(solution)/shard_map/ppermute | solution.py:514
  30.0 3.7 %copy-start.2 = (bf16[1024,512]{1,0:T(8,128)(2,1)S(1)}, bf16[1024,512]{1,0:T(8,128)(2,1)}, u32[]{:S(2)}) copy-start(bf16[1024,512]{1,0:T(8,128)(2,1)} %constant.6.clone.refs_4_) | copy-start | bytes 3145732
  35.4 5.0 %collective-permute-start.10 = (f32[2,128,128]{2,1,0:T(8,128)S(1)}, f32[2,128,128]{2,1,0:T(8,128)S(1)}, u32[]{:S(2)}, u32[]{:S(2)}) collective-permute-start(f32[2,128,128]{2,1,0:T(8,128)S(1)} %get-tuple-element.52.refs_0_), channel_id=1, source_target_pairs={{0,2},{1,3},{2,0},{3,1},{4,6},{5,7},{6,4},{7,5},{8,10},{9,11},{10,... | collective-permute-start | bytes 393224 | tf_op jit(solution)/shard_map/ppermute | solution.py:457
  37.9 1.4 %collective-permute-start.11 = (f32[2,128,128]{2,1,0:T(8,128)S(1)}, f32[2,128,128]{2,1,0:T(8,128)S(1)}, u32[]{:S(2)}, u32[]{:S(2)}) collective-permute-start(f32[2,128,128]{2,1,0:T(8,128)S(1)} %get-tuple-element.52.refs_0_), channel_id=1, source_target_pairs={{0,1},{1,0},{2,3},{3,2},{4,5},{5,4},{6,7},{7,6},{8,9},{9,8},{10,11... | collective-permute-start | bytes 393224 | tf_op jit(solution)/shard_map/ppermute | solution.py:457
  40.4 1.3 %collective-permute-start.12 = (f32[2,128,128]{2,1,0:T(8,128)S(1)}, f32[2,128,128]{2,1,0:T(8,128)S(1)}, u32[]{:S(2)}, u32[]{:S(2)}) collective-permute-start(f32[2,128,128]{2,1,0:T(8,128)S(1)} %collective-permute-done.10.refs_0_), channel_id=1, source_target_pairs={{0,1},{1,0},{2,3},{3,2},{4,5},{5,4},{6,7},{7,6},{8,9},{9,8},{10,11... | collective-permute-start | bytes 393224 | tf_op jit(solution)/shard_map/ppermute | solution.py:457

commit v7 on v6

--- a/solution.py
+++ b/solution.py
@@ -269,13 +269,15 @@
     odd = lax.rem(lax.axis_index("fcol"), 2) == 1
     at = ring_place(lax.axis_index("frow"), rows)
 
-    def add(state_ref, arrived, out_ref):
+    def add(state_ref, arrived, out_ref, gain_ref=None):
         found = [
             Message(ring_block(at + step, rows), message[...], tables, height, count, rows * height)
             for step, message in arrived
         ]
         for begin, size in chunks(rows * height):
             terms = [message.chunk(begin, size) for message in found]
+            if gain_ref is not None and begin < SG:
+                gain_ref[:, begin : begin + size] = terms[0][2]
             for i in range(3):
                 value = sum(term[i] for term in terms)
                 if state_ref is not None:
@@ -286,14 +288,21 @@
         add(None, zip(steps, refs), refs[-1])
     elif kind == "plain":
         add(refs[0], zip(steps, refs[1:]), refs[-1])
+    elif kind == "own":
+
+        @pl.when(jnp.logical_not(odd))
+        def _():
+            add(None, zip(steps, refs), refs[-1])
+
     elif kind == "skip":
 
         @pl.when(jnp.logical_not(odd))
         def _():
             add(refs[0], zip(steps, refs[1:]), refs[-1])
 
-    elif kind == "late":
-        state_ref, before_ref, early, now, waves, (out_ref, made_ref) = (
+    elif kind in ("late", "late own"):
+        whole = kind == "late own"
+        state_ref, before_ref, early, now, waves, (out_ref, made_ref, gain_ref) = (
             refs[0], refs[1], refs[2:4], refs[4:6], refs[6:9], refs[9:]
         )
 
@@ -303,7 +312,10 @@
 
         @pl.when(odd)
         def _():
-            add(before_ref, zip(steps, [*early, *now]), out_ref)
+            if whole:
+                add(None, zip((0, *steps), [before_ref, *early, *now]), out_ref, gain_ref)
+            else:
+                add(before_ref, zip(steps, [*early, *now]), out_ref)
             image_waves(*waves, made_ref)
 
     else:
@@ -319,9 +331,9 @@
             image_waves(*waves, waves_ref)
 
 
-def gather_step(kind, tables, operands, steps, count, made=None):
+def gather_step(kind, tables, operands, steps, count, *more):
     height, rows_total = tables[2].shape[2], tables[0].shape[1]
-    shapes = [jax.ShapeDtypeStruct((3, count, rows_total), F32)] + ([made] if made else [])
+    shapes = [jax.ShapeDtypeStruct((3, count, rows_total), F32), *more]
     out = pl.pallas_call(
         functools.partial(gather_kernel, kind, steps, rows_total // height, height, count),
         in_specs=[VMEM] * (len(tables) + len(operands)),
@@ -331,7 +343,7 @@
         cost_estimate=pl.CostEstimate(flops=10**9, bytes_accessed=4 << 20, transcendentals=0),
         name="gather_step",
     )(*tables, *operands)
-    return out if made else out[0]
+    return out if more else out[0]
 
 
 def back_kernel(rows, height, count, *refs):
@@ -376,28 +388,30 @@
     )(*tables, turned, state, message)
 
 
-def correct_kernel(sub_ref, gain_ref, roots_ref, out_ref):
+def correct_kernel(whole, sub_ref, gain_ref, late_ref, roots_ref, out_ref):
     count = sub_ref.shape[1]
     pieces = SG // 128
     own = lax.axis_index("frow")
     pc, ps = roots_ref[own, 0:1, :SG], roots_ref[own, 1:2, :SG]
     re, im, gain = sub_ref[0], sub_ref[1], gain_ref[2, :, :SG]
+    if whole:
+        gain = jnp.where(lax.rem(lax.axis_index("fcol"), 2) == 1, late_ref[...], gain)
     for part, value in enumerate([(re * pc + im * ps) * gain, (im * pc - re * ps) * gain]):
         for i in range(pieces):
             out_ref[pl.ds(2 * i + part, count, stride=2 * pieces), :] = value[:, 128 * i : 128 * (i + 1)]
 
 
-def correct_step(sub, first_state, roots):
+def correct_step(whole, sub, first_state, own_gain, roots):
     count = sub.shape[1]
     out = pl.pallas_call(
-        correct_kernel,
-        in_specs=[VMEM] * 3,
+        functools.partial(correct_kernel, whole),
+        in_specs=[VMEM] * 4,
         out_specs=VMEM,
         out_shape=jax.ShapeDtypeStruct((count * 2 * SG // 128, 128), F32),
         compiler_params=LIMIT,
         cost_estimate=pl.CostEstimate(flops=4 * 10**9, bytes_accessed=4 << 20, transcendentals=0),
         name="correct_step",
-    )(sub, first_state, roots)
+    )(sub, first_state, own_gain, roots)
     out = out.reshape(count, SG // 128, 2, 128)
     return jnp.transpose(out, (0, 2, 1, 3)).reshape(1, count, 2, SG)
 
@@ -490,9 +504,10 @@
     order = list(range(0, rows, 2)) + list(range(rows - 1, 0, -2))
     ahead = [(order[i], order[(i + 1) % rows]) for i in range(rows)]
     behind = [(b, a) for a, b in ahead]
-    first_state = state = gather_step("first", tables, [own], (0,), count)
     last = rows // 2 - 1
     assert last >= 3
+    whole = last == 3
+    first_state = state = gather_step("own" if whole else "first", tables, [own], (0,), count)
     made = jax.ShapeDtypeStruct((cols, 2, 2 * count, width), BF)
     up = down = own
     for step in range(1, last + 1):
@@ -504,8 +519,10 @@
             state = gather_step("skip", tables, [state, up, down], (-step, step), count)
         elif step == last - 1:
             steps = (1 - step, step - 1, -step, step)
-            operands = [state, before, *early, up, down, *waves, tilt]
-            state, image_table = gather_step("late", tables, operands, steps, count, made)
+            operands = [state, own if whole else before, *early, up, down, *waves, tilt]
+            own_gain = jax.ShapeDtypeStruct((count, SG), F32)
+            kind = "late own" if whole else "late"
+            state, image_table, own_gain = gather_step(kind, tables, operands, steps, count, made, own_gain)
         elif step == last:
             operands = [state, up, down, *waves, tilt, image_table]
             state, image_table = gather_step("last", tables, operands, (-step, step), count, made)
@@ -530,7 +547,7 @@
         bit //= 2
     del near[0]
     acc = image(near, acc)
-    corrected = correct_step(sub, first_state, roots)
+    corrected = correct_step(whole, sub, first_state, own_gain, roots)
     far[top], acc, corrected = lax.optimization_barrier((far[top], acc, corrected))
     bit = top // 2
     while bit > 1:

time: 43.5 us -> 43.4 us (level)
  no operation moved by 1% of the time
where the time goes in v7:
time: 43.4 us; the launch traced here: 43.2 us
  Pallas kernels  16.4 us (38%)
  starting transfers between devices  12.9 us (30%)
  waiting for transfers between devices  11.6 us (27%)
  between operations  2.29 us (5%)
    ppermute x4, waiting for transfers between devices, per_device(): up = lax.ppermute(up, 'frow', ahead)  7.83 us
    ppermute x4, starting transfers between devices, per_device(): up = lax.ppermute(up, 'frow', ahead)  6.42 us
    pallas_call x4, Pallas kernels, gather_step(): pl.pallas_call(functools.partial(gather_kernel, kind, steps, rows_total /...  6.36 us
    ppermute x6, starting transfers between devices, swap(): lax.ppermute(value, axis, [(i, i ^ bit) for i in range(lax.axis_size(axis...  5.2 us
    ppermute x6, waiting for transfers between devices, swap(): lax.ppermute(value, axis, [(i, i ^ bit) for i in range(lax.axis_size(axis...  3.72 us
    pallas_call x4, Pallas kernels, image_step(): pl.pallas_call(functools.partial(image_kernel, tuple(gs), first, last), i...  3.19 us
    pallas_call x1, Pallas kernels, back_step(): pl.pallas_call(functools.partial(back_kernel, rows_total // height, heigh...  1.72 us
    pallas_call x1, Pallas kernels, near_strips(): pl.pallas_call(functools.partial(near_strip_kernel, groups), in_specs=[pl...  1.47 us
  transfers between devices with their start and end apart: 13, of which 9 were waited for; matrix products, arithmetic and copies ran while one was open for 0% of the time, Pallas kernels for 26%

profile of v7, /device:TPU:0, one launch (start us, length us, event | category | flops | bytes accessed | tf_op | source)
XLA Modules:
  0.0 43.2 jit_solution(13066796899529956488)
XLA Ops:
  0.6 0.0 copy-start.5
  0.6 0.7 %waves.1 = (f32[4,2,128,128]{3,2,1,0:T(8,128)S(1)}, f32[4,2,128,128]{3,2,1,0:T(8,128)S(1)}) custom-call(), custom_call_target="tpu_custom_call" | custom-call | flops 1000000000 | bytes 2097152 | tf_op jit(solution)/shard_map/waves/pallas_call | solution.py:82
  2.0 0.0 copy-done.5
  2.0 1.1 %first_strips.1 = (f32[1,2,128,128]{3,2,1,0:T(8,128)S(1)}, bf16[2,256,1024]{2,1,0:T(8,128)(2,1)S(1)}, f32[4,128]{1,0:T(4,128)S(1)}) custom-call(s32[1,1]{1,0:T(1,128)} %bitcast.7.start_ref, f32[2,128,1024]{2,1,0:T(8,128)S(1)} %copy-done.5, f32[4,2,128,128]{3,2,1,0:T(8,128)S(1)} %get-tuple-element.31.base_ref.refs_10_.refs_7_, ...), custom_call_target="tpu_custom_call" | custom-call | flops 1000000000 | bytes 2097152 | tf_op jit(solution)/shard_map/first_strips/pallas_call | solution.py:131
  3.1 0.5 %collective-permute-start = (f32[1,2,128,128]{3,2,1,0:T(8,128)S(1)}, f32[1,2,128,128]{3,2,1,0:T(8,128)S(1)}, u32[]{:S(2)}, u32[]{:S(2)}) collective-permute-start(f32[1,2,128,128]{3,2,1,0:T(8,128)S(1)} %get-tuple-element.34), channel_id=1, source_target_pairs={{0,1},{1,0},{2,3},{3,2},{4,5},{5,4},{6,7},{7,6},{8,9},{9,8},{10,11... | collective-permute-start | bytes 393224 | tf_op jit(solution)/shard_map/ppermute | solution.py:471
  3.6 0.0 copy-start.6
  3.6 0.8 %far_strips.1 = f32[1,2,128,128]{3,2,1,0:T(8,128)S(1)} custom-call(bf16[2,256,1024]{2,1,0:T(8,128)(2,1)S(1)} %get-tuple-element.35.z_ref, f32[4,2,128,128]{3,2,1,0:T(8,128)S(1)} %get-tuple-element.31.base_ref.refs_10_.refs_7_, f32[4,2,128,128]{3,2,1,0:T(8,128)S(1)} %get-tuple-element.32.steps_ref.refs_11_.refs_8_), custom_call_target="tpu_custom_call" | custom-call | flops 1000000000 | bytes 2097152 | tf_op jit(solution)/shard_map/far_strips/pallas_call | solution.py:151
  4.4 0.2 collective-permute-done
  4.6 0.0 copy-start.3
  4.6 0.0 copy-start.4
  4.7 0.0 copy-start
  4.7 0.0 copy-start.1
  4.7 2.9 %collective-permute-start.1 = (f32[1,2,128,128]{3,2,1,0:T(8,128)S(1)}, f32[1,2,128,128]{3,2,1,0:T(8,128)S(1)}, u32[]{:S(2)}, u32[]{:S(2)}) collective-permute-start(f32[1,2,128,128]{3,2,1,0:T(8,128)S(1)} %add.6), channel_id=1, source_target_pairs={{0,2},{1,3},{2,0},{3,1},{4,6},{5,7},{6,4},{7,5},{8,10},{9,11},{10,... | collective-permute-start | bytes 393224 | tf_op jit(solution)/shard_map/ppermute | solution.py:471
  7.6 0.0 copy-done.6
  7.6 1.5 %near_strips.1 = (f32[1,2,128,128]{3,2,1,0:T(8,128)S(1)}, f32[1,2,128,128]{3,2,1,0:T(8,128)S(1)}, f32[8,2,128]{2,1,0:T(2,128)S(1)}, s32[8,1,128]{2,1,0:T(1,128)S(1)}) custom-call(s32[8]{0:T(128)S(1)} %copy-done.6, bf16[2,256,1024]{2,1,0:T(8,128)(2,1)S(1)} %get-tuple-element.35.z_ref, f32[4,2,128,128]{3,2,1,0:T(8,128)S(1)} %get-tuple-element.31.base_ref.refs_10_.refs_7_, ...), custom_call_target="tpu_custom_call" | custom-call | flops 4000000000 | bytes 2097152 | tf_op jit(solution)/shard_map/near_strips/pallas_call | solution.py:179
  9.1 0.1 collective-permute-start.2
  9.8 1.6 %collective-permute-done.1 = f32[1,2,128,128]{3,2,1,0:T(8,128)S(1)} collective-permute-done((f32[1,2,128,128]{3,2,1,0:T(8,128)S(1)}, f32[1,2,128,128]{3,2,1,0:T(8,128)S(1)}, u32[]{:S(2)}, u32[]{:S(2)}) %collective-permute-start.1) | collective-permute-done | bytes 131104 | tf_op jit(solution)/shard_map/ppermute | solution.py:471
  11.5 0.0 collective-permute-done.2.refs_1_
  11.5 0.0 copy-done.3
  11.5 0.0 copy-done.4
  11.5 0.1 pack.1.refs_4_.refs_5_
  11.6 1.8 %collective-permute-start.3 = (f32[328,128]{1,0:T(8,128)S(1)}, f32[328,128]{1,0:T(8,128)S(1)}, u32[]{:S(2)}, u32[]{:S(2)}) collective-permute-start(f32[328,128]{1,0:T(8,128)S(1)} %pack.1.refs_4_.refs_5_), channel_id=1, source_target_pairs={{0,8},{8,16},{16,24},{24,28},{28,20},{20,12},{12,4},{4,0},{1,9},{9... | collective-permute-start | bytes 503816 | tf_op jit(solution)/shard_map/ppermute | solution.py:514
  13.4 0.2 collective-permute-start.5
  13.6 0.0 copy-done
  13.6 0.0 copy-done.1
  13.6 0.8 %gather_step.4.refs_4_.gain_ref = f32[3,128,1024]{2,1,0:T(8,128)S(1)} custom-call(bf16[768,1024]{1,0:T(8,128)(2,1)S(1)} %copy-done, f32[8,2,1024]{2,1,0:T(2,128)S(1)} %copy-done.1, f32[8,2,128]{2,1,0:T(2,128)S(1)} %get-tuple-element.36.refs_2_, s32[8,1,128]{2,1,0:T(1,128)S(1)} %get-tuple-element.37.refs_3_, f32[328,128]{1,0:T(8,128)S(1)} %pack.1.refs_4_.refs_5_), custom_call_target="tpu_custom_call" | custom-call | flops 1000000000 | bytes 4194304 | tf_op jit(solution)/shard_map/gather_step/pallas_call | solution.py:337
  14.4 3.0 %collective-permute-done.3.refs_5_.refs_6_ = f32[328,128]{1,0:T(8,128)S(1)} collective-permute-done((f32[328,128]{1,0:T(8,128)S(1)}, f32[328,128]{1,0:T(8,128)S(1)}, u32[]{:S(2)}, u32[]{:S(2)}) %collective-permute-start.3) | collective-permute-done | bytes 167968 | tf_op jit(solution)/shard_map/ppermute | solution.py:514
  17.4 1.5 %collective-permute-start.4 = (f32[328,128]{1,0:T(8,128)S(1)}, f32[328,128]{1,0:T(8,128)S(1)}, u32[]{:S(2)}, u32[]{:S(2)}) collective-permute-start(f32[328,128]{1,0:T(8,128)S(1)} %collective-permute-done.3.refs_5_.refs_6_), channel_id=1, source_target_pairs={{0,8},{8,16},{16,24},{24,28},{28,20},{20,12},{12,4},{4,0},{1,9},{9... | collective-permute-start | bytes 503816 | tf_op jit(solution)/shard_map/ppermute | solution.py:514
  18.9 0.0 collective-permute-done.5.refs_6_.refs_7_
  18.9 0.5 %collective-permute-start.7 = (f32[328,128]{1,0:T(8,128)S(1)}, f32[328,128]{1,0:T(8,128)S(1)}, u32[]{:S(2)}, u32[]{:S(2)}) collective-permute-start(f32[328,128]{1,0:T(8,128)S(1)} %collective-permute-done.5.refs_6_.refs_7_), channel_id=1, source_target_pairs={{8,0},{16,8},{24,16},{28,24},{20,28},{12,20},{4,12},{0,4},{9,1},{1... | collective-permute-start | bytes 503816 | tf_op jit(solution)/shard_map/ppermute | solution.py:515
  19.4 1.4 %gather_step.5.refs_4_ = f32[3,128,1024]{2,1,0:T(8,128)S(1)} custom-call(bf16[768,1024]{1,0:T(8,128)(2,1)S(1)} %copy-done, f32[8,2,1024]{2,1,0:T(2,128)S(1)} %copy-done.1, f32[8,2,128]{2,1,0:T(2,128)S(1)} %get-tuple-element.36.refs_2_, s32[8,1,128]{2,1,0:T(1,128)S(1)} %get-tuple-element.37.refs_3_, f32[3,128,1024]{2,1,0:T(8,128)S(1)} %gather_step.4.refs_4_.gain_ref, ...), custom_call_target="tpu_custom_call" | custom-call | flops 1000000000 | bytes 4194304 | tf_op jit(solution)/shard_map/gather_step/pallas_call | solution.py:337
  20.8 2.0 %collective-permute-done.4.refs_8_ = f32[328,128]{1,0:T(8,128)S(1)} collective-permute-done((f32[328,128]{1,0:T(8,128)S(1)}, f32[328,128]{1,0:T(8,128)S(1)}, u32[]{:S(2)}, u32[]{:S(2)}) %collective-permute-start.4) | collective-permute-done | bytes 167968 | tf_op jit(solution)/shard_map/ppermute | solution.py:514
  22.8 1.6 %collective-permute-start.6 = (f32[328,128]{1,0:T(8,128)S(1)}, f32[328,128]{1,0:T(8,128)S(1)}, u32[]{:S(2)}, u32[]{:S(2)}) collective-permute-start(f32[328,128]{1,0:T(8,128)S(1)} %collective-permute-done.4.refs_8_), channel_id=1, source_target_pairs={{0,8},{8,16},{16,24},{24,28},{28,20},{20,12},{12,4},{4,0},{1,9},{9... | collective-permute-start | bytes 503816 | tf_op jit(solution)/shard_map/ppermute | solution.py:514
  24.3 0.0 collective-permute-done.7.refs_9_
  24.3 0.5 %collective-permute-start.8 = (f32[328,128]{1,0:T(8,128)S(1)}, f32[328,128]{1,0:T(8,128)S(1)}, u32[]{:S(2)}, u32[]{:S(2)}) collective-permute-start(f32[328,128]{1,0:T(8,128)S(1)} %collective-permute-done.7.refs_9_), channel_id=1, source_target_pairs={{8,0},{16,8},{24,16},{28,24},{20,28},{12,20},{4,12},{0,4},{9,1},{1... | collective-permute-start | bytes 503816 | tf_op jit(solution)/shard_map/ppermute | solution.py:515
  24.8 1.4 %gather_step.6 = (f32[3,128,1024]{2,1,0:T(8,128)S(1)}, bf16[4,2,256,1024]{3,2,1,0:T(8,128)(2,1)S(1)}, f32[128,512]{1,0:T(8,128)S(1)}) custom-call(bf16[768,1024]{1,0:T(8,128)(2,1)S(1)} %copy-done, f32[8,2,1024]{2,1,0:T(2,128)S(1)} %copy-done.1, f32[8,2,128]{2,1,0:T(2,128)S(1)} %get-tuple-element.36.refs_2_, s32[8,1,128]{2,1,0:T(1,128)S(1)} %get-tuple-element.37.refs_3_, ...), custom_call_target="tpu_custom_call" | custom-call | flops 1000000000 | bytes 4194304 | tf_op jit(solution)/shard_map/gather_step/pallas_call | solution.py:337
  26.2 1.9 %collective-permute-done.6.refs_5_ = f32[328,128]{1,0:T(8,128)S(1)} collective-permute-done((f32[328,128]{1,0:T(8,128)S(1)}, f32[328,128]{1,0:T(8,128)S(1)}, u32[]{:S(2)}, u32[]{:S(2)}) %collective-permute-start.6) | collective-permute-done | bytes 167968 | tf_op jit(solution)/shard_map/ppermute | solution.py:514
  28.1 1.6 %collective-permute-start.9 = (f32[328,128]{1,0:T(8,128)S(1)}, f32[328,128]{1,0:T(8,128)S(1)}, u32[]{:S(2)}, u32[]{:S(2)}) collective-permute-start(f32[328,128]{1,0:T(8,128)S(1)} %collective-permute-done.6.refs_5_), channel_id=1, source_target_pairs={{0,8},{8,16},{16,24},{24,28},{28,20},{20,12},{12,4},{4,0},{1,9},{9... | collective-permute-start | bytes 503816 | tf_op jit(solution)/shard_map/ppermute | solution.py:531
  29.7 0.0 collective-permute-done.8.refs_6_
  29.7 0.0 copy-start.2
  29.7 2.9 %gather_step.7 = (f32[3,128,1024]{2,1,0:T(8,128)S(1)}, bf16[4,2,256,1024]{3,2,1,0:T(8,128)(2,1)S(1)}) custom-call(bf16[768,1024]{1,0:T(8,128)(2,1)S(1)} %copy-done, f32[8,2,1024]{2,1,0:T(2,128)S(1)} %copy-done.1, f32[8,2,128]{2,1,0:T(2,128)S(1)} %get-tuple-element.36.refs_2_, s32[8,1,128]{2,1,0:T(1,128)S(1)} %get-tuple-element.37.refs_3_, ...), custom_call_target="tpu_custom_call" | custom-call | flops 1000000000 | bytes 4194304 | tf_op jit(solution)/shard_map/gather_step/pallas_call | solution.py:337
  32.6 0.9 %collective-permute-done.9.refs_6_ = f32[328,128]{1,0:T(8,128)S(1)} collective-permute-done((f32[328,128]{1,0:T(8,128)S(1)}, f32[328,128]{1,0:T(8,128)S(1)}, u32[]{:S(2)}, u32[]{:S(2)}) %collective-permute-start.9) | collective-permute-done | bytes 167968 | tf_op jit(solution)/shard_map/ppermute | solution.py:531
  33.5 0.0 copy-done.2
  33.5 1.7 %back_step.1 = (f32[2,128,128]{2,1,0:T(8,128)S(1)}, f32[2,128,512]{2,1,0:T(8,128)S(1)}) custom-call(bf16[768,1024]{1,0:T(8,128)(2,1)S(1)} %copy-done, f32[8,2,1024]{2,1,0:T(2,128)S(1)} %copy-done.1, f32[8,2,128]{2,1,0:T(2,128)S(1)} %get-tuple-element.36.refs_2_, s32[8,1,128]{2,1,0:T(1,128)S(1)} %get-tuple-element.37.refs_3_, ...), custom_call_target="tpu_custom_call" | custom-call | tf_op jit(solution)/shard_map/back_step/pallas_call | solution.py:378
  35.2 1.6 %collective-permute-start.10 = (f32[2,128,128]{2,1,0:T(8,128)S(1)}, f32[2,128,128]{2,1,0:T(8,128)S(1)}, u32[]{:S(2)}, u32[]{:S(2)}) collective-permute-start(f32[2,128,128]{2,1,0:T(8,128)S(1)} %get-tuple-element.53.refs_0_), channel_id=1, source_target_pairs={{0,2},{1,3},{2,0},{3,1},{4,6},{5,7},{6,4},{7,5},{8,10},{9,11},{10,... | collective-permute-start | bytes 393224 | tf_op jit(solution)/shard_map/ppermute | solution.py:471
  36.8 0.6 %image_step.4.refs_1_ = f32[2,128,1024]{2,1,0:T(8,128)S(1)} custom-call(bf16[4,2,256,1024]{3,2,1,0:T(8,128)(2,1)S(1)} %get-tuple-element.52.e_ref, f32[2,128,128]{2,1,0:T(8,128)S(1)} %get-tuple-element.53.refs_0_), custom_call_target="tpu_custom_call" | custom-call | flops 4000000000 | bytes 4194304 | tf_op jit(solution)/shard_map/image_step/pallas_call | solution.py:458
  37.4 0.1 collective-permute-start.11
  37.5 1.0 %correct_step.1 = f32[1024,128]{1,0:T(8,128)} custom-call(f32[2,128,512]{2,1,0:T(8,128)S(1)} %get-tuple-element.55.sub_ref, f32[3,128,1024]{2,1,0:T(8,128)S(1)} %gather_step.4.refs_4_.gain_ref, f32[128,512]{1,0:T(8,128)S(1)} %get-tuple-element.56.late_ref, f32[8,2,1024]{2,1,0:T(2,128)S(1)} %copy-done.1), custom_call_target="tpu_custom_call" | custom-call | flops 4000000000 | bytes 4194304 | tf_op jit(solution)/shard_map/correct_step/pallas_call | solution.py:406
  38.5 0.3 collective-permute-done.11.refs_0_
  38.8 0.6 %image_step.5.refs_1_ = f32[2,128,1024]{2,1,0:T(8,128)S(1)} custom-call(bf16[4,2,256,1024]{3,2,1,0:T(8,128)(2,1)S(1)} %get-tuple-element.52.e_ref, f32[2,128,128]{2,1,0:T(8,128)S(1)} %collective-permute-done.11.refs_0_, f32[2,128,1024]{2,1,0:T(8,128)S(1)} %image_step.4.refs_1_), custom_call_target="tpu_custom_call" | custom-call | flops 4000000000 | bytes 4194304 | tf_op jit(solution)/shard_map/image_step/pallas_call | solution.py:458
  39.4 0.9 %collective-permute-done.10.refs_0_ = f32[2,128,128]{2,1,0:T(8,128)S(1)} collective-permute-done((f32[2,128,128]{2,1,0:T(8,128)S(1)}, f32[2,128,128]{2,1,0:T(8,128)S(1)}, u32[]{:S(2)}, u32[]{:S(2)}) %collective-permute-start.10) | collective-permute-done | bytes 131104 | tf_op jit(solution)/shard_map/ppermute | solution.py:471
  40.3 0.0 collective-permute-start.12
  40.3 0.6 %image_step.6.refs_1_ = f32[2,128,1024]{2,1,0:T(8,128)S(1)} custom-call(bf16[4,2,256,1024]{3,2,1,0:T(8,128)(2,1)S(1)} %get-tuple-element.52.e_ref, f32[2,128,128]{2,1,0:T(8,128)S(1)} %collective-permute-done.10.refs_0_, f32[2,128,1024]{2,1,0:T(8,128)S(1)} %image_step.5.refs_1_), custom_call_target="tpu_custom_call" | custom-call | flops 4000000000 | bytes 4194304 | tf_op jit(solution)/shard_map/image_step/pallas_call | solution.py:458
  40.9 0.8 %collective-permute-done.12.refs_0_ = f32[2,128,128]{2,1,0:T(8,128)S(1)} collective-permute-done((f32[2,128,128]{2,1,0:T(8,128)S(1)}, f32[2,128,128]{2,1,0:T(8,128)S(1)}, u32[]{:S(2)}, u32[]{:S(2)}) %collective-permute-start.12) | collective-permute-done | bytes 131104 | tf_op jit(solution)/shard_map/ppermute | solution.py:471
  41.6 1.4 %image_step.7 = f32[2,128,1024]{2,1,0:T(8,128)} custom-call(bf16[4,2,256,1024]{3,2,1,0:T(8,128)(2,1)S(1)} %get-tuple-element.52.e_ref, f32[2,128,128]{2,1,0:T(8,128)S(1)} %collective-permute-done.12.refs_0_, f32[2,128,1024]{2,1,0:T(8,128)S(1)} %image_step.6.refs_1_), custom_call_target="tpu_custom_call" | custom-call | flops 4000000000 | bytes 4194304 | tf_op jit(solution)/shard_map/image_step/pallas_call | solution.py:458
  (2 shorter events, 0.0 us)
Async XLA Ops:
  0.6 1.4 %copy-start.5 = (f32[2,128,1024]{2,1,0:T(8,128)S(1)}, f32[2,128,1024]{2,1,0:T(8,128)}, u32[]{:S(2)}) copy-start(f32[2,128,1024]{2,1,0:T(8,128)} %x_ref.1) | copy-start | bytes 3145732
  3.1 1.5 %collective-permute-start = (f32[1,2,128,128]{3,2,1,0:T(8,128)S(1)}, f32[1,2,128,128]{3,2,1,0:T(8,128)S(1)}, u32[]{:S(2)}, u32[]{:S(2)}) collective-permute-start(f32[1,2,128,128]{3,2,1,0:T(8,128)S(1)} %get-tuple-element.34), channel_id=1, source_target_pairs={{0,1},{1,0},{2,3},{3,2},{4,5},{5,4},{6,7},{7,6},{8,9},{9,8},{10,11... | collective-permute-start | bytes 393224 | tf_op jit(solution)/shard_map/ppermute | solution.py:471
  3.6 4.0 %copy-start.6 = (s32[8]{0:T(128)S(1)}, s32[8]{0:T(128)}, u32[]{:S(2)}) copy-start(s32[8]{0:T(128)} %starts_ref.1) | copy-start | bytes 100
  4.6 6.8 %copy-start.3 = (f32[1,64,128]{2,1,0:T(8,128)S(1)}, f32[1,64,128]{2,1,0:T(8,128)}, u32[]{:S(2)}) copy-start(f32[1,64,128]{2,1,0:T(8,128)} %refs_2_.1) | copy-start | bytes 98308
  4.6 6.8 %copy-start.4 = (s32[1,64]{1,0:T(1,128)S(1)}, s32[1,64]{1,0:T(1,128)}, u32[]{:S(2)}) copy-start(s32[1,64]{1,0:T(1,128)} %refs_3_.1) | copy-start | bytes 772
  4.7 8.9 %copy-start = (bf16[768,1024]{1,0:T(8,128)(2,1)S(1)}, bf16[768,1024]{1,0:T(8,128)(2,1)}, u32[]{:S(2)}) copy-start(bf16[768,1024]{1,0:T(8,128)(2,1)} %constant.7.clone.refs_0_) | copy-start | bytes 4718596
  4.7 8.9 %copy-start.1 = (f32[8,2,1024]{2,1,0:T(2,128)S(1)}, f32[8,2,1024]{2,1,0:T(2,128)}, u32[]{:S(2)}) copy-start(f32[8,2,1024]{2,1,0:T(2,128)} %constant.8.clone.refs_1_.roots_ref) | copy-start | bytes 196612
  4.7 6.8 %collective-permute-start.1 = (f32[1,2,128,128]{3,2,1,0:T(8,128)S(1)}, f32[1,2,128,128]{3,2,1,0:T(8,128)S(1)}, u32[]{:S(2)}, u32[]{:S(2)}) collective-permute-start(f32[1,2,128,128]{3,2,1,0:T(8,128)S(1)} %add.6), channel_id=1, source_target_pairs={{0,2},{1,3},{2,0},{3,1},{4,6},{5,7},{6,4},{7,5},{8,10},{9,11},{10,... | collective-permute-start | bytes 393224 | tf_op jit(solution)/shard_map/ppermute | solution.py:471
  9.1 2.4 %collective-permute-start.2 = (f32[1,2,128,128]{3,2,1,0:T(8,128)S(1)}, f32[1,2,128,128]{3,2,1,0:T(8,128)S(1)}, u32[]{:S(2)}, u32[]{:S(2)}) collective-permute-start(f32[1,2,128,128]{3,2,1,0:T(8,128)S(1)} %get-tuple-element.40), channel_id=1, source_target_pairs={{0,1},{1,0},{2,3},{3,2},{4,5},{5,4},{6,7},{7,6},{8,9},{9,8},{10,11... | collective-permute-start | bytes 393224 | tf_op jit(solution)/shard_map/ppermute | solution.py:471
  11.6 5.8 %collective-permute-start.3 = (f32[328,128]{1,0:T(8,128)S(1)}, f32[328,128]{1,0:T(8,128)S(1)}, u32[]{:S(2)}, u32[]{:S(2)}) collective-permute-start(f32[328,128]{1,0:T(8,128)S(1)} %pack.1.refs_4_.refs_5_), channel_id=1, source_target_pairs={{0,8},{8,16},{16,24},{24,28},{28,20},{20,12},{12,4},{4,0},{1,9},{9... | collective-permute-start | bytes 503816 | tf_op jit(solution)/shard_map/ppermute | solution.py:514
  13.4 5.5 %collective-permute-start.5 = (f32[328,128]{1,0:T(8,128)S(1)}, f32[328,128]{1,0:T(8,128)S(1)}, u32[]{:S(2)}, u32[]{:S(2)}) collective-permute-start(f32[328,128]{1,0:T(8,128)S(1)} %pack.1.refs_4_.refs_5_), channel_id=1, source_target_pairs={{8,0},{16,8},{24,16},{28,24},{20,28},{12,20},{4,12},{0,4},{9,1},{1... | collective-permute-start | bytes 503816 | tf_op jit(solution)/shard_map/ppermute | solution.py:515
  17.4 5.4 %collective-permute-start.4 = (f32[328,128]{1,0:T(8,128)S(1)}, f32[328,128]{1,0:T(8,128)S(1)}, u32[]{:S(2)}, u32[]{:S(2)}) collective-permute-start(f32[328,128]{1,0:T(8,128)S(1)} %collective-permute-done.3.refs_5_.refs_6_), channel_id=1, source_target_pairs={{0,8},{8,16},{16,24},{24,28},{28,20},{20,12},{12,4},{4,0},{1,9},{9... | collective-permute-start | bytes 503816 | tf_op jit(solution)/shard_map/ppermute | solution.py:514
  18.9 5.5 %collective-permute-start.7 = (f32[328,128]{1,0:T(8,128)S(1)}, f32[328,128]{1,0:T(8,128)S(1)}, u32[]{:S(2)}, u32[]{:S(2)}) collective-permute-start(f32[328,128]{1,0:T(8,128)S(1)} %collective-permute-done.5.refs_6_.refs_7_), channel_id=1, source_target_pairs={{8,0},{16,8},{24,16},{28,24},{20,28},{12,20},{4,12},{0,4},{9,1},{1... | collective-permute-start | bytes 503816 | tf_op jit(solution)/shard_map/ppermute | solution.py:515
  22.8 5.4 %collective-permute-start.6 = (f32[328,128]{1,0:T(8,128)S(1)}, f32[328,128]{1,0:T(8,128)S(1)}, u32[]{:S(2)}, u32[]{:S(2)}) collective-permute-start(f32[328,128]{1,0:T(8,128)S(1)} %collective-permute-done.4.refs_8_), channel_id=1, source_target_pairs={{0,8},{8,16},{16,24},{24,28},{28,20},{20,12},{12,4},{4,0},{1,9},{9... | collective-permute-start | bytes 503816 | tf_op jit(solution)/shard_map/ppermute | solution.py:514
  24.3 5.4 %collective-permute-start.8 = (f32[328,128]{1,0:T(8,128)S(1)}, f32[328,128]{1,0:T(8,128)S(1)}, u32[]{:S(2)}, u32[]{:S(2)}) collective-permute-start(f32[328,128]{1,0:T(8,128)S(1)} %collective-permute-done.7.refs_9_), channel_id=1, source_target_pairs={{8,0},{16,8},{24,16},{28,24},{20,28},{12,20},{4,12},{0,4},{9,1},{1... | collective-permute-start | bytes 503816 | tf_op jit(solution)/shard_map/ppermute | solution.py:515
  28.1 5.4 %collective-permute-start.9 = (f32[328,128]{1,0:T(8,128)S(1)}, f32[328,128]{1,0:T(8,128)S(1)}, u32[]{:S(2)}, u32[]{:S(2)}) collective-permute-start(f32[328,128]{1,0:T(8,128)S(1)} %collective-permute-done.6.refs_5_), channel_id=1, source_target_pairs={{0,8},{8,16},{16,24},{24,28},{28,20},{20,12},{12,4},{4,0},{1,9},{9... | collective-permute-start | bytes 503816 | tf_op jit(solution)/shard_map/ppermute | solution.py:531
  29.7 3.8 %copy-start.2 = (bf16[1024,512]{1,0:T(8,128)(2,1)S(1)}, bf16[1024,512]{1,0:T(8,128)(2,1)}, u32[]{:S(2)}) copy-start(bf16[1024,512]{1,0:T(8,128)(2,1)} %constant.6.clone.refs_4_) | copy-start | bytes 3145732
  35.2 5.0 %collective-permute-start.10 = (f32[2,128,128]{2,1,0:T(8,128)S(1)}, f32[2,128,128]{2,1,0:T(8,128)S(1)}, u32[]{:S(2)}, u32[]{:S(2)}) collective-permute-start(f32[2,128,128]{2,1,0:T(8,128)S(1)} %get-tuple-element.53.refs_0_), channel_id=1, source_target_pairs={{0,2},{1,3},{2,0},{3,1},{4,6},{5,7},{6,4},{7,5},{8,10},{9,11},{10,... | collective-permute-start | bytes 393224 | tf_op jit(solution)/shard_map/ppermute | solution.py:471
  37.4 1.4 %collective-permute-start.11 = (f32[2,128,128]{2,1,0:T(8,128)S(1)}, f32[2,128,128]{2,1,0:T(8,128)S(1)}, u32[]{:S(2)}, u32[]{:S(2)}) collective-permute-start(f32[2,128,128]{2,1,0:T(8,128)S(1)} %get-tuple-element.53.refs_0_), channel_id=1, source_target_pairs={{0,1},{1,0},{2,3},{3,2},{4,5},{5,4},{6,7},{7,6},{8,9},{9,8},{10,11... | collective-permute-start | bytes 393224 | tf_op jit(solution)/shard_map/ppermute | solution.py:471
  40.3 1.3 %collective-permute-start.12 = (f32[2,128,128]{2,1,0:T(8,128)S(1)}, f32[2,128,128]{2,1,0:T(8,128)S(1)}, u32[]{:S(2)}, u32[]{:S(2)}) collective-permute-start(f32[2,128,128]{2,1,0:T(8,128)S(1)} %collective-permute-done.10.refs_0_), channel_id=1, source_target_pairs={{0,1},{1,0},{2,3},{3,2},{4,5},{5,4},{6,7},{7,6},{8,9},{9,8},{10,11... | collective-permute-start | bytes 393224 | tf_op jit(solution)/shard_map/ppermute | solution.py:471

commit v8 on v7

--- a/solution.py
+++ b/solution.py
@@ -68,13 +68,17 @@
 def wave_kernel(width, cols_total, base_ref, steps_ref):
     own = lax.axis_index("fcol")
     blocks, _, count, _ = base_ref.shape
-    row = lax.broadcasted_iota(jnp.int32, (count, 128), 0)
-    for ref, coord in ((base_ref, lanes(128)), (steps_ref, lanes(128) * 128 + own * width)):
-        cos, sin = unit(row * coord, cols_total)
-        for g in range(blocks):
-            pc, ps = unit((own ^ g) * count * coord, cols_total)
-            ref[g, 0] = cos * pc - sin * ps
-            ref[g, 1] = sin * pc + cos * ps
+    down = lax.broadcasted_iota(jnp.int32, (count, 128), 0)
+    cos, sin = unit(down * lanes(128), cols_total)
+    tiles = width // 128
+    every = own * width + 128 * lax.broadcasted_iota(jnp.int32, (tiles, 128), 0)
+    for g in range(blocks):
+        first = (own ^ g) * count
+        pc, ps = unit(first * lanes(128), cols_total)
+        base_ref[g, 0] = cos * pc - sin * ps
+        base_ref[g, 1] = sin * pc + cos * ps
+        for part, value in enumerate(unit((first + lanes(128, tiles)) * every, cols_total)):
+            steps_ref[g, part, :, :tiles] = jnp.transpose(value)[:count]
 
 
 def waves_of(count, width, cols_total):
@@ -98,15 +102,13 @@
     return halves(jnp.concatenate([jnp.concatenate(cos, 1), jnp.concatenate(sin, 1)]))
 
 
-def strip_sums(gs, z_ref, base_ref, steps_ref, out_ref):
+def strip_sums(gs, z_of, width, base_ref, steps_ref, out_ref):
     count, height = out_ref.shape[-2:]
-    z = z_ref[0], z_ref[1]
     for i, g in enumerate(gs):
         base, turn = (base_ref[g, 0], base_ref[g, 1]), (steps_ref[g, 0], steps_ref[g, 1])
         acc = None
-        for begin, size in chunks(z_ref.shape[-1]):
-            waves = waves_in(base, turn, begin, size)
-            part = dot3(waves, [value[:, begin : begin + size] for value in z], NT)
+        for begin, size in chunks(width):
+            part = dot3(waves_in(base, turn, begin, size), z_of(begin, size), NT)
             acc = part if acc is None else acc + part
         cos, sin = acc[:count], acc[count:]
         out_ref[i, 0] = cos[:, :height] + sin[:, height:]
@@ -117,12 +119,20 @@
     own = lax.axis_index("fcol")
     width = x_ref.shape[-1]
     start, scale = start_ref[0:1, 0:1], 1.0 / math.sqrt(cols_total)
-    pc, ps = unit(start * (own * width + lanes(width)), cols_total, scale)
-    re, im = x_ref[0], x_ref[1]
-    z_ref[0], z_ref[1] = halves(jnp.concatenate([re * pc + im * ps, im * pc - re * ps]))
+    made = {}
+
+    def z_of(begin, size):
+        if begin not in made:
+            columns = slice(begin, begin + size)
+            pc, ps = unit(start * (own * width + begin + lanes(size)), cols_total, scale)
+            re, im = x_ref[0, :, columns], x_ref[1, :, columns]
+            made[begin] = halves(jnp.concatenate([re * pc + im * ps, im * pc - re * ps]))
+            z_ref[0, :, columns], z_ref[1, :, columns] = made[begin]
+        return made[begin]
+
     tilt_ref[0:1], tilt_ref[1:2] = unit(start * lanes(128), cols_total)
     tilt_ref[2:3], tilt_ref[3:4] = unit(start * (own * width + 128 * lanes(128)), cols_total, scale)
-    strip_sums(gs, z_ref, base_ref, steps_ref, out_ref)
+    strip_sums(gs, z_of, width, base_ref, steps_ref, out_ref)
 
 
 def first_strips(column_start, facets, waves, gs):
@@ -143,8 +153,12 @@
     )(column_start, facets, *waves)
 
 
+def columns_of(z_ref):
+    return lambda begin, size: (z_ref[0, :, begin : begin + size], z_ref[1, :, begin : begin + size])
+
+
 def far_strip_kernel(gs, z_ref, base_ref, steps_ref, out_ref):
-    strip_sums(gs, z_ref, base_ref, steps_ref, out_ref)
+    strip_sums(gs, columns_of(z_ref), z_ref.shape[-1], base_ref, steps_ref, out_ref)
 
 
 def far_strips(z, waves, gs):
@@ -164,7 +178,7 @@
     copy = pltpu.make_async_copy(starts_ref, starts, sem)
     copy.start()
     for gs, out_ref in zip(groups, out_refs):
-        strip_sums(gs, z_ref, base_ref, steps_ref, out_ref)
+        strip_sums(gs, columns_of(z_ref), z_ref.shape[-1], base_ref, steps_ref, out_ref)
     copy.wait()
     rows, _, height = turn_ref.shape
     rows_total = rows * height
@@ -262,6 +276,10 @@
         for begin, size in chunks(out_ref.shape[-1]):
             columns = slice(begin, begin + size)
             out_ref[g, 0, :, columns], out_ref[g, 1, :, columns] = waves_in(base, turn, begin, size)
+
+
+def last_chunks(total):
+    return [(0, total // 2), (total // 2, total // 2)]
 
 
 def gather_kernel(kind, steps, rows, height, count, *refs):
@@ -429,7 +447,7 @@
         re, im = back[0], back[1]
         left.append(halves(jnp.concatenate([jnp.concatenate([re, -im], 1), jnp.concatenate([im, re], 1)])))
     copies = []
-    for begin, size in chunks(width):
+    for begin, size in (last_chunks(width) if last else chunks(width)):
         columns = slice(begin, begin + size)
         acc = None if first else jnp.concatenate([acc_ref[0, :, columns], acc_ref[1, :, columns]])
         for (high, low), g in zip(left, gs):
@@ -460,7 +478,7 @@
         in_specs=[VMEM] * (1 + len(operands)),
         out_specs=pl.BlockSpec(memory_space=pl.ANY) if last else VMEM,
         out_shape=jax.ShapeDtypeStruct((2, height, width), F32),
-        scratch_shapes=[pltpu.VMEM((2, height, width), F32), pltpu.SemaphoreType.DMA((len(chunks(width)),))] if last else [],
+        scratch_shapes=[pltpu.VMEM((2, height, width), F32), pltpu.SemaphoreType.DMA((len(last_chunks(width)),))] if last else [],
         compiler_params=LIMIT,
         cost_estimate=pl.CostEstimate(flops=4 * 10**9, bytes_accessed=4 << 20, transcendentals=0),
         name="image_step",

time: 43.4 us -> 43.2 us (level)
  transfers between devices with their start and end apart: 13 -> 13, of which waited for: 9 -> 9; matrix products, arithmetic and copies ran while one was open for 0% -> 0% of each run, Pallas kernels for 26% -> 27%
where the time goes in v8:
time: 43.2 us; the launch traced here: 43 us
  Pallas kernels  16.3 us (38%)
  starting transfers between devices  12.9 us (30%)
  waiting for transfers between devices  11.5 us (27%)
  between operations  2.29 us (5%)
    ppermute x4, waiting for transfers between devices, per_device(): up = lax.ppermute(up, 'frow', ahead)  7.82 us
    ppermute x4, starting transfers between devices, per_device(): up = lax.ppermute(up, 'frow', ahead)  6.42 us
    pallas_call x4, Pallas kernels, gather_step(): pl.pallas_call(functools.partial(gather_kernel, kind, steps, rows_total /...  6.37 us
    ppermute x6, starting transfers between devices, swap(): lax.ppermute(value, axis, [(i, i ^ bit) for i in range(lax.axis_size(axis...  5.2 us
    ppermute x6, waiting for transfers between devices, swap(): lax.ppermute(value, axis, [(i, i ^ bit) for i in range(lax.axis_size(axis...  3.7 us
    pallas_call x4, Pallas kernels, image_step(): pl.pallas_call(functools.partial(image_kernel, tuple(gs), first, last), i...  3.17 us
    pallas_call x1, Pallas kernels, back_step(): pl.pallas_call(functools.partial(back_kernel, rows_total // height, heigh...  1.72 us
    pallas_call x1, Pallas kernels, near_strips(): pl.pallas_call(functools.partial(near_strip_kernel, groups), in_specs=[pl...  1.47 us
  transfers between devices with their start and end apart: 13, of which 9 were waited for; matrix products, arithmetic and copies ran while one was open for 0% of the time, Pallas kernels for 27%

profile of v8, /device:TPU:0, one launch (start us, length us, event | category | flops | bytes accessed | tf_op | source)
XLA Modules:
  0.0 43.0 jit_solution(8228762031843995708)
XLA Ops:
  0.6 0.0 copy-start.5
  0.6 0.6 %waves.1 = (f32[4,2,128,128]{3,2,1,0:T(8,128)S(1)}, f32[4,2,128,128]{3,2,1,0:T(8,128)S(1)}) custom-call(), custom_call_target="tpu_custom_call" | custom-call | flops 1000000000 | bytes 2097152 | tf_op jit(solution)/shard_map/waves/pallas_call | solution.py:86
  1.9 0.0 copy-done.5
  1.9 1.1 %first_strips.1 = (f32[1,2,128,128]{3,2,1,0:T(8,128)S(1)}, bf16[2,256,1024]{2,1,0:T(8,128)(2,1)S(1)}, f32[4,128]{1,0:T(4,128)S(1)}) custom-call(s32[1,1]{1,0:T(1,128)} %bitcast.7.start_ref, f32[2,128,1024]{2,1,0:T(8,128)S(1)} %copy-done.5, f32[4,2,128,128]{3,2,1,0:T(8,128)S(1)} %get-tuple-element.31.base_ref.refs_10_.refs_7_, ...), custom_call_target="tpu_custom_call" | custom-call | flops 1000000000 | bytes 2097152 | tf_op jit(solution)/shard_map/first_strips/pallas_call | solution.py:141
  3.0 0.5 %collective-permute-start = (f32[1,2,128,128]{3,2,1,0:T(8,128)S(1)}, f32[1,2,128,128]{3,2,1,0:T(8,128)S(1)}, u32[]{:S(2)}, u32[]{:S(2)}) collective-permute-start(f32[1,2,128,128]{3,2,1,0:T(8,128)S(1)} %get-tuple-element.34), channel_id=1, source_target_pairs={{0,1},{1,0},{2,3},{3,2},{4,5},{5,4},{6,7},{7,6},{8,9},{9,8},{10,11... | collective-permute-start | bytes 393224 | tf_op jit(solution)/shard_map/ppermute | solution.py:489
  3.5 0.0 copy-start.6
  3.5 0.8 %far_strips.1 = f32[1,2,128,128]{3,2,1,0:T(8,128)S(1)} custom-call(bf16[2,256,1024]{2,1,0:T(8,128)(2,1)S(1)} %get-tuple-element.35.z_ref, f32[4,2,128,128]{3,2,1,0:T(8,128)S(1)} %get-tuple-element.31.base_ref.refs_10_.refs_7_, f32[4,2,128,128]{3,2,1,0:T(8,128)S(1)} %get-tuple-element.32.steps_ref.refs_11_.refs_8_), custom_call_target="tpu_custom_call" | custom-call | flops 1000000000 | bytes 2097152 | tf_op jit(solution)/shard_map/far_strips/pallas_call | solution.py:165
  4.3 0.2 collective-permute-done
  4.5 0.0 copy-start.3
  4.5 0.0 copy-start.4
  4.5 0.0 copy-start
  4.5 0.0 copy-start.1
  4.6 2.9 %collective-permute-start.1 = (f32[1,2,128,128]{3,2,1,0:T(8,128)S(1)}, f32[1,2,128,128]{3,2,1,0:T(8,128)S(1)}, u32[]{:S(2)}, u32[]{:S(2)}) collective-permute-start(f32[1,2,128,128]{3,2,1,0:T(8,128)S(1)} %add.6), channel_id=1, source_target_pairs={{0,2},{1,3},{2,0},{3,1},{4,6},{5,7},{6,4},{7,5},{8,10},{9,11},{10,... | collective-permute-start | bytes 393224 | tf_op jit(solution)/shard_map/ppermute | solution.py:489
  7.5 0.0 copy-done.6
  7.5 1.5 %near_strips.1 = (f32[1,2,128,128]{3,2,1,0:T(8,128)S(1)}, f32[1,2,128,128]{3,2,1,0:T(8,128)S(1)}, f32[8,2,128]{2,1,0:T(2,128)S(1)}, s32[8,1,128]{2,1,0:T(1,128)S(1)}) custom-call(s32[8]{0:T(128)S(1)} %copy-done.6, bf16[2,256,1024]{2,1,0:T(8,128)(2,1)S(1)} %get-tuple-element.35.z_ref, f32[4,2,128,128]{3,2,1,0:T(8,128)S(1)} %get-tuple-element.31.base_ref.refs_10_.refs_7_, ...), custom_call_target="tpu_custom_call" | custom-call | flops 4000000000 | bytes 2097152 | tf_op jit(solution)/shard_map/near_strips/pallas_call | solution.py:193
  9.0 0.1 collective-permute-start.2
  9.7 1.6 %collective-permute-done.1 = f32[1,2,128,128]{3,2,1,0:T(8,128)S(1)} collective-permute-done((f32[1,2,128,128]{3,2,1,0:T(8,128)S(1)}, f32[1,2,128,128]{3,2,1,0:T(8,128)S(1)}, u32[]{:S(2)}, u32[]{:S(2)}) %collective-permute-start.1) | collective-permute-done | bytes 131104 | tf_op jit(solution)/shard_map/ppermute | solution.py:489
  11.3 0.0 collective-permute-done.2.refs_1_
  11.3 0.0 copy-done.3
  11.3 0.0 copy-done.4
  11.4 0.1 pack.1.refs_4_.refs_5_
  11.4 1.8 %collective-permute-start.3 = (f32[328,128]{1,0:T(8,128)S(1)}, f32[328,128]{1,0:T(8,128)S(1)}, u32[]{:S(2)}, u32[]{:S(2)}) collective-permute-start(f32[328,128]{1,0:T(8,128)S(1)} %pack.1.refs_4_.refs_5_), channel_id=1, source_target_pairs={{0,8},{8,16},{16,24},{24,28},{28,20},{20,12},{12,4},{4,0},{1,9},{9... | collective-permute-start | bytes 503816 | tf_op jit(solution)/shard_map/ppermute | solution.py:532
  13.2 0.2 collective-permute-start.5
  13.5 0.0 copy-done
  13.5 0.0 copy-done.1
  13.5 0.8 %gather_step.4.refs_4_.gain_ref = f32[3,128,1024]{2,1,0:T(8,128)S(1)} custom-call(bf16[768,1024]{1,0:T(8,128)(2,1)S(1)} %copy-done, f32[8,2,1024]{2,1,0:T(2,128)S(1)} %copy-done.1, f32[8,2,128]{2,1,0:T(2,128)S(1)} %get-tuple-element.36.refs_2_, s32[8,1,128]{2,1,0:T(1,128)S(1)} %get-tuple-element.37.refs_3_, f32[328,128]{1,0:T(8,128)S(1)} %pack.1.refs_4_.refs_5_), custom_call_target="tpu_custom_call" | custom-call | flops 1000000000 | bytes 4194304 | tf_op jit(solution)/shard_map/gather_step/pallas_call | solution.py:355
  14.3 3.0 %collective-permute-done.3.refs_5_.refs_6_ = f32[328,128]{1,0:T(8,128)S(1)} collective-permute-done((f32[328,128]{1,0:T(8,128)S(1)}, f32[328,128]{1,0:T(8,128)S(1)}, u32[]{:S(2)}, u32[]{:S(2)}) %collective-permute-start.3) | collective-permute-done | bytes 167968 | tf_op jit(solution)/shard_map/ppermute | solution.py:532
  17.3 1.5 %collective-permute-start.4 = (f32[328,128]{1,0:T(8,128)S(1)}, f32[328,128]{1,0:T(8,128)S(1)}, u32[]{:S(2)}, u32[]{:S(2)}) collective-permute-start(f32[328,128]{1,0:T(8,128)S(1)} %collective-permute-done.3.refs_5_.refs_6_), channel_id=1, source_target_pairs={{0,8},{8,16},{16,24},{24,28},{28,20},{20,12},{12,4},{4,0},{1,9},{9... | collective-permute-start | bytes 503816 | tf_op jit(solution)/shard_map/ppermute | solution.py:532
  18.7 0.0 collective-permute-done.5.refs_6_.refs_7_
  18.8 0.5 %collective-permute-start.7 = (f32[328,128]{1,0:T(8,128)S(1)}, f32[328,128]{1,0:T(8,128)S(1)}, u32[]{:S(2)}, u32[]{:S(2)}) collective-permute-start(f32[328,128]{1,0:T(8,128)S(1)} %collective-permute-done.5.refs_6_.refs_7_), channel_id=1, source_target_pairs={{8,0},{16,8},{24,16},{28,24},{20,28},{12,20},{4,12},{0,4},{9,1},{1... | collective-permute-start | bytes 503816 | tf_op jit(solution)/shard_map/ppermute | solution.py:533
  19.3 1.4 %gather_step.5.refs_4_ = f32[3,128,1024]{2,1,0:T(8,128)S(1)} custom-call(bf16[768,1024]{1,0:T(8,128)(2,1)S(1)} %copy-done, f32[8,2,1024]{2,1,0:T(2,128)S(1)} %copy-done.1, f32[8,2,128]{2,1,0:T(2,128)S(1)} %get-tuple-element.36.refs_2_, s32[8,1,128]{2,1,0:T(1,128)S(1)} %get-tuple-element.37.refs_3_, f32[3,128,1024]{2,1,0:T(8,128)S(1)} %gather_step.4.refs_4_.gain_ref, ...), custom_call_target="tpu_custom_call" | custom-call | flops 1000000000 | bytes 4194304 | tf_op jit(solution)/shard_map/gather_step/pallas_call | solution.py:355
  20.7 2.0 %collective-permute-done.4.refs_8_ = f32[328,128]{1,0:T(8,128)S(1)} collective-permute-done((f32[328,128]{1,0:T(8,128)S(1)}, f32[328,128]{1,0:T(8,128)S(1)}, u32[]{:S(2)}, u32[]{:S(2)}) %collective-permute-start.4) | collective-permute-done | bytes 167968 | tf_op jit(solution)/shard_map/ppermute | solution.py:532
  22.6 1.6 %collective-permute-start.6 = (f32[328,128]{1,0:T(8,128)S(1)}, f32[328,128]{1,0:T(8,128)S(1)}, u32[]{:S(2)}, u32[]{:S(2)}) collective-permute-start(f32[328,128]{1,0:T(8,128)S(1)} %collective-permute-done.4.refs_8_), channel_id=1, source_target_pairs={{0,8},{8,16},{16,24},{24,28},{28,20},{20,12},{12,4},{4,0},{1,9},{9... | collective-permute-start | bytes 503816 | tf_op jit(solution)/shard_map/ppermute | solution.py:532
  24.2 0.0 collective-permute-done.7.refs_9_
  24.2 0.5 %collective-permute-start.8 = (f32[328,128]{1,0:T(8,128)S(1)}, f32[328,128]{1,0:T(8,128)S(1)}, u32[]{:S(2)}, u32[]{:S(2)}) collective-permute-start(f32[328,128]{1,0:T(8,128)S(1)} %collective-permute-done.7.refs_9_), channel_id=1, source_target_pairs={{8,0},{16,8},{24,16},{28,24},{20,28},{12,20},{4,12},{0,4},{9,1},{1... | collective-permute-start | bytes 503816 | tf_op jit(solution)/shard_map/ppermute | solution.py:533
  24.7 1.4 %gather_step.6 = (f32[3,128,1024]{2,1,0:T(8,128)S(1)}, bf16[4,2,256,1024]{3,2,1,0:T(8,128)(2,1)S(1)}, f32[128,512]{1,0:T(8,128)S(1)}) custom-call(bf16[768,1024]{1,0:T(8,128)(2,1)S(1)} %copy-done, f32[8,2,1024]{2,1,0:T(2,128)S(1)} %copy-done.1, f32[8,2,128]{2,1,0:T(2,128)S(1)} %get-tuple-element.36.refs_2_, s32[8,1,128]{2,1,0:T(1,128)S(1)} %get-tuple-element.37.refs_3_, ...), custom_call_target="tpu_custom_call" | custom-call | flops 1000000000 | bytes 4194304 | tf_op jit(solution)/shard_map/gather_step/pallas_call | solution.py:355
  26.0 1.9 %collective-permute-done.6.refs_5_ = f32[328,128]{1,0:T(8,128)S(1)} collective-permute-done((f32[328,128]{1,0:T(8,128)S(1)}, f32[328,128]{1,0:T(8,128)S(1)}, u32[]{:S(2)}, u32[]{:S(2)}) %collective-permute-start.6) | collective-permute-done | bytes 167968 | tf_op jit(solution)/shard_map/ppermute | solution.py:532
  28.0 1.6 %collective-permute-start.9 = (f32[328,128]{1,0:T(8,128)S(1)}, f32[328,128]{1,0:T(8,128)S(1)}, u32[]{:S(2)}, u32[]{:S(2)}) collective-permute-start(f32[328,128]{1,0:T(8,128)S(1)} %collective-permute-done.6.refs_5_), channel_id=1, source_target_pairs={{0,8},{8,16},{16,24},{24,28},{28,20},{20,12},{12,4},{4,0},{1,9},{9... | collective-permute-start | bytes 503816 | tf_op jit(solution)/shard_map/ppermute | solution.py:549
  29.6 0.0 collective-permute-done.8.refs_6_
  29.6 0.0 copy-start.2
  29.6 2.9 %gather_step.7 = (f32[3,128,1024]{2,1,0:T(8,128)S(1)}, bf16[4,2,256,1024]{3,2,1,0:T(8,128)(2,1)S(1)}) custom-call(bf16[768,1024]{1,0:T(8,128)(2,1)S(1)} %copy-done, f32[8,2,1024]{2,1,0:T(2,128)S(1)} %copy-done.1, f32[8,2,128]{2,1,0:T(2,128)S(1)} %get-tuple-element.36.refs_2_, s32[8,1,128]{2,1,0:T(1,128)S(1)} %get-tuple-element.37.refs_3_, ...), custom_call_target="tpu_custom_call" | custom-call | flops 1000000000 | bytes 4194304 | tf_op jit(solution)/shard_map/gather_step/pallas_call | solution.py:355
  32.4 0.9 %collective-permute-done.9.refs_6_ = f32[328,128]{1,0:T(8,128)S(1)} collective-permute-done((f32[328,128]{1,0:T(8,128)S(1)}, f32[328,128]{1,0:T(8,128)S(1)}, u32[]{:S(2)}, u32[]{:S(2)}) %collective-permute-start.9) | collective-permute-done | bytes 167968 | tf_op jit(solution)/shard_map/ppermute | solution.py:549
  33.4 0.0 copy-done.2
  33.4 1.7 %back_step.1 = (f32[2,128,128]{2,1,0:T(8,128)S(1)}, f32[2,128,512]{2,1,0:T(8,128)S(1)}) custom-call(bf16[768,1024]{1,0:T(8,128)(2,1)S(1)} %copy-done, f32[8,2,1024]{2,1,0:T(2,128)S(1)} %copy-done.1, f32[8,2,128]{2,1,0:T(2,128)S(1)} %get-tuple-element.36.refs_2_, s32[8,1,128]{2,1,0:T(1,128)S(1)} %get-tuple-element.37.refs_3_, ...), custom_call_target="tpu_custom_call" | custom-call | tf_op jit(solution)/shard_map/back_step/pallas_call | solution.py:396
  35.1 1.6 %collective-permute-start.10 = (f32[2,128,128]{2,1,0:T(8,128)S(1)}, f32[2,128,128]{2,1,0:T(8,128)S(1)}, u32[]{:S(2)}, u32[]{:S(2)}) collective-permute-start(f32[2,128,128]{2,1,0:T(8,128)S(1)} %get-tuple-element.53.refs_0_), channel_id=1, source_target_pairs={{0,2},{1,3},{2,0},{3,1},{4,6},{5,7},{6,4},{7,5},{8,10},{9,11},{10,... | collective-permute-start | bytes 393224 | tf_op jit(solution)/shard_map/ppermute | solution.py:489
  36.7 0.6 %image_step.4.refs_1_ = f32[2,128,1024]{2,1,0:T(8,128)S(1)} custom-call(bf16[4,2,256,1024]{3,2,1,0:T(8,128)(2,1)S(1)} %get-tuple-element.52.e_ref, f32[2,128,128]{2,1,0:T(8,128)S(1)} %get-tuple-element.53.refs_0_), custom_call_target="tpu_custom_call" | custom-call | flops 4000000000 | bytes 4194304 | tf_op jit(solution)/shard_map/image_step/pallas_call | solution.py:476
  37.3 0.1 collective-permute-start.11
  37.4 1.0 %correct_step.1 = f32[1024,128]{1,0:T(8,128)} custom-call(f32[2,128,512]{2,1,0:T(8,128)S(1)} %get-tuple-element.55.sub_ref, f32[3,128,1024]{2,1,0:T(8,128)S(1)} %gather_step.4.refs_4_.gain_ref, f32[128,512]{1,0:T(8,128)S(1)} %get-tuple-element.56.late_ref, f32[8,2,1024]{2,1,0:T(2,128)S(1)} %copy-done.1), custom_call_target="tpu_custom_call" | custom-call | flops 4000000000 | bytes 4194304 | tf_op jit(solution)/shard_map/correct_step/pallas_call | solution.py:424
  38.4 0.3 collective-permute-done.11.refs_0_
  38.7 0.6 %image_step.5.refs_1_ = f32[2,128,1024]{2,1,0:T(8,128)S(1)} custom-call(bf16[4,2,256,1024]{3,2,1,0:T(8,128)(2,1)S(1)} %get-tuple-element.52.e_ref, f32[2,128,128]{2,1,0:T(8,128)S(1)} %collective-permute-done.11.refs_0_, f32[2,128,1024]{2,1,0:T(8,128)S(1)} %image_step.4.refs_1_), custom_call_target="tpu_custom_call" | custom-call | flops 4000000000 | bytes 4194304 | tf_op jit(solution)/shard_map/image_step/pallas_call | solution.py:476
  39.3 0.8 %collective-permute-done.10.refs_0_ = f32[2,128,128]{2,1,0:T(8,128)S(1)} collective-permute-done((f32[2,128,128]{2,1,0:T(8,128)S(1)}, f32[2,128,128]{2,1,0:T(8,128)S(1)}, u32[]{:S(2)}, u32[]{:S(2)}) %collective-permute-start.10) | collective-permute-done | bytes 131104 | tf_op jit(solution)/shard_map/ppermute | solution.py:489
  40.1 0.0 collective-permute-start.12
  40.1 0.6 %image_step.6.refs_1_ = f32[2,128,1024]{2,1,0:T(8,128)S(1)} custom-call(bf16[4,2,256,1024]{3,2,1,0:T(8,128)(2,1)S(1)} %get-tuple-element.52.e_ref, f32[2,128,128]{2,1,0:T(8,128)S(1)} %collective-permute-done.10.refs_0_, f32[2,128,1024]{2,1,0:T(8,128)S(1)} %image_step.5.refs_1_), custom_call_target="tpu_custom_call" | custom-call | flops 4000000000 | bytes 4194304 | tf_op jit(solution)/shard_map/image_step/pallas_call | solution.py:476
  40.7 0.7 %collective-permute-done.12.refs_0_ = f32[2,128,128]{2,1,0:T(8,128)S(1)} collective-permute-done((f32[2,128,128]{2,1,0:T(8,128)S(1)}, f32[2,128,128]{2,1,0:T(8,128)S(1)}, u32[]{:S(2)}, u32[]{:S(2)}) %collective-permute-start.12) | collective-permute-done | bytes 131104 | tf_op jit(solution)/shard_map/ppermute | solution.py:489
  41.5 1.4 %image_step.7 = f32[2,128,1024]{2,1,0:T(8,128)} custom-call(bf16[4,2,256,1024]{3,2,1,0:T(8,128)(2,1)S(1)} %get-tuple-element.52.e_ref, f32[2,128,128]{2,1,0:T(8,128)S(1)} %collective-permute-done.12.refs_0_, f32[2,128,1024]{2,1,0:T(8,128)S(1)} %image_step.6.refs_1_), custom_call_target="tpu_custom_call" | custom-call | flops 4000000000 | bytes 4194304 | tf_op jit(solution)/shard_map/image_step/pallas_call | solution.py:476
  (2 shorter events, 0.0 us)
Async XLA Ops:
  0.6 1.2 %copy-start.5 = (f32[2,128,1024]{2,1,0:T(8,128)S(1)}, f32[2,128,1024]{2,1,0:T(8,128)}, u32[]{:S(2)}) copy-start(f32[2,128,1024]{2,1,0:T(8,128)} %x_ref.1) | copy-start | bytes 3145732
  3.0 1.5 %collective-permute-start = (f32[1,2,128,128]{3,2,1,0:T(8,128)S(1)}, f32[1,2,128,128]{3,2,1,0:T(8,128)S(1)}, u32[]{:S(2)}, u32[]{:S(2)}) collective-permute-start(f32[1,2,128,128]{3,2,1,0:T(8,128)S(1)} %get-tuple-element.34), channel_id=1, source_target_pairs={{0,1},{1,0},{2,3},{3,2},{4,5},{5,4},{6,7},{7,6},{8,9},{9,8},{10,11... | collective-permute-start | bytes 393224 | tf_op jit(solution)/shard_map/ppermute | solution.py:489
  3.5 4.0 %copy-start.6 = (s32[8]{0:T(128)S(1)}, s32[8]{0:T(128)}, u32[]{:S(2)}) copy-start(s32[8]{0:T(128)} %starts_ref.1) | copy-start | bytes 100
  4.5 6.8 %copy-start.3 = (f32[1,64,128]{2,1,0:T(8,128)S(1)}, f32[1,64,128]{2,1,0:T(8,128)}, u32[]{:S(2)}) copy-start(f32[1,64,128]{2,1,0:T(8,128)} %refs_2_.1) | copy-start | bytes 98308
  4.5 6.8 %copy-start.4 = (s32[1,64]{1,0:T(1,128)S(1)}, s32[1,64]{1,0:T(1,128)}, u32[]{:S(2)}) copy-start(s32[1,64]{1,0:T(1,128)} %refs_3_.1) | copy-start | bytes 772
  4.5 8.9 %copy-start = (bf16[768,1024]{1,0:T(8,128)(2,1)S(1)}, bf16[768,1024]{1,0:T(8,128)(2,1)}, u32[]{:S(2)}) copy-start(bf16[768,1024]{1,0:T(8,128)(2,1)} %constant.7.clone.refs_0_) | copy-start | bytes 4718596
  4.5 8.9 %copy-start.1 = (f32[8,2,1024]{2,1,0:T(2,128)S(1)}, f32[8,2,1024]{2,1,0:T(2,128)}, u32[]{:S(2)}) copy-start(f32[8,2,1024]{2,1,0:T(2,128)} %constant.8.clone.refs_1_.roots_ref) | copy-start | bytes 196612
  4.6 6.8 %collective-permute-start.1 = (f32[1,2,128,128]{3,2,1,0:T(8,128)S(1)}, f32[1,2,128,128]{3,2,1,0:T(8,128)S(1)}, u32[]{:S(2)}, u32[]{:S(2)}) collective-permute-start(f32[1,2,128,128]{3,2,1,0:T(8,128)S(1)} %add.6), channel_id=1, source_target_pairs={{0,2},{1,3},{2,0},{3,1},{4,6},{5,7},{6,4},{7,5},{8,10},{9,11},{10,... | collective-permute-start | bytes 393224 | tf_op jit(solution)/shard_map/ppermute | solution.py:489
  9.0 2.4 %collective-permute-start.2 = (f32[1,2,128,128]{3,2,1,0:T(8,128)S(1)}, f32[1,2,128,128]{3,2,1,0:T(8,128)S(1)}, u32[]{:S(2)}, u32[]{:S(2)}) collective-permute-start(f32[1,2,128,128]{3,2,1,0:T(8,128)S(1)} %get-tuple-element.40), channel_id=1, source_target_pairs={{0,1},{1,0},{2,3},{3,2},{4,5},{5,4},{6,7},{7,6},{8,9},{9,8},{10,11... | collective-permute-start | bytes 393224 | tf_op jit(solution)/shard_map/ppermute | solution.py:489
  11.4 5.8 %collective-permute-start.3 = (f32[328,128]{1,0:T(8,128)S(1)}, f32[328,128]{1,0:T(8,128)S(1)}, u32[]{:S(2)}, u32[]{:S(2)}) collective-permute-start(f32[328,128]{1,0:T(8,128)S(1)} %pack.1.refs_4_.refs_5_), channel_id=1, source_target_pairs={{0,8},{8,16},{16,24},{24,28},{28,20},{20,12},{12,4},{4,0},{1,9},{9... | collective-permute-start | bytes 503816 | tf_op jit(solution)/shard_map/ppermute | solution.py:532
  13.2 5.5 %collective-permute-start.5 = (f32[328,128]{1,0:T(8,128)S(1)}, f32[328,128]{1,0:T(8,128)S(1)}, u32[]{:S(2)}, u32[]{:S(2)}) collective-permute-start(f32[328,128]{1,0:T(8,128)S(1)} %pack.1.refs_4_.refs_5_), channel_id=1, source_target_pairs={{8,0},{16,8},{24,16},{28,24},{20,28},{12,20},{4,12},{0,4},{9,1},{1... | collective-permute-start | bytes 503816 | tf_op jit(solution)/shard_map/ppermute | solution.py:533
  17.3 5.4 %collective-permute-start.4 = (f32[328,128]{1,0:T(8,128)S(1)}, f32[328,128]{1,0:T(8,128)S(1)}, u32[]{:S(2)}, u32[]{:S(2)}) collective-permute-start(f32[328,128]{1,0:T(8,128)S(1)} %collective-permute-done.3.refs_5_.refs_6_), channel_id=1, source_target_pairs={{0,8},{8,16},{16,24},{24,28},{28,20},{20,12},{12,4},{4,0},{1,9},{9... | collective-permute-start | bytes 503816 | tf_op jit(solution)/shard_map/ppermute | solution.py:532
  18.8 5.5 %collective-permute-start.7 = (f32[328,128]{1,0:T(8,128)S(1)}, f32[328,128]{1,0:T(8,128)S(1)}, u32[]{:S(2)}, u32[]{:S(2)}) collective-permute-start(f32[328,128]{1,0:T(8,128)S(1)} %collective-permute-done.5.refs_6_.refs_7_), channel_id=1, source_target_pairs={{8,0},{16,8},{24,16},{28,24},{20,28},{12,20},{4,12},{0,4},{9,1},{1... | collective-permute-start | bytes 503816 | tf_op jit(solution)/shard_map/ppermute | solution.py:533
  22.6 5.4 %collective-permute-start.6 = (f32[328,128]{1,0:T(8,128)S(1)}, f32[328,128]{1,0:T(8,128)S(1)}, u32[]{:S(2)}, u32[]{:S(2)}) collective-permute-start(f32[328,128]{1,0:T(8,128)S(1)} %collective-permute-done.4.refs_8_), channel_id=1, source_target_pairs={{0,8},{8,16},{16,24},{24,28},{28,20},{20,12},{12,4},{4,0},{1,9},{9... | collective-permute-start | bytes 503816 | tf_op jit(solution)/shard_map/ppermute | solution.py:532
  24.2 5.4 %collective-permute-start.8 = (f32[328,128]{1,0:T(8,128)S(1)}, f32[328,128]{1,0:T(8,128)S(1)}, u32[]{:S(2)}, u32[]{:S(2)}) collective-permute-start(f32[328,128]{1,0:T(8,128)S(1)} %collective-permute-done.7.refs_9_), channel_id=1, source_target_pairs={{8,0},{16,8},{24,16},{28,24},{20,28},{12,20},{4,12},{0,4},{9,1},{1... | collective-permute-start | bytes 503816 | tf_op jit(solution)/shard_map/ppermute | solution.py:533
  28.0 5.4 %collective-permute-start.9 = (f32[328,128]{1,0:T(8,128)S(1)}, f32[328,128]{1,0:T(8,128)S(1)}, u32[]{:S(2)}, u32[]{:S(2)}) collective-permute-start(f32[328,128]{1,0:T(8,128)S(1)} %collective-permute-done.6.refs_5_), channel_id=1, source_target_pairs={{0,8},{8,16},{16,24},{24,28},{28,20},{20,12},{12,4},{4,0},{1,9},{9... | collective-permute-start | bytes 503816 | tf_op jit(solution)/shard_map/ppermute | solution.py:549
  29.6 3.8 %copy-start.2 = (bf16[1024,512]{1,0:T(8,128)(2,1)S(1)}, bf16[1024,512]{1,0:T(8,128)(2,1)}, u32[]{:S(2)}) copy-start(bf16[1024,512]{1,0:T(8,128)(2,1)} %constant.6.clone.refs_4_) | copy-start | bytes 3145732
  35.1 5.0 %collective-permute-start.10 = (f32[2,128,128]{2,1,0:T(8,128)S(1)}, f32[2,128,128]{2,1,0:T(8,128)S(1)}, u32[]{:S(2)}, u32[]{:S(2)}) collective-permute-start(f32[2,128,128]{2,1,0:T(8,128)S(1)} %get-tuple-element.53.refs_0_), channel_id=1, source_target_pairs={{0,2},{1,3},{2,0},{3,1},{4,6},{5,7},{6,4},{7,5},{8,10},{9,11},{10,... | collective-permute-start | bytes 393224 | tf_op jit(solution)/shard_map/ppermute | solution.py:489
  37.3 1.4 %collective-permute-start.11 = (f32[2,128,128]{2,1,0:T(8,128)S(1)}, f32[2,128,128]{2,1,0:T(8,128)S(1)}, u32[]{:S(2)}, u32[]{:S(2)}) collective-permute-start(f32[2,128,128]{2,1,0:T(8,128)S(1)} %get-tuple-element.53.refs_0_), channel_id=1, source_target_pairs={{0,1},{1,0},{2,3},{3,2},{4,5},{5,4},{6,7},{7,6},{8,9},{9,8},{10,11... | collective-permute-start | bytes 393224 | tf_op jit(solution)/shard_map/ppermute | solution.py:489
  40.1 1.3 %collective-permute-start.12 = (f32[2,128,128]{2,1,0:T(8,128)S(1)}, f32[2,128,128]{2,1,0:T(8,128)S(1)}, u32[]{:S(2)}, u32[]{:S(2)}) collective-permute-start(f32[2,128,128]{2,1,0:T(8,128)S(1)} %collective-permute-done.10.refs_0_), channel_id=1, source_target_pairs={{0,1},{1,0},{2,3},{3,2},{4,5},{5,4},{6,7},{7,6},{8,9},{9,8},{10,11... | collective-permute-start | bytes 393224 | tf_op jit(solution)/shard_map/ppermute | solution.py:489

commit v9 on v8

--- a/solution.py
+++ b/solution.py
@@ -102,10 +102,16 @@
     return halves(jnp.concatenate([jnp.concatenate(cos, 1), jnp.concatenate(sin, 1)]))
 
 
-def strip_sums(gs, z_of, width, base_ref, steps_ref, out_ref):
+def tilted(waves, tilt_ref, row):
+    (cos, sin), (pc, ps) = waves, (tilt_ref[row : row + 1], tilt_ref[row + 1 : row + 2])
+    return cos * pc - sin * ps, sin * pc + cos * ps
+
+
+def strip_sums(gs, z_of, width, base_ref, steps_ref, tilt_ref, out_ref):
     count, height = out_ref.shape[-2:]
     for i, g in enumerate(gs):
-        base, turn = (base_ref[g, 0], base_ref[g, 1]), (steps_ref[g, 0], steps_ref[g, 1])
+        base = tilted((base_ref[g, 0], base_ref[g, 1]), tilt_ref, 0)
+        turn = tilted((steps_ref[g, 0], steps_ref[g, 1]), tilt_ref, 2)
         acc = None
         for begin, size in chunks(width):
             part = dot3(waves_in(base, turn, begin, size), z_of(begin, size), NT)
@@ -116,23 +122,19 @@
 
 
 def first_strip_kernel(gs, cols_total, start_ref, x_ref, base_ref, steps_ref, out_ref, z_ref, tilt_ref):
-    own = lax.axis_index("fcol")
-    width = x_ref.shape[-1]
-    start, scale = start_ref[0:1, 0:1], 1.0 / math.sqrt(cols_total)
+    start, begin = start_ref[0:1, 0:1], lax.axis_index("fcol") * x_ref.shape[-1]
+    tilt_ref[0:1], tilt_ref[1:2] = unit(start * lanes(128), cols_total)
+    tilt_ref[2:3], tilt_ref[3:4] = unit(start * (begin + 128 * lanes(128)), cols_total, 1.0 / math.sqrt(cols_total))
     made = {}
 
     def z_of(begin, size):
         if begin not in made:
             columns = slice(begin, begin + size)
-            pc, ps = unit(start * (own * width + begin + lanes(size)), cols_total, scale)
-            re, im = x_ref[0, :, columns], x_ref[1, :, columns]
-            made[begin] = halves(jnp.concatenate([re * pc + im * ps, im * pc - re * ps]))
+            made[begin] = halves(jnp.concatenate([x_ref[0, :, columns], x_ref[1, :, columns]]))
             z_ref[0, :, columns], z_ref[1, :, columns] = made[begin]
         return made[begin]
 
-    tilt_ref[0:1], tilt_ref[1:2] = unit(start * lanes(128), cols_total)
-    tilt_ref[2:3], tilt_ref[3:4] = unit(start * (own * width + 128 * lanes(128)), cols_total, scale)
-    strip_sums(gs, z_of, width, base_ref, steps_ref, out_ref)
+    strip_sums(gs, z_of, x_ref.shape[-1], base_ref, steps_ref, tilt_ref, out_ref)
 
 
 def first_strips(column_start, facets, waves, gs):
@@ -157,14 +159,14 @@
     return lambda begin, size: (z_ref[0, :, begin : begin + size], z_ref[1, :, begin : begin + size])
 
 
-def far_strip_kernel(gs, z_ref, base_ref, steps_ref, out_ref):
-    strip_sums(gs, columns_of(z_ref), z_ref.shape[-1], base_ref, steps_ref, out_ref)
+def far_strip_kernel(gs, z_ref, base_ref, steps_ref, tilt_ref, out_ref):
+    strip_sums(gs, columns_of(z_ref), z_ref.shape[-1], base_ref, steps_ref, tilt_ref, out_ref)
 
 
 def far_strips(z, waves, gs):
     return pl.pallas_call(
         functools.partial(far_strip_kernel, tuple(gs)),
-        in_specs=[VMEM] * 3,
+        in_specs=[VMEM] * 4,
         out_specs=VMEM,
         out_shape=jax.ShapeDtypeStruct((len(gs), 2, waves[0].shape[2], z.shape[1] // 2), F32),
         compiler_params=LIMIT,
@@ -173,12 +175,12 @@
     )(z, *waves)
 
 
-def near_strip_kernel(groups, starts_ref, z_ref, base_ref, steps_ref, *refs):
+def near_strip_kernel(groups, starts_ref, z_ref, base_ref, steps_ref, tilt_ref, *refs):
     out_refs, (turn_ref, away_ref, starts, sem) = refs[: len(groups)], refs[len(groups) :]
     copy = pltpu.make_async_copy(starts_ref, starts, sem)
     copy.start()
     for gs, out_ref in zip(groups, out_refs):
-        strip_sums(gs, columns_of(z_ref), z_ref.shape[-1], base_ref, steps_ref, out_ref)
+        strip_sums(gs, columns_of(z_ref), z_ref.shape[-1], base_ref, steps_ref, tilt_ref, out_ref)
     copy.wait()
     rows, _, height = turn_ref.shape
     rows_total = rows * height
@@ -192,7 +194,7 @@
     rows, count, height = starts.shape[0], waves[0].shape[2], z.shape[1] // 2
     return pl.pallas_call(
         functools.partial(near_strip_kernel, groups),
-        in_specs=[pl.BlockSpec(memory_space=pl.ANY)] + [VMEM] * 3,
+        in_specs=[pl.BlockSpec(memory_space=pl.ANY)] + [VMEM] * 4,
         out_specs=[VMEM] * (len(groups) + 2),
         out_shape=[jax.ShapeDtypeStruct((len(gs), 2, count, height), F32) for gs in groups]
         + [jax.ShapeDtypeStruct((rows, 2, height), F32), jax.ShapeDtypeStruct((rows, 1, 128), jnp.int32)],
@@ -267,12 +269,9 @@
 
 
 def image_waves(base_ref, steps_ref, tilt_ref, out_ref):
-    def tilted(cos, sin, row):
-        pc, ps = tilt_ref[row : row + 1], tilt_ref[row + 1 : row + 2]
-        return cos * pc - sin * ps, sin * pc + cos * ps
-
     for g in range(out_ref.shape[0]):
-        base, turn = tilted(base_ref[g, 0], base_ref[g, 1], 0), tilted(steps_ref[g, 0], steps_ref[g, 1], 2)
+        base = tilted((base_ref[g, 0], base_ref[g, 1]), tilt_ref, 0)
+        turn = tilted((steps_ref[g, 0], steps_ref[g, 1]), tilt_ref, 2)
         for begin, size in chunks(out_ref.shape[-1]):
             columns = slice(begin, begin + size)
             out_ref[g, 0, :, columns], out_ref[g, 1, :, columns] = waves_in(base, turn, begin, size)
@@ -507,6 +506,7 @@
     column_start = column_start.reshape(1, 1)
     waves = waves_of(count, width, cols_total)
     sent, z, tilt = first_strips(column_start, facets, waves, range(top + 1, cols, 2))
+    waves = *waves, tilt
     far = far_strips(z, waves, range(top, cols, 2)) + swap(sent, "fcol", 1)
     far, z = lax.optimization_barrier((far, z))
     sent, near, *turns = near_strips(subgrid_start, z, waves, [tuple(range(1, top, 2)), tuple(range(0, top, 2))])
@@ -537,12 +537,12 @@
             state = gather_step("skip", tables, [state, up, down], (-step, step), count)
         elif step == last - 1:
             steps = (1 - step, step - 1, -step, step)
-            operands = [state, own if whole else before, *early, up, down, *waves, tilt]
+            operands = [state, own if whole else before, *early, up, down, *waves]
             own_gain = jax.ShapeDtypeStruct((count, SG), F32)
             kind = "late own" if whole else "late"
             state, image_table, own_gain = gather_step(kind, tables, operands, steps, count, made, own_gain)
         elif step == last:
-            operands = [state, up, down, *waves, tilt, image_table]
+            operands = [state, up, down, *waves, image_table]
             state, image_table = gather_step("last", tables, operands, (-step, step), count, made)
         else:
             state = gather_step("plain", tables, [state, up, down], (-step, step), count)

time: 43.2 us -> 43.1 us (level)
  transfers between devices with their start and end apart: 13 -> 13, of which waited for: 9 -> 9; matrix products, arithmetic and copies ran while one was open for 0% -> 0% of each run, Pallas kernels for 27% -> 26%
where the time goes in v9:
time: 43.1 us; the launch traced here: 43 us
  Pallas kernels  16.1 us (37%)
  starting transfers between devices  12.9 us (30%)
  waiting for transfers between devices  11.6 us (27%)
  between operations  2.29 us (5%)
    ppermute x4, waiting for transfers between devices, per_device(): up = lax.ppermute(up, 'frow', ahead)  7.82 us
    ppermute x4, starting transfers between devices, per_device(): up = lax.ppermute(up, 'frow', ahead)  6.41 us
    pallas_call x4, Pallas kernels, gather_step(): pl.pallas_call(functools.partial(gather_kernel, kind, steps, rows_total /...  6.37 us
    ppermute x6, starting transfers between devices, swap(): lax.ppermute(value, axis, [(i, i ^ bit) for i in range(lax.axis_size(axis...  5.2 us
    ppermute x6, waiting for transfers between devices, swap(): lax.ppermute(value, axis, [(i, i ^ bit) for i in range(lax.axis_size(axis...  3.82 us
    pallas_call x4, Pallas kernels, image_step(): pl.pallas_call(functools.partial(image_kernel, tuple(gs), first, last), i...  3.17 us
    pallas_call x1, Pallas kernels, back_step(): pl.pallas_call(functools.partial(back_kernel, rows_total // height, heigh...  1.72 us
    pallas_call x1, Pallas kernels, near_strips(): pl.pallas_call(functools.partial(near_strip_kernel, groups), in_specs=[pl...  1.37 us
  transfers between devices with their start and end apart: 13, of which 9 were waited for; matrix products, arithmetic and copies ran while one was open for 0% of the time, Pallas kernels for 26%

profile of v9, /device:TPU:0, one launch (start us, length us, event | category | flops | bytes accessed | tf_op | source)
XLA Modules:
  0.0 43.0 jit_solution(8922618362835462734)
XLA Ops:
  0.6 0.0 copy-start.5
  0.6 0.6 %waves.1 = (f32[4,2,128,128]{3,2,1,0:T(8,128)S(1)}, f32[4,2,128,128]{3,2,1,0:T(8,128)S(1)}) custom-call(), custom_call_target="tpu_custom_call" | custom-call | flops 1000000000 | bytes 2097152 | tf_op jit(solution)/shard_map/waves/pallas_call | solution.py:86
  1.9 0.0 copy-done.5
  1.9 1.0 %first_strips.1 = (f32[1,2,128,128]{3,2,1,0:T(8,128)S(1)}, bf16[2,256,1024]{2,1,0:T(8,128)(2,1)S(1)}, f32[4,128]{1,0:T(4,128)S(1)}) custom-call(s32[1,1]{1,0:T(1,128)} %bitcast.7.start_ref, f32[2,128,1024]{2,1,0:T(8,128)S(1)} %copy-done.5, f32[4,2,128,128]{3,2,1,0:T(8,128)S(1)} %get-tuple-element.31.base_ref.refs_10_.refs_7_, ...), custom_call_target="tpu_custom_call" | custom-call | flops 1000000000 | bytes 2097152 | tf_op jit(solution)/shard_map/first_strips/pallas_call | solution.py:143
  2.9 0.5 %collective-permute-start = (f32[1,2,128,128]{3,2,1,0:T(8,128)S(1)}, f32[1,2,128,128]{3,2,1,0:T(8,128)S(1)}, u32[]{:S(2)}, u32[]{:S(2)}) collective-permute-start(f32[1,2,128,128]{3,2,1,0:T(8,128)S(1)} %get-tuple-element.35), channel_id=1, source_target_pairs={{0,1},{1,0},{2,3},{3,2},{4,5},{5,4},{6,7},{7,6},{8,9},{9,8},{10,11... | collective-permute-start | bytes 393224 | tf_op jit(solution)/shard_map/ppermute | solution.py:488
  3.4 0.0 copy-start.6
  3.4 0.8 %far_strips.1 = f32[1,2,128,128]{3,2,1,0:T(8,128)S(1)} custom-call(bf16[2,256,1024]{2,1,0:T(8,128)(2,1)S(1)} %get-tuple-element.36.z_ref, f32[4,2,128,128]{3,2,1,0:T(8,128)S(1)} %get-tuple-element.31.base_ref.refs_10_.refs_7_, f32[4,2,128,128]{3,2,1,0:T(8,128)S(1)} %get-tuple-element.32.steps_ref.refs_11_.refs_8_, ...), custom_call_target="tpu_custom_call" | custom-call | flops 1000000000 | bytes 2097152 | tf_op jit(solution)/shard_map/far_strips/pallas_call | solution.py:167
  4.2 0.2 collective-permute-done
  4.4 0.0 copy-start.3
  4.4 0.0 copy-start.4
  4.5 0.0 copy-start
  4.5 0.0 copy-start.1
  4.5 2.9 %collective-permute-start.1 = (f32[1,2,128,128]{3,2,1,0:T(8,128)S(1)}, f32[1,2,128,128]{3,2,1,0:T(8,128)S(1)}, u32[]{:S(2)}, u32[]{:S(2)}) collective-permute-start(f32[1,2,128,128]{3,2,1,0:T(8,128)S(1)} %add.6), channel_id=1, source_target_pairs={{0,2},{1,3},{2,0},{3,1},{4,6},{5,7},{6,4},{7,5},{8,10},{9,11},{10,... | collective-permute-start | bytes 393224 | tf_op jit(solution)/shard_map/ppermute | solution.py:488
  7.4 0.0 copy-done.6
  7.4 1.4 %near_strips.1 = (f32[1,2,128,128]{3,2,1,0:T(8,128)S(1)}, f32[1,2,128,128]{3,2,1,0:T(8,128)S(1)}, f32[8,2,128]{2,1,0:T(2,128)S(1)}, s32[8,1,128]{2,1,0:T(1,128)S(1)}) custom-call(s32[8]{0:T(128)S(1)} %copy-done.6, bf16[2,256,1024]{2,1,0:T(8,128)(2,1)S(1)} %get-tuple-element.36.z_ref, f32[4,2,128,128]{3,2,1,0:T(8,128)S(1)} %get-tuple-element.31.base_ref.refs_10_.refs_7_, ...), custom_call_target="tpu_custom_call" | custom-call | flops 4000000000 | bytes 2097152 | tf_op jit(solution)/shard_map/near_strips/pallas_call | solution.py:195
  8.8 0.1 collective-permute-start.2
  9.5 1.7 %collective-permute-done.1 = f32[1,2,128,128]{3,2,1,0:T(8,128)S(1)} collective-permute-done((f32[1,2,128,128]{3,2,1,0:T(8,128)S(1)}, f32[1,2,128,128]{3,2,1,0:T(8,128)S(1)}, u32[]{:S(2)}, u32[]{:S(2)}) %collective-permute-start.1) | collective-permute-done | bytes 131104 | tf_op jit(solution)/shard_map/ppermute | solution.py:488
  11.3 0.0 collective-permute-done.2.refs_1_
  11.3 0.0 copy-done.3
  11.3 0.0 copy-done.4
  11.3 0.1 pack.1.refs_4_.refs_5_
  11.4 1.8 %collective-permute-start.3 = (f32[328,128]{1,0:T(8,128)S(1)}, f32[328,128]{1,0:T(8,128)S(1)}, u32[]{:S(2)}, u32[]{:S(2)}) collective-permute-start(f32[328,128]{1,0:T(8,128)S(1)} %pack.1.refs_4_.refs_5_), channel_id=1, source_target_pairs={{0,8},{8,16},{16,24},{24,28},{28,20},{20,12},{12,4},{4,0},{1,9},{9... | collective-permute-start | bytes 503816 | tf_op jit(solution)/shard_map/ppermute | solution.py:532
  13.2 0.2 collective-permute-start.5
  13.4 0.0 copy-done
  13.4 0.0 copy-done.1
  13.4 0.8 %gather_step.4.refs_4_.gain_ref = f32[3,128,1024]{2,1,0:T(8,128)S(1)} custom-call(bf16[768,1024]{1,0:T(8,128)(2,1)S(1)} %copy-done, f32[8,2,1024]{2,1,0:T(2,128)S(1)} %copy-done.1, f32[8,2,128]{2,1,0:T(2,128)S(1)} %get-tuple-element.37.refs_2_, s32[8,1,128]{2,1,0:T(1,128)S(1)} %get-tuple-element.38.refs_3_, f32[328,128]{1,0:T(8,128)S(1)} %pack.1.refs_4_.refs_5_), custom_call_target="tpu_custom_call" | custom-call | flops 1000000000 | bytes 4194304 | tf_op jit(solution)/shard_map/gather_step/pallas_call | solution.py:354
  14.2 3.0 %collective-permute-done.3.refs_5_.refs_6_ = f32[328,128]{1,0:T(8,128)S(1)} collective-permute-done((f32[328,128]{1,0:T(8,128)S(1)}, f32[328,128]{1,0:T(8,128)S(1)}, u32[]{:S(2)}, u32[]{:S(2)}) %collective-permute-start.3) | collective-permute-done | bytes 167968 | tf_op jit(solution)/shard_map/ppermute | solution.py:532
  17.2 1.5 %collective-permute-start.4 = (f32[328,128]{1,0:T(8,128)S(1)}, f32[328,128]{1,0:T(8,128)S(1)}, u32[]{:S(2)}, u32[]{:S(2)}) collective-permute-start(f32[328,128]{1,0:T(8,128)S(1)} %collective-permute-done.3.refs_5_.refs_6_), channel_id=1, source_target_pairs={{0,8},{8,16},{16,24},{24,28},{28,20},{20,12},{12,4},{4,0},{1,9},{9... | collective-permute-start | bytes 503816 | tf_op jit(solution)/shard_map/ppermute | solution.py:532
  18.7 0.0 collective-permute-done.5.refs_6_.refs_7_
  18.7 0.5 %collective-permute-start.7 = (f32[328,128]{1,0:T(8,128)S(1)}, f32[328,128]{1,0:T(8,128)S(1)}, u32[]{:S(2)}, u32[]{:S(2)}) collective-permute-start(f32[328,128]{1,0:T(8,128)S(1)} %collective-permute-done.5.refs_6_.refs_7_), channel_id=1, source_target_pairs={{8,0},{16,8},{24,16},{28,24},{20,28},{12,20},{4,12},{0,4},{9,1},{1... | collective-permute-start | bytes 503816 | tf_op jit(solution)/shard_map/ppermute | solution.py:533
  19.2 1.4 %gather_step.5.refs_4_ = f32[3,128,1024]{2,1,0:T(8,128)S(1)} custom-call(bf16[768,1024]{1,0:T(8,128)(2,1)S(1)} %copy-done, f32[8,2,1024]{2,1,0:T(2,128)S(1)} %copy-done.1, f32[8,2,128]{2,1,0:T(2,128)S(1)} %get-tuple-element.37.refs_2_, s32[8,1,128]{2,1,0:T(1,128)S(1)} %get-tuple-element.38.refs_3_, f32[3,128,1024]{2,1,0:T(8,128)S(1)} %gather_step.4.refs_4_.gain_ref, ...), custom_call_target="tpu_custom_call" | custom-call | flops 1000000000 | bytes 4194304 | tf_op jit(solution)/shard_map/gather_step/pallas_call | solution.py:354
  20.6 2.0 %collective-permute-done.4.refs_8_ = f32[328,128]{1,0:T(8,128)S(1)} collective-permute-done((f32[328,128]{1,0:T(8,128)S(1)}, f32[328,128]{1,0:T(8,128)S(1)}, u32[]{:S(2)}, u32[]{:S(2)}) %collective-permute-start.4) | collective-permute-done | bytes 167968 | tf_op jit(solution)/shard_map/ppermute | solution.py:532
  22.6 1.6 %collective-permute-start.6 = (f32[328,128]{1,0:T(8,128)S(1)}, f32[328,128]{1,0:T(8,128)S(1)}, u32[]{:S(2)}, u32[]{:S(2)}) collective-permute-start(f32[328,128]{1,0:T(8,128)S(1)} %collective-permute-done.4.refs_8_), channel_id=1, source_target_pairs={{0,8},{8,16},{16,24},{24,28},{28,20},{20,12},{12,4},{4,0},{1,9},{9... | collective-permute-start | bytes 503816 | tf_op jit(solution)/shard_map/ppermute | solution.py:532
  24.1 0.0 collective-permute-done.7.refs_9_
  24.1 0.5 %collective-permute-start.8 = (f32[328,128]{1,0:T(8,128)S(1)}, f32[328,128]{1,0:T(8,128)S(1)}, u32[]{:S(2)}, u32[]{:S(2)}) collective-permute-start(f32[328,128]{1,0:T(8,128)S(1)} %collective-permute-done.7.refs_9_), channel_id=1, source_target_pairs={{8,0},{16,8},{24,16},{28,24},{20,28},{12,20},{4,12},{0,4},{9,1},{1... | collective-permute-start | bytes 503816 | tf_op jit(solution)/shard_map/ppermute | solution.py:533
  24.6 1.4 %gather_step.6 = (f32[3,128,1024]{2,1,0:T(8,128)S(1)}, bf16[4,2,256,1024]{3,2,1,0:T(8,128)(2,1)S(1)}, f32[128,512]{1,0:T(8,128)S(1)}) custom-call(bf16[768,1024]{1,0:T(8,128)(2,1)S(1)} %copy-done, f32[8,2,1024]{2,1,0:T(2,128)S(1)} %copy-done.1, f32[8,2,128]{2,1,0:T(2,128)S(1)} %get-tuple-element.37.refs_2_, s32[8,1,128]{2,1,0:T(1,128)S(1)} %get-tuple-element.38.refs_3_, ...), custom_call_target="tpu_custom_call" | custom-call | flops 1000000000 | bytes 4194304 | tf_op jit(solution)/shard_map/gather_step/pallas_call | solution.py:354
  26.0 1.9 %collective-permute-done.6.refs_5_ = f32[328,128]{1,0:T(8,128)S(1)} collective-permute-done((f32[328,128]{1,0:T(8,128)S(1)}, f32[328,128]{1,0:T(8,128)S(1)}, u32[]{:S(2)}, u32[]{:S(2)}) %collective-permute-start.6) | collective-permute-done | bytes 167968 | tf_op jit(solution)/shard_map/ppermute | solution.py:532
  27.9 1.6 %collective-permute-start.9 = (f32[328,128]{1,0:T(8,128)S(1)}, f32[328,128]{1,0:T(8,128)S(1)}, u32[]{:S(2)}, u32[]{:S(2)}) collective-permute-start(f32[328,128]{1,0:T(8,128)S(1)} %collective-permute-done.6.refs_5_), channel_id=1, source_target_pairs={{0,8},{8,16},{16,24},{24,28},{28,20},{20,12},{12,4},{4,0},{1,9},{9... | collective-permute-start | bytes 503816 | tf_op jit(solution)/shard_map/ppermute | solution.py:549
  29.5 0.0 collective-permute-done.8.refs_6_
  29.5 0.0 copy-start.2
  29.5 2.9 %gather_step.7 = (f32[3,128,1024]{2,1,0:T(8,128)S(1)}, bf16[4,2,256,1024]{3,2,1,0:T(8,128)(2,1)S(1)}) custom-call(bf16[768,1024]{1,0:T(8,128)(2,1)S(1)} %copy-done, f32[8,2,1024]{2,1,0:T(2,128)S(1)} %copy-done.1, f32[8,2,128]{2,1,0:T(2,128)S(1)} %get-tuple-element.37.refs_2_, s32[8,1,128]{2,1,0:T(1,128)S(1)} %get-tuple-element.38.refs_3_, ...), custom_call_target="tpu_custom_call" | custom-call | flops 1000000000 | bytes 4194304 | tf_op jit(solution)/shard_map/gather_step/pallas_call | solution.py:354
  32.4 0.9 %collective-permute-done.9.refs_6_ = f32[328,128]{1,0:T(8,128)S(1)} collective-permute-done((f32[328,128]{1,0:T(8,128)S(1)}, f32[328,128]{1,0:T(8,128)S(1)}, u32[]{:S(2)}, u32[]{:S(2)}) %collective-permute-start.9) | collective-permute-done | bytes 167968 | tf_op jit(solution)/shard_map/ppermute | solution.py:549
  33.3 0.0 copy-done.2
  33.3 1.7 %back_step.1 = (f32[2,128,128]{2,1,0:T(8,128)S(1)}, f32[2,128,512]{2,1,0:T(8,128)S(1)}) custom-call(bf16[768,1024]{1,0:T(8,128)(2,1)S(1)} %copy-done, f32[8,2,1024]{2,1,0:T(2,128)S(1)} %copy-done.1, f32[8,2,128]{2,1,0:T(2,128)S(1)} %get-tuple-element.37.refs_2_, s32[8,1,128]{2,1,0:T(1,128)S(1)} %get-tuple-element.38.refs_3_, ...), custom_call_target="tpu_custom_call" | custom-call | tf_op jit(solution)/shard_map/back_step/pallas_call | solution.py:395
  35.0 1.6 %collective-permute-start.10 = (f32[2,128,128]{2,1,0:T(8,128)S(1)}, f32[2,128,128]{2,1,0:T(8,128)S(1)}, u32[]{:S(2)}, u32[]{:S(2)}) collective-permute-start(f32[2,128,128]{2,1,0:T(8,128)S(1)} %get-tuple-element.53.refs_0_), channel_id=1, source_target_pairs={{0,2},{1,3},{2,0},{3,1},{4,6},{5,7},{6,4},{7,5},{8,10},{9,11},{10,... | collective-permute-start | bytes 393224 | tf_op jit(solution)/shard_map/ppermute | solution.py:488
  36.6 0.6 %image_step.4.refs_1_ = f32[2,128,1024]{2,1,0:T(8,128)S(1)} custom-call(bf16[4,2,256,1024]{3,2,1,0:T(8,128)(2,1)S(1)} %get-tuple-element.52.e_ref, f32[2,128,128]{2,1,0:T(8,128)S(1)} %get-tuple-element.53.refs_0_), custom_call_target="tpu_custom_call" | custom-call | flops 4000000000 | bytes 4194304 | tf_op jit(solution)/shard_map/image_step/pallas_call | solution.py:475
  37.2 0.1 collective-permute-start.11
  37.3 1.0 %correct_step.1 = f32[1024,128]{1,0:T(8,128)} custom-call(f32[2,128,512]{2,1,0:T(8,128)S(1)} %get-tuple-element.55.sub_ref, f32[3,128,1024]{2,1,0:T(8,128)S(1)} %gather_step.4.refs_4_.gain_ref, f32[128,512]{1,0:T(8,128)S(1)} %get-tuple-element.56.late_ref, f32[8,2,1024]{2,1,0:T(2,128)S(1)} %copy-done.1), custom_call_target="tpu_custom_call" | custom-call | flops 4000000000 | bytes 4194304 | tf_op jit(solution)/shard_map/correct_step/pallas_call | solution.py:423
  38.3 0.3 collective-permute-done.11.refs_0_
  38.6 0.6 %image_step.5.refs_1_ = f32[2,128,1024]{2,1,0:T(8,128)S(1)} custom-call(bf16[4,2,256,1024]{3,2,1,0:T(8,128)(2,1)S(1)} %get-tuple-element.52.e_ref, f32[2,128,128]{2,1,0:T(8,128)S(1)} %collective-permute-done.11.refs_0_, f32[2,128,1024]{2,1,0:T(8,128)S(1)} %image_step.4.refs_1_), custom_call_target="tpu_custom_call" | custom-call | flops 4000000000 | bytes 4194304 | tf_op jit(solution)/shard_map/image_step/pallas_call | solution.py:475
  39.2 0.8 %collective-permute-done.10.refs_0_ = f32[2,128,128]{2,1,0:T(8,128)S(1)} collective-permute-done((f32[2,128,128]{2,1,0:T(8,128)S(1)}, f32[2,128,128]{2,1,0:T(8,128)S(1)}, u32[]{:S(2)}, u32[]{:S(2)}) %collective-permute-start.10) | collective-permute-done | bytes 131104 | tf_op jit(solution)/shard_map/ppermute | solution.py:488
  40.1 0.0 collective-permute-start.12
  40.1 0.6 %image_step.6.refs_1_ = f32[2,128,1024]{2,1,0:T(8,128)S(1)} custom-call(bf16[4,2,256,1024]{3,2,1,0:T(8,128)(2,1)S(1)} %get-tuple-element.52.e_ref, f32[2,128,128]{2,1,0:T(8,128)S(1)} %collective-permute-done.10.refs_0_, f32[2,128,1024]{2,1,0:T(8,128)S(1)} %image_step.5.refs_1_), custom_call_target="tpu_custom_call" | custom-call | flops 4000000000 | bytes 4194304 | tf_op jit(solution)/shard_map/image_step/pallas_call | solution.py:475
  40.7 0.7 %collective-permute-done.12.refs_0_ = f32[2,128,128]{2,1,0:T(8,128)S(1)} collective-permute-done((f32[2,128,128]{2,1,0:T(8,128)S(1)}, f32[2,128,128]{2,1,0:T(8,128)S(1)}, u32[]{:S(2)}, u32[]{:S(2)}) %collective-permute-start.12) | collective-permute-done | bytes 131104 | tf_op jit(solution)/shard_map/ppermute | solution.py:488
  41.4 1.4 %image_step.7 = f32[2,128,1024]{2,1,0:T(8,128)} custom-call(bf16[4,2,256,1024]{3,2,1,0:T(8,128)(2,1)S(1)} %get-tuple-element.52.e_ref, f32[2,128,128]{2,1,0:T(8,128)S(1)} %collective-permute-done.12.refs_0_, f32[2,128,1024]{2,1,0:T(8,128)S(1)} %image_step.6.refs_1_), custom_call_target="tpu_custom_call" | custom-call | flops 4000000000 | bytes 4194304 | tf_op jit(solution)/shard_map/image_step/pallas_call | solution.py:475
  (2 shorter events, 0.0 us)
Async XLA Ops:
  0.6 1.2 %copy-start.5 = (f32[2,128,1024]{2,1,0:T(8,128)S(1)}, f32[2,128,1024]{2,1,0:T(8,128)}, u32[]{:S(2)}) copy-start(f32[2,128,1024]{2,1,0:T(8,128)} %x_ref.1) | copy-start | bytes 3145732
  2.9 1.5 %collective-permute-start = (f32[1,2,128,128]{3,2,1,0:T(8,128)S(1)}, f32[1,2,128,128]{3,2,1,0:T(8,128)S(1)}, u32[]{:S(2)}, u32[]{:S(2)}) collective-permute-start(f32[1,2,128,128]{3,2,1,0:T(8,128)S(1)} %get-tuple-element.35), channel_id=1, source_target_pairs={{0,1},{1,0},{2,3},{3,2},{4,5},{5,4},{6,7},{7,6},{8,9},{9,8},{10,11... | collective-permute-start | bytes 393224 | tf_op jit(solution)/shard_map/ppermute | solution.py:488
  3.4 4.0 %copy-start.6 = (s32[8]{0:T(128)S(1)}, s32[8]{0:T(128)}, u32[]{:S(2)}) copy-start(s32[8]{0:T(128)} %starts_ref.1) | copy-start | bytes 100
  4.4 6.8 %copy-start.3 = (f32[1,64,128]{2,1,0:T(8,128)S(1)}, f32[1,64,128]{2,1,0:T(8,128)}, u32[]{:S(2)}) copy-start(f32[1,64,128]{2,1,0:T(8,128)} %refs_2_.1) | copy-start | bytes 98308
  4.4 6.8 %copy-start.4 = (s32[1,64]{1,0:T(1,128)S(1)}, s32[1,64]{1,0:T(1,128)}, u32[]{:S(2)}) copy-start(s32[1,64]{1,0:T(1,128)} %refs_3_.1) | copy-start | bytes 772
  4.5 8.9 %copy-start = (bf16[768,1024]{1,0:T(8,128)(2,1)S(1)}, bf16[768,1024]{1,0:T(8,128)(2,1)}, u32[]{:S(2)}) copy-start(bf16[768,1024]{1,0:T(8,128)(2,1)} %constant.7.clone.refs_0_) | copy-start | bytes 4718596
  4.5 8.9 %copy-start.1 = (f32[8,2,1024]{2,1,0:T(2,128)S(1)}, f32[8,2,1024]{2,1,0:T(2,128)}, u32[]{:S(2)}) copy-start(f32[8,2,1024]{2,1,0:T(2,128)} %constant.8.clone.refs_1_.roots_ref) | copy-start | bytes 196612
  4.5 6.8 %collective-permute-start.1 = (f32[1,2,128,128]{3,2,1,0:T(8,128)S(1)}, f32[1,2,128,128]{3,2,1,0:T(8,128)S(1)}, u32[]{:S(2)}, u32[]{:S(2)}) collective-permute-start(f32[1,2,128,128]{3,2,1,0:T(8,128)S(1)} %add.6), channel_id=1, source_target_pairs={{0,2},{1,3},{2,0},{3,1},{4,6},{5,7},{6,4},{7,5},{8,10},{9,11},{10,... | collective-permute-start | bytes 393224 | tf_op jit(solution)/shard_map/ppermute | solution.py:488
  8.8 2.5 %collective-permute-start.2 = (f32[1,2,128,128]{3,2,1,0:T(8,128)S(1)}, f32[1,2,128,128]{3,2,1,0:T(8,128)S(1)}, u32[]{:S(2)}, u32[]{:S(2)}) collective-permute-start(f32[1,2,128,128]{3,2,1,0:T(8,128)S(1)} %get-tuple-element.41), channel_id=1, source_target_pairs={{0,1},{1,0},{2,3},{3,2},{4,5},{5,4},{6,7},{7,6},{8,9},{9,8},{10,11... | collective-permute-start | bytes 393224 | tf_op jit(solution)/shard_map/ppermute | solution.py:488
  11.4 5.8 %collective-permute-start.3 = (f32[328,128]{1,0:T(8,128)S(1)}, f32[328,128]{1,0:T(8,128)S(1)}, u32[]{:S(2)}, u32[]{:S(2)}) collective-permute-start(f32[328,128]{1,0:T(8,128)S(1)} %pack.1.refs_4_.refs_5_), channel_id=1, source_target_pairs={{0,8},{8,16},{16,24},{24,28},{28,20},{20,12},{12,4},{4,0},{1,9},{9... | collective-permute-start | bytes 503816 | tf_op jit(solution)/shard_map/ppermute | solution.py:532
  13.2 5.5 %collective-permute-start.5 = (f32[328,128]{1,0:T(8,128)S(1)}, f32[328,128]{1,0:T(8,128)S(1)}, u32[]{:S(2)}, u32[]{:S(2)}) collective-permute-start(f32[328,128]{1,0:T(8,128)S(1)} %pack.1.refs_4_.refs_5_), channel_id=1, source_target_pairs={{8,0},{16,8},{24,16},{28,24},{20,28},{12,20},{4,12},{0,4},{9,1},{1... | collective-permute-start | bytes 503816 | tf_op jit(solution)/shard_map/ppermute | solution.py:533
  17.2 5.4 %collective-permute-start.4 = (f32[328,128]{1,0:T(8,128)S(1)}, f32[328,128]{1,0:T(8,128)S(1)}, u32[]{:S(2)}, u32[]{:S(2)}) collective-permute-start(f32[328,128]{1,0:T(8,128)S(1)} %collective-permute-done.3.refs_5_.refs_6_), channel_id=1, source_target_pairs={{0,8},{8,16},{16,24},{24,28},{28,20},{20,12},{12,4},{4,0},{1,9},{9... | collective-permute-start | bytes 503816 | tf_op jit(solution)/shard_map/ppermute | solution.py:532
  18.7 5.5 %collective-permute-start.7 = (f32[328,128]{1,0:T(8,128)S(1)}, f32[328,128]{1,0:T(8,128)S(1)}, u32[]{:S(2)}, u32[]{:S(2)}) collective-permute-start(f32[328,128]{1,0:T(8,128)S(1)} %collective-permute-done.5.refs_6_.refs_7_), channel_id=1, source_target_pairs={{8,0},{16,8},{24,16},{28,24},{20,28},{12,20},{4,12},{0,4},{9,1},{1... | collective-permute-start | bytes 503816 | tf_op jit(solution)/shard_map/ppermute | solution.py:533
  22.6 5.4 %collective-permute-start.6 = (f32[328,128]{1,0:T(8,128)S(1)}, f32[328,128]{1,0:T(8,128)S(1)}, u32[]{:S(2)}, u32[]{:S(2)}) collective-permute-start(f32[328,128]{1,0:T(8,128)S(1)} %collective-permute-done.4.refs_8_), channel_id=1, source_target_pairs={{0,8},{8,16},{16,24},{24,28},{28,20},{20,12},{12,4},{4,0},{1,9},{9... | collective-permute-start | bytes 503816 | tf_op jit(solution)/shard_map/ppermute | solution.py:532
  24.1 5.4 %collective-permute-start.8 = (f32[328,128]{1,0:T(8,128)S(1)}, f32[328,128]{1,0:T(8,128)S(1)}, u32[]{:S(2)}, u32[]{:S(2)}) collective-permute-start(f32[328,128]{1,0:T(8,128)S(1)} %collective-permute-done.7.refs_9_), channel_id=1, source_target_pairs={{8,0},{16,8},{24,16},{28,24},{20,28},{12,20},{4,12},{0,4},{9,1},{1... | collective-permute-start | bytes 503816 | tf_op jit(solution)/shard_map/ppermute | solution.py:533
  27.9 5.4 %collective-permute-start.9 = (f32[328,128]{1,0:T(8,128)S(1)}, f32[328,128]{1,0:T(8,128)S(1)}, u32[]{:S(2)}, u32[]{:S(2)}) collective-permute-start(f32[328,128]{1,0:T(8,128)S(1)} %collective-permute-done.6.refs_5_), channel_id=1, source_target_pairs={{0,8},{8,16},{16,24},{24,28},{28,20},{20,12},{12,4},{4,0},{1,9},{9... | collective-permute-start | bytes 503816 | tf_op jit(solution)/shard_map/ppermute | solution.py:549
  29.5 3.8 %copy-start.2 = (bf16[1024,512]{1,0:T(8,128)(2,1)S(1)}, bf16[1024,512]{1,0:T(8,128)(2,1)}, u32[]{:S(2)}) copy-start(bf16[1024,512]{1,0:T(8,128)(2,1)} %constant.6.clone.refs_4_) | copy-start | bytes 3145732
  35.0 5.0 %collective-permute-start.10 = (f32[2,128,128]{2,1,0:T(8,128)S(1)}, f32[2,128,128]{2,1,0:T(8,128)S(1)}, u32[]{:S(2)}, u32[]{:S(2)}) collective-permute-start(f32[2,128,128]{2,1,0:T(8,128)S(1)} %get-tuple-element.53.refs_0_), channel_id=1, source_target_pairs={{0,2},{1,3},{2,0},{3,1},{4,6},{5,7},{6,4},{7,5},{8,10},{9,11},{10,... | collective-permute-start | bytes 393224 | tf_op jit(solution)/shard_map/ppermute | solution.py:488
  37.2 1.4 %collective-permute-start.11 = (f32[2,128,128]{2,1,0:T(8,128)S(1)}, f32[2,128,128]{2,1,0:T(8,128)S(1)}, u32[]{:S(2)}, u32[]{:S(2)}) collective-permute-start(f32[2,128,128]{2,1,0:T(8,128)S(1)} %get-tuple-element.53.refs_0_), channel_id=1, source_target_pairs={{0,1},{1,0},{2,3},{3,2},{4,5},{5,4},{6,7},{7,6},{8,9},{9,8},{10,11... | collective-permute-start | bytes 393224 | tf_op jit(solution)/shard_map/ppermute | solution.py:488
  40.1 1.3 %collective-permute-start.12 = (f32[2,128,128]{2,1,0:T(8,128)S(1)}, f32[2,128,128]{2,1,0:T(8,128)S(1)}, u32[]{:S(2)}, u32[]{:S(2)}) collective-permute-start(f32[2,128,128]{2,1,0:T(8,128)S(1)} %collective-permute-done.10.refs_0_), channel_id=1, source_target_pairs={{0,1},{1,0},{2,3},{3,2},{4,5},{5,4},{6,7},{7,6},{8,9},{9,8},{10,11... | collective-permute-start | bytes 393224 | tf_op jit(solution)/shard_map/ppermute | solution.py:488

commit v10 on v9

--- a/solution.py
+++ b/solution.py
@@ -20,7 +20,7 @@
 NT = (((1,), (1,)), ((), ()))
 VMEM = pl.BlockSpec(memory_space=pltpu.VMEM)
 SMEM = pl.BlockSpec(memory_space=pltpu.SMEM)
-LIMIT = pltpu.CompilerParams(vmem_limit_bytes=32 << 20)
+LIMIT = pltpu.CompilerParams(vmem_limit_bytes=20 << 20)
 
 
 def halves(value):

time: 43.1 us -> 43.1 us (level)
  no operation moved by 1% of the time
where the time goes in v10:
time: 43.1 us; the launch traced here: 43 us
  Pallas kernels  16.1 us (37%)
  starting transfers between devices  12.9 us (30%)
  waiting for transfers between devices  11.6 us (27%)
  between operations  2.29 us (5%)
    ppermute x4, waiting for transfers between devices, per_device(): up = lax.ppermute(up, 'frow', ahead)  7.82 us
    ppermute x4, starting transfers between devices, per_device(): up = lax.ppermute(up, 'frow', ahead)  6.41 us
    pallas_call x4, Pallas kernels, gather_step(): pl.pallas_call(functools.partial(gather_kernel, kind, steps, rows_total /...  6.37 us
    ppermute x6, starting transfers between devices, swap(): lax.ppermute(value, axis, [(i, i ^ bit) for i in range(lax.axis_size(axis...  5.2 us
    ppermute x6, waiting for transfers between devices, swap(): lax.ppermute(value, axis, [(i, i ^ bit) for i in range(lax.axis_size(axis...  3.82 us
    pallas_call x4, Pallas kernels, image_step(): pl.pallas_call(functools.partial(image_kernel, tuple(gs), first, last), i...  3.17 us
    pallas_call x1, Pallas kernels, back_step(): pl.pallas_call(functools.partial(back_kernel, rows_total // height, heigh...  1.72 us
    pallas_call x1, Pallas kernels, near_strips(): pl.pallas_call(functools.partial(near_strip_kernel, groups), in_specs=[pl...  1.37 us
  transfers between devices with their start and end apart: 13, of which 9 were waited for; matrix products, arithmetic and copies ran while one was open for 0% of the time, Pallas kernels for 26%

profile of v10, /device:TPU:0, one launch (start us, length us, event | category | flops | bytes accessed | tf_op | source)
XLA Modules:
  0.0 43.0 jit_solution(4668376521981087794)
XLA Ops:
  0.6 0.0 copy-start.5
  0.6 0.6 %waves.1 = (f32[4,2,128,128]{3,2,1,0:T(8,128)S(1)}, f32[4,2,128,128]{3,2,1,0:T(8,128)S(1)}) custom-call(), custom_call_target="tpu_custom_call" | custom-call | flops 1000000000 | bytes 2097152 | tf_op jit(solution)/shard_map/waves/pallas_call | solution.py:86
  1.9 0.0 copy-done.5
  1.9 1.0 %first_strips.1 = (f32[1,2,128,128]{3,2,1,0:T(8,128)S(1)}, bf16[2,256,1024]{2,1,0:T(8,128)(2,1)S(1)}, f32[4,128]{1,0:T(4,128)S(1)}) custom-call(s32[1,1]{1,0:T(1,128)} %bitcast.7.start_ref, f32[2,128,1024]{2,1,0:T(8,128)S(1)} %copy-done.5, f32[4,2,128,128]{3,2,1,0:T(8,128)S(1)} %get-tuple-element.31.base_ref.refs_10_.refs_7_, ...), custom_call_target="tpu_custom_call" | custom-call | flops 1000000000 | bytes 2097152 | tf_op jit(solution)/shard_map/first_strips/pallas_call | solution.py:143
  2.9 0.5 %collective-permute-start = (f32[1,2,128,128]{3,2,1,0:T(8,128)S(1)}, f32[1,2,128,128]{3,2,1,0:T(8,128)S(1)}, u32[]{:S(2)}, u32[]{:S(2)}) collective-permute-start(f32[1,2,128,128]{3,2,1,0:T(8,128)S(1)} %get-tuple-element.35), channel_id=1, source_target_pairs={{0,1},{1,0},{2,3},{3,2},{4,5},{5,4},{6,7},{7,6},{8,9},{9,8},{10,11... | collective-permute-start | bytes 393224 | tf_op jit(solution)/shard_map/ppermute | solution.py:488
  3.4 0.0 copy-start.6
  3.4 0.8 %far_strips.1 = f32[1,2,128,128]{3,2,1,0:T(8,128)S(1)} custom-call(bf16[2,256,1024]{2,1,0:T(8,128)(2,1)S(1)} %get-tuple-element.36.z_ref, f32[4,2,128,128]{3,2,1,0:T(8,128)S(1)} %get-tuple-element.31.base_ref.refs_10_.refs_7_, f32[4,2,128,128]{3,2,1,0:T(8,128)S(1)} %get-tuple-element.32.steps_ref.refs_11_.refs_8_, ...), custom_call_target="tpu_custom_call" | custom-call | flops 1000000000 | bytes 2097152 | tf_op jit(solution)/shard_map/far_strips/pallas_call | solution.py:167
  4.2 0.2 collective-permute-done
  4.4 0.0 copy-start.3
  4.4 0.0 copy-start.4
  4.5 0.0 copy-start
  4.5 0.0 copy-start.1
  4.5 2.9 %collective-permute-start.1 = (f32[1,2,128,128]{3,2,1,0:T(8,128)S(1)}, f32[1,2,128,128]{3,2,1,0:T(8,128)S(1)}, u32[]{:S(2)}, u32[]{:S(2)}) collective-permute-start(f32[1,2,128,128]{3,2,1,0:T(8,128)S(1)} %add.6), channel_id=1, source_target_pairs={{0,2},{1,3},{2,0},{3,1},{4,6},{5,7},{6,4},{7,5},{8,10},{9,11},{10,... | collective-permute-start | bytes 393224 | tf_op jit(solution)/shard_map/ppermute | solution.py:488
  7.4 0.0 copy-done.6
  7.4 1.4 %near_strips.1 = (f32[1,2,128,128]{3,2,1,0:T(8,128)S(1)}, f32[1,2,128,128]{3,2,1,0:T(8,128)S(1)}, f32[8,2,128]{2,1,0:T(2,128)S(1)}, s32[8,1,128]{2,1,0:T(1,128)S(1)}) custom-call(s32[8]{0:T(128)S(1)} %copy-done.6, bf16[2,256,1024]{2,1,0:T(8,128)(2,1)S(1)} %get-tuple-element.36.z_ref, f32[4,2,128,128]{3,2,1,0:T(8,128)S(1)} %get-tuple-element.31.base_ref.refs_10_.refs_7_, ...), custom_call_target="tpu_custom_call" | custom-call | flops 4000000000 | bytes 2097152 | tf_op jit(solution)/shard_map/near_strips/pallas_call | solution.py:195
  8.8 0.1 collective-permute-start.2
  9.5 1.7 %collective-permute-done.1 = f32[1,2,128,128]{3,2,1,0:T(8,128)S(1)} collective-permute-done((f32[1,2,128,128]{3,2,1,0:T(8,128)S(1)}, f32[1,2,128,128]{3,2,1,0:T(8,128)S(1)}, u32[]{:S(2)}, u32[]{:S(2)}) %collective-permute-start.1) | collective-permute-done | bytes 131104 | tf_op jit(solution)/shard_map/ppermute | solution.py:488
  11.3 0.0 collective-permute-done.2.refs_1_
  11.3 0.0 copy-done.3
  11.3 0.0 copy-done.4
  11.3 0.1 pack.1.refs_4_.refs_5_
  11.4 1.8 %collective-permute-start.3 = (f32[328,128]{1,0:T(8,128)S(1)}, f32[328,128]{1,0:T(8,128)S(1)}, u32[]{:S(2)}, u32[]{:S(2)}) collective-permute-start(f32[328,128]{1,0:T(8,128)S(1)} %pack.1.refs_4_.refs_5_), channel_id=1, source_target_pairs={{0,8},{8,16},{16,24},{24,28},{28,20},{20,12},{12,4},{4,0},{1,9},{9... | collective-permute-start | bytes 503816 | tf_op jit(solution)/shard_map/ppermute | solution.py:532
  13.2 0.2 collective-permute-start.5
  13.4 0.0 copy-done
  13.4 0.0 copy-done.1
  13.4 0.8 %gather_step.4.refs_4_.gain_ref = f32[3,128,1024]{2,1,0:T(8,128)S(1)} custom-call(bf16[768,1024]{1,0:T(8,128)(2,1)S(1)} %copy-done, f32[8,2,1024]{2,1,0:T(2,128)S(1)} %copy-done.1, f32[8,2,128]{2,1,0:T(2,128)S(1)} %get-tuple-element.37.refs_2_, s32[8,1,128]{2,1,0:T(1,128)S(1)} %get-tuple-element.38.refs_3_, f32[328,128]{1,0:T(8,128)S(1)} %pack.1.refs_4_.refs_5_), custom_call_target="tpu_custom_call" | custom-call | flops 1000000000 | bytes 4194304 | tf_op jit(solution)/shard_map/gather_step/pallas_call | solution.py:354
  14.2 3.0 %collective-permute-done.3.refs_5_.refs_6_ = f32[328,128]{1,0:T(8,128)S(1)} collective-permute-done((f32[328,128]{1,0:T(8,128)S(1)}, f32[328,128]{1,0:T(8,128)S(1)}, u32[]{:S(2)}, u32[]{:S(2)}) %collective-permute-start.3) | collective-permute-done | bytes 167968 | tf_op jit(solution)/shard_map/ppermute | solution.py:532
  17.2 1.5 %collective-permute-start.4 = (f32[328,128]{1,0:T(8,128)S(1)}, f32[328,128]{1,0:T(8,128)S(1)}, u32[]{:S(2)}, u32[]{:S(2)}) collective-permute-start(f32[328,128]{1,0:T(8,128)S(1)} %collective-permute-done.3.refs_5_.refs_6_), channel_id=1, source_target_pairs={{0,8},{8,16},{16,24},{24,28},{28,20},{20,12},{12,4},{4,0},{1,9},{9... | collective-permute-start | bytes 503816 | tf_op jit(solution)/shard_map/ppermute | solution.py:532
  18.7 0.0 collective-permute-done.5.refs_6_.refs_7_
  18.7 0.5 %collective-permute-start.7 = (f32[328,128]{1,0:T(8,128)S(1)}, f32[328,128]{1,0:T(8,128)S(1)}, u32[]{:S(2)}, u32[]{:S(2)}) collective-permute-start(f32[328,128]{1,0:T(8,128)S(1)} %collective-permute-done.5.refs_6_.refs_7_), channel_id=1, source_target_pairs={{8,0},{16,8},{24,16},{28,24},{20,28},{12,20},{4,12},{0,4},{9,1},{1... | collective-permute-start | bytes 503816 | tf_op jit(solution)/shard_map/ppermute | solution.py:533
  19.2 1.4 %gather_step.5.refs_4_ = f32[3,128,1024]{2,1,0:T(8,128)S(1)} custom-call(bf16[768,1024]{1,0:T(8,128)(2,1)S(1)} %copy-done, f32[8,2,1024]{2,1,0:T(2,128)S(1)} %copy-done.1, f32[8,2,128]{2,1,0:T(2,128)S(1)} %get-tuple-element.37.refs_2_, s32[8,1,128]{2,1,0:T(1,128)S(1)} %get-tuple-element.38.refs_3_, f32[3,128,1024]{2,1,0:T(8,128)S(1)} %gather_step.4.refs_4_.gain_ref, ...), custom_call_target="tpu_custom_call" | custom-call | flops 1000000000 | bytes 4194304 | tf_op jit(solution)/shard_map/gather_step/pallas_call | solution.py:354
  20.6 2.0 %collective-permute-done.4.refs_8_ = f32[328,128]{1,0:T(8,128)S(1)} collective-permute-done((f32[328,128]{1,0:T(8,128)S(1)}, f32[328,128]{1,0:T(8,128)S(1)}, u32[]{:S(2)}, u32[]{:S(2)}) %collective-permute-start.4) | collective-permute-done | bytes 167968 | tf_op jit(solution)/shard_map/ppermute | solution.py:532
  22.6 1.6 %collective-permute-start.6 = (f32[328,128]{1,0:T(8,128)S(1)}, f32[328,128]{1,0:T(8,128)S(1)}, u32[]{:S(2)}, u32[]{:S(2)}) collective-permute-start(f32[328,128]{1,0:T(8,128)S(1)} %collective-permute-done.4.refs_8_), channel_id=1, source_target_pairs={{0,8},{8,16},{16,24},{24,28},{28,20},{20,12},{12,4},{4,0},{1,9},{9... | collective-permute-start | bytes 503816 | tf_op jit(solution)/shard_map/ppermute | solution.py:532
  24.1 0.0 collective-permute-done.7.refs_9_
  24.1 0.5 %collective-permute-start.8 = (f32[328,128]{1,0:T(8,128)S(1)}, f32[328,128]{1,0:T(8,128)S(1)}, u32[]{:S(2)}, u32[]{:S(2)}) collective-permute-start(f32[328,128]{1,0:T(8,128)S(1)} %collective-permute-done.7.refs_9_), channel_id=1, source_target_pairs={{8,0},{16,8},{24,16},{28,24},{20,28},{12,20},{4,12},{0,4},{9,1},{1... | collective-permute-start | bytes 503816 | tf_op jit(solution)/shard_map/ppermute | solution.py:533
  24.6 1.4 %gather_step.6 = (f32[3,128,1024]{2,1,0:T(8,128)S(1)}, bf16[4,2,256,1024]{3,2,1,0:T(8,128)(2,1)S(1)}, f32[128,512]{1,0:T(8,128)S(1)}) custom-call(bf16[768,1024]{1,0:T(8,128)(2,1)S(1)} %copy-done, f32[8,2,1024]{2,1,0:T(2,128)S(1)} %copy-done.1, f32[8,2,128]{2,1,0:T(2,128)S(1)} %get-tuple-element.37.refs_2_, s32[8,1,128]{2,1,0:T(1,128)S(1)} %get-tuple-element.38.refs_3_, ...), custom_call_target="tpu_custom_call" | custom-call | flops 1000000000 | bytes 4194304 | tf_op jit(solution)/shard_map/gather_step/pallas_call | solution.py:354
  26.0 1.9 %collective-permute-done.6.refs_5_ = f32[328,128]{1,0:T(8,128)S(1)} collective-permute-done((f32[328,128]{1,0:T(8,128)S(1)}, f32[328,128]{1,0:T(8,128)S(1)}, u32[]{:S(2)}, u32[]{:S(2)}) %collective-permute-start.6) | collective-permute-done | bytes 167968 | tf_op jit(solution)/shard_map/ppermute | solution.py:532
  27.9 1.6 %collective-permute-start.9 = (f32[328,128]{1,0:T(8,128)S(1)}, f32[328,128]{1,0:T(8,128)S(1)}, u32[]{:S(2)}, u32[]{:S(2)}) collective-permute-start(f32[328,128]{1,0:T(8,128)S(1)} %collective-permute-done.6.refs_5_), channel_id=1, source_target_pairs={{0,8},{8,16},{16,24},{24,28},{28,20},{20,12},{12,4},{4,0},{1,9},{9... | collective-permute-start | bytes 503816 | tf_op jit(solution)/shard_map/ppermute | solution.py:549
  29.5 0.0 collective-permute-done.8.refs_6_
  29.5 0.0 copy-start.2
  29.5 2.9 %gather_step.7 = (f32[3,128,1024]{2,1,0:T(8,128)S(1)}, bf16[4,2,256,1024]{3,2,1,0:T(8,128)(2,1)S(1)}) custom-call(bf16[768,1024]{1,0:T(8,128)(2,1)S(1)} %copy-done, f32[8,2,1024]{2,1,0:T(2,128)S(1)} %copy-done.1, f32[8,2,128]{2,1,0:T(2,128)S(1)} %get-tuple-element.37.refs_2_, s32[8,1,128]{2,1,0:T(1,128)S(1)} %get-tuple-element.38.refs_3_, ...), custom_call_target="tpu_custom_call" | custom-call | flops 1000000000 | bytes 4194304 | tf_op jit(solution)/shard_map/gather_step/pallas_call | solution.py:354
  32.4 0.9 %collective-permute-done.9.refs_6_ = f32[328,128]{1,0:T(8,128)S(1)} collective-permute-done((f32[328,128]{1,0:T(8,128)S(1)}, f32[328,128]{1,0:T(8,128)S(1)}, u32[]{:S(2)}, u32[]{:S(2)}) %collective-permute-start.9) | collective-permute-done | bytes 167968 | tf_op jit(solution)/shard_map/ppermute | solution.py:549
  33.3 0.0 copy-done.2
  33.3 1.7 %back_step.1 = (f32[2,128,128]{2,1,0:T(8,128)S(1)}, f32[2,128,512]{2,1,0:T(8,128)S(1)}) custom-call(bf16[768,1024]{1,0:T(8,128)(2,1)S(1)} %copy-done, f32[8,2,1024]{2,1,0:T(2,128)S(1)} %copy-done.1, f32[8,2,128]{2,1,0:T(2,128)S(1)} %get-tuple-element.37.refs_2_, s32[8,1,128]{2,1,0:T(1,128)S(1)} %get-tuple-element.38.refs_3_, ...), custom_call_target="tpu_custom_call" | custom-call | tf_op jit(solution)/shard_map/back_step/pallas_call | solution.py:395
  35.0 1.6 %collective-permute-start.10 = (f32[2,128,128]{2,1,0:T(8,128)S(1)}, f32[2,128,128]{2,1,0:T(8,128)S(1)}, u32[]{:S(2)}, u32[]{:S(2)}) collective-permute-start(f32[2,128,128]{2,1,0:T(8,128)S(1)} %get-tuple-element.53.refs_0_), channel_id=1, source_target_pairs={{0,2},{1,3},{2,0},{3,1},{4,6},{5,7},{6,4},{7,5},{8,10},{9,11},{10,... | collective-permute-start | bytes 393224 | tf_op jit(solution)/shard_map/ppermute | solution.py:488
  36.6 0.6 %image_step.4.refs_1_ = f32[2,128,1024]{2,1,0:T(8,128)S(1)} custom-call(bf16[4,2,256,1024]{3,2,1,0:T(8,128)(2,1)S(1)} %get-tuple-element.52.e_ref, f32[2,128,128]{2,1,0:T(8,128)S(1)} %get-tuple-element.53.refs_0_), custom_call_target="tpu_custom_call" | custom-call | flops 4000000000 | bytes 4194304 | tf_op jit(solution)/shard_map/image_step/pallas_call | solution.py:475
  37.2 0.1 collective-permute-start.11
  37.3 1.0 %correct_step.1 = f32[1024,128]{1,0:T(8,128)} custom-call(f32[2,128,512]{2,1,0:T(8,128)S(1)} %get-tuple-element.55.sub_ref, f32[3,128,1024]{2,1,0:T(8,128)S(1)} %gather_step.4.refs_4_.gain_ref, f32[128,512]{1,0:T(8,128)S(1)} %get-tuple-element.56.late_ref, f32[8,2,1024]{2,1,0:T(2,128)S(1)} %copy-done.1), custom_call_target="tpu_custom_call" | custom-call | flops 4000000000 | bytes 4194304 | tf_op jit(solution)/shard_map/correct_step/pallas_call | solution.py:423
  38.3 0.3 collective-permute-done.11.refs_0_
  38.6 0.6 %image_step.5.refs_1_ = f32[2,128,1024]{2,1,0:T(8,128)S(1)} custom-call(bf16[4,2,256,1024]{3,2,1,0:T(8,128)(2,1)S(1)} %get-tuple-element.52.e_ref, f32[2,128,128]{2,1,0:T(8,128)S(1)} %collective-permute-done.11.refs_0_, f32[2,128,1024]{2,1,0:T(8,128)S(1)} %image_step.4.refs_1_), custom_call_target="tpu_custom_call" | custom-call | flops 4000000000 | bytes 4194304 | tf_op jit(solution)/shard_map/image_step/pallas_call | solution.py:475
  39.2 0.8 %collective-permute-done.10.refs_0_ = f32[2,128,128]{2,1,0:T(8,128)S(1)} collective-permute-done((f32[2,128,128]{2,1,0:T(8,128)S(1)}, f32[2,128,128]{2,1,0:T(8,128)S(1)}, u32[]{:S(2)}, u32[]{:S(2)}) %collective-permute-start.10) | collective-permute-done | bytes 131104 | tf_op jit(solution)/shard_map/ppermute | solution.py:488
  40.1 0.0 collective-permute-start.12
  40.1 0.6 %image_step.6.refs_1_ = f32[2,128,1024]{2,1,0:T(8,128)S(1)} custom-call(bf16[4,2,256,1024]{3,2,1,0:T(8,128)(2,1)S(1)} %get-tuple-element.52.e_ref, f32[2,128,128]{2,1,0:T(8,128)S(1)} %collective-permute-done.10.refs_0_, f32[2,128,1024]{2,1,0:T(8,128)S(1)} %image_step.5.refs_1_), custom_call_target="tpu_custom_call" | custom-call | flops 4000000000 | bytes 4194304 | tf_op jit(solution)/shard_map/image_step/pallas_call | solution.py:475
  40.7 0.7 %collective-permute-done.12.refs_0_ = f32[2,128,128]{2,1,0:T(8,128)S(1)} collective-permute-done((f32[2,128,128]{2,1,0:T(8,128)S(1)}, f32[2,128,128]{2,1,0:T(8,128)S(1)}, u32[]{:S(2)}, u32[]{:S(2)}) %collective-permute-start.12) | collective-permute-done | bytes 131104 | tf_op jit(solution)/shard_map/ppermute | solution.py:488
  41.4 1.4 %image_step.7 = f32[2,128,1024]{2,1,0:T(8,128)} custom-call(bf16[4,2,256,1024]{3,2,1,0:T(8,128)(2,1)S(1)} %get-tuple-element.52.e_ref, f32[2,128,128]{2,1,0:T(8,128)S(1)} %collective-permute-done.12.refs_0_, f32[2,128,1024]{2,1,0:T(8,128)S(1)} %image_step.6.refs_1_), custom_call_target="tpu_custom_call" | custom-call | flops 4000000000 | bytes 4194304 | tf_op jit(solution)/shard_map/image_step/pallas_call | solution.py:475
  (2 shorter events, 0.0 us)
Async XLA Ops:
  0.6 1.2 %copy-start.5 = (f32[2,128,1024]{2,1,0:T(8,128)S(1)}, f32[2,128,1024]{2,1,0:T(8,128)}, u32[]{:S(2)}) copy-start(f32[2,128,1024]{2,1,0:T(8,128)} %x_ref.1) | copy-start | bytes 3145732
  2.9 1.5 %collective-permute-start = (f32[1,2,128,128]{3,2,1,0:T(8,128)S(1)}, f32[1,2,128,128]{3,2,1,0:T(8,128)S(1)}, u32[]{:S(2)}, u32[]{:S(2)}) collective-permute-start(f32[1,2,128,128]{3,2,1,0:T(8,128)S(1)} %get-tuple-element.35), channel_id=1, source_target_pairs={{0,1},{1,0},{2,3},{3,2},{4,5},{5,4},{6,7},{7,6},{8,9},{9,8},{10,11... | collective-permute-start | bytes 393224 | tf_op jit(solution)/shard_map/ppermute | solution.py:488
  3.4 4.0 %copy-start.6 = (s32[8]{0:T(128)S(1)}, s32[8]{0:T(128)}, u32[]{:S(2)}) copy-start(s32[8]{0:T(128)} %starts_ref.1) | copy-start | bytes 100
  4.4 6.8 %copy-start.3 = (f32[1,64,128]{2,1,0:T(8,128)S(1)}, f32[1,64,128]{2,1,0:T(8,128)}, u32[]{:S(2)}) copy-start(f32[1,64,128]{2,1,0:T(8,128)} %refs_2_.1) | copy-start | bytes 98308
  4.4 6.8 %copy-start.4 = (s32[1,64]{1,0:T(1,128)S(1)}, s32[1,64]{1,0:T(1,128)}, u32[]{:S(2)}) copy-start(s32[1,64]{1,0:T(1,128)} %refs_3_.1) | copy-start | bytes 772
  4.5 8.9 %copy-start = (bf16[768,1024]{1,0:T(8,128)(2,1)S(1)}, bf16[768,1024]{1,0:T(8,128)(2,1)}, u32[]{:S(2)}) copy-start(bf16[768,1024]{1,0:T(8,128)(2,1)} %constant.7.clone.refs_0_) | copy-start | bytes 4718596
  4.5 8.9 %copy-start.1 = (f32[8,2,1024]{2,1,0:T(2,128)S(1)}, f32[8,2,1024]{2,1,0:T(2,128)}, u32[]{:S(2)}) copy-start(f32[8,2,1024]{2,1,0:T(2,128)} %constant.8.clone.refs_1_.roots_ref) | copy-start | bytes 196612
  4.5 6.8 %collective-permute-start.1 = (f32[1,2,128,128]{3,2,1,0:T(8,128)S(1)}, f32[1,2,128,128]{3,2,1,0:T(8,128)S(1)}, u32[]{:S(2)}, u32[]{:S(2)}) collective-permute-start(f32[1,2,128,128]{3,2,1,0:T(8,128)S(1)} %add.6), channel_id=1, source_target_pairs={{0,2},{1,3},{2,0},{3,1},{4,6},{5,7},{6,4},{7,5},{8,10},{9,11},{10,... | collective-permute-start | bytes 393224 | tf_op jit(solution)/shard_map/ppermute | solution.py:488
  8.8 2.5 %collective-permute-start.2 = (f32[1,2,128,128]{3,2,1,0:T(8,128)S(1)}, f32[1,2,128,128]{3,2,1,0:T(8,128)S(1)}, u32[]{:S(2)}, u32[]{:S(2)}) collective-permute-start(f32[1,2,128,128]{3,2,1,0:T(8,128)S(1)} %get-tuple-element.41), channel_id=1, source_target_pairs={{0,1},{1,0},{2,3},{3,2},{4,5},{5,4},{6,7},{7,6},{8,9},{9,8},{10,11... | collective-permute-start | bytes 393224 | tf_op jit(solution)/shard_map/ppermute | solution.py:488
  11.4 5.8 %collective-permute-start.3 = (f32[328,128]{1,0:T(8,128)S(1)}, f32[328,128]{1,0:T(8,128)S(1)}, u32[]{:S(2)}, u32[]{:S(2)}) collective-permute-start(f32[328,128]{1,0:T(8,128)S(1)} %pack.1.refs_4_.refs_5_), channel_id=1, source_target_pairs={{0,8},{8,16},{16,24},{24,28},{28,20},{20,12},{12,4},{4,0},{1,9},{9... | collective-permute-start | bytes 503816 | tf_op jit(solution)/shard_map/ppermute | solution.py:532
  13.2 5.5 %collective-permute-start.5 = (f32[328,128]{1,0:T(8,128)S(1)}, f32[328,128]{1,0:T(8,128)S(1)}, u32[]{:S(2)}, u32[]{:S(2)}) collective-permute-start(f32[328,128]{1,0:T(8,128)S(1)} %pack.1.refs_4_.refs_5_), channel_id=1, source_target_pairs={{8,0},{16,8},{24,16},{28,24},{20,28},{12,20},{4,12},{0,4},{9,1},{1... | collective-permute-start | bytes 503816 | tf_op jit(solution)/shard_map/ppermute | solution.py:533
  17.2 5.4 %collective-permute-start.4 = (f32[328,128]{1,0:T(8,128)S(1)}, f32[328,128]{1,0:T(8,128)S(1)}, u32[]{:S(2)}, u32[]{:S(2)}) collective-permute-start(f32[328,128]{1,0:T(8,128)S(1)} %collective-permute-done.3.refs_5_.refs_6_), channel_id=1, source_target_pairs={{0,8},{8,16},{16,24},{24,28},{28,20},{20,12},{12,4},{4,0},{1,9},{9... | collective-permute-start | bytes 503816 | tf_op jit(solution)/shard_map/ppermute | solution.py:532
  18.7 5.5 %collective-permute-start.7 = (f32[328,128]{1,0:T(8,128)S(1)}, f32[328,128]{1,0:T(8,128)S(1)}, u32[]{:S(2)}, u32[]{:S(2)}) collective-permute-start(f32[328,128]{1,0:T(8,128)S(1)} %collective-permute-done.5.refs_6_.refs_7_), channel_id=1, source_target_pairs={{8,0},{16,8},{24,16},{28,24},{20,28},{12,20},{4,12},{0,4},{9,1},{1... | collective-permute-start | bytes 503816 | tf_op jit(solution)/shard_map/ppermute | solution.py:533
  22.6 5.4 %collective-permute-start.6 = (f32[328,128]{1,0:T(8,128)S(1)}, f32[328,128]{1,0:T(8,128)S(1)}, u32[]{:S(2)}, u32[]{:S(2)}) collective-permute-start(f32[328,128]{1,0:T(8,128)S(1)} %collective-permute-done.4.refs_8_), channel_id=1, source_target_pairs={{0,8},{8,16},{16,24},{24,28},{28,20},{20,12},{12,4},{4,0},{1,9},{9... | collective-permute-start | bytes 503816 | tf_op jit(solution)/shard_map/ppermute | solution.py:532
  24.1 5.4 %collective-permute-start.8 = (f32[328,128]{1,0:T(8,128)S(1)}, f32[328,128]{1,0:T(8,128)S(1)}, u32[]{:S(2)}, u32[]{:S(2)}) collective-permute-start(f32[328,128]{1,0:T(8,128)S(1)} %collective-permute-done.7.refs_9_), channel_id=1, source_target_pairs={{8,0},{16,8},{24,16},{28,24},{20,28},{12,20},{4,12},{0,4},{9,1},{1... | collective-permute-start | bytes 503816 | tf_op jit(solution)/shard_map/ppermute | solution.py:533
  27.9 5.4 %collective-permute-start.9 = (f32[328,128]{1,0:T(8,128)S(1)}, f32[328,128]{1,0:T(8,128)S(1)}, u32[]{:S(2)}, u32[]{:S(2)}) collective-permute-start(f32[328,128]{1,0:T(8,128)S(1)} %collective-permute-done.6.refs_5_), channel_id=1, source_target_pairs={{0,8},{8,16},{16,24},{24,28},{28,20},{20,12},{12,4},{4,0},{1,9},{9... | collective-permute-start | bytes 503816 | tf_op jit(solution)/shard_map/ppermute | solution.py:549
  29.5 3.8 %copy-start.2 = (bf16[1024,512]{1,0:T(8,128)(2,1)S(1)}, bf16[1024,512]{1,0:T(8,128)(2,1)}, u32[]{:S(2)}) copy-start(bf16[1024,512]{1,0:T(8,128)(2,1)} %constant.6.clone.refs_4_) | copy-start | bytes 3145732
  35.0 5.0 %collective-permute-start.10 = (f32[2,128,128]{2,1,0:T(8,128)S(1)}, f32[2,128,128]{2,1,0:T(8,128)S(1)}, u32[]{:S(2)}, u32[]{:S(2)}) collective-permute-start(f32[2,128,128]{2,1,0:T(8,128)S(1)} %get-tuple-element.53.refs_0_), channel_id=1, source_target_pairs={{0,2},{1,3},{2,0},{3,1},{4,6},{5,7},{6,4},{7,5},{8,10},{9,11},{10,... | collective-permute-start | bytes 393224 | tf_op jit(solution)/shard_map/ppermute | solution.py:488
  37.2 1.4 %collective-permute-start.11 = (f32[2,128,128]{2,1,0:T(8,128)S(1)}, f32[2,128,128]{2,1,0:T(8,128)S(1)}, u32[]{:S(2)}, u32[]{:S(2)}) collective-permute-start(f32[2,128,128]{2,1,0:T(8,128)S(1)} %get-tuple-element.53.refs_0_), channel_id=1, source_target_pairs={{0,1},{1,0},{2,3},{3,2},{4,5},{5,4},{6,7},{7,6},{8,9},{9,8},{10,11... | collective-permute-start | bytes 393224 | tf_op jit(solution)/shard_map/ppermute | solution.py:488
  40.1 1.3 %collective-permute-start.12 = (f32[2,128,128]{2,1,0:T(8,128)S(1)}, f32[2,128,128]{2,1,0:T(8,128)S(1)}, u32[]{:S(2)}, u32[]{:S(2)}) collective-permute-start(f32[2,128,128]{2,1,0:T(8,128)S(1)} %collective-permute-done.10.refs_0_), channel_id=1, source_target_pairs={{0,1},{1,0},{2,3},{3,2},{4,5},{5,4},{6,7},{7,6},{8,9},{9,8},{10,11... | collective-permute-start | bytes 393224 | tf_op jit(solution)/shard_map/ppermute | solution.py:488

commit v11 on v9

--- a/solution.py
+++ b/solution.py
@@ -242,19 +242,22 @@
         high, low = halves(jnp.concatenate([jnp.concatenate([re, im], 1), jnp.concatenate([im, -re], 1)]))
         self.left = jnp.concatenate([high, low, high], 1)
 
-        width = message.shape[1]
-        flat = jnp.concatenate([rest, jnp.zeros((width - rest.shape[0], width), F32)])
-        turned = jnp.transpose(flat)
-        self.weight = jnp.concatenate(halves(turned[:count, :MAXB]), 1)
-        row = turned[:MAXB, MAXB : MAXB + 1].astype(jnp.int32)
-        self.away = away_ref[r][0:1, 0:1]
-        self.place = jnp.where(row < 0, -1, (row - self.away) & (rows_total - 1))
+        self.rest, self.away, self.place = rest, away_ref[r][0:1, 0:1], None
         self.turn = lax.rem(r - own + rows_total // height, rows_total // height)
         self.refs, self.count, self.rows_total = (b_ref, roots_ref), count, rows_total
+
+    def prepare(self):
+        width = self.rest.shape[1]
+        turned = jnp.transpose(jnp.concatenate([self.rest, jnp.zeros((width - self.rest.shape[0], width), F32)]))
+        self.weight = jnp.concatenate(halves(turned[: self.count, :MAXB]), 1)
+        row = turned[:MAXB, MAXB : MAXB + 1].astype(jnp.int32)
+        self.place = jnp.where(row < 0, -1, (row - self.away) & (self.rows_total - 1))
 
     def chunk(self, begin, size):
         b_ref, roots_ref = self.refs
         part = lax.dot_general(self.left, b_ref[:, begin : begin + size], NN, preferred_element_type=F32)
+        if self.place is None:
+            self.prepare()
         pc, ps = roots_ref[self.turn, 0:1, begin : begin + size], roots_ref[self.turn, 1:2, begin : begin + size]
         re, im = part[: self.count], part[self.count :]
         freq = begin + lanes(size)

time: 43.1 us -> 43.1 us (level)
  no operation moved by 1% of the time
where the time goes in v11:
time: 43.1 us; the launch traced here: 43 us
  Pallas kernels  16.1 us (37%)
  starting transfers between devices  12.9 us (30%)
  waiting for transfers between devices  11.6 us (27%)
  between operations  2.29 us (5%)
    ppermute x4, waiting for transfers between devices, per_device(): up = lax.ppermute(up, 'frow', ahead)  7.82 us
    ppermute x4, starting transfers between devices, per_device(): up = lax.ppermute(up, 'frow', ahead)  6.41 us
    pallas_call x4, Pallas kernels, gather_step(): pl.pallas_call(functools.partial(gather_kernel, kind, steps, rows_total /...  6.37 us
    ppermute x6, starting transfers between devices, swap(): lax.ppermute(value, axis, [(i, i ^ bit) for i in range(lax.axis_size(axis...  5.21 us
    ppermute x6, waiting for transfers between devices, swap(): lax.ppermute(value, axis, [(i, i ^ bit) for i in range(lax.axis_size(axis...  3.8 us
    pallas_call x4, Pallas kernels, image_step(): pl.pallas_call(functools.partial(image_kernel, tuple(gs), first, last), i...  3.17 us
    pallas_call x1, Pallas kernels, back_step(): pl.pallas_call(functools.partial(back_kernel, rows_total // height, heigh...  1.72 us
    pallas_call x1, Pallas kernels, near_strips(): pl.pallas_call(functools.partial(near_strip_kernel, groups), in_specs=[pl...  1.37 us
  transfers between devices with their start and end apart: 13, of which 9 were waited for; matrix products, arithmetic and copies ran while one was open for 0% of the time, Pallas kernels for 26%

profile of v11, /device:TPU:0, one launch (start us, length us, event | category | flops | bytes accessed | tf_op | source)
XLA Modules:
  0.0 43.0 jit_solution(9519053748980253538)
XLA Ops:
  0.6 0.0 copy-start.5
  0.6 0.6 %waves.1 = (f32[4,2,128,128]{3,2,1,0:T(8,128)S(1)}, f32[4,2,128,128]{3,2,1,0:T(8,128)S(1)}) custom-call(), custom_call_target="tpu_custom_call" | custom-call | flops 1000000000 | bytes 2097152 | tf_op jit(solution)/shard_map/waves/pallas_call | solution.py:86
  1.9 0.0 copy-done.5
  1.9 1.0 %first_strips.1 = (f32[1,2,128,128]{3,2,1,0:T(8,128)S(1)}, bf16[2,256,1024]{2,1,0:T(8,128)(2,1)S(1)}, f32[4,128]{1,0:T(4,128)S(1)}) custom-call(s32[1,1]{1,0:T(1,128)} %bitcast.7.start_ref, f32[2,128,1024]{2,1,0:T(8,128)S(1)} %copy-done.5, f32[4,2,128,128]{3,2,1,0:T(8,128)S(1)} %get-tuple-element.31.base_ref.refs_10_.refs_7_, ...), custom_call_target="tpu_custom_call" | custom-call | flops 1000000000 | bytes 2097152 | tf_op jit(solution)/shard_map/first_strips/pallas_call | solution.py:143
  2.9 0.5 %collective-permute-start = (f32[1,2,128,128]{3,2,1,0:T(8,128)S(1)}, f32[1,2,128,128]{3,2,1,0:T(8,128)S(1)}, u32[]{:S(2)}, u32[]{:S(2)}) collective-permute-start(f32[1,2,128,128]{3,2,1,0:T(8,128)S(1)} %get-tuple-element.35), channel_id=1, source_target_pairs={{0,1},{1,0},{2,3},{3,2},{4,5},{5,4},{6,7},{7,6},{8,9},{9,8},{10,11... | collective-permute-start | bytes 393224 | tf_op jit(solution)/shard_map/ppermute | solution.py:491
  3.4 0.0 copy-start.6
  3.4 0.8 %far_strips.1 = f32[1,2,128,128]{3,2,1,0:T(8,128)S(1)} custom-call(bf16[2,256,1024]{2,1,0:T(8,128)(2,1)S(1)} %get-tuple-element.36.z_ref, f32[4,2,128,128]{3,2,1,0:T(8,128)S(1)} %get-tuple-element.31.base_ref.refs_10_.refs_7_, f32[4,2,128,128]{3,2,1,0:T(8,128)S(1)} %get-tuple-element.32.steps_ref.refs_11_.refs_8_, ...), custom_call_target="tpu_custom_call" | custom-call | flops 1000000000 | bytes 2097152 | tf_op jit(solution)/shard_map/far_strips/pallas_call | solution.py:167
  4.2 0.2 collective-permute-done
  4.4 0.0 copy-start.3
  4.4 0.0 copy-start.4
  4.5 0.0 copy-start
  4.5 0.0 copy-start.1
  4.5 2.9 %collective-permute-start.1 = (f32[1,2,128,128]{3,2,1,0:T(8,128)S(1)}, f32[1,2,128,128]{3,2,1,0:T(8,128)S(1)}, u32[]{:S(2)}, u32[]{:S(2)}) collective-permute-start(f32[1,2,128,128]{3,2,1,0:T(8,128)S(1)} %add.6), channel_id=1, source_target_pairs={{0,2},{1,3},{2,0},{3,1},{4,6},{5,7},{6,4},{7,5},{8,10},{9,11},{10,... | collective-permute-start | bytes 393224 | tf_op jit(solution)/shard_map/ppermute | solution.py:491
  7.4 0.0 copy-done.6
  7.4 1.4 %near_strips.1 = (f32[1,2,128,128]{3,2,1,0:T(8,128)S(1)}, f32[1,2,128,128]{3,2,1,0:T(8,128)S(1)}, f32[8,2,128]{2,1,0:T(2,128)S(1)}, s32[8,1,128]{2,1,0:T(1,128)S(1)}) custom-call(s32[8]{0:T(128)S(1)} %copy-done.6, bf16[2,256,1024]{2,1,0:T(8,128)(2,1)S(1)} %get-tuple-element.36.z_ref, f32[4,2,128,128]{3,2,1,0:T(8,128)S(1)} %get-tuple-element.31.base_ref.refs_10_.refs_7_, ...), custom_call_target="tpu_custom_call" | custom-call | flops 4000000000 | bytes 2097152 | tf_op jit(solution)/shard_map/near_strips/pallas_call | solution.py:195
  8.8 0.1 collective-permute-start.2
  9.5 1.7 %collective-permute-done.1 = f32[1,2,128,128]{3,2,1,0:T(8,128)S(1)} collective-permute-done((f32[1,2,128,128]{3,2,1,0:T(8,128)S(1)}, f32[1,2,128,128]{3,2,1,0:T(8,128)S(1)}, u32[]{:S(2)}, u32[]{:S(2)}) %collective-permute-start.1) | collective-permute-done | bytes 131104 | tf_op jit(solution)/shard_map/ppermute | solution.py:491
  11.3 0.0 collective-permute-done.2.refs_1_
  11.3 0.0 copy-done.3
  11.3 0.0 copy-done.4
  11.3 0.1 pack.1.refs_4_.refs_5_
  11.4 1.8 %collective-permute-start.3 = (f32[328,128]{1,0:T(8,128)S(1)}, f32[328,128]{1,0:T(8,128)S(1)}, u32[]{:S(2)}, u32[]{:S(2)}) collective-permute-start(f32[328,128]{1,0:T(8,128)S(1)} %pack.1.refs_4_.refs_5_), channel_id=1, source_target_pairs={{0,8},{8,16},{16,24},{24,28},{28,20},{20,12},{12,4},{4,0},{1,9},{9... | collective-permute-start | bytes 503816 | tf_op jit(solution)/shard_map/ppermute | solution.py:535
  13.2 0.2 collective-permute-start.5
  13.4 0.0 copy-done
  13.4 0.0 copy-done.1
  13.4 0.8 %gather_step.4.refs_4_.gain_ref = f32[3,128,1024]{2,1,0:T(8,128)S(1)} custom-call(bf16[768,1024]{1,0:T(8,128)(2,1)S(1)} %copy-done, f32[8,2,1024]{2,1,0:T(2,128)S(1)} %copy-done.1, f32[8,2,128]{2,1,0:T(2,128)S(1)} %get-tuple-element.37.refs_2_, s32[8,1,128]{2,1,0:T(1,128)S(1)} %get-tuple-element.38.refs_3_, f32[328,128]{1,0:T(8,128)S(1)} %pack.1.refs_4_.refs_5_), custom_call_target="tpu_custom_call" | custom-call | flops 1000000000 | bytes 4194304 | tf_op jit(solution)/shard_map/gather_step/pallas_call | solution.py:357
  14.2 3.0 %collective-permute-done.3.refs_5_.refs_6_ = f32[328,128]{1,0:T(8,128)S(1)} collective-permute-done((f32[328,128]{1,0:T(8,128)S(1)}, f32[328,128]{1,0:T(8,128)S(1)}, u32[]{:S(2)}, u32[]{:S(2)}) %collective-permute-start.3) | collective-permute-done | bytes 167968 | tf_op jit(solution)/shard_map/ppermute | solution.py:535
  17.2 1.5 %collective-permute-start.4 = (f32[328,128]{1,0:T(8,128)S(1)}, f32[328,128]{1,0:T(8,128)S(1)}, u32[]{:S(2)}, u32[]{:S(2)}) collective-permute-start(f32[328,128]{1,0:T(8,128)S(1)} %collective-permute-done.3.refs_5_.refs_6_), channel_id=1, source_target_pairs={{0,8},{8,16},{16,24},{24,28},{28,20},{20,12},{12,4},{4,0},{1,9},{9... | collective-permute-start | bytes 503816 | tf_op jit(solution)/shard_map/ppermute | solution.py:535
  18.7 0.0 collective-permute-done.5.refs_6_.refs_7_
  18.7 0.5 %collective-permute-start.7 = (f32[328,128]{1,0:T(8,128)S(1)}, f32[328,128]{1,0:T(8,128)S(1)}, u32[]{:S(2)}, u32[]{:S(2)}) collective-permute-start(f32[328,128]{1,0:T(8,128)S(1)} %collective-permute-done.5.refs_6_.refs_7_), channel_id=1, source_target_pairs={{8,0},{16,8},{24,16},{28,24},{20,28},{12,20},{4,12},{0,4},{9,1},{1... | collective-permute-start | bytes 503816 | tf_op jit(solution)/shard_map/ppermute | solution.py:536
  19.2 1.4 %gather_step.5.refs_4_ = f32[3,128,1024]{2,1,0:T(8,128)S(1)} custom-call(bf16[768,1024]{1,0:T(8,128)(2,1)S(1)} %copy-done, f32[8,2,1024]{2,1,0:T(2,128)S(1)} %copy-done.1, f32[8,2,128]{2,1,0:T(2,128)S(1)} %get-tuple-element.37.refs_2_, s32[8,1,128]{2,1,0:T(1,128)S(1)} %get-tuple-element.38.refs_3_, f32[3,128,1024]{2,1,0:T(8,128)S(1)} %gather_step.4.refs_4_.gain_ref, ...), custom_call_target="tpu_custom_call" | custom-call | flops 1000000000 | bytes 4194304 | tf_op jit(solution)/shard_map/gather_step/pallas_call | solution.py:357
  20.6 2.0 %collective-permute-done.4.refs_8_ = f32[328,128]{1,0:T(8,128)S(1)} collective-permute-done((f32[328,128]{1,0:T(8,128)S(1)}, f32[328,128]{1,0:T(8,128)S(1)}, u32[]{:S(2)}, u32[]{:S(2)}) %collective-permute-start.4) | collective-permute-done | bytes 167968 | tf_op jit(solution)/shard_map/ppermute | solution.py:535
  22.6 1.6 %collective-permute-start.6 = (f32[328,128]{1,0:T(8,128)S(1)}, f32[328,128]{1,0:T(8,128)S(1)}, u32[]{:S(2)}, u32[]{:S(2)}) collective-permute-start(f32[328,128]{1,0:T(8,128)S(1)} %collective-permute-done.4.refs_8_), channel_id=1, source_target_pairs={{0,8},{8,16},{16,24},{24,28},{28,20},{20,12},{12,4},{4,0},{1,9},{9... | collective-permute-start | bytes 503816 | tf_op jit(solution)/shard_map/ppermute | solution.py:535
  24.1 0.0 collective-permute-done.7.refs_9_
  24.1 0.5 %collective-permute-start.8 = (f32[328,128]{1,0:T(8,128)S(1)}, f32[328,128]{1,0:T(8,128)S(1)}, u32[]{:S(2)}, u32[]{:S(2)}) collective-permute-start(f32[328,128]{1,0:T(8,128)S(1)} %collective-permute-done.7.refs_9_), channel_id=1, source_target_pairs={{8,0},{16,8},{24,16},{28,24},{20,28},{12,20},{4,12},{0,4},{9,1},{1... | collective-permute-start | bytes 503816 | tf_op jit(solution)/shard_map/ppermute | solution.py:536
  24.6 1.4 %gather_step.6 = (f32[3,128,1024]{2,1,0:T(8,128)S(1)}, bf16[4,2,256,1024]{3,2,1,0:T(8,128)(2,1)S(1)}, f32[128,512]{1,0:T(8,128)S(1)}) custom-call(bf16[768,1024]{1,0:T(8,128)(2,1)S(1)} %copy-done, f32[8,2,1024]{2,1,0:T(2,128)S(1)} %copy-done.1, f32[8,2,128]{2,1,0:T(2,128)S(1)} %get-tuple-element.37.refs_2_, s32[8,1,128]{2,1,0:T(1,128)S(1)} %get-tuple-element.38.refs_3_, ...), custom_call_target="tpu_custom_call" | custom-call | flops 1000000000 | bytes 4194304 | tf_op jit(solution)/shard_map/gather_step/pallas_call | solution.py:357
  26.0 1.9 %collective-permute-done.6.refs_5_ = f32[328,128]{1,0:T(8,128)S(1)} collective-permute-done((f32[328,128]{1,0:T(8,128)S(1)}, f32[328,128]{1,0:T(8,128)S(1)}, u32[]{:S(2)}, u32[]{:S(2)}) %collective-permute-start.6) | collective-permute-done | bytes 167968 | tf_op jit(solution)/shard_map/ppermute | solution.py:535
  27.9 1.6 %collective-permute-start.9 = (f32[328,128]{1,0:T(8,128)S(1)}, f32[328,128]{1,0:T(8,128)S(1)}, u32[]{:S(2)}, u32[]{:S(2)}) collective-permute-start(f32[328,128]{1,0:T(8,128)S(1)} %collective-permute-done.6.refs_5_), channel_id=1, source_target_pairs={{0,8},{8,16},{16,24},{24,28},{28,20},{20,12},{12,4},{4,0},{1,9},{9... | collective-permute-start | bytes 503816 | tf_op jit(solution)/shard_map/ppermute | solution.py:552
  29.5 0.0 collective-permute-done.8.refs_6_
  29.5 0.0 copy-start.2
  29.5 2.9 %gather_step.7 = (f32[3,128,1024]{2,1,0:T(8,128)S(1)}, bf16[4,2,256,1024]{3,2,1,0:T(8,128)(2,1)S(1)}) custom-call(bf16[768,1024]{1,0:T(8,128)(2,1)S(1)} %copy-done, f32[8,2,1024]{2,1,0:T(2,128)S(1)} %copy-done.1, f32[8,2,128]{2,1,0:T(2,128)S(1)} %get-tuple-element.37.refs_2_, s32[8,1,128]{2,1,0:T(1,128)S(1)} %get-tuple-element.38.refs_3_, ...), custom_call_target="tpu_custom_call" | custom-call | flops 1000000000 | bytes 4194304 | tf_op jit(solution)/shard_map/gather_step/pallas_call | solution.py:357
  32.4 0.9 %collective-permute-done.9.refs_6_ = f32[328,128]{1,0:T(8,128)S(1)} collective-permute-done((f32[328,128]{1,0:T(8,128)S(1)}, f32[328,128]{1,0:T(8,128)S(1)}, u32[]{:S(2)}, u32[]{:S(2)}) %collective-permute-start.9) | collective-permute-done | bytes 167968 | tf_op jit(solution)/shard_map/ppermute | solution.py:552
  33.3 0.0 copy-done.2
  33.3 1.7 %back_step.1 = (f32[2,128,128]{2,1,0:T(8,128)S(1)}, f32[2,128,512]{2,1,0:T(8,128)S(1)}) custom-call(bf16[768,1024]{1,0:T(8,128)(2,1)S(1)} %copy-done, f32[8,2,1024]{2,1,0:T(2,128)S(1)} %copy-done.1, f32[8,2,128]{2,1,0:T(2,128)S(1)} %get-tuple-element.37.refs_2_, s32[8,1,128]{2,1,0:T(1,128)S(1)} %get-tuple-element.38.refs_3_, ...), custom_call_target="tpu_custom_call" | custom-call | tf_op jit(solution)/shard_map/back_step/pallas_call | solution.py:398
  35.0 1.6 %collective-permute-start.10 = (f32[2,128,128]{2,1,0:T(8,128)S(1)}, f32[2,128,128]{2,1,0:T(8,128)S(1)}, u32[]{:S(2)}, u32[]{:S(2)}) collective-permute-start(f32[2,128,128]{2,1,0:T(8,128)S(1)} %get-tuple-element.53.refs_0_), channel_id=1, source_target_pairs={{0,2},{1,3},{2,0},{3,1},{4,6},{5,7},{6,4},{7,5},{8,10},{9,11},{10,... | collective-permute-start | bytes 393224 | tf_op jit(solution)/shard_map/ppermute | solution.py:491
  36.6 0.6 %image_step.4.refs_1_ = f32[2,128,1024]{2,1,0:T(8,128)S(1)} custom-call(bf16[4,2,256,1024]{3,2,1,0:T(8,128)(2,1)S(1)} %get-tuple-element.52.e_ref, f32[2,128,128]{2,1,0:T(8,128)S(1)} %get-tuple-element.53.refs_0_), custom_call_target="tpu_custom_call" | custom-call | flops 4000000000 | bytes 4194304 | tf_op jit(solution)/shard_map/image_step/pallas_call | solution.py:478
  37.2 0.1 collective-permute-start.11
  37.3 1.0 %correct_step.1 = f32[1024,128]{1,0:T(8,128)} custom-call(f32[2,128,512]{2,1,0:T(8,128)S(1)} %get-tuple-element.55.sub_ref, f32[3,128,1024]{2,1,0:T(8,128)S(1)} %gather_step.4.refs_4_.gain_ref, f32[128,512]{1,0:T(8,128)S(1)} %get-tuple-element.56.late_ref, f32[8,2,1024]{2,1,0:T(2,128)S(1)} %copy-done.1), custom_call_target="tpu_custom_call" | custom-call | flops 4000000000 | bytes 4194304 | tf_op jit(solution)/shard_map/correct_step/pallas_call | solution.py:426
  38.3 0.3 collective-permute-done.11.refs_0_
  38.6 0.6 %image_step.5.refs_1_ = f32[2,128,1024]{2,1,0:T(8,128)S(1)} custom-call(bf16[4,2,256,1024]{3,2,1,0:T(8,128)(2,1)S(1)} %get-tuple-element.52.e_ref, f32[2,128,128]{2,1,0:T(8,128)S(1)} %collective-permute-done.11.refs_0_, f32[2,128,1024]{2,1,0:T(8,128)S(1)} %image_step.4.refs_1_), custom_call_target="tpu_custom_call" | custom-call | flops 4000000000 | bytes 4194304 | tf_op jit(solution)/shard_map/image_step/pallas_call | solution.py:478
  39.2 0.8 %collective-permute-done.10.refs_0_ = f32[2,128,128]{2,1,0:T(8,128)S(1)} collective-permute-done((f32[2,128,128]{2,1,0:T(8,128)S(1)}, f32[2,128,128]{2,1,0:T(8,128)S(1)}, u32[]{:S(2)}, u32[]{:S(2)}) %collective-permute-start.10) | collective-permute-done | bytes 131104 | tf_op jit(solution)/shard_map/ppermute | solution.py:491
  40.1 0.0 collective-permute-start.12
  40.1 0.6 %image_step.6.refs_1_ = f32[2,128,1024]{2,1,0:T(8,128)S(1)} custom-call(bf16[4,2,256,1024]{3,2,1,0:T(8,128)(2,1)S(1)} %get-tuple-element.52.e_ref, f32[2,128,128]{2,1,0:T(8,128)S(1)} %collective-permute-done.10.refs_0_, f32[2,128,1024]{2,1,0:T(8,128)S(1)} %image_step.5.refs_1_), custom_call_target="tpu_custom_call" | custom-call | flops 4000000000 | bytes 4194304 | tf_op jit(solution)/shard_map/image_step/pallas_call | solution.py:478
  40.7 0.7 %collective-permute-done.12.refs_0_ = f32[2,128,128]{2,1,0:T(8,128)S(1)} collective-permute-done((f32[2,128,128]{2,1,0:T(8,128)S(1)}, f32[2,128,128]{2,1,0:T(8,128)S(1)}, u32[]{:S(2)}, u32[]{:S(2)}) %collective-permute-start.12) | collective-permute-done | bytes 131104 | tf_op jit(solution)/shard_map/ppermute | solution.py:491
  41.4 1.4 %image_step.7 = f32[2,128,1024]{2,1,0:T(8,128)} custom-call(bf16[4,2,256,1024]{3,2,1,0:T(8,128)(2,1)S(1)} %get-tuple-element.52.e_ref, f32[2,128,128]{2,1,0:T(8,128)S(1)} %collective-permute-done.12.refs_0_, f32[2,128,1024]{2,1,0:T(8,128)S(1)} %image_step.6.refs_1_), custom_call_target="tpu_custom_call" | custom-call | flops 4000000000 | bytes 4194304 | tf_op jit(solution)/shard_map/image_step/pallas_call | solution.py:478
  (2 shorter events, 0.0 us)
Async XLA Ops:
  0.6 1.2 %copy-start.5 = (f32[2,128,1024]{2,1,0:T(8,128)S(1)}, f32[2,128,1024]{2,1,0:T(8,128)}, u32[]{:S(2)}) copy-start(f32[2,128,1024]{2,1,0:T(8,128)} %x_ref.1) | copy-start | bytes 3145732
  2.9 1.5 %collective-permute-start = (f32[1,2,128,128]{3,2,1,0:T(8,128)S(1)}, f32[1,2,128,128]{3,2,1,0:T(8,128)S(1)}, u32[]{:S(2)}, u32[]{:S(2)}) collective-permute-start(f32[1,2,128,128]{3,2,1,0:T(8,128)S(1)} %get-tuple-element.35), channel_id=1, source_target_pairs={{0,1},{1,0},{2,3},{3,2},{4,5},{5,4},{6,7},{7,6},{8,9},{9,8},{10,11... | collective-permute-start | bytes 393224 | tf_op jit(solution)/shard_map/ppermute | solution.py:491
  3.4 4.0 %copy-start.6 = (s32[8]{0:T(128)S(1)}, s32[8]{0:T(128)}, u32[]{:S(2)}) copy-start(s32[8]{0:T(128)} %starts_ref.1) | copy-start | bytes 100
  4.4 6.8 %copy-start.3 = (f32[1,64,128]{2,1,0:T(8,128)S(1)}, f32[1,64,128]{2,1,0:T(8,128)}, u32[]{:S(2)}) copy-start(f32[1,64,128]{2,1,0:T(8,128)} %refs_2_.1) | copy-start | bytes 98308
  4.4 6.8 %copy-start.4 = (s32[1,64]{1,0:T(1,128)S(1)}, s32[1,64]{1,0:T(1,128)}, u32[]{:S(2)}) copy-start(s32[1,64]{1,0:T(1,128)} %refs_3_.1) | copy-start | bytes 772
  4.5 8.9 %copy-start = (bf16[768,1024]{1,0:T(8,128)(2,1)S(1)}, bf16[768,1024]{1,0:T(8,128)(2,1)}, u32[]{:S(2)}) copy-start(bf16[768,1024]{1,0:T(8,128)(2,1)} %constant.7.clone.refs_0_) | copy-start | bytes 4718596
  4.5 8.9 %copy-start.1 = (f32[8,2,1024]{2,1,0:T(2,128)S(1)}, f32[8,2,1024]{2,1,0:T(2,128)}, u32[]{:S(2)}) copy-start(f32[8,2,1024]{2,1,0:T(2,128)} %constant.8.clone.refs_1_.roots_ref) | copy-start | bytes 196612
  4.5 6.8 %collective-permute-start.1 = (f32[1,2,128,128]{3,2,1,0:T(8,128)S(1)}, f32[1,2,128,128]{3,2,1,0:T(8,128)S(1)}, u32[]{:S(2)}, u32[]{:S(2)}) collective-permute-start(f32[1,2,128,128]{3,2,1,0:T(8,128)S(1)} %add.6), channel_id=1, source_target_pairs={{0,2},{1,3},{2,0},{3,1},{4,6},{5,7},{6,4},{7,5},{8,10},{9,11},{10,... | collective-permute-start | bytes 393224 | tf_op jit(solution)/shard_map/ppermute | solution.py:491
  8.8 2.5 %collective-permute-start.2 = (f32[1,2,128,128]{3,2,1,0:T(8,128)S(1)}, f32[1,2,128,128]{3,2,1,0:T(8,128)S(1)}, u32[]{:S(2)}, u32[]{:S(2)}) collective-permute-start(f32[1,2,128,128]{3,2,1,0:T(8,128)S(1)} %get-tuple-element.41), channel_id=1, source_target_pairs={{0,1},{1,0},{2,3},{3,2},{4,5},{5,4},{6,7},{7,6},{8,9},{9,8},{10,11... | collective-permute-start | bytes 393224 | tf_op jit(solution)/shard_map/ppermute | solution.py:491
  11.4 5.8 %collective-permute-start.3 = (f32[328,128]{1,0:T(8,128)S(1)}, f32[328,128]{1,0:T(8,128)S(1)}, u32[]{:S(2)}, u32[]{:S(2)}) collective-permute-start(f32[328,128]{1,0:T(8,128)S(1)} %pack.1.refs_4_.refs_5_), channel_id=1, source_target_pairs={{0,8},{8,16},{16,24},{24,28},{28,20},{20,12},{12,4},{4,0},{1,9},{9... | collective-permute-start | bytes 503816 | tf_op jit(solution)/shard_map/ppermute | solution.py:535
  13.2 5.5 %collective-permute-start.5 = (f32[328,128]{1,0:T(8,128)S(1)}, f32[328,128]{1,0:T(8,128)S(1)}, u32[]{:S(2)}, u32[]{:S(2)}) collective-permute-start(f32[328,128]{1,0:T(8,128)S(1)} %pack.1.refs_4_.refs_5_), channel_id=1, source_target_pairs={{8,0},{16,8},{24,16},{28,24},{20,28},{12,20},{4,12},{0,4},{9,1},{1... | collective-permute-start | bytes 503816 | tf_op jit(solution)/shard_map/ppermute | solution.py:536
  17.2 5.4 %collective-permute-start.4 = (f32[328,128]{1,0:T(8,128)S(1)}, f32[328,128]{1,0:T(8,128)S(1)}, u32[]{:S(2)}, u32[]{:S(2)}) collective-permute-start(f32[328,128]{1,0:T(8,128)S(1)} %collective-permute-done.3.refs_5_.refs_6_), channel_id=1, source_target_pairs={{0,8},{8,16},{16,24},{24,28},{28,20},{20,12},{12,4},{4,0},{1,9},{9... | collective-permute-start | bytes 503816 | tf_op jit(solution)/shard_map/ppermute | solution.py:535
  18.7 5.5 %collective-permute-start.7 = (f32[328,128]{1,0:T(8,128)S(1)}, f32[328,128]{1,0:T(8,128)S(1)}, u32[]{:S(2)}, u32[]{:S(2)}) collective-permute-start(f32[328,128]{1,0:T(8,128)S(1)} %collective-permute-done.5.refs_6_.refs_7_), channel_id=1, source_target_pairs={{8,0},{16,8},{24,16},{28,24},{20,28},{12,20},{4,12},{0,4},{9,1},{1... | collective-permute-start | bytes 503816 | tf_op jit(solution)/shard_map/ppermute | solution.py:536
  22.6 5.4 %collective-permute-start.6 = (f32[328,128]{1,0:T(8,128)S(1)}, f32[328,128]{1,0:T(8,128)S(1)}, u32[]{:S(2)}, u32[]{:S(2)}) collective-permute-start(f32[328,128]{1,0:T(8,128)S(1)} %collective-permute-done.4.refs_8_), channel_id=1, source_target_pairs={{0,8},{8,16},{16,24},{24,28},{28,20},{20,12},{12,4},{4,0},{1,9},{9... | collective-permute-start | bytes 503816 | tf_op jit(solution)/shard_map/ppermute | solution.py:535
  24.1 5.4 %collective-permute-start.8 = (f32[328,128]{1,0:T(8,128)S(1)}, f32[328,128]{1,0:T(8,128)S(1)}, u32[]{:S(2)}, u32[]{:S(2)}) collective-permute-start(f32[328,128]{1,0:T(8,128)S(1)} %collective-permute-done.7.refs_9_), channel_id=1, source_target_pairs={{8,0},{16,8},{24,16},{28,24},{20,28},{12,20},{4,12},{0,4},{9,1},{1... | collective-permute-start | bytes 503816 | tf_op jit(solution)/shard_map/ppermute | solution.py:536
  27.9 5.4 %collective-permute-start.9 = (f32[328,128]{1,0:T(8,128)S(1)}, f32[328,128]{1,0:T(8,128)S(1)}, u32[]{:S(2)}, u32[]{:S(2)}) collective-permute-start(f32[328,128]{1,0:T(8,128)S(1)} %collective-permute-done.6.refs_5_), channel_id=1, source_target_pairs={{0,8},{8,16},{16,24},{24,28},{28,20},{20,12},{12,4},{4,0},{1,9},{9... | collective-permute-start | bytes 503816 | tf_op jit(solution)/shard_map/ppermute | solution.py:552
  29.5 3.8 %copy-start.2 = (bf16[1024,512]{1,0:T(8,128)(2,1)S(1)}, bf16[1024,512]{1,0:T(8,128)(2,1)}, u32[]{:S(2)}) copy-start(bf16[1024,512]{1,0:T(8,128)(2,1)} %constant.6.clone.refs_4_) | copy-start | bytes 3145732
  35.0 5.0 %collective-permute-start.10 = (f32[2,128,128]{2,1,0:T(8,128)S(1)}, f32[2,128,128]{2,1,0:T(8,128)S(1)}, u32[]{:S(2)}, u32[]{:S(2)}) collective-permute-start(f32[2,128,128]{2,1,0:T(8,128)S(1)} %get-tuple-element.53.refs_0_), channel_id=1, source_target_pairs={{0,2},{1,3},{2,0},{3,1},{4,6},{5,7},{6,4},{7,5},{8,10},{9,11},{10,... | collective-permute-start | bytes 393224 | tf_op jit(solution)/shard_map/ppermute | solution.py:491
  37.2 1.4 %collective-permute-start.11 = (f32[2,128,128]{2,1,0:T(8,128)S(1)}, f32[2,128,128]{2,1,0:T(8,128)S(1)}, u32[]{:S(2)}, u32[]{:S(2)}) collective-permute-start(f32[2,128,128]{2,1,0:T(8,128)S(1)} %get-tuple-element.53.refs_0_), channel_id=1, source_target_pairs={{0,1},{1,0},{2,3},{3,2},{4,5},{5,4},{6,7},{7,6},{8,9},{9,8},{10,11... | collective-permute-start | bytes 393224 | tf_op jit(solution)/shard_map/ppermute | solution.py:491
  40.1 1.3 %collective-permute-start.12 = (f32[2,128,128]{2,1,0:T(8,128)S(1)}, f32[2,128,128]{2,1,0:T(8,128)S(1)}, u32[]{:S(2)}, u32[]{:S(2)}) collective-permute-start(f32[2,128,128]{2,1,0:T(8,128)S(1)} %collective-permute-done.10.refs_0_), channel_id=1, source_target_pairs={{0,1},{1,0},{2,3},{3,2},{4,5},{5,4},{6,7},{7,6},{8,9},{9,8},{10,11... | collective-permute-start | bytes 393224 | tf_op jit(solution)/shard_map/ppermute | solution.py:491
